TPU v7x, 32 devices: a whole 2x2x4 slice. The times are simulated.
32 devices in a mesh: seq: 32 (over z, y, x, core).
Axes of the slice: x: 2, y: 2, z: 4, core: 2. Of those that a mesh axis runs over, the one named last changes fastest.
Arguments:
- tokens: bfloat16 [4096, 1024], P('seq'), may hold values from -6 to 6
- scene_lengths: int32 [8], replicated, may hold values from 1 to 1024, 4096 in all
- cotangent: bfloat16 [4096, 1024], P('seq'), may hold values from -6 to 6
- attend_weight: float32 [1024, 3072], P('seq'), may hold values from -0.09375 to 0.09375
- output_weight: float32 [1024, 1024], P('seq'), may hold values from -2 to 2
- expand_weight: float32 [1024, 4096], P('seq'), may hold values from -0.1875 to 0.1875
- reduce_weight: float32 [4096, 1024], P('seq'), may hold values from -0.09375 to 0.09375
- vector_params: float32 [9, 1024], P(None, 'seq'), may hold values from -1.2 to 7.2, as said below
- attend_momentum: float32 [1024, 3072], P('seq'), may hold values from -0.0048828125 to 0.0048828125
- output_momentum: float32 [1024, 1024], P('seq'), may hold values from -0.0048828125 to 0.0048828125
- expand_momentum: float32 [1024, 4096], P('seq'), may hold values from -0.0048828125 to 0.0048828125
- reduce_momentum: float32 [4096, 1024], P('seq'), may hold values from -0.0048828125 to 0.0048828125
- vector_momentum: float32 [9, 1024], P(None, 'seq'), may hold values from -0.0048828125 to 0.0048828125
- attend_average: float32 [1024, 3072], P('seq'), may hold values from -0.09375 to 0.09375
- output_average: float32 [1024, 1024], P('seq'), may hold values from -2 to 2
- expand_average: float32 [1024, 4096], P('seq'), may hold values from -0.1875 to 0.1875
- reduce_average: float32 [4096, 1024], P('seq'), may hold values from -0.09375 to 0.09375
- vector_average: float32 [9, 1024], P(None, 'seq'), may hold values from 0.1 to 1.9
Outputs:
- block_output: bfloat16 [4096, 1024], P('seq')
- input_gradient: bfloat16 [4096, 1024], P('seq')
- gradient_norm: float32 [], replicated
- attend_velocity: float32 [1024, 3072], P('seq')
- attend_updated: float32 [1024, 3072], P('seq')
- attend_smoothed: float32 [1024, 3072], P('seq')
- output_velocity: float32 [1024, 1024], P('seq')
- output_updated: float32 [1024, 1024], P('seq')
- output_smoothed: float32 [1024, 1024], P('seq')
- expand_velocity: float32 [1024, 4096], P('seq')
- expand_updated: float32 [1024, 4096], P('seq')
- expand_smoothed: float32 [1024, 4096], P('seq')
- reduce_velocity: float32 [4096, 1024], P('seq')
- reduce_updated: float32 [4096, 1024], P('seq')
- reduce_smoothed: float32 [4096, 1024], P('seq')
- vector_velocity: float32 [9, 1024], P(None, 'seq')
- vector_updated: float32 [9, 1024], P(None, 'seq')
- vector_smoothed: float32 [9, 1024], P(None, 'seq')
Inputs may be any that keep to these rules, and one draw needn't show every extreme that they name: `scene_lengths`: the lengths sum to 4096; no scene holds more than 1024 tokens. `vector_params`: rows 0 and 2 are positive.
All inputs are finite; a program needn't handle non-finite values.
Results may differ from a plain program's by a relative error of at most 0.015.
The roundings to bfloat16 on the way count: a program that leaves them out, or rounds other values in their place, can miss the bound.
Values may be sent and summed in bfloat16 or wider, within the bound.
No kernel may reach another device: no remote copies, remote signals or barrier semaphores. Data moves between devices by JAX's collectives and lax.ppermute only.
A program may use at most 256 MiB of HBM per device.

v0:
```python
import jax
import jax.numpy as jnp
from jax import lax
from jax.sharding import PartitionSpec as P

HEADS = 16
SPAN = 8
STEP = 10


EPSILON = 1e-05
MOMENTUM = 0.9
LEARNING_RATES = (60.0, 480.0, 60.0, 60.0, 600.0)
WEIGHT_DECAY = 0.0001
CLIP_NORM = 1.0
MASK_FLOOR = -1e30
group_heads = 4


def shifted(block, axis, distance):
    devices = range(lax.axis_size(axis))
    route = [(i - distance, i) for i in devices if i - distance in devices]
    return lax.ppermute(block, axis, route)


def layer_norm(values, scales, shifts):
    centre = values - jnp.mean(values, axis=-1, keepdims=True)
    spread = jnp.mean(centre * centre, axis=-1, keepdims=True)
    return centre * lax.rsqrt(spread + EPSILON) * scales + shifts


def gelu_exact(values):
    return jax.nn.gelu(values, approximate=False)


def scene_labels(finish, positions):
    return jnp.sum((positions[:, None] >= finish[None, :]).astype(jnp.int32), axis=1)


def masked_scores(queries, keyset, allowed):
    scores = jnp.einsum(
        "qhd,khd->hqk", queries, keyset, preferred_element_type=jnp.float32
    ) * queries.shape[2] ** (-0.5)
    return jnp.where(allowed[None], scores, MASK_FLOOR)


def group_columns(array, start, extent, heads_here, head_size):
    return lax.dynamic_slice_in_dim(array, start, extent, 1).reshape(
        array.shape[0], heads_here, head_size
    )


def on_device(
    tokens,
    scene_lengths,
    cotangent,
    attend_weight,
    output_weight,
    expand_weight,
    reduce_weight,
    vector_params,
    attend_momentum,
    output_momentum,
    expand_momentum,
    reduce_momentum,
    vector_momentum,
    attend_average,
    output_average,
    expand_average,
    reduce_average,
    vector_average,
):
    attend, output, expand, shrink, vectors = (
        lax.all_gather(attend_weight.astype(jnp.bfloat16), "seq", axis=0, tiled=True),
        lax.all_gather(output_weight.astype(jnp.bfloat16), "seq", axis=0, tiled=True),
        lax.all_gather(expand_weight.astype(jnp.bfloat16), "seq", axis=0, tiled=True),
        lax.all_gather(reduce_weight.astype(jnp.bfloat16), "seq", axis=0, tiled=True),
        lax.all_gather(vector_params.astype(jnp.bfloat16), "seq", axis=1, tiled=True),
    )
    vector_full = vectors.astype(jnp.float32)
    number, columns = tokens.shape
    head_size = columns // HEADS
    scale_factor = head_size ** (-0.5)
    group_width = group_heads * head_size
    group_count = HEADS // group_heads
    total_tokens = number * lax.axis_size("seq")
    device_index = lax.axis_index("seq")
    window = (2 * SPAN + 1) * number
    finish = jnp.cumsum(scene_lengths)
    query_pos = device_index * number + jnp.arange(number, dtype=jnp.int32)
    key_pos = (device_index - SPAN) * number + jnp.arange(window, dtype=jnp.int32)
    inside = (key_pos >= 0) & (key_pos < total_tokens)
    key_label = jnp.where(inside, scene_labels(finish, key_pos), -1)
    allowed = scene_labels(finish, query_pos)[:, None] == key_label[None, :]
    rows_in = tokens.astype(jnp.float32)
    first, first_back = jax.vjp(layer_norm, rows_in, vector_full[0], vector_full[1])
    first_low = first.astype(jnp.bfloat16)
    joined = jnp.dot(first_low, attend, preferred_element_type=jnp.float32).astype(jnp.bfloat16)
    query_all = joined[:, :columns]
    pairs_local = joined[:, columns:]
    window_blocks = []
    for offset in range(-SPAN, SPAN + 1):
        if offset == 0:
            window_blocks.append(pairs_local)
        else:
            window_blocks.append(shifted(pairs_local, "seq", -offset))
    pair_window = jnp.concatenate(window_blocks, axis=0)

    def group_inputs(group_index):
        start = group_index * group_width
        queries = group_columns(query_all, start, group_width, group_heads, head_size)
        keyset = group_columns(pair_window, start, group_width, group_heads, head_size)
        valueset = group_columns(pair_window, columns + start, group_width, group_heads, head_size)
        return (queries, keyset, valueset)

    def attend_group(group_index):
        queries, keyset, valueset = group_inputs(group_index)
        masked = masked_scores(queries, keyset, allowed)
        row_peak = jnp.max(masked, axis=-1, keepdims=True)
        raised = jnp.exp(masked - row_peak)
        totals = jnp.sum(raised, axis=-1, keepdims=True)
        log_total = row_peak + jnp.log(totals)
        shares_low = (raised / totals).astype(jnp.bfloat16)
        mixed = jnp.einsum("hqk,khd->qhd", shares_low, valueset, preferred_element_type=jnp.float32)
        return (mixed.reshape(number, group_width), log_total)

    group_ids = jnp.arange(group_count, dtype=jnp.int32)
    mixed_groups, log_totals = lax.map(attend_group, group_ids)
    mixed_heads = jnp.moveaxis(mixed_groups, 0, 1).reshape(number, columns).astype(jnp.bfloat16)
    second = rows_in + jnp.dot(mixed_heads, output, preferred_element_type=jnp.float32)
    normed, normed_back = jax.vjp(layer_norm, second, vector_full[2], vector_full[3])
    normed_low = normed.astype(jnp.bfloat16)
    upper_part = jnp.dot(normed_low, expand, preferred_element_type=jnp.float32) + vector_full[
        5:
    ].reshape(-1)
    active, active_back = jax.vjp(gelu_exact, upper_part)
    active_low = active.astype(jnp.bfloat16)
    block_output = (
        second + jnp.dot(active_low, shrink, preferred_element_type=jnp.float32) + vector_full[4]
    ).astype(jnp.bfloat16)
    sliced = active_low
    shrink_grad = jnp.einsum("tf,td->fd", sliced, cotangent, preferred_element_type=jnp.float32)
    active_grad = jnp.einsum("td,fd->tf", cotangent, shrink, preferred_element_type=jnp.float32)
    upper_grad = active_back(active_grad)[0].astype(jnp.bfloat16)
    sliced = normed_low
    expand_grad = jnp.einsum("td,tf->df", sliced, upper_grad, preferred_element_type=jnp.float32)
    normed_grad = jnp.einsum("tf,df->td", upper_grad, expand, preferred_element_type=jnp.float32)
    second_part, gain_two, shift_two = normed_back(normed_grad)
    second_grad = cotangent.astype(jnp.float32) + second_part
    branch_grad = second_grad.astype(jnp.bfloat16)
    sliced = mixed_heads
    output_grad = jnp.einsum("ti,to->io", sliced, branch_grad, preferred_element_type=jnp.float32)
    mixed_grad = jnp.einsum(
        "to,io->ti", branch_grad, output, preferred_element_type=jnp.float32
    ).astype(jnp.bfloat16)

    def attend_back(inputs):
        group_index, log_total = inputs
        queries, keyset, valueset = group_inputs(group_index)
        grad_group = group_columns(
            mixed_grad, group_index * group_width, group_width, group_heads, head_size
        )
        shares = jnp.exp(masked_scores(queries, keyset, allowed) - log_total)
        shares_again = shares.astype(jnp.bfloat16)
        value_grad = jnp.einsum(
            "hqk,qhd->khd", shares_again, grad_group, preferred_element_type=jnp.float32
        )
        share_grad = jnp.einsum(
            "qhd,khd->hqk", grad_group, valueset, preferred_element_type=jnp.float32
        )
        centred = jnp.sum(shares * share_grad, axis=-1, keepdims=True)
        score_grad = (shares * (share_grad - centred)).astype(jnp.bfloat16)
        query_grad = (
            jnp.einsum("hqk,khd->qhd", score_grad, keyset, preferred_element_type=jnp.float32)
            * scale_factor
        )
        key_grad = (
            jnp.einsum("hqk,qhd->khd", score_grad, queries, preferred_element_type=jnp.float32)
            * scale_factor
        )
        return (
            query_grad.reshape(number, group_width),
            key_grad.reshape(window, group_width),
            value_grad.reshape(window, group_width),
        )

    query_groups, key_groups, value_groups = lax.map(attend_back, (group_ids, log_totals))
    query_grad = jnp.moveaxis(query_groups, 0, 1).reshape(number, columns)
    key_grad = jnp.moveaxis(key_groups, 0, 1).reshape(window, columns)
    value_grad = jnp.moveaxis(value_groups, 0, 1).reshape(window, columns)
    pair_grad = jnp.concatenate([key_grad, value_grad], axis=1)
    returned = lax.slice_in_dim(pair_grad, SPAN * number, (SPAN + 1) * number, axis=0)
    for offset in range(-SPAN, SPAN + 1):
        if offset != 0:
            grad_part = lax.slice_in_dim(
                pair_grad, (offset + SPAN) * number, (offset + SPAN + 1) * number, axis=0
            )
            returned = returned + shifted(grad_part.astype(jnp.bfloat16), "seq", offset).astype(
                grad_part.dtype
            )
    joined_grad = jnp.concatenate([query_grad, returned], axis=1).astype(jnp.bfloat16)
    first_grad = jnp.einsum("tj,ij->ti", joined_grad, attend, preferred_element_type=jnp.float32)
    rows_part, gain_one, shift_one = first_back(first_grad)
    input_gradient = (second_grad + rows_part).astype(jnp.bfloat16)
    vector_grad_full = jnp.concatenate(
        [
            jnp.stack(
                [
                    gain_one,
                    shift_one,
                    gain_two,
                    shift_two,
                    jnp.sum(cotangent.astype(jnp.float32), axis=0),
                ]
            ),
            jnp.sum(upper_grad.astype(jnp.float32), axis=0).reshape(-1, columns),
        ],
        axis=0,
    )
    sliced = first_low
    attend_grad, output_grad, expand_grad, shrink_grad, vector_grad = (
        lax.psum_scatter(
            jnp.einsum("ti,tj->ij", sliced, joined_grad, preferred_element_type=jnp.float32),
            "seq",
            scatter_dimension=0,
            tiled=True,
        ),
        lax.psum_scatter(output_grad, "seq", scatter_dimension=0, tiled=True),
        lax.psum_scatter(expand_grad, "seq", scatter_dimension=0, tiled=True),
        lax.psum_scatter(shrink_grad, "seq", scatter_dimension=0, tiled=True),
        lax.psum_scatter(vector_grad_full, "seq", scatter_dimension=1, tiled=True),
    )
    groups = (
        (attend_weight, attend_momentum, attend_average, attend_grad),
        (output_weight, output_momentum, output_average, output_grad),
        (expand_weight, expand_momentum, expand_average, expand_grad),
        (reduce_weight, reduce_momentum, reduce_average, shrink_grad),
        (vector_params, vector_momentum, vector_average, vector_grad),
    )
    local_square = jnp.zeros((), jnp.float32)
    for weight_now, moment_now, average_now, gradient_now in groups:
        local_square = local_square + jnp.sum(gradient_now * gradient_now)
    norm_square = lax.psum(local_square, "seq")
    gradient_norm = jnp.sqrt(norm_square)
    factor = jnp.minimum(1.0, CLIP_NORM / (gradient_norm + 1e-06))
    smooth_rate = min(0.999, (1.0 + STEP) / (10.0 + STEP))
    updates = []
    for position, (weight_now, moment_now, average_now, gradient_now) in enumerate(groups):
        rate_now = LEARNING_RATES[position]
        clipped = factor * gradient_now + WEIGHT_DECAY * weight_now
        velocity = MOMENTUM * moment_now + clipped
        updated = weight_now - rate_now * (clipped + MOMENTUM * velocity)
        smoothed = smooth_rate * average_now + (1.0 - smooth_rate) * updated
        updates.append((velocity, updated, smoothed))
    return (
        block_output,
        input_gradient,
        gradient_norm,
        updates[0][0],
        updates[0][1],
        updates[0][2],
        updates[1][0],
        updates[1][1],
        updates[1][2],
        updates[2][0],
        updates[2][1],
        updates[2][2],
        updates[3][0],
        updates[3][1],
        updates[3][2],
        updates[4][0],
        updates[4][1],
        updates[4][2],
    )


def solution(mesh):
    return jax.shard_map(
        on_device,
        mesh=mesh,
        in_specs=(
            P("seq", None),
            P(),
            P("seq", None),
            P("seq", None),
            P("seq", None),
            P("seq", None),
            P("seq", None),
            P(None, "seq"),
            P("seq", None),
            P("seq", None),
            P("seq", None),
            P("seq", None),
            P(None, "seq"),
            P("seq", None),
            P("seq", None),
            P("seq", None),
            P("seq", None),
            P(None, "seq"),
        ),
        out_specs=(
            P("seq", None),
            P("seq", None),
            P(),
            P("seq", None),
            P("seq", None),
            P("seq", None),
            P("seq", None),
            P("seq", None),
            P("seq", None),
            P("seq", None),
            P("seq", None),
            P("seq", None),
            P("seq", None),
            P("seq", None),
            P("seq", None),
            P(None, "seq"),
            P(None, "seq"),
            P(None, "seq"),
        ),
        check_vma=False,
    )
```

profile of v0, /device:TPU:0, one launch (start us, length us, event | category | flops | bytes accessed | tf_op | source)
XLA Modules:
  0.0 1455.5 jit_solution(269246412776002761)
XLA Ops:
  14.3 43.9 %all-gather = bf16[32,32,9]{1,2,0:T(8,128)(2,1)S(1)} all-gather(bf16[1,32,9]{1,2,0:T(8,128)(2,1)S(1)} %convert_bitcast_fusion), channel_id=1, replica_groups=mesh['seq'=32] {'seq'}, dimensions={0}, use_global_device_ids=true | all-gather | bytes 19008 | tf_op jit(solution)/shard_map/all_gather | solution.py:78
  59.3 24.7 %all-gather.6.cloned.1.call-done = bf16[1024,3072]{1,0:T(8,128)(2,1)} async-done(((bf16[32,3072]{1,0:T(8,128)(2,1)}), bf16[1024,3072]{1,0:T(8,128)(2,1)}) %all-gather.6.cloned.1.call-update) | async-done | bytes 6291472 | tf_op jit(solution)/shard_map/all_gather | solution.py:74
  84.0 3.9 convolution_convert_fusion
  87.9 4.2 collective-permute-start
  92.1 3.8 collective-permute-start.1
  95.9 3.7 collective-permute-start.2
  108.4 11.3 collective-permute-start.4
  122.4 11.5 collective-permute-start.5
  135.8 4.0 collective-permute-start.6
  140.6 3.3 collective-permute-start.7
  146.9 8.1 collective-permute-done.6
  160.2 10.1 collective-permute-done.8
  174.5 13.6 collective-permute-done.10
  190.4 13.5 collective-permute-done.11
  204.8 35.1 %collective-permute-done.12 = bf16[128,2048]{1,0:T(8,128)(2,1)S(1)} collective-permute-done((bf16[128,2048]{1,0:T(8,128)(2,1)S(1)}, bf16[128,2048]{1,0:T(8,128)(2,1)S(1)}, u32[]{:S(2)}, u32[]{:S(2)}) %collective-permute-start.12) | collective-permute-done | bytes 524320 | tf_op jit(solution)/shard_map/ppermute | solution.py:23
  243.3 11.8 copy.60
  255.2 25.0 %while.32 = (s32[]{:T(128)}, bf16[4,128,256]{1,2,0:T(8,128)(2,1)S(1)}, f32[4,4,128,1]{2,1,3,0:T(4,128)S(1)}, s32[4]{0:T(128)S(1)}, bf16[2176,2048]{0,1:T(8,128)(...) while((s32[]{:T(128)}, ...), condition=%wide.region_8.9_spmd.clone, body=%wide.region_5.8_spmd.clone.sunk | while | flops 294403584 | bytes 21030164 | solution.py:128
  283.5 4.8 convolution_add_fusion
  288.2 77.6 %all-gather.12.cloned.1.call-done = bf16[4096,1024]{1,0:T(8,128)(2,1)} async-done(((bf16[128,1024]{1,0:T(8,128)(2,1)}), bf16[4096,1024]{1,0:T(8,128)(2,1)}) %all-gather.12.cloned.1.call-update) | async-done | bytes 8388624 | tf_op jit(solution)/shard_map/all_gather | solution.py:77
  365.9 10.5 convert_reduce_fusion
  376.4 3.0 multiply_reduce_fusion.1
  382.0 43.1 %while.33 = (s32[]{:T(128)}, bf16[4,128,256]{1,2,0:T(8,128)(2,1)S(1)}, f32[4,2176,256]{1,2,0:T(8,128)}, f32[4,2176,256]{1,2,0:T(8,128)}, s32[4]{0:T(128)S(1)}, /...) while((s32[]{:T(128)}, ...), condition=%wide.region_15.16_spmd.clone, body=%wide.region_13.15_spmd.clone.sunk | while | flops 723959296 | bytes 56020276 | solution.py:187
  425.0 7.7 fusion.12
  436.6 4.6 collective-permute-start.31
  441.2 2.7 collective-permute-start.30
  443.9 4.3 collective-permute-start.29
  448.2 3.0 collective-permute-start.28
  451.3 3.4 collective-permute-start.27
  456.6 11.5 collective-permute-start.25
  470.8 24.0 %collective-permute-done.27 = bf16[128,2048]{0,1:T(8,128)(2,1)S(1)} collective-permute-done((bf16[128,2048]{0,1:T(8,128)(2,1)S(1)}, bf16[128,2048]{0,1:T(8,128)(2,1)S(1)}, u32[]{:S(2)}, u32[]{:S(2)}) %collective-permute-start.27) | collective-permute-done | bytes 524320 | tf_op jit(solution)/shard_map/ppermute | solution.py:23
  501.3 9.2 collective-permute-done.22
  511.9 10.2 collective-permute-done.20
  522.1 6.0 collective-permute-done.19
  528.1 19.3 %collective-permute-done.18 = bf16[128,2048]{0,1:T(8,128)(2,1)} collective-permute-done((bf16[128,2048]{0,1:T(8,128)(2,1)}, bf16[128,2048]{0,1:T(8,128)(2,1)}, u32[]{:S(2)}, u32[]{:S(2)}) %collective-permute-start.18) | collective-permute-done | bytes 524320 | tf_op jit(solution)/shard_map/ppermute | solution.py:23
  547.4 4.1 collective-permute-done.17
  551.5 4.7 add_convert_fusion.1
  556.3 5.1 fusion.45
  564.3 2.7 fusion.53
  567.9 6.4 fusion.34
  575.6 8.2 fusion.44
  586.3 8.1 fusion.54
  594.5 124.2 %reduce-scatter.16.cloned.1.call-done = f32[32,9]{1,0:T(8,128)} async-done(((f32[1024,9]{1,0:T(8,128)}), f32[32,9]{1,0:T(8,128)}) %reduce-scatter.16.cloned.1.call-update) | async-done | bytes 1168
  720.1 137.5 %reduce-scatter.10.cloned.1.call-done = f32[32,1024]{1,0:T(8,128)} async-done(((f32[1024,1024]{1,0:T(8,128)}), f32[32,1024]{1,0:T(8,128)}) %reduce-scatter.10.cloned.1.call-update) | async-done | bytes 131088 | tf_op jit(solution)/shard_map/reduce_scatter | solution.py:228
  859.2 156.8 %reduce-scatter.8.cloned.1.call-done = f32[32,3072]{1,0:T(8,128)} async-done(((f32[1024,3072]{1,0:T(8,128)}), f32[32,3072]{1,0:T(8,128)}) %reduce-scatter.8.cloned.1.call-update) | async-done | bytes 393232 | tf_op jit(solution)/shard_map/reduce_scatter | solution.py:222
  1019.0 181.3 %reduce-scatter.12.cloned.1.call-done = f32[32,4096]{1,0:T(8,128)} async-done(((f32[1024,4096]{1,0:T(8,128)}), f32[32,4096]{1,0:T(8,128)}) %reduce-scatter.12.cloned.1.call-update) | async-done | bytes 524304 | tf_op jit(solution)/shard_map/reduce_scatter | solution.py:229
  1202.8 184.4 %reduce-scatter.14.cloned.1.call-done = f32[128,1024]{1,0:T(8,128)} async-done(((f32[4096,1024]{1,0:T(8,128)}), f32[128,1024]{1,0:T(8,128)}) %reduce-scatter.14.cloned.1.call-update) | async-done | bytes 524304 | tf_op jit(solution)/shard_map/reduce_scatter | solution.py:230
  1390.3 5.5 fusion.20
  1395.7 42.2 %psum.7 = f32[]{:T(128)} all-reduce(f32[]{:T(128)S(6)} %add.350), channel_id=1, replica_groups=mesh['seq'=32] {'seq'}, use_global_device_ids=true, to_apply=%region_34.35 | all-reduce | flops 1 | bytes 8 | tf_op jit(solution)/shard_map/psum | solution.py:243
  (332 shorter events, 149.4 us)
Async XLA Ops:
  7.2 76.7 %all-gather.6.cloned.1.call-start = ((), (), s32[]{:S(2)}) async-start(), calls=%async_computation.5 | async-start | bytes 6488064 | tf_op jit(solution)/shard_map/all_gather | solution.py:74
  9.1 271.2 %all-gather.8.cloned.1.call-start = ((), (), s32[]{:S(2)}) async-start(), calls=%async_computation.6 | async-start | bytes 2162688 | tf_op jit(solution)/shard_map/all_gather | solution.py:75
  10.7 272.8 %all-gather.10.cloned.1.call-start = ((), (), s32[]{:S(2)}) async-start(), calls=%async_computation.7 | async-start | bytes 8650752 | tf_op jit(solution)/shard_map/all_gather | solution.py:76
  12.5 353.3 %all-gather.12.cloned.1.call-start = ((), (), s32[]{:S(2)}) async-start(), calls=%async_computation.8 | async-start | bytes 8650752 | tf_op jit(solution)/shard_map/all_gather | solution.py:77
  13.3 705.4 %reduce-scatter.16.cloned.1.call-start = ((), (), s32[]{:S(2)}) async-start(), calls=%async_computation.13 | async-start | bytes 540672
  13.5 74.3 %copy-start.42 = (f32[128]{0:T(128)}, f32[128]{0:T(128)S(1)}, u32[]{:S(2)}) copy-start(f32[128]{0:T(128)S(1)} %broadcast_multiply_fusion.1) | copy-start | bytes 1540
  14.3 69.7 %copy-start.44 = (f32[128]{0:T(128)}, f32[128]{0:T(128)S(1)}, u32[]{:S(2)}) copy-start(f32[128]{0:T(128)S(1)} %fusion.37) | copy-start | bytes 1540
  87.9 17.1 %collective-permute-start = (bf16[128,2048]{1,0:T(8,128)(2,1)S(1)}, bf16[128,2048]{1,0:T(8,128)(2,1)}, u32[]{:S(2)}, u32[]{:S(2)}) collective-permute-start(bf16[128,2048]{1,0:T(8,128)(2,1)S(1)} %slice.118), channel_id=1, source_target_pairs={{0,8},{1,9},{2,10},{3,11},{4,12},{5,13},{6,14},{7,15},{8,16},{9,17... | collective-permute-start | bytes 1572872 | tf_op jit(solution)/shard_map/ppermute | solution.py:23
  92.1 16.3 %collective-permute-start.1 = (bf16[128,2048]{1,0:T(8,128)(2,1)S(1)}, bf16[128,2048]{1,0:T(8,128)(2,1)}, u32[]{:S(2)}, u32[]{:S(2)}) collective-permute-start(bf16[128,2048]{1,0:T(8,128)(2,1)S(1)} %slice.118), channel_id=1, source_target_pairs={{0,7},{1,8},{2,9},{3,10},{4,11},{5,12},{6,13},{7,14},{8,15},{9,16}... | collective-permute-start | bytes 1572872 | tf_op jit(solution)/shard_map/ppermute | solution.py:23
  95.9 26.5 %collective-permute-start.2 = (bf16[128,2048]{1,0:T(8,128)(2,1)S(1)}, bf16[128,2048]{1,0:T(8,128)(2,1)}, u32[]{:S(2)}, u32[]{:S(2)}) collective-permute-start(bf16[128,2048]{1,0:T(8,128)(2,1)S(1)} %slice.118), channel_id=1, source_target_pairs={{0,6},{1,7},{2,8},{3,9},{4,10},{5,11},{6,12},{7,13},{8,14},{9,15},... | collective-permute-start | bytes 1572872 | tf_op jit(solution)/shard_map/ppermute | solution.py:23
  99.7 142.8 %collective-permute-start.15 = (bf16[128,2048]{1,0:T(8,128)(2,1)S(1)}, bf16[128,2048]{1,0:T(8,128)(2,1)S(1)}, u32[]{:S(2)}, u32[]{:S(2)}) collective-permute-start(bf16[128,2048]{1,0:T(8,128)(2,1)S(1)} %slice.118), channel_id=1, source_target_pairs={{8,0},{9,1},{10,2},{11,3},{12,4},{13,5},{14,6},{15,7},{16,8},{17,9... | collective-permute-start | bytes 1572872 | tf_op jit(solution)/shard_map/ppermute | solution.py:23
  101.0 140.6 %collective-permute-start.14 = (bf16[128,2048]{1,0:T(8,128)(2,1)S(1)}, bf16[128,2048]{1,0:T(8,128)(2,1)S(1)}, u32[]{:S(2)}, u32[]{:S(2)}) collective-permute-start(bf16[128,2048]{1,0:T(8,128)(2,1)S(1)} %slice.118), channel_id=1, source_target_pairs={{7,0},{8,1},{9,2},{10,3},{11,4},{12,5},{13,6},{14,7},{15,8},{16,9}... | collective-permute-start | bytes 1572872 | tf_op jit(solution)/shard_map/ppermute | solution.py:23
  105.0 30.8 %collective-permute-start.3 = (bf16[128,2048]{1,0:T(8,128)(2,1)S(1)}, bf16[128,2048]{1,0:T(8,128)(2,1)S(1)}, u32[]{:S(2)}, u32[]{:S(2)}) collective-permute-start(bf16[128,2048]{1,0:T(8,128)(2,1)S(1)} %slice.118), channel_id=1, source_target_pairs={{0,5},{1,6},{2,7},{3,8},{4,9},{5,10},{6,11},{7,12},{8,13},{9,14},{... | collective-permute-start | bytes 1572872 | tf_op jit(solution)/shard_map/ppermute | solution.py:23
  108.4 32.2 %collective-permute-start.4 = (bf16[128,2048]{1,0:T(8,128)(2,1)S(1)}, bf16[128,2048]{1,0:T(8,128)(2,1)S(1)}, u32[]{:S(2)}, u32[]{:S(2)}) collective-permute-start(bf16[128,2048]{1,0:T(8,128)(2,1)S(1)} %slice.118), channel_id=1, source_target_pairs={{0,4},{1,5},{2,6},{3,7},{4,8},{5,9},{6,10},{7,11},{8,12},{9,13},{1... | collective-permute-start | bytes 1572872 | tf_op jit(solution)/shard_map/ppermute | solution.py:23
  122.4 22.4 %collective-permute-start.5 = (bf16[128,2048]{1,0:T(8,128)(2,1)S(1)}, bf16[128,2048]{1,0:T(8,128)(2,1)S(1)}, u32[]{:S(2)}, u32[]{:S(2)}) collective-permute-start(bf16[128,2048]{1,0:T(8,128)(2,1)S(1)} %slice.118), channel_id=1, source_target_pairs={{0,3},{1,4},{2,5},{3,6},{4,7},{5,8},{6,9},{7,10},{8,11},{9,12},{10... | collective-permute-start | bytes 1572872 | tf_op jit(solution)/shard_map/ppermute | solution.py:23
  135.8 19.3 %collective-permute-start.6 = (bf16[128,2048]{1,0:T(8,128)(2,1)S(1)}, bf16[128,2048]{1,0:T(8,128)(2,1)S(1)}, u32[]{:S(2)}, u32[]{:S(2)}) collective-permute-start(bf16[128,2048]{1,0:T(8,128)(2,1)S(1)} %slice.118), channel_id=1, source_target_pairs={{0,2},{1,3},{2,4},{3,5},{4,6},{5,7},{6,8},{7,9},{8,10},{9,11},{10,... | collective-permute-start | bytes 1572872 | tf_op jit(solution)/shard_map/ppermute | solution.py:23
  140.6 16.6 %collective-permute-start.7 = (bf16[128,2048]{1,0:T(8,128)(2,1)S(1)}, bf16[128,2048]{1,0:T(8,128)(2,1)S(1)}, u32[]{:S(2)}, u32[]{:S(2)}) collective-permute-start(bf16[128,2048]{1,0:T(8,128)(2,1)S(1)} %slice.118), channel_id=1, source_target_pairs={{0,1},{1,2},{2,3},{3,4},{4,5},{5,6},{6,7},{7,8},{8,9},{9,10},{10,1... | collective-permute-start | bytes 1572872 | tf_op jit(solution)/shard_map/ppermute | solution.py:23
  144.8 43.3 %collective-permute-start.10 = (bf16[128,2048]{1,0:T(8,128)(2,1)S(1)}, bf16[128,2048]{1,0:T(8,128)(2,1)S(1)}, u32[]{:S(2)}, u32[]{:S(2)}) collective-permute-start(bf16[128,2048]{1,0:T(8,128)(2,1)S(1)} %slice.118), channel_id=1, source_target_pairs={{3,0},{4,1},{5,2},{6,3},{7,4},{8,5},{9,6},{10,7},{11,8},{12,9},{13... | collective-permute-start | bytes 1572872 | tf_op jit(solution)/shard_map/ppermute | solution.py:23
  155.1 17.3 %collective-permute-start.9 = (bf16[128,2048]{1,0:T(8,128)(2,1)S(1)}, bf16[128,2048]{1,0:T(8,128)(2,1)S(1)}, u32[]{:S(2)}, u32[]{:S(2)}) collective-permute-start(bf16[128,2048]{1,0:T(8,128)(2,1)S(1)} %slice.118), channel_id=1, source_target_pairs={{2,0},{3,1},{4,2},{5,3},{6,4},{7,5},{8,6},{9,7},{10,8},{11,9},{12,... | collective-permute-start | bytes 1572872 | tf_op jit(solution)/shard_map/ppermute | solution.py:23
  157.2 13.1 collective-permute-start.8
  170.3 33.7 %collective-permute-start.11 = (bf16[128,2048]{1,0:T(8,128)(2,1)S(1)}, bf16[128,2048]{1,0:T(8,128)(2,1)S(1)}, u32[]{:S(2)}, u32[]{:S(2)}) collective-permute-start(bf16[128,2048]{1,0:T(8,128)(2,1)S(1)} %slice.118), channel_id=1, source_target_pairs={{4,0},{5,1},{6,2},{7,3},{8,4},{9,5},{10,6},{11,7},{12,8},{13,9},{1... | collective-permute-start | bytes 1572872 | tf_op jit(solution)/shard_map/ppermute | solution.py:23
  172.4 67.5 %collective-permute-start.12 = (bf16[128,2048]{1,0:T(8,128)(2,1)S(1)}, bf16[128,2048]{1,0:T(8,128)(2,1)S(1)}, u32[]{:S(2)}, u32[]{:S(2)}) collective-permute-start(bf16[128,2048]{1,0:T(8,128)(2,1)S(1)} %slice.118), channel_id=1, source_target_pairs={{5,0},{6,1},{7,2},{8,3},{9,4},{10,5},{11,6},{12,7},{13,8},{14,9},{... | collective-permute-start | bytes 1572872 | tf_op jit(solution)/shard_map/ppermute | solution.py:23
  188.1 52.7 %collective-permute-start.13 = (bf16[128,2048]{1,0:T(8,128)(2,1)S(1)}, bf16[128,2048]{1,0:T(8,128)(2,1)S(1)}, u32[]{:S(2)}, u32[]{:S(2)}) collective-permute-start(bf16[128,2048]{1,0:T(8,128)(2,1)S(1)} %slice.118), channel_id=1, source_target_pairs={{6,0},{7,1},{8,2},{9,3},{10,4},{11,5},{12,6},{13,7},{14,8},{15,9},... | collective-permute-start | bytes 1572872 | tf_op jit(solution)/shard_map/ppermute | solution.py:23
  283.5 82.4 %copy-start.6 = (bf16[128,1024]{1,0:T(8,128)(2,1)S(1)}, bf16[128,1024]{1,0:T(8,128)(2,1)}, u32[]{:S(2)}) copy-start(bf16[128,1024]{1,0:T(8,128)(2,1)} %param.24) | copy-start | bytes 786436
  288.2 88.2 %copy-start.2 = (f32[128,4096]{1,0:T(8,128)}, f32[128,4096]{1,0:T(8,128)S(1)}, u32[]{:S(2)}) copy-start(f32[128,4096]{1,0:T(8,128)S(1)} %convolution_add_fusion) | copy-start | bytes 6291460
  435.3 16.0 %collective-permute-start.16 = (bf16[128,2048]{0,1:T(8,128)(2,1)S(1)}, bf16[128,2048]{0,1:T(8,128)(2,1)S(1)}, u32[]{:S(2)}, u32[]{:S(2)}) collective-permute-start(bf16[128,2048]{0,1:T(8,128)(2,1)S(1)} %get-tuple-element.456), channel_id=1, source_target_pairs={{8,0},{9,1},{10,2},{11,3},{12,4},{13,5},{14,6},{15,7},{16,8},{17,9... | collective-permute-start | bytes 1572872 | tf_op jit(solution)/shard_map/ppermute | solution.py:23
  436.6 18.1 %collective-permute-start.31 = (bf16[128,2048]{0,1:T(8,128)(2,1)S(1)}, bf16[128,2048]{0,1:T(8,128)(2,1)S(1)}, u32[]{:S(2)}, u32[]{:S(2)}) collective-permute-start(bf16[128,2048]{0,1:T(8,128)(2,1)S(1)} %get-tuple-element.457), channel_id=1, source_target_pairs={{0,8},{1,9},{2,10},{3,11},{4,12},{5,13},{6,14},{7,15},{8,16},{9,17... | collective-permute-start | bytes 1572872 | tf_op jit(solution)/shard_map/ppermute | solution.py:23
  441.2 15.4 %collective-permute-start.30 = (bf16[128,2048]{0,1:T(8,128)(2,1)S(1)}, bf16[128,2048]{0,1:T(8,128)(2,1)S(1)}, u32[]{:S(2)}, u32[]{:S(2)}) collective-permute-start(bf16[128,2048]{0,1:T(8,128)(2,1)S(1)} %get-tuple-element.458), channel_id=1, source_target_pairs={{0,7},{1,8},{2,9},{3,10},{4,11},{5,12},{6,13},{7,14},{8,15},{9,16}... | collective-permute-start | bytes 1572872 | tf_op jit(solution)/shard_map/ppermute | solution.py:23
  443.9 24.2 %collective-permute-start.29 = (bf16[128,2048]{0,1:T(8,128)(2,1)S(1)}, bf16[128,2048]{0,1:T(8,128)(2,1)S(1)}, u32[]{:S(2)}, u32[]{:S(2)}) collective-permute-start(bf16[128,2048]{0,1:T(8,128)(2,1)S(1)} %get-tuple-element.459), channel_id=1, source_target_pairs={{0,6},{1,7},{2,8},{3,9},{4,10},{5,11},{6,12},{7,13},{8,14},{9,15},... | collective-permute-start | bytes 1572872 | tf_op jit(solution)/shard_map/ppermute | solution.py:23
  448.2 21.2 %collective-permute-start.28 = (bf16[128,2048]{0,1:T(8,128)(2,1)S(1)}, bf16[128,2048]{0,1:T(8,128)(2,1)S(1)}, u32[]{:S(2)}, u32[]{:S(2)}) collective-permute-start(bf16[128,2048]{0,1:T(8,128)(2,1)S(1)} %get-tuple-element.460), channel_id=1, source_target_pairs={{0,5},{1,6},{2,7},{3,8},{4,9},{5,10},{6,11},{7,12},{8,13},{9,14},{... | collective-permute-start | bytes 1572872 | tf_op jit(solution)/shard_map/ppermute | solution.py:23
  451.3 43.4 %collective-permute-start.27 = (bf16[128,2048]{0,1:T(8,128)(2,1)S(1)}, bf16[128,2048]{0,1:T(8,128)(2,1)S(1)}, u32[]{:S(2)}, u32[]{:S(2)}) collective-permute-start(bf16[128,2048]{0,1:T(8,128)(2,1)S(1)} %get-tuple-element.461), channel_id=1, source_target_pairs={{0,4},{1,5},{2,6},{3,7},{4,8},{5,9},{6,10},{7,11},{8,12},{9,13},{1... | collective-permute-start | bytes 1572872 | tf_op jit(solution)/shard_map/ppermute | solution.py:23
  454.7 57.0 %copy-start.19 = (bf16[128,2048]{0,1:T(8,128)(2,1)}, bf16[128,2048]{0,1:T(8,128)(2,1)S(1)}, u32[]{:S(2)}) copy-start(bf16[128,2048]{0,1:T(8,128)(2,1)S(1)} %collective-permute-done.31) | copy-start | bytes 1572868
  454.7 41.3 %collective-permute-start.26 = (bf16[128,2048]{0,1:T(8,128)(2,1)S(1)}, bf16[128,2048]{0,1:T(8,128)(2,1)S(1)}, u32[]{:S(2)}, u32[]{:S(2)}) collective-permute-start(bf16[128,2048]{0,1:T(8,128)(2,1)S(1)} %get-tuple-element.462), channel_id=1, source_target_pairs={{0,3},{1,4},{2,5},{3,6},{4,7},{5,8},{6,9},{7,10},{8,11},{9,12},{10... | collective-permute-start | bytes 1572872 | tf_op jit(solution)/shard_map/ppermute | solution.py:23
  456.6 55.2 %copy-start.20 = (bf16[128,2048]{0,1:T(8,128)(2,1)}, bf16[128,2048]{0,1:T(8,128)(2,1)S(1)}, u32[]{:S(2)}) copy-start(bf16[128,2048]{0,1:T(8,128)(2,1)S(1)} %collective-permute-done.30) | copy-start | bytes 1572868
  456.6 40.7 %collective-permute-start.25 = (bf16[128,2048]{0,1:T(8,128)(2,1)S(1)}, bf16[128,2048]{0,1:T(8,128)(2,1)S(1)}, u32[]{:S(2)}, u32[]{:S(2)}) collective-permute-start(bf16[128,2048]{0,1:T(8,128)(2,1)S(1)} %get-tuple-element.463), channel_id=1, source_target_pairs={{0,2},{1,3},{2,4},{3,5},{4,6},{5,7},{6,8},{7,9},{8,10},{9,11},{10,... | collective-permute-start | bytes 1572872 | tf_op jit(solution)/shard_map/ppermute | solution.py:23
  468.1 30.6 %collective-permute-start.24 = (bf16[128,2048]{0,1:T(8,128)(2,1)S(1)}, bf16[128,2048]{0,1:T(8,128)(2,1)S(1)}, u32[]{:S(2)}, u32[]{:S(2)}) collective-permute-start(bf16[128,2048]{0,1:T(8,128)(2,1)S(1)} %get-tuple-element.464), channel_id=1, source_target_pairs={{0,1},{1,2},{2,3},{3,4},{4,5},{5,6},{6,7},{7,8},{8,9},{9,10},{10,1... | collective-permute-start | bytes 1572872 | tf_op jit(solution)/shard_map/ppermute | solution.py:23
  469.5 30.5 %collective-permute-start.23 = (bf16[128,2048]{0,1:T(8,128)(2,1)S(1)}, bf16[128,2048]{0,1:T(8,128)(2,1)S(1)}, u32[]{:S(2)}, u32[]{:S(2)}) collective-permute-start(bf16[128,2048]{0,1:T(8,128)(2,1)S(1)} %get-tuple-element.465), channel_id=1, source_target_pairs={{1,0},{2,1},{3,2},{4,3},{5,4},{6,5},{7,6},{8,7},{9,8},{10,9},{11,1... | collective-permute-start | bytes 1572872 | tf_op jit(solution)/shard_map/ppermute | solution.py:23
  494.7 15.7 %collective-permute-start.22 = (bf16[128,2048]{0,1:T(8,128)(2,1)S(1)}, bf16[128,2048]{0,1:T(8,128)(2,1)S(1)}, u32[]{:S(2)}, u32[]{:S(2)}) collective-permute-start(bf16[128,2048]{0,1:T(8,128)(2,1)S(1)} %get-tuple-element.466), channel_id=1, source_target_pairs={{2,0},{3,1},{4,2},{5,3},{6,4},{7,5},{8,6},{9,7},{10,8},{11,9},{12,... | collective-permute-start | bytes 1572872 | tf_op jit(solution)/shard_map/ppermute | solution.py:23
  496.0 15.9 %collective-permute-start.21 = (bf16[128,2048]{0,1:T(8,128)(2,1)}, bf16[128,2048]{0,1:T(8,128)(2,1)}, u32[]{:S(2)}, u32[]{:S(2)}) collective-permute-start(bf16[128,2048]{0,1:T(8,128)(2,1)} %get-tuple-element.467), channel_id=1, source_target_pairs={{3,0},{4,1},{5,2},{6,3},{7,4},{8,5},{9,6},{10,7},{11,8},{12,9},{13... | collective-permute-start | bytes 1572872 | tf_op jit(solution)/shard_map/ppermute | solution.py:23
  497.4 24.7 %collective-permute-start.20 = (bf16[128,2048]{0,1:T(8,128)(2,1)}, bf16[128,2048]{0,1:T(8,128)(2,1)}, u32[]{:S(2)}, u32[]{:S(2)}) collective-permute-start(bf16[128,2048]{0,1:T(8,128)(2,1)} %get-tuple-element.468), channel_id=1, source_target_pairs={{4,0},{5,1},{6,2},{7,3},{8,4},{9,5},{10,6},{11,7},{12,8},{13,9},{1... | collective-permute-start | bytes 1572872 | tf_op jit(solution)/shard_map/ppermute | solution.py:23
  498.7 29.4 %collective-permute-start.19 = (bf16[128,2048]{0,1:T(8,128)(2,1)}, bf16[128,2048]{0,1:T(8,128)(2,1)}, u32[]{:S(2)}, u32[]{:S(2)}) collective-permute-start(bf16[128,2048]{0,1:T(8,128)(2,1)} %get-tuple-element.469), channel_id=1, source_target_pairs={{5,0},{6,1},{7,2},{8,3},{9,4},{10,5},{11,6},{12,7},{13,8},{14,9},{... | collective-permute-start | bytes 1572872 | tf_op jit(solution)/shard_map/ppermute | solution.py:23
  500.0 47.4 %collective-permute-start.18 = (bf16[128,2048]{0,1:T(8,128)(2,1)}, bf16[128,2048]{0,1:T(8,128)(2,1)}, u32[]{:S(2)}, u32[]{:S(2)}) collective-permute-start(bf16[128,2048]{0,1:T(8,128)(2,1)} %get-tuple-element.470), channel_id=1, source_target_pairs={{6,0},{7,1},{8,2},{9,3},{10,4},{11,5},{12,6},{13,7},{14,8},{15,9},... | collective-permute-start | bytes 1572872 | tf_op jit(solution)/shard_map/ppermute | solution.py:23
  510.5 41.1 %collective-permute-start.17 = (bf16[128,2048]{0,1:T(8,128)(2,1)S(1)}, bf16[128,2048]{0,1:T(8,128)(2,1)}, u32[]{:S(2)}, u32[]{:S(2)}) collective-permute-start(bf16[128,2048]{0,1:T(8,128)(2,1)S(1)} %get-tuple-element.471), channel_id=1, source_target_pairs={{7,0},{8,1},{9,2},{10,3},{11,4},{12,5},{13,6},{14,7},{15,8},{16,9}... | collective-permute-start | bytes 1572872 | tf_op jit(solution)/shard_map/ppermute | solution.py:23
  563.9 293.7 %reduce-scatter.10.cloned.1.call-start = ((), (), s32[]{:S(2)}) async-start(), calls=%async_computation.10 | async-start | bytes 4325376 | tf_op jit(solution)/shard_map/reduce_scatter | solution.py:228
  567.0 449.0 %reduce-scatter.8.cloned.1.call-start = ((), (), s32[]{:S(2)}) async-start(), calls=%async_computation.9 | async-start | bytes 12976128 | tf_op jit(solution)/shard_map/reduce_scatter | solution.py:222
  574.4 626.0 %reduce-scatter.12.cloned.1.call-start = ((), (), s32[]{:S(2)}) async-start(), calls=%async_computation.11 | async-start | bytes 17301504 | tf_op jit(solution)/shard_map/reduce_scatter | solution.py:229
  583.8 803.3 %reduce-scatter.14.cloned.1.call-start = ((), (), s32[]{:S(2)}) async-start(), calls=%async_computation.12 | async-start | bytes 17301504 | tf_op jit(solution)/shard_map/reduce_scatter | solution.py:230
  594.4 795.8 %copy-start.46 = (f32[1,1024]{1,0:T(1,128)S(1)}, f32[1,1024]{1,0:T(1,128)}, u32[]{:S(2)}) copy-start(f32[1,1024]{1,0:T(1,128)} %get-tuple-element.474) | copy-start | bytes 12292
  (43 other events, 958.6 us)
Sparse Core Ops, SparseCore 0:
  11.5 72.4 all-gather.5
  87.4 73.0 all-gather.7
  164.0 119.4 all-gather.9
  286.7 79.0 all-gather.11
  564.1 154.5 reduce-scatter.15
  720.9 136.6 reduce-scatter.9
  864.7 151.2 reduce-scatter.7
  1018.3 181.9 reduce-scatter.11
  1202.6 184.4 reduce-scatter.13
where the time goes:
time: 1460 us
  waiting for transfers between devices  1040 us (71%)
  starting transfers between devices  97.3 us (7%)
  matrix products  87.8 us (6%)
  blocking collectives  86.1 us (6%)
  local copies, waits for them, and re-layouts  68.5 us (5%)
  other arithmetic  45.2 us (3%)
  between operations  20.4 us (1%)
    reduce_scatter x1, waiting for transfers between devices, on_device(): lax.psum_scatter(shrink_grad, 'seq', scatter_dimension=0, tiled=True)  184 us
    reduce_scatter x1, waiting for transfers between devices, on_device(): lax.psum_scatter(expand_grad, 'seq', scatter_dimension=0, tiled=True)  181 us
    reduce_scatter x1, waiting for transfers between devices, on_device(): lax.psum_scatter(jnp.einsum('ti,tj->ij', sliced, joined_grad, preferred_e...  157 us
    ppermute x32, waiting for transfers between devices, shifted(): return lax.ppermute(block, axis, route)  157 us
    reduce_scatter x1, waiting for transfers between devices, on_device(): lax.psum_scatter(output_grad, 'seq', scatter_dimension=0, tiled=True)  138 us
    unnamed x10, waiting for transfers between devices  124 us
    ppermute x32, starting transfers between devices, shifted(): return lax.ppermute(block, axis, route)  96.7 us
    all_gather x1, waiting for transfers between devices, on_device(): lax.all_gather(reduce_weight.astype(jnp.bfloat16), 'seq', axis=0, tiled=T...  77.6 us
  transfers between devices with their start and end apart: 41, of which 22 were waited for; matrix products, arithmetic and copies ran while one was open for 7% of the time, Pallas kernels for 0%

commit v1 on v0

v1 whole, which is shorter than its diff:
```python
import functools

import jax
import jax.numpy as jnp
from jax import lax
from jax.experimental import pallas as pl
from jax.experimental.pallas import tpu as pltpu
from jax.sharding import PartitionSpec as P

HEADS = 16
STEP = 10
EPSILON = 1e-05
MOMENTUM = 0.9
LEARNING_RATES = (60.0, 480.0, 60.0, 60.0, 600.0)
WEIGHT_DECAY = 0.0001
CLIP_NORM = 1.0
MASK_FLOOR = -1e30
PLANE = 8
QUERY_TILE = 256
KEY_TILE = 256
F32 = jnp.float32
LOW = jnp.bfloat16


def swap(block, bit):
    n = lax.axis_size("seq")
    return lax.ppermute(block, "seq", [(i, i ^ bit) for i in range(n)])


def move(block, distance):
    n = lax.axis_size("seq")
    return lax.ppermute(
        block, "seq", [(i, i + distance) for i in range(n) if 0 <= i + distance < n]
    )


def plane_groups():
    n = lax.axis_size("seq")
    return [[g * PLANE + j for j in range(PLANE)] for g in range(n // PLANE)]


def cross_groups():
    n = lax.axis_size("seq")
    return [[g * PLANE + j for g in range(n // PLANE)] for j in range(PLANE)]


def exchange(blocks, groups=None):
    return lax.all_to_all(blocks, "seq", 0, 0, axis_index_groups=groups)


def spread(block):
    half = block.shape[0] // 2
    across = swap(block, 2)
    along = swap(block, 4)
    corner = jnp.concatenate([swap(across[:half], 4), swap(along[half:], 2)], axis=0)
    mine = jnp.stack([block, across, along, corner])
    return jnp.stack([mine, swap(mine, 1)])


def collect(parts):
    half = parts.shape[2] // 2
    pair = parts[0] + swap(parts[1].astype(LOW), 1).astype(F32)
    corner = pair[3].astype(LOW)
    by_across = swap(corner[:half], 2).astype(F32)
    by_along = swap(corner[half:], 4).astype(F32)
    across = jnp.concatenate([pair[1][:half], pair[1][half:] + by_along], axis=0).astype(LOW)
    along = jnp.concatenate([pair[2][:half] + by_across, pair[2][half:]], axis=0).astype(LOW)
    return pair[0] + swap(across, 2).astype(F32) + swap(along, 4).astype(F32)


def norm_parts(values):
    centre = values - jnp.mean(values, axis=-1, keepdims=True)
    spread_of = jnp.mean(centre * centre, axis=-1, keepdims=True)
    inverse = lax.rsqrt(spread_of + EPSILON)
    return centre * inverse, inverse


def norm_back(unit, inverse, gain, incoming):
    scaled = incoming * gain
    return inverse * (
        scaled
        - jnp.mean(scaled, axis=-1, keepdims=True)
        - unit * jnp.mean(scaled * unit, axis=-1, keepdims=True)
    )


def dot(a, b, dims=((1,), (0,))):
    return lax.dot_general(a, b, (dims, ((), ())), preferred_element_type=F32)


def project_kernel(order_ref, tokens_ref, gain_ref, shift_ref, weight_ref, first_ref, joined_ref):
    unit, _ = norm_parts(tokens_ref[0].astype(F32))
    first = (unit * gain_ref[...] + shift_ref[...]).astype(LOW)
    first_ref[0] = first
    joined_ref[0] = dot(first, weight_ref[...]).astype(LOW)


def project(place, tokens, gain, shift, weight):
    blocks, number, columns = tokens.shape
    wide = weight.shape[1]
    return pl.pallas_call(
        project_kernel,
        grid_spec=pltpu.PrefetchScalarGridSpec(
            num_scalar_prefetch=1,
            grid=(blocks,),
            in_specs=[
                pl.BlockSpec((1, number, columns), lambda i, s: (i, 0, 0)),
                pl.BlockSpec((1, columns), lambda i, s: (0, 0)),
                pl.BlockSpec((1, columns), lambda i, s: (0, 0)),
                pl.BlockSpec((columns, wide), lambda i, s: (0, 0)),
            ],
            out_specs=[
                pl.BlockSpec((1, number, columns), lambda i, s: (s[i], 0, 0)),
                pl.BlockSpec((1, number, wide), lambda i, s: (s[i], 0, 0)),
            ],
        ),
        out_shape=[
            jax.ShapeDtypeStruct((blocks, number, columns), LOW),
            jax.ShapeDtypeStruct((blocks, number, wide), LOW),
        ],
        cost_estimate=pl.CostEstimate(
            flops=2 * blocks * number * columns * wide, bytes_accessed=2 * tokens.size * 3, transcendentals=0
        ),
        compiler_params=pltpu.CompilerParams(vmem_limit_bytes=40 << 20),
    )(place, tokens, gain, shift, weight)


def head_mask(shape, head):
    return lax.broadcasted_iota(jnp.int32, shape, len(shape) - 1) // 64 == head


def attend_kernel(
    range_ref, query_ref, before_ref, own_ref, after_ref, span_ref, mixed_ref, log_ref, keys, values
):
    step = pl.program_id(0)
    tokens = own_ref.shape[0]
    wide = query_ref.shape[1]

    @pl.when(step == 0)
    def _():
        for place, ref in enumerate((before_ref, own_ref, after_ref)):
            keys[pl.ds(place * tokens, tokens), :] = ref[:, :wide]
            values[:, pl.ds(place * tokens, tokens)] = ref[:, wide:].T

    queries = query_ref[...] * jnp.asarray(0.125, LOW)
    begin = span_ref[0:1, :]
    end = span_ref[1:2, :]
    here = query_ref.shape[0]
    split = [jnp.where(head_mask(queries.shape, h), queries, jnp.zeros_like(queries)) for h in range(2)]

    def body(index, carry):
        start = pl.multiple_of(index * KEY_TILE, KEY_TILE)
        block = keys[pl.ds(start, KEY_TILE), :]
        place = start + lax.broadcasted_iota(jnp.int32, (KEY_TILE, here), 0)
        allowed = (place >= begin) & (place < end)
        out = []
        for h in range(2):
            peak, total, mixed = carry[h]
            scores = jnp.where(allowed, dot(block, split[h], ((1,), (1,))), MASK_FLOOR)
            raised_peak = jnp.maximum(peak, jnp.max(scores, axis=0, keepdims=True))
            raised = jnp.exp(scores - raised_peak)
            fade = jnp.exp(peak - raised_peak)
            total = total * fade + jnp.sum(raised, axis=0, keepdims=True)
            turned = values[64 * h : 64 * h + 64, pl.ds(start, KEY_TILE)]
            mixed = mixed * fade + dot(turned, raised.astype(LOW))
            out.append((raised_peak, total, mixed))
        return tuple(out)

    init = tuple(
        (jnp.full((1, here), MASK_FLOOR, F32), jnp.zeros((1, here), F32), jnp.zeros((64, here), F32))
        for _ in range(2)
    )
    done = lax.fori_loop(range_ref[0, step], range_ref[1, step], body, init)
    mixed_ref[...] = jnp.concatenate([m / t for _, t, m in done], axis=0).T
    log_ref[...] = jnp.concatenate([k + jnp.log(t) for k, t, _ in done], axis=0)


def attend_back_kernel(
    range_ref,
    query_ref,
    before_ref,
    own_ref,
    after_ref,
    span_ref,
    mixed_ref,
    log_ref,
    grad_ref,
    query_grad_ref,
    before_grad_ref,
    own_grad_ref,
    after_grad_ref,
    keys,
    values,
    turned_keys,
    key_grad,
    value_grad,
):
    step = pl.program_id(0)
    tokens = own_ref.shape[0]
    wide = query_ref.shape[1]

    @pl.when(step == 0)
    def _():
        for place, ref in enumerate((before_ref, own_ref, after_ref)):
            keys[pl.ds(place * tokens, tokens), :] = ref[:, :wide]
            values[pl.ds(place * tokens, tokens), :] = ref[:, wide:]
            turned_keys[:, pl.ds(place * tokens, tokens)] = ref[:, :wide].T
        key_grad[...] = jnp.zeros_like(key_grad)
        value_grad[...] = jnp.zeros_like(value_grad)

    queries = query_ref[...] * jnp.asarray(0.125, LOW)
    grads = grad_ref[...]
    here = queries.shape[0]
    zero = jnp.zeros_like(queries)
    split = [jnp.where(head_mask(queries.shape, h), queries, zero) for h in range(2)]
    split_grads = [jnp.where(head_mask(queries.shape, h), grads, zero) for h in range(2)]
    product = (grads.astype(F32) * mixed_ref[...]).T
    centred = [jnp.sum(product[64 * h : 64 * h + 64], axis=0, keepdims=True) for h in range(2)]
    begin = span_ref[0:1, :]
    end = span_ref[1:2, :]

    def body(index, carry):
        start = pl.multiple_of(index * KEY_TILE, KEY_TILE)
        rows = pl.ds(start, KEY_TILE)
        place = start + lax.broadcasted_iota(jnp.int32, (KEY_TILE, here), 0)
        allowed = (place >= begin) & (place < end)
        out, key_part, value_part = [], 0, 0
        for h in range(2):
            scores = dot(keys[rows, :], split[h], ((1,), (1,)))
            shares = jnp.exp(jnp.where(allowed, scores - log_ref[h : h + 1, :], MASK_FLOOR))
            value_part += dot(shares.astype(LOW), split_grads[h])
            share_grad = dot(values[rows, :], split_grads[h], ((1,), (1,)))
            score_grad = (shares * (share_grad - centred[h])).astype(LOW)
            key_part += dot(score_grad, split[h])
            out.append(carry[h] + dot(turned_keys[64 * h : 64 * h + 64, rows], score_grad))
        key_grad[rows, :] += key_part
        value_grad[rows, :] += value_part
        return tuple(out)

    init = tuple(jnp.zeros((64, here), F32) for _ in range(2))
    done = lax.fori_loop(range_ref[0, step], range_ref[1, step], body, init)
    query_grad_ref[...] = (jnp.concatenate(done, axis=0).T * 0.125).astype(LOW)

    @pl.when(step == pl.num_programs(0) - 1)
    def _():
        for place, ref in enumerate((before_grad_ref, own_grad_ref, after_grad_ref)):
            ref[:, :wide] = key_grad[pl.ds(place * tokens, tokens), :].astype(ref.dtype)
            ref[:, wide:] = value_grad[pl.ds(place * tokens, tokens), :].astype(ref.dtype)


def attention(ranges, queries, before, own, after, spans):
    tokens, wide = queries.shape
    whole = lambda shape: pl.BlockSpec(shape, lambda i, s: (0, 0))
    tile = pl.BlockSpec((QUERY_TILE, wide), lambda i, s: (i, 0))
    row = pl.BlockSpec((2, QUERY_TILE), lambda i, s: (0, i))
    return pl.pallas_call(
        attend_kernel,
        grid_spec=pltpu.PrefetchScalarGridSpec(
            num_scalar_prefetch=1,
            grid=(tokens // QUERY_TILE,),
            in_specs=[tile] + [whole((tokens, 2 * wide))] * 3 + [row],
            out_specs=[tile, row],
            scratch_shapes=[
                pltpu.VMEM((3 * tokens, wide), LOW),
                pltpu.VMEM((wide, 3 * tokens), LOW),
            ],
        ),
        out_shape=[
            jax.ShapeDtypeStruct((tokens, wide), F32),
            jax.ShapeDtypeStruct((2, tokens), F32),
        ],
        cost_estimate=pl.CostEstimate(
            flops=4 * tokens * tokens * wide * 2, bytes_accessed=16 * tokens * wide, transcendentals=2 * tokens * tokens
        ),
        compiler_params=pltpu.CompilerParams(vmem_limit_bytes=40 << 20),
    )(ranges, queries, before, own, after, spans)


def attention_back(ranges, queries, before, own, after, spans, mixed, logs, grads):
    tokens, wide = queries.shape
    whole = lambda shape: pl.BlockSpec(shape, lambda i, s: (0, 0))
    tile = pl.BlockSpec((QUERY_TILE, wide), lambda i, s: (i, 0))
    row = pl.BlockSpec((2, QUERY_TILE), lambda i, s: (0, i))
    return pl.pallas_call(
        attend_back_kernel,
        grid_spec=pltpu.PrefetchScalarGridSpec(
            num_scalar_prefetch=1,
            grid=(tokens // QUERY_TILE,),
            in_specs=[tile] + [whole((tokens, 2 * wide))] * 3 + [row, tile, row, tile],
            out_specs=[tile] + [whole((tokens, 2 * wide))] * 3,
            scratch_shapes=[
                pltpu.VMEM((3 * tokens, wide), LOW),
                pltpu.VMEM((3 * tokens, wide), LOW),
                pltpu.VMEM((wide, 3 * tokens), LOW),
                pltpu.VMEM((3 * tokens, wide), F32),
                pltpu.VMEM((3 * tokens, wide), F32),
            ],
        ),
        out_shape=[
            jax.ShapeDtypeStruct((tokens, wide), LOW),
            jax.ShapeDtypeStruct((tokens, 2 * wide), LOW),
            jax.ShapeDtypeStruct((tokens, 2 * wide), F32),
            jax.ShapeDtypeStruct((tokens, 2 * wide), LOW),
        ],
        cost_estimate=pl.CostEstimate(
            flops=10 * tokens * tokens * wide * 2, bytes_accessed=32 * tokens * wide, transcendentals=2 * tokens * tokens
        ),
        compiler_params=pltpu.CompilerParams(vmem_limit_bytes=48 << 20),
    )(ranges, queries, before, own, after, spans, mixed, logs, grads)


def on_device(
    tokens,
    scene_lengths,
    cotangent,
    attend_weight,
    output_weight,
    expand_weight,
    reduce_weight,
    vector_params,
    attend_momentum,
    output_momentum,
    expand_momentum,
    reduce_momentum,
    vector_momentum,
    attend_average,
    output_average,
    expand_average,
    reduce_average,
    vector_average,
):
    n = lax.axis_size("seq")
    planes = n // PLANE
    device = lax.axis_index("seq")
    plane, spot = device // PLANE, device % PLANE
    number, columns = tokens.shape
    shared = number * PLANE
    rows = columns // n
    hidden = reduce_weight.shape[0]
    wide = columns // PLANE

    vectors = exchange(jnp.broadcast_to(vector_params.astype(LOW)[None], (n,) + vector_params.shape))
    vectors = jnp.moveaxis(vectors, 0, 1).reshape(-1, columns).astype(F32)
    bias_up = lax.dynamic_index_in_dim(
        vectors[5:].reshape(planes, PLANE, hidden), spot, axis=1, keepdims=False
    ).reshape(1, planes * hidden)

    attend = (
        attend_weight.astype(LOW).reshape(rows, 3, PLANE, wide).transpose(2, 0, 1, 3).reshape(PLANE, rows, 3 * wide)
    )
    attend = exchange(jnp.broadcast_to(attend[None], (planes,) + attend.shape).reshape(n, rows, 3 * wide))
    attend = attend.reshape(columns, 3 * wide)
    expand = (
        expand_weight.astype(LOW)
        .reshape(rows, planes, PLANE, hidden)
        .transpose(2, 0, 1, 3)
        .reshape(PLANE, rows, planes * hidden)
    )
    expand = exchange(jnp.broadcast_to(expand[None], (planes,) + expand.shape).reshape(n, rows, -1))
    expand = expand.reshape(columns, planes * hidden)
    shrink = exchange(
        jnp.broadcast_to(reduce_weight.astype(LOW)[None], (planes,) + reduce_weight.shape), cross_groups()
    ).reshape(planes * hidden, columns)
    output = exchange(
        jnp.broadcast_to(output_weight.astype(LOW)[None], (planes,) + output_weight.shape), cross_groups()
    )
    output = exchange(jnp.broadcast_to(output[None], (PLANE,) + output.shape), plane_groups())
    output = output.transpose(1, 0, 2, 3).reshape(columns, columns)

    order = spot ^ jnp.array([2 * m + k for k in range(2) for m in range(4)], jnp.int32)
    gathered = spread(tokens).reshape(PLANE, number, columns)
    first_low, joined = project(order, gathered, vectors[0:1], vectors[1:2], attend)
    first_low = first_low.reshape(shared, columns)
    joined = joined.reshape(shared, 3 * wide)
    queries, pairs = joined[:, :wide], joined[:, wide:]
    before, after = move(pairs, PLANE), move(pairs, -PLANE)

    finish = jnp.cumsum(scene_lengths)
    begin = finish - scene_lengths
    base = (plane - 1) * shared
    position = plane * shared + jnp.arange(shared, dtype=jnp.int32)
    past = begin[None, :] <= position[:, None]
    span_begin = jnp.max(jnp.where(past, begin[None, :], 0), axis=1) - base
    span_end = jnp.min(jnp.where(finish[None, :] > position[:, None], finish[None, :], 1 << 30), axis=1) - base
    spans = jnp.stack([span_begin, span_end])
    ranges = jnp.stack(
        [span_begin[::QUERY_TILE] // KEY_TILE, (span_end[QUERY_TILE - 1 :: QUERY_TILE] + KEY_TILE - 1) // KEY_TILE]
    )
    mixed_exact, logs = attention(ranges, queries, before, pairs, after, spans)
    mixed_mine = mixed_exact.astype(LOW)
    mixed = exchange(mixed_mine.reshape(PLANE, number, wide), plane_groups())
    mixed = mixed.transpose(1, 0, 2).reshape(number, columns)

    second = tokens.astype(F32) + dot(mixed, output)
    unit_two, inverse_two = norm_parts(second)
    normed = (unit_two * vectors[2:3] + vectors[3:4]).astype(LOW)
    normed_all = spread(normed).reshape(shared, columns)
    cotangent_all = spread(cotangent).reshape(shared, columns)

    upper = dot(normed_all, expand) + bias_up
    active, active_back = jax.vjp(lambda v: jax.nn.gelu(v, approximate=False), upper)
    active_low = active.astype(LOW)
    upper_grad = active_back(dot(cotangent_all, shrink, ((1,), (1,))))[0].astype(LOW)
    normed_grad = collect(dot(upper_grad, expand, ((1,), (1,))).reshape(2, 4, number, columns))
    block_output = collect(dot(active_low, shrink).reshape(2, 4, number, columns))
    block_output = (second + block_output + vectors[4:5]).astype(LOW)

    second_grad = cotangent.astype(F32) + norm_back(unit_two, inverse_two, vectors[2:3], normed_grad)
    branch_grad = second_grad.astype(LOW)
    mixed_grad = dot(branch_grad, output, ((1,), (1,))).astype(LOW)
    mixed_grad = exchange(mixed_grad.reshape(number, PLANE, wide).transpose(1, 0, 2), plane_groups())
    mixed_grad = mixed_grad.reshape(shared, wide)

    query_grad, before_grad, own_grad, after_grad = attention_back(
        ranges, queries, before, pairs, after, spans, mixed_exact, logs, mixed_grad
    )
    pair_grad = own_grad + move(before_grad, -PLANE).astype(F32) + move(after_grad, PLANE).astype(F32)
    joined_grad = jnp.concatenate([query_grad, pair_grad.astype(LOW)], axis=1)

    attend_grad = dot(first_low, joined_grad, ((0,), (0,))).astype(LOW)
    attend_grad = exchange(attend_grad.reshape(n, rows, 3 * wide)).astype(F32)
    attend_grad = attend_grad.reshape(planes, PLANE, rows, 3, wide).sum(0).transpose(1, 2, 0, 3).reshape(rows, -1)

    expand_grad = dot(normed_all, upper_grad, ((0,), (0,))).astype(LOW)
    expand_grad = exchange(expand_grad.reshape(n, rows, planes * hidden)).astype(F32)
    expand_grad = (
        expand_grad.reshape(planes, PLANE, rows, planes, hidden).sum(0).transpose(1, 2, 0, 3).reshape(rows, -1)
    )
    shrink_grad = dot(active_low, cotangent_all, ((0,), (0,))).astype(LOW)
    shrink_grad = exchange(shrink_grad.reshape(planes, hidden, columns), cross_groups()).astype(F32).sum(0)
    branch_all = exchange(jnp.broadcast_to(branch_grad[None], (PLANE,) + branch_grad.shape), plane_groups())
    output_grad = dot(mixed_mine, branch_all.reshape(shared, columns), ((0,), (0,))).astype(LOW)
    output_grad = exchange(output_grad.reshape(planes, rows, columns), cross_groups()).astype(F32).sum(0)
    output_grad = lax.ppermute(
        output_grad,
        "seq",
        [(g * PLANE + j, j * planes + g) for g in range(planes) for j in range(PLANE)],
    )

    first_grad = collect(
        jnp.take(dot(joined_grad, attend, ((1,), (1,))).reshape(PLANE, number, columns), order, axis=0).reshape(
            2, 4, number, columns
        )
    )
    unit_one, inverse_one = norm_parts(tokens.astype(F32))
    input_gradient = (second_grad + norm_back(unit_one, inverse_one, vectors[0:1], first_grad)).astype(LOW)

    up_sum = jnp.sum(upper_grad.astype(F32), axis=0).reshape(planes, 1, hidden)
    up_sum = lax.dynamic_update_slice_in_dim(jnp.zeros((planes, PLANE, hidden), F32), up_sum, spot, axis=1)
    vector_grad = jnp.concatenate(
        [
            jnp.stack(
                [
                    jnp.sum(first_grad * unit_one, axis=0),
                    jnp.sum(first_grad, axis=0),
                    jnp.sum(normed_grad * unit_two, axis=0),
                    jnp.sum(normed_grad, axis=0),
                    jnp.sum(cotangent.astype(F32), axis=0),
                ]
            ),
            up_sum.reshape(-1, columns),
        ],
        axis=0,
    )
    vector_grad = exchange(jnp.moveaxis(vector_grad.reshape(-1, n, rows), 1, 0)).sum(0)

    groups = (
        (attend_weight, attend_momentum, attend_average, attend_grad),
        (output_weight, output_momentum, output_average, output_grad),
        (expand_weight, expand_momentum, expand_average, expand_grad),
        (reduce_weight, reduce_momentum, reduce_average, shrink_grad),
        (vector_params, vector_momentum, vector_average, vector_grad),
    )
    local_square = sum(jnp.sum(g[3] * g[3]) for g in groups)
    norm_square = jnp.sum(exchange(jnp.full((n, 1, 128), local_square, F32))[:, 0, 0])
    gradient_norm = jnp.sqrt(norm_square)
    factor = jnp.minimum(1.0, CLIP_NORM / (gradient_norm + 1e-06))
    smooth_rate = min(0.999, (1.0 + STEP) / (10.0 + STEP))
    updates = []
    for rate, (weight, moment, average, gradient) in zip(LEARNING_RATES, groups):
        clipped = factor * gradient + WEIGHT_DECAY * weight
        velocity = MOMENTUM * moment + clipped
        updated = weight - rate * (clipped + MOMENTUM * velocity)
        smoothed = smooth_rate * average + (1.0 - smooth_rate) * updated
        updates += [velocity, updated, smoothed]
    return (block_output, input_gradient, gradient_norm, *updates)


def solution(mesh):
    split, turned = P("seq", None), P(None, "seq")
    return jax.shard_map(
        on_device,
        mesh=mesh,
        in_specs=(split, P()) + (split,) * 5 + (turned,) + ((split,) * 4 + (turned,)) * 2,
        out_specs=(split, split, P()) + (split,) * 12 + (turned,) * 3,
        check_vma=False,
    )
```

time: 1460 us -> 445 us (0.30)
  waiting for transfers between devices: 1040 us -> 148 us
  blocking collectives: 86.1 us -> 0 us
  matrix products: 87.8 us -> 36.3 us
  Pallas kernels: 0 us -> 31.3 us
    reduce_scatter x4 -> x0, waiting for transfers between devices: 660 us -> none  [the longest x1 184 us: on_device(): lax.psum_scatter(shrink_grad, 'seq', scatter_dimension=0, tiled=True)]
    unnamed x10 -> x0, waiting for transfers between devices: 124 us -> none
    all_gather x4 -> x0, waiting for transfers between devices: 103 us -> none  [the longest x1 77.6 us: on_device(): lax.all_gather(reduce_weight.astype(jnp.bfloat16), 'seq', axis=0, tiled=T...]
    ppermute x32 -> x35, waiting for transfers between devices: 157 us -> 78.2 us  [the longest x30 54.1 us: swap(): return lax.ppermute(block, 'seq', [(i, i ^ bit) for i in range(n)])]
    all_to_all x0 -> x15, waiting for transfers between devices: none -> 69.7 us  [exchange(): return lax.all_to_all(blocks, 'seq', 0, 0, axis_index_groups=groups)]
    all_to_all x0 -> x15, starting transfers between devices: none -> 65.9 us  [exchange(): return lax.all_to_all(blocks, 'seq', 0, 0, axis_index_groups=groups)]
    ppermute x32 -> x35, starting transfers between devices: 96.7 us -> 42.5 us  [the longest x30 26.7 us: swap(): return lax.ppermute(block, 'seq', [(i, i ^ bit) for i in range(n)])]
    dot_general x40 -> x11, matrix products: 87.8 us -> 36.3 us  [dot(): return lax.dot_general(a, b, (dims, ((), ())), preferred_element_type=F32)]
  transfers between devices with their start and end apart: 41 -> 50, of which waited for: 22 -> 26; matrix products, arithmetic and copies ran while one was open for 7% -> 24% of each run, Pallas kernels for 0% -> 7%
where the time goes in v1:
time: 445 us; the launch traced here: 443 us
  waiting for transfers between devices  148 us (33%)
  starting transfers between devices  108 us (24%)
  other arithmetic  57.1 us (13%)
  local copies, waits for them, and re-layouts  55.5 us (12%)
  matrix products  36.3 us (8%)
  Pallas kernels  31.3 us (7%)
  between operations  6.78 us (2%)
    all_to_all x15, waiting for transfers between devices, exchange(): return lax.all_to_all(blocks, 'seq', 0, 0, axis_index_groups=groups)  69.7 us
    all_to_all x15, starting transfers between devices, exchange(): return lax.all_to_all(blocks, 'seq', 0, 0, axis_index_groups=groups)  65.9 us
    ppermute x30, waiting for transfers between devices, swap(): return lax.ppermute(block, 'seq', [(i, i ^ bit) for i in range(n)])  54.1 us
    dot_general x11, matrix products, dot(): return lax.dot_general(a, b, (dims, ((), ())), preferred_element_type=F32)  36.3 us
    ppermute x30, starting transfers between devices, swap(): return lax.ppermute(block, 'seq', [(i, i ^ bit) for i in range(n)])  26.7 us
    ppermute x4, waiting for transfers between devices, move(): lax.ppermute(block, 'seq', [(i, i + distance) for i in range(n) if 0 <= i...  24.1 us
    unnamed x95, local copies, waits for them, and re-layouts  14.2 us
    ppermute x4, starting transfers between devices, move(): lax.ppermute(block, 'seq', [(i, i + distance) for i in range(n) if 0 <= i...  13.6 us
  transfers between devices with their start and end apart: 50, of which 26 were waited for; matrix products, arithmetic and copies ran while one was open for 24% of the time, Pallas kernels for 7%

profile of v1, /device:TPU:0, one launch (start us, length us, event | category | flops | bytes accessed | tf_op | source)
XLA Modules:
  0.0 443.3 jit_solution(9913984939105817512)
XLA Ops:
  2.1 7.3 %all-to-all-start = ((bf16[32,2,144]{2,1,0:T(2,128)(2,1)}), bf16[32,2,144]{2,1,0:T(2,128)(2,1)S(1)}, u32[]{:S(2)}, u32[]{:S(2)}) async-start(bf16[32,2,144]{2,1,0:T(2,128)(2,1)} %reshape.374), calls=%async_computation | async-start | bytes 65536 | tf_op jit(solution)/shard_map/all_to_all | solution.py:48
  10.4 6.3 %all-to-all-done = bf16[32,2,144]{2,1,0:T(2,128)(2,1)S(1)} async-done(((bf16[32,2,144]{2,1,0:T(2,128)(2,1)}), bf16[32,2,144]{2,1,0:T(2,128)(2,1)S(1)}, u32[]{:S(2)}, u32[]{:S(2)}) %all-to-all-start) | async-done | bytes 18464 | tf_op jit(solution)/shard_map/all_to_all | solution.py:48
  17.4 3.4 all-to-all-start.3
  22.2 8.0 %all-to-all-done.3 = bf16[4,32,1024]{2,1,0:T(8,128)(2,1)S(1)} async-done(((bf16[4,32,1024]{2,1,0:T(8,128)(2,1)}), bf16[4,32,1024]{2,1,0:T(8,128)(2,1)S(1)}, u32[]{:S(2)}, u32[]{:S(2)}) %all-to-all-start.3) | async-done | bytes 262176 | tf_op jit(solution)/shard_map/all_to_all | solution.py:48
  38.1 11.6 %collective-permute-done.1 = bf16[128,1024]{1,0:T(8,128)(2,1)S(1)} collective-permute-done((bf16[128,1024]{1,0:T(8,128)(2,1)S(1)}, bf16[128,1024]{1,0:T(8,128)(2,1)S(1)}, u32[]{:S(2)}, u32[]{:S(2)}) %collective-permute-start.1) | collective-permute-done | bytes 262176 | tf_op jit(solution)/shard_map/ppermute | solution.py:27
  51.5 7.6 %collective-permute-done.3 = bf16[64,1024]{1,0:T(8,128)(2,1)S(1)} collective-permute-done((bf16[64,1024]{1,0:T(8,128)(2,1)S(1)}, bf16[64,1024]{1,0:T(8,128)(2,1)S(1)}, u32[]{:S(2)}, u32[]{:S(2)}) %collective-permute-start.3) | collective-permute-done | bytes 131104 | tf_op jit(solution)/shard_map/ppermute | solution.py:27
  62.0 4.5 %all-to-all-start.4 = ((bf16[8,4,32,1024]{3,2,1,0:T(8,128)(2,1)}), bf16[8,4,32,1024]{3,2,1,0:T(8,128)(2,1)}, u32[]{:S(2)}, u32[]{:S(2)}) async-start(bf16[8,4,32,1024]{3,2,1,0:T(8,128)(2,1)} %broadcast_in_dim.98), calls=%async_computation.4 | async-start | bytes 4194304 | tf_op jit(solution)/shard_map/all_to_all | solution.py:48
  68.6 4.5 %shard_map.322 = (bf16[8,128,1024]{2,1,0:T(8,128)(2,1)S(1)}, bf16[8,128,384]{2,1,0:T(8,128)(2,1)S(1)}) custom-call(s32[8]{0:T(128)S(1)} %broadcast_xor_fusion.order_ref, bf16[8,128,1024]{2,1,0:T(8,128)(2,1)S(1)} %bitcast.225, f32[1,1024]{1,0:T(1,128)S(1)} %slice.254.gain_ref, f32[1,1024]{1,0:T(1,128)S(1)} %slice.256.shift_ref, bf16[1024,384]{1,0:T(8,128)(2,1)S(1)} %bitcast.223), custom_call_target="tpu_custom_call" | custom-call | flops 805306368 | bytes 6291456 | tf_op jit(solution)/shard_map/pallas_call | solution.py:101
  75.9 5.4 %collective-permute-start.5 = (bf16[1024,256]{1,0:T(8,128)(2,1)S(1)}, bf16[1024,256]{1,0:T(8,128)(2,1)}, u32[]{:S(2)}, u32[]{:S(2)}) collective-permute-start(bf16[1024,256]{1,0:T(8,128)(2,1)S(1)} %slice.320.own_ref), channel_id=1, source_target_pairs={{0,8},{1,9},{2,10},{3,11},{4,12},{5,13},{6,14},{7,15},{8,16},{9,17... | collective-permute-start | bytes 1572872 | tf_op jit(solution)/shard_map/ppermute | solution.py:32
  81.4 9.3 %collective-permute-done.6.after_ref = bf16[1024,256]{1,0:T(8,128)(2,1)S(1)} collective-permute-done((bf16[1024,256]{1,0:T(8,128)(2,1)S(1)}, bf16[1024,256]{1,0:T(8,128)(2,1)S(1)}, u32[]{:S(2)}, u32[]{:S(2)}) %collective-permute-start.6) | collective-permute-done | bytes 524320 | tf_op jit(solution)/shard_map/ppermute | solution.py:32
  92.0 13.3 %shard_map.323 = (f32[1024,128]{1,0:T(8,128)S(1)}, f32[2,1024]{1,0:T(2,128)S(1)}) custom-call(s32[2,4]{1,0:T(2,128)S(1)} %pad_add_fusion.1.range_ref, bf16[1024,128]{1,0:T(8,128)(2,1)S(1)} %slice.319.query_ref, bf16[1024,256]{1,0:T(8,128)(2,1)} %collective-permute-done.5.before_ref, bf16[1024,256]{1,0:T(8,128)(2,1)S(1)} %slice.320.own_ref, ...), custom_call_target="tpu_custom_call" | custom-call | flops 1073741824 | bytes 2097152 | tf_op jit(solution)/shard_map/pallas_call | solution.py:256
  106.1 4.1 all-to-all-start.2
  113.2 4.0 all-to-all-done.2
  118.2 7.6 %all-to-all-start.5 = ((bf16[32,32,512]{2,1,0:T(8,128)(2,1)}), bf16[32,32,512]{2,1,0:T(8,128)(2,1)}, u32[]{:S(2)}, u32[]{:S(2)}) async-start(bf16[32,32,512]{2,1,0:T(8,128)(2,1)} %bitcast.236), calls=%async_computation.5 | async-start | bytes 2097152 | tf_op jit(solution)/shard_map/all_to_all | solution.py:48
  135.9 4.4 collective-permute-done.20
  142.9 3.9 collective-permute-done.7
  149.2 3.8 collective-permute-done.9
  156.0 5.9 %all-to-all-start.6 = ((bf16[4,128,1024]{2,1,0:T(8,128)(2,1)}), bf16[4,128,1024]{2,1,0:T(8,128)(2,1)}, u32[]{:S(2)}, u32[]{:S(2)}) async-start(bf16[4,128,1024]{2,1,0:T(8,128)(2,1)} %broadcast_in_dim.101), calls=%async_computation.6 | async-start | bytes 2097152 | tf_op jit(solution)/shard_map/all_to_all | solution.py:48
  163.0 3.1 pad_maximum_fusion.2
  168.9 3.9 fusion.53
  172.7 15.7 %all-to-all-done.6 = bf16[4,128,1024]{2,1,0:T(8,128)(2,1)} async-done(((bf16[4,128,1024]{2,1,0:T(8,128)(2,1)}), bf16[4,128,1024]{2,1,0:T(8,128)(2,1)}, u32[]{:S(2)}, u32[]{:S(2)}) %all-to-all-start.6) | async-done | bytes 1048608 | tf_op jit(solution)/shard_map/all_to_all | solution.py:48
  188.4 7.9 %convert_reduce_fusion = (f32[512]{0:T(512)S(1)}, bf16[1024,512]{1,0:T(8,128)(2,1)S(1)}, f32[1024,512]{1,0:T(8,128)S(1)}) fusion(f32[1024,512]{1,0:T(8,128)} %fusion.53, f32[512]{0:T(512)S(1)} %bitcast.259, bf16[1024,1024]{1,0:T(8,128)(2,1)} %bitcast.234, bf16[512,1024]{1,0:T(8,128)(2,1)} %bitcast.34), kind=kOutput, calls=%fused_computation.10 | convolution fusion | flops 1113062912 | bytes 8392704 | tf_op jit(solution)/shard_map/dot_general | solution.py:88
  204.4 4.9 %fusion.54 = f32[1024,1024]{1,0:T(8,128)} fusion(bf16[1024,512]{1,0:T(8,128)(2,1)S(1)} %multiply_convert_fusion, bf16[512,1024]{1,0:T(8,128)(2,1)} %bitcast.34), kind=kOutput, calls=%fused_computation.202 | convolution fusion | flops 1073741824 | bytes 6291456 | tf_op jit(solution)/shard_map/dot_general | solution.py:88
  212.1 3.2 slice.326
  232.4 3.3 collective-permute-done.26
  236.1 3.9 collective-permute-done.16
  243.7 3.4 all-to-all-start.7
  247.2 4.1 convolution_convert_fusion
  251.3 2.7 all-to-all-done.7
  254.0 4.5 %all-to-all-start.12 = ((bf16[4,128,1024]{2,1,0:T(8,128)(2,1)}), bf16[4,128,1024]{2,1,0:T(8,128)(2,1)}, u32[]{:S(2)}, u32[]{:S(2)}) async-start(bf16[4,128,1024]{2,1,0:T(8,128)(2,1)} %bitcast.237), calls=%async_computation.12 | async-start | bytes 2097152 | tf_op jit(solution)/shard_map/all_to_all | solution.py:48
  258.5 13.5 %shard_map.324 = (bf16[1024,128]{1,0:T(8,128)(2,1)S(1)}, bf16[1024,256]{1,0:T(8,128)(2,1)S(1)}, f32[1024,256]{1,0:T(8,128)S(1)}, bf16[1024,256]{1,0:T(8,128)(2,1)S(1)}) custom-call(s32[2,4]{1,0:T(2,128)S(1)} %pad_add_fusion.1.range_ref, bf16[1024,128]{1,0:T(8,128)(2,1)S(1)} %slice.319.query_ref, bf16[1024,256]{1,0:T(8,128)(2,1)} %collective-permute-done.5.before_ref, ...), custom_call_target="tpu_custom_call" | custom-call | flops 2684354560 | bytes 4194304 | tf_op jit(solution)/shard_map/pallas_call | solution.py:284
  273.3 5.7 %collective-permute-start.28 = (bf16[1024,256]{1,0:T(8,128)(2,1)S(1)}, bf16[1024,256]{1,0:T(8,128)(2,1)S(1)}, u32[]{:S(2)}, u32[]{:S(2)}) collective-permute-start(bf16[1024,256]{1,0:T(8,128)(2,1)S(1)} %get-tuple-element.32), channel_id=1, source_target_pairs={{0,8},{1,9},{2,10},{3,11},{4,12},{5,13},{6,14},{7,15},{8,16},{9,17... | collective-permute-start | bytes 1572872 | tf_op jit(solution)/shard_map/ppermute | solution.py:32
  279.0 13.5 %collective-permute-done.27 = bf16[1024,256]{1,0:T(8,128)(2,1)S(1)} collective-permute-done((bf16[1024,256]{1,0:T(8,128)(2,1)S(1)}, bf16[1024,256]{1,0:T(8,128)(2,1)S(1)}, u32[]{:S(2)}, u32[]{:S(2)}) %collective-permute-start.27) | collective-permute-done | bytes 524320 | tf_op jit(solution)/shard_map/ppermute | solution.py:32
  295.1 4.4 all-to-all-start.9
  299.4 3.2 fusion.56
  302.7 5.0 %gather_fusion = f32[8,128,1024]{2,1,0:T(8,128)} fusion(f32[8,128,1024]{2,1,0:T(8,128)} %fusion.56, s32[1024]{0:T(1024)S(1)} %pad_clamp_fusion), kind=kCustom, calls=%fused_computation | custom fusion | bytes 8388640 | tf_op jit(solution)/shard_map/jit(_take)/gather | solution.py:441
  307.7 5.2 %broadcast_select_fusion = f32[8,128,1024]{2,1,0:T(8,128)} fusion(f32[8,128,1024]{2,1,0:T(8,128)} %gather_fusion, pred[8]{0:T(512)(128)(4,1)S(1)} %get-tuple-element.70), kind=kLoop, calls=%fused_computation.12 | loop fusion | flops 1048576 | bytes 8388616 | tf_op jit(solution)/shard_map/jit(_take)/select_n | solution.py:441
  317.9 8.2 %all-to-all-done.9 = bf16[8,128,1024]{2,1,0:T(8,128)(2,1)} async-done(((bf16[8,128,1024]{2,1,0:T(8,128)(2,1)}), bf16[8,128,1024]{2,1,0:T(8,128)(2,1)}, u32[]{:S(2)}, u32[]{:S(2)}) %all-to-all-start.9) | async-done | bytes 2097184 | tf_op jit(solution)/shard_map/all_to_all | solution.py:48
  326.1 4.4 all-to-all-start.11
  337.1 6.8 %collective-permute-done.32 = bf16[64,1024]{1,0:T(8,128)(2,1)S(1)} collective-permute-done((bf16[64,1024]{1,0:T(8,128)(2,1)}, bf16[64,1024]{1,0:T(8,128)(2,1)S(1)}, u32[]{:S(2)}, u32[]{:S(2)}) %collective-permute-start.32) | collective-permute-done | bytes 131104 | tf_op jit(solution)/shard_map/ppermute | solution.py:27
  348.3 2.8 convolution_convert_fusion.3
  351.1 5.1 %collective-permute-done.33 = bf16[128,1024]{1,0:T(8,128)(2,1)S(1)} collective-permute-done((bf16[128,1024]{1,0:T(8,128)(2,1)S(1)}, bf16[128,1024]{1,0:T(8,128)(2,1)S(1)}, u32[]{:S(2)}, u32[]{:S(2)}) %collective-permute-start.33) | collective-permute-done | bytes 262176 | tf_op jit(solution)/shard_map/ppermute | solution.py:27
  360.1 5.0 %all-to-all-start.10 = ((bf16[4,32,1024]{2,1,0:T(8,128)(2,1)}), bf16[4,32,1024]{2,1,0:T(8,128)(2,1)S(1)}, u32[]{:S(2)}, u32[]{:S(2)}) async-start(bf16[4,32,1024]{2,1,0:T(8,128)(2,1)} %bitcast.244), calls=%async_computation.10 | async-start | bytes 524288 | tf_op jit(solution)/shard_map/all_to_all | solution.py:48
  377.9 5.1 %all-to-all-done.13 = f32[32,1,288]{2,1,0:T(1,128)S(1)} async-done(((f32[32,1,288]{2,1,0:T(1,128)}), f32[32,1,288]{2,1,0:T(1,128)S(1)}, u32[]{:S(2)}, u32[]{:S(2)}) %all-to-all-start.13) | async-done | bytes 36896 | tf_op jit(solution)/shard_map/all_to_all | solution.py:48
  383.1 3.3 all-to-all-start.8
  397.7 12.6 %all-to-all-done.8 = bf16[32,32,384]{2,1,0:T(8,128)(2,1)} async-done(((bf16[32,32,384]{2,1,0:T(8,128)(2,1)}), bf16[32,32,384]{2,1,0:T(8,128)(2,1)}, u32[]{:S(2)}, u32[]{:S(2)}) %all-to-all-start.8) | async-done | bytes 786464 | tf_op jit(solution)/shard_map/all_to_all | solution.py:48
  421.5 3.1 all-to-all-start.14
  426.8 4.9 %all-to-all-done.14 = f32[32,1,128]{2,1,0:T(1,128)S(1)} async-done(((f32[32,1,128]{2,1,0:T(1,128)}), f32[32,1,128]{2,1,0:T(1,128)S(1)}, u32[]{:S(2)}, u32[]{:S(2)}) %all-to-all-start.14) | async-done | bytes 16416 | tf_op jit(solution)/shard_map/all_to_all | solution.py:48
  (302 shorter events, 149.4 us)
Async XLA Ops:
  2.1 14.6 %all-to-all-start = ((bf16[32,2,144]{2,1,0:T(2,128)(2,1)}), bf16[32,2,144]{2,1,0:T(2,128)(2,1)S(1)}, u32[]{:S(2)}, u32[]{:S(2)}) async-start(bf16[32,2,144]{2,1,0:T(2,128)(2,1)} %reshape.374), calls=%async_computation | async-start | bytes 65536 | tf_op jit(solution)/shard_map/all_to_all | solution.py:48
  17.4 12.8 %all-to-all-start.3 = ((bf16[4,32,1024]{2,1,0:T(8,128)(2,1)}), bf16[4,32,1024]{2,1,0:T(8,128)(2,1)S(1)}, u32[]{:S(2)}, u32[]{:S(2)}) async-start(bf16[4,32,1024]{2,1,0:T(8,128)(2,1)} %broadcast_in_dim.55), calls=%async_computation.3 | async-start | bytes 524288 | tf_op jit(solution)/shard_map/all_to_all | solution.py:48
  31.2 29.2 %all-to-all-start.1 = ((bf16[32,32,384]{2,1,0:T(8,128)(2,1)}), bf16[32,32,384]{2,1,0:T(8,128)(2,1)S(1)}, u32[]{:S(2)}, u32[]{:S(2)}) async-start(bf16[32,32,384]{2,1,0:T(8,128)(2,1)} %bitcast.13), calls=%async_computation.1 | async-start | bytes 1572864 | tf_op jit(solution)/shard_map/all_to_all | solution.py:48
  33.8 15.9 %collective-permute-start.1 = (bf16[128,1024]{1,0:T(8,128)(2,1)S(1)}, bf16[128,1024]{1,0:T(8,128)(2,1)S(1)}, u32[]{:S(2)}, u32[]{:S(2)}) collective-permute-start(bf16[128,1024]{1,0:T(8,128)(2,1)S(1)} %copy-done.6), channel_id=1, source_target_pairs={{0,4},{1,5},{2,6},{3,7},{4,0},{5,1},{6,2},{7,3},{8,12},{9,13},{10,... | collective-permute-start | bytes 786440 | tf_op jit(solution)/shard_map/ppermute | solution.py:27
  35.6 15.8 %collective-permute-start = (bf16[128,1024]{1,0:T(8,128)(2,1)S(1)}, bf16[128,1024]{1,0:T(8,128)(2,1)S(1)}, u32[]{:S(2)}, u32[]{:S(2)}) collective-permute-start(bf16[128,1024]{1,0:T(8,128)(2,1)S(1)} %copy-done.6), channel_id=1, source_target_pairs={{0,2},{1,3},{2,0},{3,1},{4,6},{5,7},{6,4},{7,5},{8,10},{9,11},{10,... | collective-permute-start | bytes 786440 | tf_op jit(solution)/shard_map/ppermute | solution.py:27
  37.0 88.9 %collective-permute-start.18 = (bf16[128,1024]{1,0:T(8,128)(2,1)}, bf16[128,1024]{1,0:T(8,128)(2,1)}, u32[]{:S(2)}, u32[]{:S(2)}) collective-permute-start(bf16[128,1024]{1,0:T(8,128)(2,1)} %param.21), channel_id=1, source_target_pairs={{0,4},{1,5},{2,6},{3,7},{4,0},{5,1},{6,2},{7,3},{8,12},{9,13},{10,... | collective-permute-start | bytes 786440 | tf_op jit(solution)/shard_map/ppermute | solution.py:27
  37.6 91.1 %collective-permute-start.17 = (bf16[128,1024]{1,0:T(8,128)(2,1)}, bf16[128,1024]{1,0:T(8,128)(2,1)}, u32[]{:S(2)}, u32[]{:S(2)}) collective-permute-start(bf16[128,1024]{1,0:T(8,128)(2,1)} %param.21), channel_id=1, source_target_pairs={{0,2},{1,3},{2,0},{3,1},{4,6},{5,7},{6,4},{7,5},{8,10},{9,11},{10,... | collective-permute-start | bytes 786440 | tf_op jit(solution)/shard_map/ppermute | solution.py:27
  49.8 9.2 %collective-permute-start.3 = (bf16[64,1024]{1,0:T(8,128)(2,1)S(1)}, bf16[64,1024]{1,0:T(8,128)(2,1)S(1)}, u32[]{:S(2)}, u32[]{:S(2)}) collective-permute-start(bf16[64,1024]{1,0:T(8,128)(2,1)S(1)} %slice.316), channel_id=1, source_target_pairs={{0,2},{1,3},{2,0},{3,1},{4,6},{5,7},{6,4},{7,5},{8,10},{9,11},{10,... | collective-permute-start | bytes 393224 | tf_op jit(solution)/shard_map/ppermute | solution.py:27
  51.4 7.7 %collective-permute-start.2 = (bf16[64,1024]{1,0:T(8,128)(2,1)S(1)}, bf16[64,1024]{1,0:T(8,128)(2,1)S(1)}, u32[]{:S(2)}, u32[]{:S(2)}) collective-permute-start(bf16[64,1024]{1,0:T(8,128)(2,1)S(1)} %slice.315), channel_id=1, source_target_pairs={{0,4},{1,5},{2,6},{3,7},{4,0},{5,1},{6,2},{7,3},{8,12},{9,13},{10,... | collective-permute-start | bytes 393224 | tf_op jit(solution)/shard_map/ppermute | solution.py:27
  60.3 6.9 %collective-permute-start.4 = (bf16[4,128,1024]{2,1,0:T(8,128)(2,1)}, bf16[4,128,1024]{2,1,0:T(8,128)(2,1)}, u32[]{:S(2)}, u32[]{:S(2)}) collective-permute-start(bf16[4,128,1024]{2,1,0:T(8,128)(2,1)} %get-tuple-element.102), channel_id=1, source_target_pairs={{0,1},{1,0},{2,3},{3,2},{4,5},{5,4},{6,7},{7,6},{8,9},{9,8},{10,11... | collective-permute-start | bytes 3145736 | tf_op jit(solution)/shard_map/ppermute | solution.py:27
  62.0 44.1 %all-to-all-start.4 = ((bf16[8,4,32,1024]{3,2,1,0:T(8,128)(2,1)}), bf16[8,4,32,1024]{3,2,1,0:T(8,128)(2,1)}, u32[]{:S(2)}, u32[]{:S(2)}) async-start(bf16[8,4,32,1024]{3,2,1,0:T(8,128)(2,1)} %broadcast_in_dim.98), calls=%async_computation.4 | async-start | bytes 4194304 | tf_op jit(solution)/shard_map/all_to_all | solution.py:48
  74.6 16.2 %collective-permute-start.6 = (bf16[1024,256]{1,0:T(8,128)(2,1)S(1)}, bf16[1024,256]{1,0:T(8,128)(2,1)S(1)}, u32[]{:S(2)}, u32[]{:S(2)}) collective-permute-start(bf16[1024,256]{1,0:T(8,128)(2,1)S(1)} %slice.320.own_ref), channel_id=1, source_target_pairs={{8,0},{9,1},{10,2},{11,3},{12,4},{13,5},{14,6},{15,7},{16,8},{17,9... | collective-permute-start | bytes 1572872 | tf_op jit(solution)/shard_map/ppermute | solution.py:32
  75.9 16.1 %collective-permute-start.5 = (bf16[1024,256]{1,0:T(8,128)(2,1)S(1)}, bf16[1024,256]{1,0:T(8,128)(2,1)}, u32[]{:S(2)}, u32[]{:S(2)}) collective-permute-start(bf16[1024,256]{1,0:T(8,128)(2,1)S(1)} %slice.320.own_ref), channel_id=1, source_target_pairs={{0,8},{1,9},{2,10},{3,11},{4,12},{5,13},{6,14},{7,15},{8,16},{9,17... | collective-permute-start | bytes 1572872 | tf_op jit(solution)/shard_map/ppermute | solution.py:32
  106.1 11.0 %all-to-all-start.2 = ((bf16[8,128,128]{1,2,0:T(8,128)(2,1)}), bf16[8,128,128]{1,2,0:T(8,128)(2,1)}, u32[]{:S(2)}, u32[]{:S(2)}) async-start(bf16[8,128,128]{1,2,0:T(8,128)(2,1)} %copy.66), calls=%async_computation.2 | async-start | bytes 524288 | tf_op jit(solution)/shard_map/all_to_all | solution.py:48
  118.2 36.7 %all-to-all-start.5 = ((bf16[32,32,512]{2,1,0:T(8,128)(2,1)}), bf16[32,32,512]{2,1,0:T(8,128)(2,1)}, u32[]{:S(2)}, u32[]{:S(2)}) async-start(bf16[32,32,512]{2,1,0:T(8,128)(2,1)} %bitcast.236), calls=%async_computation.5 | async-start | bytes 2097152 | tf_op jit(solution)/shard_map/all_to_all | solution.py:48
  126.9 13.4 %collective-permute-start.20 = (bf16[64,1024]{1,0:T(8,128)(2,1)S(1)}, bf16[64,1024]{1,0:T(8,128)(2,1)S(1)}, u32[]{:S(2)}, u32[]{:S(2)}) collective-permute-start(bf16[64,1024]{1,0:T(8,128)(2,1)S(1)} %slice.337), channel_id=1, source_target_pairs={{0,2},{1,3},{2,0},{3,1},{4,6},{5,7},{6,4},{7,5},{8,10},{9,11},{10,... | collective-permute-start | bytes 393224 | tf_op jit(solution)/shard_map/ppermute | solution.py:27
  129.6 10.7 %collective-permute-start.19 = (bf16[64,1024]{1,0:T(8,128)(2,1)S(1)}, bf16[64,1024]{1,0:T(8,128)(2,1)S(1)}, u32[]{:S(2)}, u32[]{:S(2)}) collective-permute-start(bf16[64,1024]{1,0:T(8,128)(2,1)S(1)} %slice.336), channel_id=1, source_target_pairs={{0,4},{1,5},{2,6},{3,7},{4,0},{5,1},{6,2},{7,3},{8,12},{9,13},{10,... | collective-permute-start | bytes 393224 | tf_op jit(solution)/shard_map/ppermute | solution.py:27
  135.0 11.8 %collective-permute-start.7 = (bf16[128,1024]{1,0:T(8,128)(2,1)S(1)}, bf16[128,1024]{1,0:T(8,128)(2,1)S(1)}, u32[]{:S(2)}, u32[]{:S(2)}) collective-permute-start(bf16[128,1024]{1,0:T(8,128)(2,1)S(1)} %add_convert_fusion.2), channel_id=1, source_target_pairs={{0,2},{1,3},{2,0},{3,1},{4,6},{5,7},{6,4},{7,5},{8,10},{9,11},{10,... | collective-permute-start | bytes 786440 | tf_op jit(solution)/shard_map/ppermute | solution.py:27
  135.6 12.4 %collective-permute-start.8 = (bf16[128,1024]{1,0:T(8,128)(2,1)S(1)}, bf16[128,1024]{1,0:T(8,128)(2,1)S(1)}, u32[]{:S(2)}, u32[]{:S(2)}) collective-permute-start(bf16[128,1024]{1,0:T(8,128)(2,1)S(1)} %add_convert_fusion.2), channel_id=1, source_target_pairs={{0,4},{1,5},{2,6},{3,7},{4,0},{5,1},{6,2},{7,3},{8,12},{9,13},{10,... | collective-permute-start | bytes 786440 | tf_op jit(solution)/shard_map/ppermute | solution.py:27
  142.9 20.1 %collective-permute-start.21 = (bf16[4,128,1024]{2,1,0:T(8,128)(2,1)}, bf16[4,128,1024]{2,1,0:T(8,128)(2,1)}, u32[]{:S(2)}, u32[]{:S(2)}) collective-permute-start(bf16[4,128,1024]{2,1,0:T(8,128)(2,1)} %get-tuple-element.100), channel_id=1, source_target_pairs={{0,1},{1,0},{2,3},{3,2},{4,5},{5,4},{6,7},{7,6},{8,9},{9,8},{10,11... | collective-permute-start | bytes 3145736 | tf_op jit(solution)/shard_map/ppermute | solution.py:27
  146.8 6.2 %collective-permute-start.9 = (bf16[64,1024]{1,0:T(8,128)(2,1)S(1)}, bf16[64,1024]{1,0:T(8,128)(2,1)S(1)}, u32[]{:S(2)}, u32[]{:S(2)}) collective-permute-start(bf16[64,1024]{1,0:T(8,128)(2,1)S(1)} %slice.323), channel_id=1, source_target_pairs={{0,4},{1,5},{2,6},{3,7},{4,0},{5,1},{6,2},{7,3},{8,12},{9,13},{10,... | collective-permute-start | bytes 393224 | tf_op jit(solution)/shard_map/ppermute | solution.py:27
  154.9 11.2 %collective-permute-start.11 = (bf16[4,128,1024]{2,1,0:T(8,128)(2,1)}, bf16[4,128,1024]{2,1,0:T(8,128)(2,1)}, u32[]{:S(2)}, u32[]{:S(2)}) collective-permute-start(bf16[4,128,1024]{2,1,0:T(8,128)(2,1)} %get-tuple-element.98), channel_id=1, source_target_pairs={{0,1},{1,0},{2,3},{3,2},{4,5},{5,4},{6,7},{7,6},{8,9},{9,8},{10,11... | collective-permute-start | bytes 3145736 | tf_op jit(solution)/shard_map/ppermute | solution.py:27
  156.0 32.4 %all-to-all-start.6 = ((bf16[4,128,1024]{2,1,0:T(8,128)(2,1)}), bf16[4,128,1024]{2,1,0:T(8,128)(2,1)}, u32[]{:S(2)}, u32[]{:S(2)}) async-start(bf16[4,128,1024]{2,1,0:T(8,128)(2,1)} %broadcast_in_dim.101), calls=%async_computation.6 | async-start | bytes 2097152 | tf_op jit(solution)/shard_map/all_to_all | solution.py:48
  203.0 12.3 %collective-permute-start.22 = (bf16[4,128,1024]{2,1,0:T(8,128)(2,1)}, bf16[4,128,1024]{2,1,0:T(8,128)(2,1)}, u32[]{:S(2)}, u32[]{:S(2)}) collective-permute-start(bf16[4,128,1024]{2,1,0:T(8,128)(2,1)} %bitcast.52), channel_id=1, source_target_pairs={{0,1},{1,0},{2,3},{3,2},{4,5},{5,4},{6,7},{7,6},{8,9},{9,8},{10,11... | collective-permute-start | bytes 3145736 | tf_op jit(solution)/shard_map/ppermute | solution.py:27
  212.0 7.5 %collective-permute-start.12 = (bf16[4,128,1024]{2,1,0:T(8,128)(2,1)}, bf16[4,128,1024]{2,1,0:T(8,128)(2,1)}, u32[]{:S(2)}, u32[]{:S(2)}) collective-permute-start(bf16[4,128,1024]{2,1,0:T(8,128)(2,1)} %bitcast.36), channel_id=1, source_target_pairs={{0,1},{1,0},{2,3},{3,2},{4,5},{5,4},{6,7},{7,6},{8,9},{9,8},{10,11... | collective-permute-start | bytes 3145736 | tf_op jit(solution)/shard_map/ppermute | solution.py:27
  218.7 6.5 %collective-permute-start.25 = (bf16[64,1024]{1,0:T(8,128)(2,1)S(1)}, bf16[64,1024]{1,0:T(8,128)(2,1)S(1)}, u32[]{:S(2)}, u32[]{:S(2)}) collective-permute-start(bf16[64,1024]{1,0:T(8,128)(2,1)S(1)} %get-tuple-element.91), channel_id=1, source_target_pairs={{0,2},{1,3},{2,0},{3,1},{4,6},{5,7},{6,4},{7,5},{8,10},{9,11},{10,... | collective-permute-start | bytes 393224 | tf_op jit(solution)/shard_map/ppermute | solution.py:27
  219.3 5.9 %collective-permute-start.23 = (bf16[64,1024]{1,0:T(8,128)(2,1)S(1)}, bf16[64,1024]{1,0:T(8,128)(2,1)S(1)}, u32[]{:S(2)}, u32[]{:S(2)}) collective-permute-start(bf16[64,1024]{1,0:T(8,128)(2,1)S(1)} %get-tuple-element.92), channel_id=1, source_target_pairs={{0,4},{1,5},{2,6},{3,7},{4,0},{5,1},{6,2},{7,3},{8,12},{9,13},{10,... | collective-permute-start | bytes 393224 | tf_op jit(solution)/shard_map/ppermute | solution.py:27
  223.7 6.4 %collective-permute-start.13 = (bf16[64,1024]{1,0:T(8,128)(2,1)S(1)}, bf16[64,1024]{1,0:T(8,128)(2,1)S(1)}, u32[]{:S(2)}, u32[]{:S(2)}) collective-permute-start(bf16[64,1024]{1,0:T(8,128)(2,1)S(1)} %get-tuple-element.96), channel_id=1, source_target_pairs={{0,4},{1,5},{2,6},{3,7},{4,0},{5,1},{6,2},{7,3},{8,12},{9,13},{10,... | collective-permute-start | bytes 393224 | tf_op jit(solution)/shard_map/ppermute | solution.py:27
  225.3 10.5 %collective-permute-start.26 = (bf16[128,1024]{1,0:T(8,128)(2,1)S(1)}, bf16[128,1024]{1,0:T(8,128)(2,1)S(1)}, u32[]{:S(2)}, u32[]{:S(2)}) collective-permute-start(bf16[128,1024]{1,0:T(8,128)(2,1)S(1)} %pad_maximum_fusion.10), channel_id=1, source_target_pairs={{0,4},{1,5},{2,6},{3,7},{4,0},{5,1},{6,2},{7,3},{8,12},{9,13},{10,... | collective-permute-start | bytes 786440 | tf_op jit(solution)/shard_map/ppermute | solution.py:27
  225.9 9.8 %collective-permute-start.24 = (bf16[128,1024]{1,0:T(8,128)(2,1)S(1)}, bf16[128,1024]{1,0:T(8,128)(2,1)S(1)}, u32[]{:S(2)}, u32[]{:S(2)}) collective-permute-start(bf16[128,1024]{1,0:T(8,128)(2,1)S(1)} %pad_maximum_fusion.9), channel_id=1, source_target_pairs={{0,2},{1,3},{2,0},{3,1},{4,6},{5,7},{6,4},{7,5},{8,10},{9,11},{10,... | collective-permute-start | bytes 786440 | tf_op jit(solution)/shard_map/ppermute | solution.py:27
  230.2 9.8 %collective-permute-start.16 = (bf16[128,1024]{1,0:T(8,128)(2,1)S(1)}, bf16[128,1024]{1,0:T(8,128)(2,1)S(1)}, u32[]{:S(2)}, u32[]{:S(2)}) collective-permute-start(bf16[128,1024]{1,0:T(8,128)(2,1)S(1)} %pad_maximum_fusion.8), channel_id=1, source_target_pairs={{0,4},{1,5},{2,6},{3,7},{4,0},{5,1},{6,2},{7,3},{8,12},{9,13},{10,... | collective-permute-start | bytes 786440 | tf_op jit(solution)/shard_map/ppermute | solution.py:27
  231.8 8.3 %collective-permute-start.14 = (bf16[128,1024]{1,0:T(8,128)(2,1)S(1)}, bf16[128,1024]{1,0:T(8,128)(2,1)S(1)}, u32[]{:S(2)}, u32[]{:S(2)}) collective-permute-start(bf16[128,1024]{1,0:T(8,128)(2,1)S(1)} %pad_maximum_fusion.7), channel_id=1, source_target_pairs={{0,2},{1,3},{2,0},{3,1},{4,6},{5,7},{6,4},{7,5},{8,10},{9,11},{10,... | collective-permute-start | bytes 786440 | tf_op jit(solution)/shard_map/ppermute | solution.py:27
  243.7 10.3 %all-to-all-start.7 = ((bf16[8,128,128]{2,1,0:T(8,128)(2,1)}), bf16[8,128,128]{2,1,0:T(8,128)(2,1)S(1)}, u32[]{:S(2)}, u32[]{:S(2)}) async-start(bf16[8,128,128]{2,1,0:T(8,128)(2,1)} %bitcast.246), calls=%async_computation.7 | async-start | bytes 524288 | tf_op jit(solution)/shard_map/all_to_all | solution.py:48
  254.0 38.8 %all-to-all-start.12 = ((bf16[4,128,1024]{2,1,0:T(8,128)(2,1)}), bf16[4,128,1024]{2,1,0:T(8,128)(2,1)}, u32[]{:S(2)}, u32[]{:S(2)}) async-start(bf16[4,128,1024]{2,1,0:T(8,128)(2,1)} %bitcast.237), calls=%async_computation.12 | async-start | bytes 2097152 | tf_op jit(solution)/shard_map/all_to_all | solution.py:48
  272.0 20.5 %collective-permute-start.27 = (bf16[1024,256]{1,0:T(8,128)(2,1)S(1)}, bf16[1024,256]{1,0:T(8,128)(2,1)S(1)}, u32[]{:S(2)}, u32[]{:S(2)}) collective-permute-start(bf16[1024,256]{1,0:T(8,128)(2,1)S(1)} %get-tuple-element.31), channel_id=1, source_target_pairs={{8,0},{9,1},{10,2},{11,3},{12,4},{13,5},{14,6},{15,7},{16,8},{17,9... | collective-permute-start | bytes 1572872 | tf_op jit(solution)/shard_map/ppermute | solution.py:32
  273.3 19.2 %collective-permute-start.28 = (bf16[1024,256]{1,0:T(8,128)(2,1)S(1)}, bf16[1024,256]{1,0:T(8,128)(2,1)S(1)}, u32[]{:S(2)}, u32[]{:S(2)}) collective-permute-start(bf16[1024,256]{1,0:T(8,128)(2,1)S(1)} %get-tuple-element.32), channel_id=1, source_target_pairs={{0,8},{1,9},{2,10},{3,11},{4,12},{5,13},{6,14},{7,15},{8,16},{9,17... | collective-permute-start | bytes 1572872 | tf_op jit(solution)/shard_map/ppermute | solution.py:32
  295.1 31.0 %all-to-all-start.9 = ((bf16[8,128,1024]{2,1,0:T(8,128)(2,1)}), bf16[8,128,1024]{2,1,0:T(8,128)(2,1)}, u32[]{:S(2)}, u32[]{:S(2)}) async-start(bf16[8,128,1024]{2,1,0:T(8,128)(2,1)} %broadcast_in_dim.105), calls=%async_computation.9 | async-start | bytes 4194304 | tf_op jit(solution)/shard_map/all_to_all | solution.py:48
  314.8 15.6 %collective-permute-start.29 = (bf16[4,128,1024]{2,1,0:T(8,128)(2,1)S(1)}, bf16[4,128,1024]{2,1,0:T(8,128)(2,1)}, u32[]{:S(2)}, u32[]{:S(2)}) collective-permute-start(bf16[4,128,1024]{2,1,0:T(8,128)(2,1)S(1)} %slice.430), channel_id=1, source_target_pairs={{0,1},{1,0},{2,3},{3,2},{4,5},{5,4},{6,7},{7,6},{8,9},{9,8},{10,11... | collective-permute-start | bytes 3145736 | tf_op jit(solution)/shard_map/ppermute | solution.py:27
  326.1 34.0 %all-to-all-start.11 = ((bf16[32,32,512]{2,1,0:T(8,128)(2,1)}), bf16[32,32,512]{2,1,0:T(8,128)(2,1)}, u32[]{:S(2)}, u32[]{:S(2)}) async-start(bf16[32,32,512]{2,1,0:T(8,128)(2,1)} %bitcast.76), calls=%async_computation.11 | async-start | bytes 2097152 | tf_op jit(solution)/shard_map/all_to_all | solution.py:48
  333.5 10.4 %collective-permute-start.32 = (bf16[64,1024]{1,0:T(8,128)(2,1)}, bf16[64,1024]{1,0:T(8,128)(2,1)S(1)}, u32[]{:S(2)}, u32[]{:S(2)}) collective-permute-start(bf16[64,1024]{1,0:T(8,128)(2,1)} %get-tuple-element.87), channel_id=1, source_target_pairs={{0,2},{1,3},{2,0},{3,1},{4,6},{5,7},{6,4},{7,5},{8,10},{9,11},{10,... | collective-permute-start | bytes 393224 | tf_op jit(solution)/shard_map/ppermute | solution.py:27
  335.2 8.7 %collective-permute-start.30 = (bf16[64,1024]{1,0:T(8,128)(2,1)S(1)}, bf16[64,1024]{1,0:T(8,128)(2,1)}, u32[]{:S(2)}, u32[]{:S(2)}) collective-permute-start(bf16[64,1024]{1,0:T(8,128)(2,1)S(1)} %get-tuple-element.88), channel_id=1, source_target_pairs={{0,4},{1,5},{2,6},{3,7},{4,0},{5,1},{6,2},{7,3},{8,12},{9,13},{10,... | collective-permute-start | bytes 393224 | tf_op jit(solution)/shard_map/ppermute | solution.py:27
  345.6 10.6 %collective-permute-start.33 = (bf16[128,1024]{1,0:T(8,128)(2,1)S(1)}, bf16[128,1024]{1,0:T(8,128)(2,1)S(1)}, u32[]{:S(2)}, u32[]{:S(2)}) collective-permute-start(bf16[128,1024]{1,0:T(8,128)(2,1)S(1)} %pad_maximum_fusion.12), channel_id=1, source_target_pairs={{0,4},{1,5},{2,6},{3,7},{4,0},{5,1},{6,2},{7,3},{8,12},{9,13},{10,... | collective-permute-start | bytes 786440 | tf_op jit(solution)/shard_map/ppermute | solution.py:27
  347.3 9.3 %collective-permute-start.31 = (bf16[128,1024]{1,0:T(8,128)(2,1)S(1)}, bf16[128,1024]{1,0:T(8,128)(2,1)S(1)}, u32[]{:S(2)}, u32[]{:S(2)}) collective-permute-start(bf16[128,1024]{1,0:T(8,128)(2,1)S(1)} %pad_maximum_fusion.11), channel_id=1, source_target_pairs={{0,2},{1,3},{2,0},{3,1},{4,6},{5,7},{6,4},{7,5},{8,10},{9,11},{10,... | collective-permute-start | bytes 786440 | tf_op jit(solution)/shard_map/ppermute | solution.py:27
  360.1 13.1 %all-to-all-start.10 = ((bf16[4,32,1024]{2,1,0:T(8,128)(2,1)}), bf16[4,32,1024]{2,1,0:T(8,128)(2,1)S(1)}, u32[]{:S(2)}, u32[]{:S(2)}) async-start(bf16[4,32,1024]{2,1,0:T(8,128)(2,1)} %bitcast.244), calls=%async_computation.10 | async-start | bytes 524288 | tf_op jit(solution)/shard_map/all_to_all | solution.py:48
  373.2 9.9 %all-to-all-start.13 = ((f32[32,1,288]{2,1,0:T(1,128)}), f32[32,1,288]{2,1,0:T(1,128)S(1)}, u32[]{:S(2)}, u32[]{:S(2)}) async-start(f32[32,1,288]{2,1,0:T(1,128)} %reshape.376), calls=%async_computation.13 | async-start | bytes 98304 | tf_op jit(solution)/shard_map/all_to_all | solution.py:48
  383.1 27.2 %all-to-all-start.8 = ((bf16[32,32,384]{2,1,0:T(8,128)(2,1)}), bf16[32,32,384]{2,1,0:T(8,128)(2,1)}, u32[]{:S(2)}, u32[]{:S(2)}) async-start(bf16[32,32,384]{2,1,0:T(8,128)(2,1)} %bitcast.250), calls=%async_computation.8 | async-start | bytes 1572864 | tf_op jit(solution)/shard_map/all_to_all | solution.py:48
  393.5 22.6 %collective-permute-start.34 = (f32[32,1024]{1,0:T(8,128)}, f32[32,1024]{1,0:T(8,128)}, u32[]{:S(2)}, u32[]{:S(2)}) collective-permute-start(f32[32,1024]{1,0:T(8,128)} %convert_reduce_fusion.4), channel_id=1, source_target_pairs={{0,0},{1,4},{2,8},{3,12},{4,16},{5,20},{6,24},{7,28},{8,1},{9,5},{... | collective-permute-start | bytes 393224 | tf_op jit(solution)/shard_map/ppermute | solution.py:434
  421.5 10.2 %all-to-all-start.14 = ((f32[32,1,128]{2,1,0:T(1,128)}), f32[32,1,128]{2,1,0:T(1,128)S(1)}, u32[]{:S(2)}, u32[]{:S(2)}) async-start(f32[32,1,128]{2,1,0:T(1,128)} %broadcast_in_dim.107), calls=%async_computation.14 | async-start | bytes 32768 | tf_op jit(solution)/shard_map/all_to_all | solution.py:48
  (45 other events, 287.3 us)

commit v2 on v1

v2 whole, which is shorter than its diff:
```python
import functools

import jax
import jax.numpy as jnp
from jax import lax
from jax.experimental import pallas as pl
from jax.experimental.pallas import tpu as pltpu
from jax.sharding import PartitionSpec as P

HEADS = 16
STEP = 10
EPSILON = 1e-05
MOMENTUM = 0.9
LEARNING_RATES = (60.0, 480.0, 60.0, 60.0, 600.0)
WEIGHT_DECAY = 0.0001
CLIP_NORM = 1.0
MASK_FLOOR = -1e30
PLANE = 8
EXTRA = 8
LANES = 128
QUERY_TILE = 256
KEY_TILE = 256
F32 = jnp.float32
LOW = jnp.bfloat16
WHOLE = pl.BlockSpec()
SMEM = pl.BlockSpec(memory_space=pltpu.SMEM)


def like(shape, dtype):
    return jax.ShapeDtypeStruct(shape, dtype)


def kernel_call(body, outs, *args, scalars=(), scratch=(), flops=0, limit=60):
    moved = sum(a.size * a.dtype.itemsize for a in list(args) + list(outs))
    return pl.pallas_call(
        body,
        in_specs=[SMEM] * len(scalars) + [WHOLE] * len(args),
        out_specs=[WHOLE] * len(outs),
        out_shape=list(outs),
        scratch_shapes=list(scratch),
        cost_estimate=pl.CostEstimate(flops=flops, bytes_accessed=moved, transcendentals=0),
        compiler_params=pltpu.CompilerParams(vmem_limit_bytes=limit << 20),
    )(*scalars, *args)


def after(value, *others):
    return lax.optimization_barrier((value, *others))[0]


def tie(*values):
    return lax.optimization_barrier(values)


def swap(block, bit):
    n = lax.axis_size("seq")
    return lax.ppermute(block, "seq", [(i, i ^ bit) for i in range(n)])


def move(block, distance):
    n = lax.axis_size("seq")
    return lax.ppermute(
        block, "seq", [(i, i + distance) for i in range(n) if 0 <= i + distance < n]
    )


def turn(block, planes_on):
    n = lax.axis_size("seq")
    return lax.ppermute(block, "seq", [(i, (i + planes_on * PLANE) % n) for i in range(n)])


def plane_groups():
    n = lax.axis_size("seq")
    return [[g * PLANE + j for j in range(PLANE)] for g in range(n // PLANE)]


def cross_groups():
    n = lax.axis_size("seq")
    return [[g * PLANE + j for g in range(n // PLANE)] for j in range(PLANE)]


def exchange(blocks, groups=None):
    return lax.all_to_all(blocks, "seq", 0, 0, axis_index_groups=groups)


def spread_sides(block):
    return swap(block, 2), swap(block, 4)


def spread_corner(across, along):
    half = across.shape[0] // 2
    return swap(across[:half], 4), swap(along[half:], 2)


def spread_far(block, sides, corner):
    far = swap(jnp.stack([block, *sides]), 1)
    return [block, *sides, *corner, far, *[swap(c, 1) for c in corner]]


def spread(block):
    sides = spread_sides(block)
    return spread_far(block, sides, spread_corner(*sides))


SPREAD = 8


def join(refs, out):
    number = refs[0].shape[0]
    place = 0
    for ref in refs:
        if len(ref.shape) == 3:
            for m in range(ref.shape[0]):
                out[pl.ds(place, number), :] = ref[m]
                place += number
        else:
            out[pl.ds(place, ref.shape[0]), :] = ref[...]
            place += ref.shape[0]


def collect(near, far, far_corner):
    half = near.shape[1] // 2
    came_corner = swap(far_corner, 1)
    came = swap(far, 1)
    corner = (near[3] + came_corner.astype(F32)).astype(LOW)
    by_across = swap(corner[:half], 2).astype(F32)
    by_along = swap(corner[half:], 4).astype(F32)
    across = near[1] + came[1].astype(F32)
    along = near[2] + came[2].astype(F32)
    across = jnp.concatenate([across[:half], across[half:] + by_along], axis=0).astype(LOW)
    along = jnp.concatenate([along[:half] + by_across, along[half:]], axis=0).astype(LOW)
    return near[0] + came[0].astype(F32), swap(across, 2), swap(along, 4)


def put_block(outs, k, m, value):
    if k == 0:
        outs[0][m] = value
    elif m < 3:
        outs[1][m] = value.astype(LOW)
    else:
        outs[2][...] = value.astype(LOW)


def total(terms):
    return terms[0] + terms[1].astype(F32) + terms[2].astype(F32)


def norm_parts(values):
    centre = values - jnp.mean(values, axis=-1, keepdims=True)
    spread_of = jnp.mean(centre * centre, axis=-1, keepdims=True)
    inverse = lax.rsqrt(spread_of + EPSILON)
    return centre * inverse, inverse


def norm_back(unit, inverse, gain, incoming):
    scaled = incoming * gain
    return inverse * (
        scaled
        - jnp.mean(scaled, axis=-1, keepdims=True)
        - unit * jnp.mean(scaled * unit, axis=-1, keepdims=True)
    )


def dot(a, b, dims=((1,), (0,))):
    return lax.dot_general(a, b, (dims, ((), ())), preferred_element_type=F32)


NT = ((1,), (1,))
TN = ((0,), (0,))


def block_rows(place, number):
    return pl.ds(pl.multiple_of(place * number, number), number)


def gather_planes(plane, refs, out):
    planes = len(refs)
    rows = refs[0].shape[0]
    for s, ref in enumerate(refs):
        out[block_rows(lax.rem(plane - s + planes, planes), rows), :] = ref[...]


def project_kernel(spot_ref, *refs):
    token_refs, refs = refs[:SPREAD], refs[SPREAD:]
    sent_ref, lots_ref, unit_ref, first_ref, pair_ref, weight_ref, vector_ref, held = refs
    spot = spot_ref[0]
    number, columns = token_refs[0].shape
    devices = sent_ref.shape[0]
    rows = columns // devices
    for d in range(devices):
        weight_ref[pl.ds(d * rows, rows), :] = sent_ref[d, :rows, :]
    for g in range(lots_ref.shape[0]):
        lanes = slice(g * LANES, (g + 1) * LANES)
        vector_ref[:EXTRA, lanes] = lots_ref[g, :, :LANES]
        vector_ref[EXTRA:, lanes] = lots_ref[g, :, LANES : 2 * LANES]
    join(token_refs, held)
    gain, shift = vector_ref[0:1, :], vector_ref[1:2, :]
    for r in range(PLANE):
        here = pl.ds(r * number, number)
        unit, _ = norm_parts(held[here, :].astype(F32))
        first = (unit * gain + shift).astype(LOW)
        unit_ref[here, :] = unit.astype(LOW)
        held[here, :] = first
        first_ref[block_rows(spot ^ relative(r), number), :] = first
    pairs = dot(held[...], weight_ref[...]).astype(LOW)
    for r in range(PLANE):
        pair_ref[block_rows(spot ^ relative(r), number), :] = pairs[r * number : (r + 1) * number]


def relative(r):
    return 2 * (r % 4) + r // 4


def head_mask(shape, head):
    return lax.broadcasted_iota(jnp.int32, shape, len(shape) - 1) // 64 == head


def attend_kernel(
    range_ref, query_ref, before_ref, own_ref, after_ref, span_ref, mixed_ref, low_ref, log_ref, keys, values
):
    step = pl.program_id(0)
    tokens = own_ref.shape[0]
    wide = query_ref.shape[1]

    @pl.when(step == 0)
    def _():
        for place, ref in enumerate((before_ref, own_ref, after_ref)):
            keys[pl.ds(place * tokens, tokens), :] = ref[:, :wide]
            values[:, pl.ds(place * tokens, tokens)] = ref[:, wide:].T

    queries = query_ref[...] * jnp.asarray(0.125, LOW)
    begin = span_ref[0:1, :]
    end = span_ref[1:2, :]
    here = query_ref.shape[0]
    split = [jnp.where(head_mask(queries.shape, h), queries, jnp.zeros_like(queries)) for h in range(2)]

    def body(index, carry):
        start = pl.multiple_of(index * KEY_TILE, KEY_TILE)
        block = keys[pl.ds(start, KEY_TILE), :]
        place = start + lax.broadcasted_iota(jnp.int32, (KEY_TILE, here), 0)
        allowed = (place >= begin) & (place < end)
        out = []
        for h in range(2):
            peak, whole, mixed = carry[h]
            scores = jnp.where(allowed, dot(block, split[h], NT), MASK_FLOOR)
            raised_peak = jnp.maximum(peak, jnp.max(scores, axis=0, keepdims=True))
            raised = jnp.exp(scores - raised_peak)
            fade = jnp.exp(peak - raised_peak)
            whole = whole * fade + jnp.sum(raised, axis=0, keepdims=True)
            turned = values[64 * h : 64 * h + 64, pl.ds(start, KEY_TILE)]
            mixed = mixed * fade + dot(turned, raised.astype(LOW))
            out.append((raised_peak, whole, mixed))
        return tuple(out)

    init = tuple(
        (jnp.full((1, here), MASK_FLOOR, F32), jnp.zeros((1, here), F32), jnp.zeros((64, here), F32))
        for _ in range(2)
    )
    done = lax.fori_loop(range_ref[0, step], range_ref[1, step], body, init)
    mixed = jnp.concatenate([m / t for _, t, m in done], axis=0).T
    mixed_ref[...] = mixed
    low_ref[...] = mixed.astype(LOW)
    log_ref[...] = jnp.concatenate([k + jnp.log(t) for k, t, _ in done], axis=0)


def attend_back_kernel(
    range_ref,
    query_ref,
    before_ref,
    own_ref,
    after_ref,
    span_ref,
    mixed_ref,
    log_ref,
    grad_ref,
    query_grad_ref,
    before_grad_ref,
    own_grad_ref,
    after_grad_ref,
    keys,
    values,
    turned_keys,
    key_grad,
    value_grad,
):
    step = pl.program_id(0)
    tokens = own_ref.shape[0]
    wide = query_ref.shape[1]

    @pl.when(step == 0)
    def _():
        for place, ref in enumerate((before_ref, own_ref, after_ref)):
            keys[pl.ds(place * tokens, tokens), :] = ref[:, :wide]
            values[pl.ds(place * tokens, tokens), :] = ref[:, wide:]
            turned_keys[:, pl.ds(place * tokens, tokens)] = ref[:, :wide].T
        key_grad[...] = jnp.zeros_like(key_grad)
        value_grad[...] = jnp.zeros_like(value_grad)

    queries = query_ref[...] * jnp.asarray(0.125, LOW)
    grads = grad_ref[...]
    here = queries.shape[0]
    zero = jnp.zeros_like(queries)
    split = [jnp.where(head_mask(queries.shape, h), queries, zero) for h in range(2)]
    split_grads = [jnp.where(head_mask(queries.shape, h), grads, zero) for h in range(2)]
    product = (grads.astype(F32) * mixed_ref[...]).T
    centred = [jnp.sum(product[64 * h : 64 * h + 64], axis=0, keepdims=True) for h in range(2)]
    begin = span_ref[0:1, :]
    end = span_ref[1:2, :]

    def body(index, carry):
        start = pl.multiple_of(index * KEY_TILE, KEY_TILE)
        rows = pl.ds(start, KEY_TILE)
        place = start + lax.broadcasted_iota(jnp.int32, (KEY_TILE, here), 0)
        allowed = (place >= begin) & (place < end)
        out, key_part, value_part = [], 0, 0
        for h in range(2):
            scores = dot(keys[rows, :], split[h], NT)
            shares = jnp.exp(jnp.where(allowed, scores - log_ref[h : h + 1, :], MASK_FLOOR))
            value_part += dot(shares.astype(LOW), split_grads[h])
            share_grad = dot(values[rows, :], split_grads[h], NT)
            score_grad = (shares * (share_grad - centred[h])).astype(LOW)
            key_part += dot(score_grad, split[h])
            out.append(carry[h] + dot(turned_keys[64 * h : 64 * h + 64, rows], score_grad))
        key_grad[rows, :] += key_part
        value_grad[rows, :] += value_part
        return tuple(out)

    init = tuple(jnp.zeros((64, here), F32) for _ in range(2))
    done = lax.fori_loop(range_ref[0, step], range_ref[1, step], body, init)
    query_grad_ref[...] = (jnp.concatenate(done, axis=0).T * 0.125).astype(LOW)

    @pl.when(step == pl.num_programs(0) - 1)
    def _():
        for place, ref in enumerate((before_grad_ref, own_grad_ref, after_grad_ref)):
            ref[:, :wide] = key_grad[pl.ds(place * tokens, tokens), :].astype(ref.dtype)
            ref[:, wide:] = value_grad[pl.ds(place * tokens, tokens), :].astype(ref.dtype)


def attention(ranges, queries, before, own, behind, spans):
    tokens, wide = queries.shape
    whole = lambda shape: pl.BlockSpec(shape, lambda i, s: (0, 0))
    tile = pl.BlockSpec((QUERY_TILE, wide), lambda i, s: (i, 0))
    row = pl.BlockSpec((2, QUERY_TILE), lambda i, s: (0, i))
    return pl.pallas_call(
        attend_kernel,
        grid_spec=pltpu.PrefetchScalarGridSpec(
            num_scalar_prefetch=1,
            grid=(tokens // QUERY_TILE,),
            in_specs=[tile] + [whole((tokens, 2 * wide))] * 3 + [row],
            out_specs=[tile, tile, row],
            scratch_shapes=[
                pltpu.VMEM((3 * tokens, wide), LOW),
                pltpu.VMEM((wide, 3 * tokens), LOW),
            ],
        ),
        out_shape=[like((tokens, wide), F32), like((tokens, wide), LOW), like((2, tokens), F32)],
        cost_estimate=pl.CostEstimate(
            flops=40 * tokens * tokens * wide, bytes_accessed=16 * tokens * wide, transcendentals=2 * tokens * tokens
        ),
        compiler_params=pltpu.CompilerParams(vmem_limit_bytes=60 << 20),
    )(ranges, queries, before, own, behind, spans)


def attention_back(ranges, queries, before, own, behind, spans, mixed, logs, grads):
    tokens, wide = queries.shape
    whole = lambda shape: pl.BlockSpec(shape, lambda i, s: (0, 0))
    tile = pl.BlockSpec((QUERY_TILE, wide), lambda i, s: (i, 0))
    row = pl.BlockSpec((2, QUERY_TILE), lambda i, s: (0, i))
    return pl.pallas_call(
        attend_back_kernel,
        grid_spec=pltpu.PrefetchScalarGridSpec(
            num_scalar_prefetch=1,
            grid=(tokens // QUERY_TILE,),
            in_specs=[tile] + [whole((tokens, 2 * wide))] * 3 + [row, tile, row, tile],
            out_specs=[tile] + [whole((tokens, 2 * wide))] * 3,
            scratch_shapes=[
                pltpu.VMEM((3 * tokens, wide), LOW),
                pltpu.VMEM((3 * tokens, wide), LOW),
                pltpu.VMEM((wide, 3 * tokens), LOW),
                pltpu.VMEM((3 * tokens, wide), F32),
                pltpu.VMEM((3 * tokens, wide), F32),
            ],
        ),
        out_shape=[
            like((tokens, wide), LOW),
            like((tokens, 2 * wide), LOW),
            like((tokens, 2 * wide), F32),
            like((tokens, 2 * wide), LOW),
        ],
        cost_estimate=pl.CostEstimate(
            flops=60 * tokens * tokens * wide, bytes_accessed=32 * tokens * wide, transcendentals=2 * tokens * tokens
        ),
        compiler_params=pltpu.CompilerParams(vmem_limit_bytes=60 << 20),
    )(ranges, queries, before, own, behind, spans, mixed, logs, grads)


def place_output(planes, place_ref, refs, held, out):
    if len(refs) == 1:
        out[...] = refs[0][...]
        return
    join(refs, held)
    rows = out.shape[0] // (PLANE * planes)
    for r in range(PLANE):
        for s in range(planes):
            device = lax.rem(place_ref[1] - s + planes, planes) * PLANE + (place_ref[0] ^ relative(r))
            out[block_rows(device, rows), :] = held[pl.ds((r * planes + s) * rows, rows), :]


def ordered_output(spot, plane, refs, planes):
    rows = refs[0].shape[0] // planes
    if rows % 16 == 0:
        return refs
    whole = jnp.concatenate([r.reshape(-1, r.shape[-1]) for r in refs], axis=0)
    whole = whole.reshape(PLANE, planes, rows, -1)
    device = jnp.arange(PLANE * planes)
    turns = (plane - device // PLANE) % planes
    bits = device % PLANE ^ spot
    return [whole[bits // 2 + 4 * (bits % 2), turns].reshape(PLANE * planes * rows, -1)]


def mix_out_kernel(planes, place_ref, mixed_ref, tokens_ref, vector_ref, *refs):
    output_refs, (second_ref, normed_ref, held, output) = refs[:-4], refs[-4:]
    place_output(planes, place_ref, output_refs, held, output)
    mixed = jnp.concatenate([mixed_ref[j] for j in range(PLANE)], axis=1)
    second = tokens_ref[...].astype(F32) + dot(mixed, output[...])
    second_ref[...] = second
    unit, _ = norm_parts(second)
    normed_ref[...] = (unit * vector_ref[2:3, :] + vector_ref[3:4, :]).astype(LOW)


def feed_kernel(planes, place_ref, *refs):
    normed_refs, refs = refs[:SPREAD], refs[SPREAD:]
    cot_refs, refs = refs[:SPREAD], refs[SPREAD:]
    shrink_refs, refs = refs[:planes], refs[planes:]
    expand_refs, refs = refs[:2], refs[2:]
    bias_ref, near_out, far_out, corner_out, active_ref, grad_ref, bias_out, expand, shrink, x, c = refs
    part = expand.shape[1] // 2
    expand[:, :part] = expand_refs[0][...]
    expand[:, part:] = expand_refs[1][...]
    gather_planes(place_ref[1], shrink_refs, shrink)
    join(normed_refs, x)
    join(cot_refs, c)
    number = near_out.shape[1]
    sums = jnp.zeros(bias_ref.shape, F32)
    for k, m in ((1, 2), (1, 0), (0, 2), (0, 0)):
        rows = pl.ds((4 * k + m) * number, 2 * number)
        upper = dot(x[rows, :], expand[...]) + bias_ref[...]
        share = 0.5 + 0.5 * lax.erf(upper * 0.7071067811865476)
        density = 0.3989422804014327 * jnp.exp(-0.5 * upper * upper)
        active_ref[rows, :] = (upper * share).astype(LOW)
        grad = (dot(c[rows, :], shrink[...], NT) * (share + upper * density)).astype(LOW)
        grad_ref[rows, :] = grad
        sums += jnp.sum(grad.astype(F32), axis=0, keepdims=True)
        down = dot(grad, expand[...], NT)
        put_block((near_out, far_out, corner_out), k, m, down[:number])
        put_block((near_out, far_out, corner_out), k, m + 1, down[number:])
    bias_out[...] = sums


def lower_kernel(planes, place_ref, active_ref, *refs):
    shrink_refs, (near_out, far_out, corner_out, shrink) = refs[:planes], refs[planes:]
    gather_planes(place_ref[1], shrink_refs, shrink)
    number = near_out.shape[1]
    for k, m in ((1, 2), (1, 0), (0, 2), (0, 0)):
        lower = dot(active_ref[pl.ds((4 * k + m) * number, 2 * number), :], shrink[...])
        put_block((near_out, far_out, corner_out), k, m, lower[:number])
        put_block((near_out, far_out, corner_out), k, m + 1, lower[number:])


def plane_blocks(plane, whole, outs):
    planes = len(outs)
    tall = whole.shape[0] // planes
    for s, out in enumerate(outs):
        out[...] = whole[block_rows(lax.rem(plane + s, planes), tall), :].astype(out.dtype)


def shrink_grad_kernel(place_ref, active_ref, *refs):
    cot_refs, outs, (whole, cotangents) = refs[:SPREAD], refs[SPREAD:-2], refs[-2:]
    join(cot_refs, cotangents)
    whole[...] = dot(active_ref[...], cotangents[...], TN)
    plane_blocks(place_ref[1], whole, outs)


def expand_grad_kernel(grad_ref, *refs):
    normed_refs, (out_ref, other_ref, normed) = refs[:SPREAD], refs[SPREAD:]
    join(normed_refs, normed)
    half = grad_ref.shape[1] // 2
    out_ref[...] = dot(normed[...], grad_ref[:, :half], TN).astype(LOW)
    other_ref[...] = dot(normed[...], grad_ref[:, half:], TN).astype(LOW)


def norm_two_back_kernel(
    planes, place_ref, one_ref, two_ref, three_ref, second_ref, cotangent_ref, vector_ref, *refs
):
    output_refs, (second_grad_ref, branch_ref, mixed_ref, sums_ref, held, output) = refs[:-6], refs[-6:]
    place_output(planes, place_ref, output_refs, held, output)
    incoming = one_ref[...] + two_ref[...].astype(F32) + three_ref[...].astype(F32)
    unit, inverse = norm_parts(second_ref[...])
    cotangent = cotangent_ref[...].astype(F32)
    second_grad = cotangent + norm_back(unit, inverse, vector_ref[2:3, :], incoming)
    second_grad_ref[...] = second_grad
    branch = second_grad.astype(LOW)
    branch_ref[...] = branch
    mixed = dot(branch, output[...], NT).astype(LOW)
    wide = mixed_ref.shape[2]
    for j in range(PLANE):
        mixed_ref[j] = mixed[:, wide * j : wide * j + wide]
    sums_ref[...] = jnp.concatenate(
        [
            jnp.sum(incoming * unit, axis=0, keepdims=True),
            jnp.sum(incoming, axis=0, keepdims=True),
            jnp.sum(cotangent, axis=0, keepdims=True),
        ],
        axis=0,
    )


def output_grad_kernel(place_ref, mixed_ref, *refs):
    branch_refs, outs, (whole, left, right) = refs[:SPREAD], refs[SPREAD:-3], refs[-3:]
    join(branch_refs, right)
    number = branch_refs[0].shape[0]
    for r in range(PLANE):
        left[pl.ds(r * number, number), :] = mixed_ref[block_rows(place_ref[0] ^ relative(r), number), :]
    whole[...] = dot(left[...], right[...], TN)
    if len(outs) == 1:
        outs[0][...] = whole[...].astype(LOW)
    else:
        plane_blocks(place_ref[1], whole, outs)


def first_back_kernel(
    place_ref, own_ref, from_after_ref, from_before_ref, query_ref, first_ref, unit_ref,
    pair_weight_ref, query_weight_ref, grad_ref, near_ref, far_ref, corner_ref, sums_ref, joined, weight,
):
    spot = place_ref[0]
    number, columns = near_ref.shape[1:]
    wide = query_ref.shape[1]
    pairs = (own_ref[...] + from_after_ref[...].astype(F32) + from_before_ref[...].astype(F32)).astype(LOW)
    joined[:, :wide] = query_ref[...]
    joined[:, wide:] = pairs
    weight[:, :wide] = query_weight_ref[...]
    weight[:, wide:] = pair_weight_ref[...]
    grad_ref[...] = dot(first_ref[...], joined[...], TN).astype(LOW)
    gain = jnp.zeros((1, columns), F32)
    shift = jnp.zeros((1, columns), F32)
    for k, m in ((1, 2), (1, 0), (0, 2), (0, 0)):
        part = jnp.concatenate(
            [joined[block_rows(spot ^ (2 * (m + i) + k), number), :] for i in range(2)], axis=0
        )
        down = dot(part, weight[...], NT)
        unit = unit_ref[pl.ds((4 * k + m) * number, 2 * number), :].astype(F32)
        gain += jnp.sum(down * unit, axis=0, keepdims=True)
        shift += jnp.sum(down, axis=0, keepdims=True)
        put_block((near_ref, far_ref, corner_ref), k, m, down[:number])
        put_block((near_ref, far_ref, corner_ref), k, m + 1, down[number:])
    sums_ref[...] = jnp.concatenate([gain, shift], axis=0)


def first_norm_back_kernel(one_ref, two_ref, three_ref, tokens_ref, second_grad_ref, vector_ref, out_ref):
    incoming = one_ref[...] + two_ref[...].astype(F32) + three_ref[...].astype(F32)
    unit, inverse = norm_parts(tokens_ref[...].astype(F32))
    out_ref[...] = (second_grad_ref[...] + norm_back(unit, inverse, vector_ref[0:1, :], incoming)).astype(LOW)


def sum_kernel(wide, *refs):
    part_refs, (grad_ref, square_ref) = refs[:-2], refs[-2:]
    rows = grad_ref.shape[0]
    square = jnp.zeros((rows, wide), F32)
    start = 0
    for ref in part_refs:
        for c in range(ref.shape[2] // wide):
            for j in range(PLANE):
                sources = range(j, ref.shape[0], PLANE)
                whole = sum(ref[d, :rows, c * wide : (c + 1) * wide].astype(F32) for d in sources)
                grad_ref[:, start : start + wide] = whole
                square += whole * whole
                start += wide
    square_ref[...] = jnp.sum(square, keepdims=True)


def sum_parts(wide, rows, *parts):
    if wide % LANES == 0:
        columns = PLANE * sum(p.shape[2] for p in parts)
        return kernel_call(
            functools.partial(sum_kernel, wide), [like((rows, columns), F32), like((1, 1), F32)], *parts
        )
    whole = jnp.concatenate([p[:, :rows] for p in parts], axis=2).astype(F32)
    whole = whole.reshape(-1, PLANE, rows, whole.shape[2] // wide, wide).sum(0)
    whole = whole.transpose(1, 2, 0, 3).reshape(rows, -1)
    return whole, jnp.sum(whole * whole).reshape(1, 1)


def update_kernel(factor_ref, *refs):
    factor = factor_ref[0]
    smooth_rate = min(0.999, (1.0 + STEP) / (10.0 + STEP))
    count = len(LEARNING_RATES)
    states, grads, outs = refs[: 3 * count], refs[3 * count : 4 * count], refs[4 * count :]
    for place, rate in enumerate(LEARNING_RATES):
        weight, moment, average = (ref[...] for ref in states[3 * place : 3 * place + 3])
        clipped = factor * grads[place][...] + WEIGHT_DECAY * weight
        velocity = MOMENTUM * moment + clipped
        updated = weight - rate * (clipped + MOMENTUM * velocity)
        outs[3 * place][...] = velocity
        outs[3 * place + 1][...] = updated
        outs[3 * place + 2][...] = smooth_rate * average + (1.0 - smooth_rate) * updated


def on_device(
    tokens,
    scene_lengths,
    cotangent,
    attend_weight,
    output_weight,
    expand_weight,
    reduce_weight,
    vector_params,
    attend_momentum,
    output_momentum,
    expand_momentum,
    reduce_momentum,
    vector_momentum,
    attend_average,
    output_average,
    expand_average,
    reduce_average,
    vector_average,
):
    n = lax.axis_size("seq")
    planes = n // PLANE
    device = lax.axis_index("seq")
    plane, spot = device // PLANE, device % PLANE
    place = jnp.stack([spot, plane]).astype(jnp.int32)
    number, columns = tokens.shape
    shared = number * PLANE
    rows = columns // n
    hidden = reduce_weight.shape[0]
    wide = columns // PLANE
    lots = columns // LANES
    in_lot = LANES // rows
    inner = planes * hidden
    near_like, far_like = like((4, number, columns), F32), like((3, number, columns), LOW)
    block_like, block_exact = like((number, columns), LOW), like((number, columns), F32)
    shared_scratch = pltpu.VMEM((shared, columns), LOW)
    square_scratch = pltpu.VMEM((columns, columns), LOW)

    sides = spread_sides(tokens)
    attend_low = attend_weight.astype(LOW).reshape(rows, 3, PLANE, wide)
    pair_weight = attend_low[:, 1:].transpose(2, 0, 1, 3).reshape(PLANE, rows, 2 * wide)
    vector_part = lax.dynamic_update_slice(
        jnp.zeros((2 * EXTRA, LANES), LOW), vector_params.astype(LOW), (0, rows * (device % in_lot))
    )
    vector_part = jnp.concatenate([vector_part[:EXTRA], vector_part[EXTRA:]], axis=1)
    pair_weight = jnp.concatenate(
        [
            jnp.broadcast_to(pair_weight[None], (planes,) + pair_weight.shape).reshape(n, rows, 2 * wide),
            jnp.broadcast_to(vector_part[None], (n,) + vector_part.shape),
        ],
        axis=1,
    )
    pair_weight = exchange(pair_weight)
    lot_vectors = pair_weight[:, rows:].reshape(lots, in_lot, EXTRA, 2 * wide).astype(F32).sum(1)
    corner = spread_corner(*sides)
    output = after(output_weight, *sides).astype(LOW)
    output = jnp.concatenate([output] + [turn(output, s) for s in range(1, planes)], axis=0)
    gathered = spread_far(tokens, sides, corner)
    query_weight = attend_low[:, 0].transpose(1, 0, 2)
    query_weight = jnp.broadcast_to(query_weight[None], (planes,) + query_weight.shape).reshape(n, rows, wide)
    expand = (
        expand_weight.astype(LOW)
        .reshape(rows, planes, PLANE, hidden)
        .transpose(2, 0, 1, 3)
        .reshape(PLANE, rows, inner)
    )
    expand = jnp.broadcast_to(expand[None], (planes,) + expand.shape).reshape(n, rows, inner)
    expand = [expand[:, :, : inner // 2], expand[:, :, inner // 2 :]]
    shrink = reduce_weight.astype(LOW)
    gathered, output, query_weight, expand, shrink = tie(gathered, output, query_weight, expand, shrink)

    units, first_low, pairs, pair_weight, vectors = kernel_call(
        project_kernel,
        [
            like((shared, columns), LOW),
            like((shared, columns), LOW),
            like((shared, 2 * wide), LOW),
            like((columns, 2 * wide), LOW),
            like((2 * EXTRA, columns), F32),
        ],
        *gathered,
        pair_weight,
        lot_vectors,
        scalars=(place,),
        scratch=[shared_scratch],
        flops=4 * shared * columns * wide,
    )
    bias_up = lax.dynamic_index_in_dim(
        vectors[5 : vector_params.shape[0]].reshape(planes, PLANE, hidden), spot, axis=1, keepdims=False
    ).reshape(1, inner)

    before, behind = move(pairs, PLANE), move(pairs, -PLANE)
    query_weight = exchange(after(query_weight, pairs)).reshape(columns, wide)
    queries = dot(first_low, query_weight).astype(LOW)
    expand[0] = exchange(after(expand[0], query_weight)).reshape(columns, inner // 2)
    output_sides = spread_sides(after(output, pairs))
    queries, output_sides = tie(queries, output_sides)

    finish = jnp.cumsum(scene_lengths)
    begin = finish - scene_lengths
    base = (plane - 1) * shared
    position = plane * shared + jnp.arange(shared, dtype=jnp.int32)
    past = begin[None, :] <= position[:, None]
    span_begin = jnp.max(jnp.where(past, begin[None, :], 0), axis=1) - base
    span_end = jnp.min(jnp.where(finish[None, :] > position[:, None], finish[None, :], 1 << 30), axis=1) - base
    spans = jnp.stack([span_begin, span_end])
    ranges = jnp.stack(
        [span_begin[::QUERY_TILE] // KEY_TILE, (span_end[QUERY_TILE - 1 :: QUERY_TILE] + KEY_TILE - 1) // KEY_TILE]
    )
    output_corner = spread_corner(*output_sides)
    cot_sides = spread_sides(after(cotangent, queries))
    mixed_exact, mixed_low, logs = attention(ranges, queries, before, pairs, behind, spans)
    mixed_low, output_corner, cot_sides, expand[0] = tie(mixed_low, output_corner, cot_sides, expand[0])

    mixed = exchange(mixed_low.reshape(PLANE, number, wide), plane_groups())
    output = spread_far(output, output_sides, output_corner)
    cot_corner = spread_corner(*cot_sides)
    shrink = after(shrink, mixed_low)
    shrink_turns = [turn(shrink, s) for s in range(1, planes)]
    output = ordered_output(spot, plane, output, planes)
    second, normed = kernel_call(
        functools.partial(mix_out_kernel, planes),
        [block_exact, block_like],
        mixed,
        tokens,
        vectors,
        *output,
        scalars=(place,),
        scratch=[square_scratch, square_scratch],
        flops=2 * number * columns * columns,
    )

    expand[1] = exchange(after(expand[1], mixed)).reshape(columns, inner // 2)
    sides = spread_sides(normed)
    sides, shrink_turns[::2], cot_corner = tie(sides, shrink_turns[::2], cot_corner)
    cotangents = spread_far(cotangent, cot_sides, cot_corner)
    corner = spread_corner(*sides)
    corner, shrink_turns = tie(corner, shrink_turns)
    shrink = [shrink] + shrink_turns
    normed_all = spread_far(normed, sides, corner)

    inner_low = like((shared, inner), LOW)
    grad_near, grad_far, grad_corner, active, upper_grad, up_sums = kernel_call(
        functools.partial(feed_kernel, planes),
        [near_like, far_like, block_like, inner_low, inner_low, like((1, inner), F32)],
        *normed_all,
        *cotangents,
        *shrink,
        *expand,
        bias_up,
        scalars=(place,),
        scratch=[pltpu.VMEM((columns, inner), LOW), pltpu.VMEM((inner, columns), LOW), shared_scratch, shared_scratch],
        flops=6 * shared * columns * inner,
    )

    normed_grad = collect(grad_near, grad_far, grad_corner)
    shrink_grad = kernel_call(
        shrink_grad_kernel,
        [like((hidden, columns), LOW)] * planes,
        active,
        *cotangents,
        scalars=(place,),
        scratch=[pltpu.VMEM((inner, columns), F32), shared_scratch],
        flops=2 * shared * columns * inner,
    )
    shrink_turns = [turn(shrink_grad[s], s) for s in range(1, planes)]
    normed_grad, shrink_turns[:1] = tie(normed_grad, shrink_turns[:1])
    second_grad, branch_grad, mixed_grad, two_sums = kernel_call(
        functools.partial(norm_two_back_kernel, planes),
        [block_exact, block_like, like((PLANE, number, wide), LOW), like((3, columns), F32)],
        *normed_grad,
        second,
        cotangent,
        vectors,
        *output,
        scalars=(place,),
        scratch=[square_scratch, square_scratch],
        flops=2 * number * columns * columns,
    )

    mixed_grad = exchange(mixed_grad, plane_groups()).reshape(shared, wide)
    expand_grad = kernel_call(
        expand_grad_kernel,
        [like((columns, inner // 2), LOW)] * 2,
        after(upper_grad, branch_grad),
        *normed_all,
        scratch=[shared_scratch],
        flops=2 * shared * columns * inner,
    )
    branch_sides = spread_sides(branch_grad)
    mixed_grad, expand_grad, branch_sides, shrink_turns = tie(mixed_grad, expand_grad, branch_sides, shrink_turns)
    shrink_grad = sum(g.astype(F32) for g in [shrink_grad[0], *shrink_turns])

    expand_part = [exchange(expand_grad[0].reshape(n, rows, inner // 2))]
    branch_corner = spread_corner(*branch_sides)
    query_grad, before_grad, own_grad, behind_grad = attention_back(
        ranges, queries, before, pairs, behind, spans, mixed_exact, logs, mixed_grad
    )
    before_grad, behind_grad, branch_corner, expand_part = tie(before_grad, behind_grad, branch_corner, expand_part)

    from_after, from_before = move(before_grad, -PLANE), move(behind_grad, PLANE)
    expand_part = expand_part + [exchange(after(expand_grad[1], before_grad).reshape(n, rows, inner // 2))]
    branch_all = spread_far(branch_grad, branch_sides, branch_corner)
    lower = kernel_call(
        functools.partial(lower_kernel, planes),
        [near_like, far_like, block_like],
        after(active, before_grad),
        *shrink,
        scalars=(place,),
        scratch=[pltpu.VMEM((inner, columns), LOW)],
        flops=2 * shared * columns * inner,
    )
    output_grad = kernel_call(
        output_grad_kernel,
        [like((rows, columns), LOW)] * planes if rows % 16 == 0 else [like((wide, columns), LOW)],
        mixed_low,
        *branch_all,
        scalars=(place,),
        scratch=[pltpu.VMEM((wide, columns), F32), pltpu.VMEM((shared, wide), LOW), shared_scratch],
        flops=2 * shared * columns * wide,
    )
    from_after, from_before, output_grad, lower, expand_part = tie(
        from_after, from_before, output_grad, lower, expand_part
    )

    attend_grad, first_near, first_far, first_corner, one_sums = kernel_call(
        first_back_kernel,
        [like((columns, 3 * wide), LOW), near_like, far_like, block_like, like((2, columns), F32)],
        own_grad,
        from_after,
        from_before,
        query_grad,
        first_low,
        units,
        pair_weight,
        query_weight,
        scalars=(place,),
        scratch=[pltpu.VMEM((shared, 3 * wide), LOW), pltpu.VMEM((columns, 3 * wide), LOW)],
        flops=2 * shared * columns * 6 * wide,
    )
    up_sums = lax.dynamic_update_slice_in_dim(
        jnp.zeros((planes, PLANE, hidden), F32), up_sums.reshape(planes, 1, hidden), spot, axis=1
    )
    vector_part = jnp.concatenate([two_sums, up_sums.reshape(-1, columns)], axis=0)
    vector_part = jnp.concatenate([one_sums, vector_part], axis=0).astype(LOW).reshape(-1, lots, LANES)
    vector_part = jnp.moveaxis(vector_part, 1, 0)
    more = vector_part.shape[1] - EXTRA
    vector_part = jnp.concatenate(
        [
            vector_part[:, :EXTRA],
            jnp.pad(vector_part[:, EXTRA:], ((0, 0), (0, EXTRA - more), (0, 3 * wide - 2 * LANES))),
        ],
        axis=2,
    )
    vector_part = jnp.repeat(vector_part, in_lot, axis=0)
    attend_part = jnp.concatenate([attend_grad.reshape(n, rows, 3 * wide), vector_part], axis=1)
    attend_part, output_grad, first_near, first_far, first_corner, lower, expand_part = tie(
        attend_part, output_grad, first_near, first_far, first_corner, lower, expand_part
    )
    attend_part = exchange(attend_part)
    expand_grad, expand_square = sum_parts(hidden, rows, *expand_part)
    vector_grad = attend_part[:, rows:].astype(F32).sum(0)
    vector_grad = jnp.concatenate([vector_grad[:, :LANES], vector_grad[:more, LANES : 2 * LANES]], axis=0)
    vector_grad = lax.dynamic_slice_in_dim(vector_grad, rows * (device % in_lot), rows, axis=1)
    attend_grad, attend_square = sum_parts(wide, rows, attend_part)

    if len(output_grad) == 1:
        output_grad = jnp.take(
            output_grad[0].reshape(planes, rows, columns), (plane + jnp.arange(planes)) % planes, axis=0, mode="clip"
        )
    output_grad = sum(
        [output_grad[0].astype(F32)] + [turn(output_grad[s], s).astype(F32) for s in range(1, planes)]
    )
    output_grad = lax.ppermute(
        output_grad, "seq", [(g * PLANE + j, j * planes + g) for g in range(planes) for j in range(PLANE)]
    )
    first_grad = collect(first_near, first_far, first_corner)
    (input_gradient,) = kernel_call(
        first_norm_back_kernel, [block_like], *first_grad, tokens, second_grad, vectors
    )
    block_output = collect(*lower)
    block_output = (second + total(block_output) + vectors[4:5]).astype(LOW)

    squares = [jnp.sum(g * g) for g in (output_grad, shrink_grad, vector_grad)]
    local_square = sum(squares) + expand_square[0, 0] + attend_square[0, 0]
    norm_square = jnp.sum(exchange(jnp.full((n, 1, LANES), local_square, F32))[:, 0, 0])
    gradient_norm = jnp.sqrt(norm_square)
    factor = jnp.minimum(1.0, CLIP_NORM / (gradient_norm + 1e-06))
    states = (
        (attend_weight, attend_momentum, attend_average),
        (output_weight, output_momentum, output_average),
        (expand_weight, expand_momentum, expand_average),
        (reduce_weight, reduce_momentum, reduce_average),
        (vector_params, vector_momentum, vector_average),
    )
    updates = kernel_call(
        update_kernel,
        [like(g[0].shape, F32) for g in states for _ in range(3)],
        *[a for g in states for a in g],
        attend_grad,
        output_grad,
        expand_grad,
        shrink_grad,
        vector_grad,
        scalars=(factor.reshape(1),),
    )
    return (block_output, input_gradient, gradient_norm, *updates)


def solution(mesh):
    split, turned = P("seq", None), P(None, "seq")
    return jax.shard_map(
        on_device,
        mesh=mesh,
        in_specs=(split, P()) + (split,) * 5 + (turned,) + ((split,) * 4 + (turned,)) * 2,
        out_specs=(split, split, P()) + (split,) * 12 + (turned,) * 3,
        check_vma=False,
    )
```

time: 445 us -> 330 us (0.74)
  waiting for transfers between devices: 148 us -> 55.8 us
  Pallas kernels: 31.3 us -> 88.4 us
  local copies, waits for them, and re-layouts: 55.5 us -> 14 us
  matrix products: 36.3 us -> 3.05 us
  other arithmetic: 57.1 us -> 27.4 us
  starting transfers between devices: 108 us -> 134 us
    all_to_all x15 -> x10, waiting for transfers between devices: 69.7 us -> 5.94 us  [exchange(): return lax.all_to_all(blocks, 'seq', 0, 0, axis_index_groups=groups)]
    pallas_call x1 -> x13, Pallas kernels: 4.54 us -> 56.7 us  [kernel_call(): pl.pallas_call(body, in_specs=[SMEM] * len(scalars) + [WHOLE] * len(args)...]
    ppermute x30 -> x53, waiting for transfers between devices: 54.1 us -> 15.3 us  [swap(): return lax.ppermute(block, 'seq', [(i, i ^ bit) for i in range(n)])]
    dot_general x11 -> x1, matrix products: 36.3 us -> 3.05 us  [dot(): return lax.dot_general(a, b, (dims, ((), ())), preferred_element_type=F32)]
    ppermute x0 -> x12, waiting for transfers between devices: none -> 24.5 us  [turn(): lax.ppermute(block, 'seq', [(i, (i + planes_on * PLANE) % n) for i in ran...]
    ppermute x30 -> x53, starting transfers between devices: 26.7 us -> 48.6 us  [swap(): return lax.ppermute(block, 'seq', [(i, i ^ bit) for i in range(n)])]
    ppermute x0 -> x12, starting transfers between devices: none -> 20.6 us  [turn(): lax.ppermute(block, 'seq', [(i, (i + planes_on * PLANE) % n) for i in ran...]
    another operation x17 -> x13, other arithmetic: 19.2 us -> 1.4 us  [the longest x1 0.59 us: on_device(): place = jnp.stack([spot, plane]).astype(jnp.int32)]
  transfers between devices with their start and end apart: 50 -> 80, of which waited for: 26 -> 18; matrix products, arithmetic and copies ran while one was open for 24% -> 10% of each run, Pallas kernels for 7% -> 19%
where the time goes in v2:
time: 330 us
  starting transfers between devices  134 us (41%)
  Pallas kernels  88.4 us (27%)
  waiting for transfers between devices  55.8 us (17%)
  other arithmetic  27.4 us (8%)
  local copies, waits for them, and re-layouts  14 us (4%)
  between operations  7.24 us (2%)
    pallas_call x13, Pallas kernels, kernel_call(): pl.pallas_call(body, in_specs=[SMEM] * len(scalars) + [WHOLE] * len(args)...  56.7 us
    all_to_all x10, starting transfers between devices, exchange(): return lax.all_to_all(blocks, 'seq', 0, 0, axis_index_groups=groups)  51.9 us
    ppermute x53, starting transfers between devices, swap(): return lax.ppermute(block, 'seq', [(i, i ^ bit) for i in range(n)])  48.6 us
    ppermute x12, waiting for transfers between devices, turn(): lax.ppermute(block, 'seq', [(i, (i + planes_on * PLANE) % n) for i in ran...  24.5 us
    ppermute x12, starting transfers between devices, turn(): lax.ppermute(block, 'seq', [(i, (i + planes_on * PLANE) % n) for i in ran...  20.6 us
    pallas_call x1, Pallas kernels, attention_back(): pl.pallas_call(attend_back_kernel, grid_spec=pltpu.PrefetchScalarGridSpec...  16.4 us
    ppermute x53, waiting for transfers between devices, swap(): return lax.ppermute(block, 'seq', [(i, i ^ bit) for i in range(n)])  15.3 us
    pallas_call x1, Pallas kernels, attention(): pl.pallas_call(attend_kernel, grid_spec=pltpu.PrefetchScalarGridSpec(num_...  15.2 us
  transfers between devices with their start and end apart: 80, of which 18 were waited for; matrix products, arithmetic and copies ran while one was open for 10% of the time, Pallas kernels for 19%

profile of v2, /device:TPU:0, one launch (start us, length us, event | category | flops | bytes accessed | tf_op | source)
XLA Modules:
  0.0 329.8 jit_solution(13907609485241601495)
XLA Ops:
  0.7 3.0 collective-permute-start
  8.4 4.2 %all-to-all-start = ((bf16[32,40,256]{2,1,0:T(8,128)(2,1)}), bf16[32,40,256]{2,1,0:T(8,128)(2,1)S(1)}, u32[]{:S(2)}, u32[]{:S(2)}) async-start(bf16[32,40,256]{2,1,0:T(8,128)(2,1)} %pad_maximum_fusion.6), calls=%async_computation | async-start | bytes 1310720 | tf_op jit(solution)/shard_map/all_to_all | solution.py:82
  21.1 2.5 collective-permute-start.8
  23.5 6.3 %collective-permute-done.7 = bf16[32,1024]{1,0:T(8,128)(2,1)S(1)} collective-permute-done((bf16[32,1024]{1,0:T(8,128)(2,1)}, bf16[32,1024]{1,0:T(8,128)(2,1)S(1)}, u32[]{:S(2)}, u32[]{:S(2)}) %collective-permute-start.7) | collective-permute-done | bytes 65568 | tf_op jit(solution)/shard_map/ppermute | solution.py:68
  32.0 2.8 collective-permute-done.8
  38.9 5.9 %shard_map.313 = (bf16[1024,1024]{1,0:T(8,128)(2,1)}, bf16[1024,1024]{1,0:T(8,128)(2,1)}, bf16[1024,256]{1,0:T(8,128)(2,1)}, bf16[1024,256]{1,0:T(8,128)(2,1)}, f32[16,1024]{1,0:T(8,128)}) custom-call(s32[2]{0:T(128)} %pad_add_fusion.2.spot_ref.place_ref, bf16[128,1024]{1,0:T(8,128)(2,1)} %tokens_ref.3, bf16[128,1024]{1,0:T(8,128)(2,1)} %copy-done.15, ...), custom_call_target="tpu_custom_call" | custom-call | flops 536870912 | bytes 8126464 | tf_op jit(solution)/shard_map/pallas_call | solution.py:35
  44.8 5.9 %all-to-all-start.1 = ((bf16[32,32,128]{2,1,0:T(8,128)(2,1)}), bf16[32,32,128]{2,1,0:T(8,128)(2,1)S(1)}, u32[]{:S(2)}, u32[]{:S(2)}) async-start(bf16[32,32,128]{2,1,0:T(8,128)(2,1)} %bitcast.11), calls=%async_computation.1 | async-start | bytes 524288 | tf_op jit(solution)/shard_map/all_to_all | solution.py:82
  54.8 4.2 %collective-permute-start.12 = (bf16[1024,256]{1,0:T(8,128)(2,1)}, bf16[1024,256]{1,0:T(8,128)(2,1)}, u32[]{:S(2)}, u32[]{:S(2)}) collective-permute-start(bf16[1024,256]{1,0:T(8,128)(2,1)} %get-tuple-element.174.own_ref), channel_id=1, source_target_pairs={{0,8},{1,9},{2,10},{3,11},{4,12},{5,13},{6,14},{7,15},{8,16},{9,17... | collective-permute-start | bytes 1572872 | tf_op jit(solution)/shard_map/ppermute | solution.py:61
  61.3 3.9 %all-to-all-start.2 = ((bf16[32,32,256]{2,1,0:T(8,128)(2,1)}), bf16[32,32,256]{2,1,0:T(8,128)(2,1)}, u32[]{:S(2)}, u32[]{:S(2)}) async-start(bf16[32,32,256]{2,1,0:T(8,128)(2,1)} %get-tuple-element.184), calls=%async_computation.2 | async-start | bytes 1048576 | tf_op jit(solution)/shard_map/all_to_all | solution.py:82
  65.3 3.0 convolution_convert_fusion.query_ref
  73.1 3.7 %collective-permute-done.13.after_ref = bf16[1024,256]{1,0:T(8,128)(2,1)} collective-permute-done((bf16[1024,256]{1,0:T(8,128)(2,1)}, bf16[1024,256]{1,0:T(8,128)(2,1)}, u32[]{:S(2)}, u32[]{:S(2)}) %collective-permute-start.13) | collective-permute-done | bytes 524320 | tf_op jit(solution)/shard_map/ppermute | solution.py:61
  77.8 15.2 %shard_map.314 = (f32[1024,128]{1,0:T(8,128)}, bf16[1024,128]{1,0:T(8,128)(2,1)}, f32[2,1024]{1,0:T(2,128)}) custom-call(s32[2,4]{1,0:T(2,128)} %pad_add_fusion.1.range_ref, bf16[1024,128]{1,0:T(8,128)(2,1)} %convolution_convert_fusion.query_ref, bf16[1024,256]{1,0:T(8,128)(2,1)} %collective-permute-done.12.before_ref, ...), custom_call_target="tpu_custom_call" | custom-call | flops 5368709120 | bytes 2097152 | tf_op jit(solution)/shard_map/pallas_call | solution.py:343
  93.2 3.4 %all-to-all-start.3 = ((bf16[8,128,128]{2,1,0:T(8,128)(2,1)}), bf16[8,128,128]{2,1,0:T(8,128)(2,1)S(1)}, u32[]{:S(2)}, u32[]{:S(2)}) async-start(bf16[8,128,128]{2,1,0:T(8,128)(2,1)} %bitcast.161), calls=%async_computation.3 | async-start | bytes 524288 | tf_op jit(solution)/shard_map/all_to_all | solution.py:82
  97.2 3.8 %collective-permute-start.24 = (bf16[128,1024]{1,0:T(8,128)(2,1)S(1)}, bf16[128,1024]{1,0:T(8,128)(2,1)}, u32[]{:S(2)}, u32[]{:S(2)}) collective-permute-start(bf16[128,1024]{1,0:T(8,128)(2,1)S(1)} %convert_element_type.145.refs_16_.refs_0_), channel_id=1, source_target_pairs={{0,24},{1,25},{2,26},{3,27},{4,28},{5,29},{6,30},{7,31},{8,0},{9,1... | collective-permute-start | bytes 786440 | tf_op jit(solution)/shard_map/ppermute | solution.py:68
  101.0 1.9 collective-permute-start.25
  104.2 3.2 shard_map.315
  109.0 7.2 %all-to-all-start.4 = ((bf16[32,32,256]{2,1,0:T(8,128)(2,1)}), bf16[32,32,256]{2,1,0:T(8,128)(2,1)}, u32[]{:S(2)}, u32[]{:S(2)}) async-start(bf16[32,32,256]{2,1,0:T(8,128)(2,1)} %get-tuple-element.210), calls=%async_computation.4 | async-start | bytes 1048576 | tf_op jit(solution)/shard_map/all_to_all | solution.py:82
  117.9 7.9 %collective-permute-done.26.refs_12_.refs_4_ = bf16[64,1024]{1,0:T(8,128)(2,1)S(1)} collective-permute-done((bf16[64,1024]{1,0:T(8,128)(2,1)S(1)}, bf16[64,1024]{1,0:T(8,128)(2,1)S(1)}, u32[]{:S(2)}, u32[]{:S(2)}) %collective-permute-start.26) | collective-permute-done | bytes 131104 | tf_op jit(solution)/shard_map/ppermute | solution.py:56
  126.5 2.2 collective-permute-start.29
  131.0 11.1 %collective-permute-done.29.refs_18_.refs_2_ = bf16[128,1024]{1,0:T(8,128)(2,1)S(1)} collective-permute-done((bf16[128,1024]{1,0:T(8,128)(2,1)S(1)}, bf16[128,1024]{1,0:T(8,128)(2,1)S(1)}, u32[]{:S(2)}, u32[]{:S(2)}) %collective-permute-start.29) | collective-permute-done | bytes 262176 | tf_op jit(solution)/shard_map/ppermute | solution.py:68
  145.8 8.7 %shard_map.316 = (f32[4,128,1024]{2,1,0:T(8,128)}, bf16[3,128,1024]{2,1,0:T(8,128)(2,1)}, bf16[128,1024]{1,0:T(8,128)(2,1)}, bf16[1024,512]{1,0:T(8,128)(2,1)}, ...) custom-call(s32[2]{0:T(128)} %pad_add_fusion.2.spot_ref.place_ref, bf16[128,1024]{1,0:T(8,128)(2,1)} %get-tuple-element.192.refs_0_, ...), custom_call_target="tpu_custom_call" | custom-call | flops 3221225472 | bytes 11538432 | tf_op jit(solution)/shard_map/pallas_call | solution.py:35
  155.1 4.3 %shard_map.317 = (bf16[128,1024]{1,0:T(8,128)(2,1)}, bf16[128,1024]{1,0:T(8,128)(2,1)}, bf16[128,1024]{1,0:T(8,128)(2,1)}, bf16[128,1024]{1,0:T(8,128)(2,1)}) custom-call(s32[2]{0:T(128)} %pad_add_fusion.2.spot_ref.place_ref, bf16[1024,512]{1,0:T(8,128)(2,1)} %get-tuple-element.243.active_ref, bf16[128,1024]{1,0:T(8,128)(2,1)} %cotangent_ref.1, ...), custom_call_target="tpu_custom_call" | custom-call | flops 1073741824 | bytes 4194304 | tf_op jit(solution)/shard_map/pallas_call | solution.py:35
  175.3 4.1 %shard_map.318 = (f32[128,1024]{1,0:T(8,128)}, bf16[128,1024]{1,0:T(8,128)(2,1)}, bf16[8,128,128]{2,1,0:T(8,128)(2,1)}, f32[3,1024]{1,0:T(4,128)}) custom-call(s32[2]{0:T(128)} %pad_add_fusion.2.spot_ref.place_ref, f32[128,1024]{1,0:T(8,128)} %get-tuple-element.216.one_ref, bf16[128,1024]{1,0:T(8,128)(2,1)} %copy-done.39, bf16[128,1024]{1,0:T(8,128)(2,1)} %copy-done.38, ...), custom_call_target="tpu_custom_call" | custom-call | flops 268435456 | bytes 5058560 | tf_op jit(solution)/shard_map/pallas_call | solution.py:35
  181.5 3.4 %all-to-all-start.5 = ((bf16[8,128,128]{2,1,0:T(8,128)(2,1)}), bf16[8,128,128]{2,1,0:T(8,128)(2,1)S(1)}, u32[]{:S(2)}, u32[]{:S(2)}) async-start(bf16[8,128,128]{2,1,0:T(8,128)(2,1)} %get-tuple-element.219), calls=%async_computation.5 | async-start | bytes 524288 | tf_op jit(solution)/shard_map/all_to_all | solution.py:82
  184.9 4.1 %shard_map.319 = (bf16[1024,256]{1,0:T(8,128)(2,1)}, bf16[1024,256]{1,0:T(8,128)(2,1)}) custom-call(bf16[1024,512]{1,0:T(8,128)(2,1)} %get-tuple-element.222.grad_ref, bf16[128,1024]{1,0:T(8,128)(2,1)} %get-tuple-element.192.refs_0_, bf16[128,1024]{1,0:T(8,128)(2,1)} %copy-done.24, bf16[128,1024]{1,0:T(8,128)(2,1)} %copy-done.25, ...), custom_call_target="tpu_custom_call" | custom-call | flops 1073741824 | bytes 4194304 | tf_op jit(solution)/shard_map/pallas_call | solution.py:35
  189.1 2.7 all-to-all-done.5
  191.8 4.1 %all-to-all-start.6 = ((bf16[32,32,256]{2,1,0:T(8,128)(2,1)}), bf16[32,32,256]{2,1,0:T(8,128)(2,1)S(1)}, u32[]{:S(2)}, u32[]{:S(2)}) async-start(bf16[32,32,256]{2,1,0:T(8,128)(2,1)} %bitcast.174), calls=%async_computation.6 | async-start | bytes 1048576 | tf_op jit(solution)/shard_map/all_to_all | solution.py:82
  199.1 16.4 %shard_map.320 = (bf16[1024,128]{1,0:T(8,128)(2,1)}, bf16[1024,256]{1,0:T(8,128)(2,1)}, f32[1024,256]{1,0:T(8,128)}, bf16[1024,256]{1,0:T(8,128)(2,1)}) custom-call(s32[2,4]{1,0:T(2,128)} %pad_add_fusion.1.range_ref, bf16[1024,128]{1,0:T(8,128)(2,1)} %convolution_convert_fusion.query_ref, bf16[1024,256]{1,0:T(8,128)(2,1)} %collective-permute-done.12.before_ref, ...), custom_call_target="tpu_custom_call" | custom-call | flops 8053063680 | bytes 4194304 | tf_op jit(solution)/shard_map/pallas_call | solution.py:368
  215.5 6.8 %all-to-all-start.7 = ((bf16[32,32,256]{2,1,0:T(8,128)(2,1)}), bf16[32,32,256]{2,1,0:T(8,128)(2,1)S(1)}, u32[]{:S(2)}, u32[]{:S(2)}) async-start(bf16[32,32,256]{2,1,0:T(8,128)(2,1)} %bitcast.45), calls=%async_computation.7 | async-start | bytes 1048576 | tf_op jit(solution)/shard_map/all_to_all | solution.py:82
  224.1 4.6 %collective-permute-start.50 = (bf16[1024,256]{1,0:T(8,128)(2,1)}, bf16[1024,256]{1,0:T(8,128)(2,1)S(1)}, u32[]{:S(2)}, u32[]{:S(2)}) collective-permute-start(bf16[1024,256]{1,0:T(8,128)(2,1)} %get-tuple-element.236), channel_id=1, source_target_pairs={{0,8},{1,9},{2,10},{3,11},{4,12},{5,13},{6,14},{7,15},{8,16},{9,17... | collective-permute-start | bytes 1572872 | tf_op jit(solution)/shard_map/ppermute | solution.py:61
  229.9 4.3 %shard_map.322 = (f32[4,128,1024]{2,1,0:T(8,128)}, bf16[3,128,1024]{2,1,0:T(8,128)(2,1)}, bf16[128,1024]{1,0:T(8,128)(2,1)}) custom-call(s32[2]{0:T(128)} %pad_add_fusion.2.spot_ref.place_ref, bf16[1024,512]{1,0:T(8,128)(2,1)} %get-tuple-element.243.active_ref, bf16[128,1024]{1,0:T(8,128)(2,1)} %copy-done.36, ...), custom_call_target="tpu_custom_call" | custom-call | flops 1073741824 | bytes 5242880 | tf_op jit(solution)/shard_map/pallas_call | solution.py:35
  235.8 2.8 shard_map.321
  238.6 6.3 %collective-permute-done.49.from_after_ref = bf16[1024,256]{1,0:T(8,128)(2,1)S(1)} collective-permute-done((bf16[1024,256]{1,0:T(8,128)(2,1)}, bf16[1024,256]{1,0:T(8,128)(2,1)S(1)}, u32[]{:S(2)}, u32[]{:S(2)}) %collective-permute-start.49) | collective-permute-done | bytes 524320 | tf_op jit(solution)/shard_map/ppermute | solution.py:61
  245.8 7.2 %shard_map.323 = (bf16[1024,384]{1,0:T(8,128)(2,1)}, f32[4,128,1024]{2,1,0:T(8,128)}, bf16[3,128,1024]{2,1,0:T(8,128)(2,1)}, bf16[128,1024]{1,0:T(8,128)(2,1)}, f32[2,1024]{1,0:T(2,128)}) custom-call(s32[2]{0:T(128)} %pad_add_fusion.2.spot_ref.place_ref, f32[1024,256]{1,0:T(8,128)} %get-tuple-element.229.own_ref, bf16[1024,256]{1,0:T(8,128)(2,1)} %copy-done.34, ...), custom_call_target="tpu_custom_call" | custom-call | flops 1610612736 | bytes 11280384 | tf_op jit(solution)/shard_map/pallas_call | solution.py:35
  254.0 2.2 pad_maximum_fusion
  256.2 4.3 %collective-permute-start.66 = (bf16[32,1024]{1,0:T(8,128)(2,1)S(1)}, bf16[32,1024]{1,0:T(8,128)(2,1)S(1)}, u32[]{:S(2)}, u32[]{:S(2)}) collective-permute-start(bf16[32,1024]{1,0:T(8,128)(2,1)S(1)} %copy-done.70), channel_id=1, source_target_pairs={{0,8},{1,9},{2,10},{3,11},{4,12},{5,13},{6,14},{7,15},{8,16},{9,17... | collective-permute-start | bytes 196616 | tf_op jit(solution)/shard_map/ppermute | solution.py:68
  260.5 2.6 collective-permute-start.68
  263.9 2.9 collective-permute-done.67
  270.6 5.7 %all-to-all-start.8 = ((bf16[32,40,384]{2,1,0:T(8,128)(2,1)}), bf16[32,40,384]{2,1,0:T(8,128)(2,1)S(1)}, u32[]{:S(2)}, u32[]{:S(2)}) async-start(bf16[32,40,384]{2,1,0:T(8,128)(2,1)} %pad_maximum_fusion), calls=%async_computation.8 | async-start | bytes 1966080 | tf_op jit(solution)/shard_map/all_to_all | solution.py:82
  277.1 2.1 shard_map.325
  287.7 2.2 convert_add_fusion.1
  292.0 1.9 collective-permute-start.65
  299.6 2.0 collective-permute-start.63
  304.4 2.0 shard_map.326
  307.7 7.3 %all-to-all-start.9 = ((f32[32,1,128]{2,1,0:T(1,128)}), f32[32,1,128]{2,1,0:T(1,128)S(1)}, u32[]{:S(2)}, u32[]{:S(2)}) async-start(f32[32,1,128]{2,1,0:T(1,128)} %broadcast_in_dim.71), calls=%async_computation.9 | async-start | bytes 32768 | tf_op jit(solution)/shard_map/all_to_all | solution.py:82
  315.0 2.2 fusion.5
  317.9 2.6 shard_map.324
  323.5 5.2 %shard_map.327 = (f32[32,3072]{1,0:T(8,128)}, f32[32,3072]{1,0:T(8,128)}, f32[32,3072]{1,0:T(8,128)}, f32[32,1024]{1,0:T(8,128)}, f32[32,1024]{1,0:T(8,128)}, /*...) custom-call(f32[1]{0:T(128)} %bitcast.67.factor_ref, ...), custom_call_target="tpu_custom_call" | custom-call | bytes 11018112 | tf_op jit(solution)/shard_map/pallas_call | solution.py:35
  (375 shorter events, 96.1 us)
Async XLA Ops:
  0.7 13.2 %collective-permute-start = (bf16[128,1024]{1,0:T(8,128)(2,1)}, bf16[128,1024]{1,0:T(8,128)(2,1)S(1)}, u32[]{:S(2)}, u32[]{:S(2)}) collective-permute-start(bf16[128,1024]{1,0:T(8,128)(2,1)} %tokens_ref.3), channel_id=1, source_target_pairs={{0,2},{1,3},{2,0},{3,1},{4,6},{5,7},{6,4},{7,5},{8,10},{9,11},{10,... | collective-permute-start | bytes 786440 | tf_op jit(solution)/shard_map/ppermute | solution.py:56
  8.4 29.6 %all-to-all-start = ((bf16[32,40,256]{2,1,0:T(8,128)(2,1)}), bf16[32,40,256]{2,1,0:T(8,128)(2,1)S(1)}, u32[]{:S(2)}, u32[]{:S(2)}) async-start(bf16[32,40,256]{2,1,0:T(8,128)(2,1)} %pad_maximum_fusion.6), calls=%async_computation | async-start | bytes 1310720 | tf_op jit(solution)/shard_map/all_to_all | solution.py:82
  14.0 23.2 %collective-permute-start.4 = (bf16[3,128,1024]{2,1,0:T(8,128)(2,1)S(1)}, bf16[3,128,1024]{2,1,0:T(8,128)(2,1)S(1)}, u32[]{:S(2)}, u32[]{:S(2)}) collective-permute-start(bf16[3,128,1024]{2,1,0:T(8,128)(2,1)S(1)} %pad_maximum_fusion.1), channel_id=1, source_target_pairs={{0,1},{1,0},{2,3},{3,2},{4,5},{5,4},{6,7},{7,6},{8,9},{9,8},{10,11... | collective-permute-start | bytes 2359304 | tf_op jit(solution)/shard_map/ppermute | solution.py:56
  16.3 13.5 %collective-permute-start.7 = (bf16[32,1024]{1,0:T(8,128)(2,1)}, bf16[32,1024]{1,0:T(8,128)(2,1)S(1)}, u32[]{:S(2)}, u32[]{:S(2)}) collective-permute-start(bf16[32,1024]{1,0:T(8,128)(2,1)} %convert_element_type.142), channel_id=1, source_target_pairs={{0,8},{1,9},{2,10},{3,11},{4,12},{5,13},{6,14},{7,15},{8,16},{9,17... | collective-permute-start | bytes 196616 | tf_op jit(solution)/shard_map/ppermute | solution.py:68
  18.0 11.8 %collective-permute-start.2 = (bf16[64,1024]{1,0:T(8,128)(2,1)S(1)}, bf16[64,1024]{1,0:T(8,128)(2,1)}, u32[]{:S(2)}, u32[]{:S(2)}) collective-permute-start(bf16[64,1024]{1,0:T(8,128)(2,1)S(1)} %slice.318), channel_id=1, source_target_pairs={{0,4},{1,5},{2,6},{3,7},{4,0},{5,1},{6,2},{7,3},{8,12},{9,13},{10,... | collective-permute-start | bytes 393224 | tf_op jit(solution)/shard_map/ppermute | solution.py:56
  21.1 13.7 %collective-permute-start.8 = (bf16[32,1024]{1,0:T(8,128)(2,1)}, bf16[32,1024]{1,0:T(8,128)(2,1)S(1)}, u32[]{:S(2)}, u32[]{:S(2)}) collective-permute-start(bf16[32,1024]{1,0:T(8,128)(2,1)} %convert_element_type.142), channel_id=1, source_target_pairs={{0,16},{1,17},{2,18},{3,19},{4,20},{5,21},{6,22},{7,23},{8,24},{9,... | collective-permute-start | bytes 196616 | tf_op jit(solution)/shard_map/ppermute | solution.py:68
  44.8 16.5 %all-to-all-start.1 = ((bf16[32,32,128]{2,1,0:T(8,128)(2,1)}), bf16[32,32,128]{2,1,0:T(8,128)(2,1)S(1)}, u32[]{:S(2)}, u32[]{:S(2)}) async-start(bf16[32,32,128]{2,1,0:T(8,128)(2,1)} %bitcast.11), calls=%async_computation.1 | async-start | bytes 524288 | tf_op jit(solution)/shard_map/all_to_all | solution.py:82
  51.5 16.9 %collective-permute-start.10 = (bf16[128,1024]{1,0:T(8,128)(2,1)S(1)}, bf16[128,1024]{1,0:T(8,128)(2,1)S(1)}, u32[]{:S(2)}, u32[]{:S(2)}) collective-permute-start(bf16[128,1024]{1,0:T(8,128)(2,1)S(1)} %pad_maximum_fusion.7.refs_0_), channel_id=1, source_target_pairs={{0,2},{1,3},{2,0},{3,1},{4,6},{5,7},{6,4},{7,5},{8,10},{9,11},{10,... | collective-permute-start | bytes 786440 | tf_op jit(solution)/shard_map/ppermute | solution.py:56
  53.3 15.1 %collective-permute-start.11 = (bf16[128,1024]{1,0:T(8,128)(2,1)S(1)}, bf16[128,1024]{1,0:T(8,128)(2,1)S(1)}, u32[]{:S(2)}, u32[]{:S(2)}) collective-permute-start(bf16[128,1024]{1,0:T(8,128)(2,1)S(1)} %pad_maximum_fusion.7.refs_0_), channel_id=1, source_target_pairs={{0,4},{1,5},{2,6},{3,7},{4,0},{5,1},{6,2},{7,3},{8,12},{9,13},{10,... | collective-permute-start | bytes 786440 | tf_op jit(solution)/shard_map/ppermute | solution.py:56
  54.8 17.7 %collective-permute-start.12 = (bf16[1024,256]{1,0:T(8,128)(2,1)}, bf16[1024,256]{1,0:T(8,128)(2,1)}, u32[]{:S(2)}, u32[]{:S(2)}) collective-permute-start(bf16[1024,256]{1,0:T(8,128)(2,1)} %get-tuple-element.174.own_ref), channel_id=1, source_target_pairs={{0,8},{1,9},{2,10},{3,11},{4,12},{5,13},{6,14},{7,15},{8,16},{9,17... | collective-permute-start | bytes 1572872 | tf_op jit(solution)/shard_map/ppermute | solution.py:61
  58.9 17.9 %collective-permute-start.13 = (bf16[1024,256]{1,0:T(8,128)(2,1)}, bf16[1024,256]{1,0:T(8,128)(2,1)}, u32[]{:S(2)}, u32[]{:S(2)}) collective-permute-start(bf16[1024,256]{1,0:T(8,128)(2,1)} %get-tuple-element.174.own_ref), channel_id=1, source_target_pairs={{8,0},{9,1},{10,2},{11,3},{12,4},{13,5},{14,6},{15,7},{16,8},{17,9... | collective-permute-start | bytes 1572872 | tf_op jit(solution)/shard_map/ppermute | solution.py:61
  61.3 31.8 %all-to-all-start.2 = ((bf16[32,32,256]{2,1,0:T(8,128)(2,1)}), bf16[32,32,256]{2,1,0:T(8,128)(2,1)}, u32[]{:S(2)}, u32[]{:S(2)}) async-start(bf16[32,32,256]{2,1,0:T(8,128)(2,1)} %get-tuple-element.184), calls=%async_computation.2 | async-start | bytes 1048576 | tf_op jit(solution)/shard_map/all_to_all | solution.py:82
  68.5 32.5 %collective-permute-start.18 = (bf16[3,128,1024]{2,1,0:T(8,128)(2,1)S(1)}, bf16[3,128,1024]{2,1,0:T(8,128)(2,1)S(1)}, u32[]{:S(2)}, u32[]{:S(2)}) collective-permute-start(bf16[3,128,1024]{2,1,0:T(8,128)(2,1)S(1)} %pad_maximum_fusion.2), channel_id=1, source_target_pairs={{0,1},{1,0},{2,3},{3,2},{4,5},{5,4},{6,7},{7,6},{8,9},{9,8},{10,11... | collective-permute-start | bytes 2359304 | tf_op jit(solution)/shard_map/ppermute | solution.py:56
  69.3 23.8 %collective-permute-start.16 = (bf16[128,1024]{1,0:T(8,128)(2,1)S(1)}, bf16[128,1024]{1,0:T(8,128)(2,1)S(1)}, u32[]{:S(2)}, u32[]{:S(2)}) collective-permute-start(bf16[128,1024]{1,0:T(8,128)(2,1)S(1)} %copy-done.20), channel_id=1, source_target_pairs={{0,2},{1,3},{2,0},{3,1},{4,6},{5,7},{6,4},{7,5},{8,10},{9,11},{10,... | collective-permute-start | bytes 786440 | tf_op jit(solution)/shard_map/ppermute | solution.py:56
  71.0 22.1 %collective-permute-start.17 = (bf16[128,1024]{1,0:T(8,128)(2,1)S(1)}, bf16[128,1024]{1,0:T(8,128)(2,1)S(1)}, u32[]{:S(2)}, u32[]{:S(2)}) collective-permute-start(bf16[128,1024]{1,0:T(8,128)(2,1)S(1)} %copy-done.20), channel_id=1, source_target_pairs={{0,4},{1,5},{2,6},{3,7},{4,0},{5,1},{6,2},{7,3},{8,12},{9,13},{10,... | collective-permute-start | bytes 786440 | tf_op jit(solution)/shard_map/ppermute | solution.py:56
  72.5 20.6 %collective-permute-start.14 = (bf16[64,1024]{1,0:T(8,128)(2,1)S(1)}, bf16[64,1024]{1,0:T(8,128)(2,1)S(1)}, u32[]{:S(2)}, u32[]{:S(2)}) collective-permute-start(bf16[64,1024]{1,0:T(8,128)(2,1)S(1)} %slice.251), channel_id=1, source_target_pairs={{0,4},{1,5},{2,6},{3,7},{4,0},{5,1},{6,2},{7,3},{8,12},{9,13},{10,... | collective-permute-start | bytes 393224 | tf_op jit(solution)/shard_map/ppermute | solution.py:56
  76.9 16.2 %collective-permute-start.15 = (bf16[64,1024]{1,0:T(8,128)(2,1)S(1)}, bf16[64,1024]{1,0:T(8,128)(2,1)S(1)}, u32[]{:S(2)}, u32[]{:S(2)}) collective-permute-start(bf16[64,1024]{1,0:T(8,128)(2,1)S(1)} %slice.252), channel_id=1, source_target_pairs={{0,2},{1,3},{2,0},{3,1},{4,6},{5,7},{6,4},{7,5},{8,10},{9,11},{10,... | collective-permute-start | bytes 393224 | tf_op jit(solution)/shard_map/ppermute | solution.py:56
  97.2 28.6 %collective-permute-start.23 = (bf16[128,1024]{1,0:T(8,128)(2,1)S(1)}, bf16[128,1024]{1,0:T(8,128)(2,1)}, u32[]{:S(2)}, u32[]{:S(2)}) collective-permute-start(bf16[128,1024]{1,0:T(8,128)(2,1)S(1)} %convert_element_type.145.refs_16_.refs_0_), channel_id=1, source_target_pairs={{0,8},{1,9},{2,10},{3,11},{4,12},{5,13},{6,14},{7,15},{8,16},{9,17... | collective-permute-start | bytes 786440 | tf_op jit(solution)/shard_map/ppermute | solution.py:68
  97.2 28.6 %collective-permute-start.24 = (bf16[128,1024]{1,0:T(8,128)(2,1)S(1)}, bf16[128,1024]{1,0:T(8,128)(2,1)}, u32[]{:S(2)}, u32[]{:S(2)}) collective-permute-start(bf16[128,1024]{1,0:T(8,128)(2,1)S(1)} %convert_element_type.145.refs_16_.refs_0_), channel_id=1, source_target_pairs={{0,24},{1,25},{2,26},{3,27},{4,28},{5,29},{6,30},{7,31},{8,0},{9,1... | collective-permute-start | bytes 786440 | tf_op jit(solution)/shard_map/ppermute | solution.py:68
  101.0 15.2 %collective-permute-start.25 = (bf16[64,1024]{1,0:T(8,128)(2,1)S(1)}, bf16[64,1024]{1,0:T(8,128)(2,1)S(1)}, u32[]{:S(2)}, u32[]{:S(2)}) collective-permute-start(bf16[64,1024]{1,0:T(8,128)(2,1)S(1)} %slice.253), channel_id=1, source_target_pairs={{0,4},{1,5},{2,6},{3,7},{4,0},{5,1},{6,2},{7,3},{8,12},{9,13},{10,... | collective-permute-start | bytes 393224 | tf_op jit(solution)/shard_map/ppermute | solution.py:56
  107.4 18.4 %collective-permute-start.21 = (bf16[128,1024]{1,0:T(8,128)(2,1)}, bf16[128,1024]{1,0:T(8,128)(2,1)S(1)}, u32[]{:S(2)}, u32[]{:S(2)}) collective-permute-start(bf16[128,1024]{1,0:T(8,128)(2,1)} %get-tuple-element.192.refs_0_), channel_id=1, source_target_pairs={{0,2},{1,3},{2,0},{3,1},{4,6},{5,7},{6,4},{7,5},{8,10},{9,11},{10,... | collective-permute-start | bytes 786440 | tf_op jit(solution)/shard_map/ppermute | solution.py:56
  108.5 17.3 %collective-permute-start.22 = (bf16[128,1024]{1,0:T(8,128)(2,1)}, bf16[128,1024]{1,0:T(8,128)(2,1)S(1)}, u32[]{:S(2)}, u32[]{:S(2)}) collective-permute-start(bf16[128,1024]{1,0:T(8,128)(2,1)} %get-tuple-element.192.refs_0_), channel_id=1, source_target_pairs={{0,4},{1,5},{2,6},{3,7},{4,0},{5,1},{6,2},{7,3},{8,12},{9,13},{10,... | collective-permute-start | bytes 786440 | tf_op jit(solution)/shard_map/ppermute | solution.py:56
  109.0 36.1 %all-to-all-start.4 = ((bf16[32,32,256]{2,1,0:T(8,128)(2,1)}), bf16[32,32,256]{2,1,0:T(8,128)(2,1)}, u32[]{:S(2)}, u32[]{:S(2)}) async-start(bf16[32,32,256]{2,1,0:T(8,128)(2,1)} %get-tuple-element.210), calls=%async_computation.4 | async-start | bytes 1048576 | tf_op jit(solution)/shard_map/all_to_all | solution.py:82
  125.7 19.3 %collective-permute-start.33 = (bf16[3,128,1024]{2,1,0:T(8,128)(2,1)S(1)}, bf16[3,128,1024]{2,1,0:T(8,128)(2,1)}, u32[]{:S(2)}, u32[]{:S(2)}) collective-permute-start(bf16[3,128,1024]{2,1,0:T(8,128)(2,1)S(1)} %pad_maximum_fusion.4), channel_id=1, source_target_pairs={{0,1},{1,0},{2,3},{3,2},{4,5},{5,4},{6,7},{7,6},{8,9},{9,8},{10,11... | collective-permute-start | bytes 2359304 | tf_op jit(solution)/shard_map/ppermute | solution.py:56
  125.9 19.2 %collective-permute-start.30 = (bf16[3,128,1024]{2,1,0:T(8,128)(2,1)S(1)}, bf16[3,128,1024]{2,1,0:T(8,128)(2,1)}, u32[]{:S(2)}, u32[]{:S(2)}) collective-permute-start(bf16[3,128,1024]{2,1,0:T(8,128)(2,1)S(1)} %pad_maximum_fusion.3), channel_id=1, source_target_pairs={{0,1},{1,0},{2,3},{3,2},{4,5},{5,4},{6,7},{7,6},{8,9},{9,8},{10,11... | collective-permute-start | bytes 2359304 | tf_op jit(solution)/shard_map/ppermute | solution.py:56
  126.5 15.6 %collective-permute-start.29 = (bf16[128,1024]{1,0:T(8,128)(2,1)S(1)}, bf16[128,1024]{1,0:T(8,128)(2,1)S(1)}, u32[]{:S(2)}, u32[]{:S(2)}) collective-permute-start(bf16[128,1024]{1,0:T(8,128)(2,1)S(1)} %convert_element_type.145.refs_16_.refs_0_), channel_id=1, source_target_pairs={{0,16},{1,17},{2,18},{3,19},{4,20},{5,21},{6,22},{7,23},{8,24},{9,... | collective-permute-start | bytes 786440 | tf_op jit(solution)/shard_map/ppermute | solution.py:68
  128.8 13.4 %collective-permute-start.27 = (bf16[64,1024]{1,0:T(8,128)(2,1)S(1)}, bf16[64,1024]{1,0:T(8,128)(2,1)S(1)}, u32[]{:S(2)}, u32[]{:S(2)}) collective-permute-start(bf16[64,1024]{1,0:T(8,128)(2,1)S(1)} %slice.255), channel_id=1, source_target_pairs={{0,4},{1,5},{2,6},{3,7},{4,0},{5,1},{6,2},{7,3},{8,12},{9,13},{10,... | collective-permute-start | bytes 393224 | tf_op jit(solution)/shard_map/ppermute | solution.py:56
  130.3 12.3 %collective-permute-start.28 = (bf16[64,1024]{1,0:T(8,128)(2,1)S(1)}, bf16[64,1024]{1,0:T(8,128)(2,1)S(1)}, u32[]{:S(2)}, u32[]{:S(2)}) collective-permute-start(bf16[64,1024]{1,0:T(8,128)(2,1)S(1)} %slice.256), channel_id=1, source_target_pairs={{0,2},{1,3},{2,0},{3,1},{4,6},{5,7},{6,4},{7,5},{8,10},{9,11},{10,... | collective-permute-start | bytes 393224 | tf_op jit(solution)/shard_map/ppermute | solution.py:56
  159.4 12.8 %collective-permute-start.42 = (bf16[128,1024]{1,0:T(8,128)(2,1)}, bf16[128,1024]{1,0:T(8,128)(2,1)S(1)}, u32[]{:S(2)}, u32[]{:S(2)}) collective-permute-start(bf16[128,1024]{1,0:T(8,128)(2,1)} %get-tuple-element.215), channel_id=1, source_target_pairs={{0,8},{1,9},{2,10},{3,11},{4,12},{5,13},{6,14},{7,15},{8,16},{9,17... | collective-permute-start | bytes 786440 | tf_op jit(solution)/shard_map/ppermute | solution.py:68
  168.6 20.4 %collective-permute-start.45 = (bf16[128,1024]{1,0:T(8,128)(2,1)S(1)}, bf16[128,1024]{1,0:T(8,128)(2,1)S(1)}, u32[]{:S(2)}, u32[]{:S(2)}) collective-permute-start(bf16[128,1024]{1,0:T(8,128)(2,1)S(1)} %copy-done.58), channel_id=1, source_target_pairs={{0,16},{1,17},{2,18},{3,19},{4,20},{5,21},{6,22},{7,23},{8,24},{9,... | collective-permute-start | bytes 786440 | tf_op jit(solution)/shard_map/ppermute | solution.py:68
  170.4 18.7 %collective-permute-start.46 = (bf16[128,1024]{1,0:T(8,128)(2,1)S(1)}, bf16[128,1024]{1,0:T(8,128)(2,1)S(1)}, u32[]{:S(2)}, u32[]{:S(2)}) collective-permute-start(bf16[128,1024]{1,0:T(8,128)(2,1)S(1)} %copy-done.57), channel_id=1, source_target_pairs={{0,24},{1,25},{2,26},{3,27},{4,28},{5,29},{6,30},{7,31},{8,0},{9,1... | collective-permute-start | bytes 786440 | tf_op jit(solution)/shard_map/ppermute | solution.py:68
  179.4 12.3 %collective-permute-start.43 = (bf16[128,1024]{1,0:T(8,128)(2,1)}, bf16[128,1024]{1,0:T(8,128)(2,1)S(1)}, u32[]{:S(2)}, u32[]{:S(2)}) collective-permute-start(bf16[128,1024]{1,0:T(8,128)(2,1)} %get-tuple-element.221.refs_0_), channel_id=1, source_target_pairs={{0,2},{1,3},{2,0},{3,1},{4,6},{5,7},{6,4},{7,5},{8,10},{9,11},{10,... | collective-permute-start | bytes 786440 | tf_op jit(solution)/shard_map/ppermute | solution.py:56
  191.8 23.7 %all-to-all-start.6 = ((bf16[32,32,256]{2,1,0:T(8,128)(2,1)}), bf16[32,32,256]{2,1,0:T(8,128)(2,1)S(1)}, u32[]{:S(2)}, u32[]{:S(2)}) async-start(bf16[32,32,256]{2,1,0:T(8,128)(2,1)} %bitcast.174), calls=%async_computation.6 | async-start | bytes 1048576 | tf_op jit(solution)/shard_map/all_to_all | solution.py:82
  195.9 19.6 %collective-permute-start.47 = (bf16[64,1024]{1,0:T(8,128)(2,1)S(1)}, bf16[64,1024]{1,0:T(8,128)(2,1)S(1)}, u32[]{:S(2)}, u32[]{:S(2)}) collective-permute-start(bf16[64,1024]{1,0:T(8,128)(2,1)S(1)} %slice.275), channel_id=1, source_target_pairs={{0,4},{1,5},{2,6},{3,7},{4,0},{5,1},{6,2},{7,3},{8,12},{9,13},{10,... | collective-permute-start | bytes 393224 | tf_op jit(solution)/shard_map/ppermute | solution.py:56
  197.5 18.0 %collective-permute-start.48 = (bf16[64,1024]{1,0:T(8,128)(2,1)S(1)}, bf16[64,1024]{1,0:T(8,128)(2,1)}, u32[]{:S(2)}, u32[]{:S(2)}) collective-permute-start(bf16[64,1024]{1,0:T(8,128)(2,1)S(1)} %slice.276), channel_id=1, source_target_pairs={{0,2},{1,3},{2,0},{3,1},{4,6},{5,7},{6,4},{7,5},{8,10},{9,11},{10,... | collective-permute-start | bytes 393224 | tf_op jit(solution)/shard_map/ppermute | solution.py:56
  215.5 29.4 %all-to-all-start.7 = ((bf16[32,32,256]{2,1,0:T(8,128)(2,1)}), bf16[32,32,256]{2,1,0:T(8,128)(2,1)S(1)}, u32[]{:S(2)}, u32[]{:S(2)}) async-start(bf16[32,32,256]{2,1,0:T(8,128)(2,1)} %bitcast.45), calls=%async_computation.7 | async-start | bytes 1048576 | tf_op jit(solution)/shard_map/all_to_all | solution.py:82
  222.8 22.1 %collective-permute-start.49 = (bf16[1024,256]{1,0:T(8,128)(2,1)}, bf16[1024,256]{1,0:T(8,128)(2,1)S(1)}, u32[]{:S(2)}, u32[]{:S(2)}) collective-permute-start(bf16[1024,256]{1,0:T(8,128)(2,1)} %get-tuple-element.235), channel_id=1, source_target_pairs={{8,0},{9,1},{10,2},{11,3},{12,4},{13,5},{14,6},{15,7},{16,8},{17,9... | collective-permute-start | bytes 1572872 | tf_op jit(solution)/shard_map/ppermute | solution.py:61
  224.1 20.8 %collective-permute-start.50 = (bf16[1024,256]{1,0:T(8,128)(2,1)}, bf16[1024,256]{1,0:T(8,128)(2,1)S(1)}, u32[]{:S(2)}, u32[]{:S(2)}) collective-permute-start(bf16[1024,256]{1,0:T(8,128)(2,1)} %get-tuple-element.236), channel_id=1, source_target_pairs={{0,8},{1,9},{2,10},{3,11},{4,12},{5,13},{6,14},{7,15},{8,16},{9,17... | collective-permute-start | bytes 1572872 | tf_op jit(solution)/shard_map/ppermute | solution.py:61
  263.9 17.3 %collective-permute-start.61 = (bf16[128,1024]{1,0:T(8,128)(2,1)}, bf16[128,1024]{1,0:T(8,128)(2,1)S(1)}, u32[]{:S(2)}, u32[]{:S(2)}) collective-permute-start(bf16[128,1024]{1,0:T(8,128)(2,1)} %get-tuple-element.276), channel_id=1, source_target_pairs={{0,1},{1,0},{2,3},{3,2},{4,5},{5,4},{6,7},{7,6},{8,9},{9,8},{10,11... | collective-permute-start | bytes 786440 | tf_op jit(solution)/shard_map/ppermute | solution.py:56
  267.5 11.8 %collective-permute-start.69 = (f32[32,1024]{1,0:T(8,128)}, f32[32,1024]{1,0:T(8,128)S(1)}, u32[]{:S(2)}, u32[]{:S(2)}) collective-permute-start(f32[32,1024]{1,0:T(8,128)} %convert_add_fusion.7), channel_id=1, source_target_pairs={{0,0},{1,4},{2,8},{3,12},{4,16},{5,20},{6,24},{7,28},{8,1},{9,5},{... | collective-permute-start | bytes 393224 | tf_op jit(solution)/shard_map/ppermute | solution.py:880
  270.6 31.1 %all-to-all-start.8 = ((bf16[32,40,384]{2,1,0:T(8,128)(2,1)}), bf16[32,40,384]{2,1,0:T(8,128)(2,1)S(1)}, u32[]{:S(2)}, u32[]{:S(2)}) async-start(bf16[32,40,384]{2,1,0:T(8,128)(2,1)} %pad_maximum_fusion), calls=%async_computation.8 | async-start | bytes 1966080 | tf_op jit(solution)/shard_map/all_to_all | solution.py:82
  276.8 17.1 %collective-permute-start.54 = (bf16[3,128,1024]{2,1,0:T(8,128)(2,1)}, bf16[3,128,1024]{2,1,0:T(8,128)(2,1)}, u32[]{:S(2)}, u32[]{:S(2)}) collective-permute-start(bf16[3,128,1024]{2,1,0:T(8,128)(2,1)} %get-tuple-element.272), channel_id=1, source_target_pairs={{0,1},{1,0},{2,3},{3,2},{4,5},{5,4},{6,7},{7,6},{8,9},{9,8},{10,11... | collective-permute-start | bytes 2359304 | tf_op jit(solution)/shard_map/ppermute | solution.py:56
  284.2 14.6 %collective-permute-start.62 = (bf16[64,1024]{1,0:T(8,128)(2,1)S(1)}, bf16[64,1024]{1,0:T(8,128)(2,1)S(1)}, u32[]{:S(2)}, u32[]{:S(2)}) collective-permute-start(bf16[64,1024]{1,0:T(8,128)(2,1)S(1)} %get-tuple-element.325), channel_id=1, source_target_pairs={{0,4},{1,5},{2,6},{3,7},{4,0},{5,1},{6,2},{7,3},{8,12},{9,13},{10,... | collective-permute-start | bytes 393224 | tf_op jit(solution)/shard_map/ppermute | solution.py:56
  292.0 25.2 %collective-permute-start.65 = (bf16[128,1024]{1,0:T(8,128)(2,1)}, bf16[128,1024]{1,0:T(8,128)(2,1)S(1)}, u32[]{:S(2)}, u32[]{:S(2)}) collective-permute-start(bf16[128,1024]{1,0:T(8,128)(2,1)} %pad_maximum_fusion.13), channel_id=1, source_target_pairs={{0,4},{1,5},{2,6},{3,7},{4,0},{5,1},{6,2},{7,3},{8,12},{9,13},{10,... | collective-permute-start | bytes 786440 | tf_op jit(solution)/shard_map/ppermute | solution.py:56
  297.0 18.0 %collective-permute-start.57 = (bf16[128,1024]{1,0:T(8,128)(2,1)}, bf16[128,1024]{1,0:T(8,128)(2,1)}, u32[]{:S(2)}, u32[]{:S(2)}) collective-permute-start(bf16[128,1024]{1,0:T(8,128)(2,1)} %pad_maximum_fusion.10), channel_id=1, source_target_pairs={{0,2},{1,3},{2,0},{3,1},{4,6},{5,7},{6,4},{7,5},{8,10},{9,11},{10,... | collective-permute-start | bytes 786440 | tf_op jit(solution)/shard_map/ppermute | solution.py:56
  298.5 16.5 %collective-permute-start.59 = (bf16[128,1024]{1,0:T(8,128)(2,1)}, bf16[128,1024]{1,0:T(8,128)(2,1)}, u32[]{:S(2)}, u32[]{:S(2)}) collective-permute-start(bf16[128,1024]{1,0:T(8,128)(2,1)} %pad_maximum_fusion.11), channel_id=1, source_target_pairs={{0,4},{1,5},{2,6},{3,7},{4,0},{5,1},{6,2},{7,3},{8,12},{9,13},{10,... | collective-permute-start | bytes 786440 | tf_op jit(solution)/shard_map/ppermute | solution.py:56
  299.6 17.6 %collective-permute-start.63 = (bf16[128,1024]{1,0:T(8,128)(2,1)}, bf16[128,1024]{1,0:T(8,128)(2,1)}, u32[]{:S(2)}, u32[]{:S(2)}) collective-permute-start(bf16[128,1024]{1,0:T(8,128)(2,1)} %pad_maximum_fusion.12), channel_id=1, source_target_pairs={{0,2},{1,3},{2,0},{3,1},{4,6},{5,7},{6,4},{7,5},{8,10},{9,11},{10,... | collective-permute-start | bytes 786440 | tf_op jit(solution)/shard_map/ppermute | solution.py:56
  307.7 14.4 %all-to-all-start.9 = ((f32[32,1,128]{2,1,0:T(1,128)}), f32[32,1,128]{2,1,0:T(1,128)S(1)}, u32[]{:S(2)}, u32[]{:S(2)}) async-start(f32[32,1,128]{2,1,0:T(1,128)} %broadcast_in_dim.71), calls=%async_computation.9 | async-start | bytes 32768 | tf_op jit(solution)/shard_map/all_to_all | solution.py:82
  (104 other events, 987.4 us)

commit v3 on v2

v3 whole, which is shorter than its diff:
```python
import functools

import jax
import jax.numpy as jnp
from jax import lax
from jax.experimental import pallas as pl
from jax.experimental.pallas import tpu as pltpu
from jax.sharding import PartitionSpec as P

HEADS = 16
STEP = 10
EPSILON = 1e-05
MOMENTUM = 0.9
LEARNING_RATES = (60.0, 480.0, 60.0, 60.0, 600.0)
WEIGHT_DECAY = 0.0001
CLIP_NORM = 1.0
MASK_FLOOR = -1e30
PLANE = 8
EXTRA = 8
LANES = 128
QUERY_TILE = 512
KEY_TILE = 640
F32 = jnp.float32
LOW = jnp.bfloat16
WHOLE = pl.BlockSpec()
SMEM = pl.BlockSpec(memory_space=pltpu.SMEM)


def like(shape, dtype):
    return jax.ShapeDtypeStruct(shape, dtype)


def kernel_call(body, outs, *args, scalars=(), scratch=(), flops=0, limit=60):
    moved = sum(a.size * a.dtype.itemsize for a in list(args) + list(outs))
    return pl.pallas_call(
        body,
        in_specs=[SMEM] * len(scalars) + [WHOLE] * len(args),
        out_specs=[WHOLE] * len(outs),
        out_shape=list(outs),
        scratch_shapes=list(scratch),
        cost_estimate=pl.CostEstimate(flops=flops, bytes_accessed=moved, transcendentals=0),
        compiler_params=pltpu.CompilerParams(vmem_limit_bytes=limit << 20),
    )(*scalars, *args)


def after(value, *others):
    return lax.optimization_barrier((value, *others))[0]


def tie(*values):
    return lax.optimization_barrier(values)


def swap(block, bit):
    n = lax.axis_size("seq")
    return lax.ppermute(block, "seq", [(i, i ^ bit) for i in range(n)])


def move(block, distance):
    n = lax.axis_size("seq")
    return lax.ppermute(
        block, "seq", [(i, i + distance) for i in range(n) if 0 <= i + distance < n]
    )


def turn(block, planes_on):
    n = lax.axis_size("seq")
    return lax.ppermute(block, "seq", [(i, (i + planes_on * PLANE) % n) for i in range(n)])


def plane_groups():
    n = lax.axis_size("seq")
    return [[g * PLANE + j for j in range(PLANE)] for g in range(n // PLANE)]


def cross_groups():
    n = lax.axis_size("seq")
    return [[g * PLANE + j for g in range(n // PLANE)] for j in range(PLANE)]


def exchange(blocks, groups=None):
    return lax.all_to_all(blocks, "seq", 0, 0, axis_index_groups=groups)


def spread_sides(block):
    return swap(block, 2), swap(block, 4)


def spread_corner(across, along):
    half = across.shape[0] // 2
    return swap(across[:half], 4), swap(along[half:], 2)


def grow(block, bit):
    return jnp.concatenate([block, swap(block, bit)], axis=0)


def spread_far(block, sides, corner):
    far = swap(jnp.stack([block, *sides]), 1)
    return [block, *sides, *corner, far, *[swap(c, 1) for c in corner]]


def spread(block):
    sides = spread_sides(block)
    return spread_far(block, sides, spread_corner(*sides))


SPREAD = 8


def join(refs, out):
    number = refs[0].shape[0]
    place = 0
    for ref in refs:
        if len(ref.shape) == 3:
            for m in range(ref.shape[0]):
                out[pl.ds(place, number), :] = ref[m]
                place += number
        else:
            out[pl.ds(place, ref.shape[0]), :] = ref[...]
            place += ref.shape[0]


def collect(near, far, far_corner):
    return collect_came(near, swap(far_corner, 1), swap(far, 1))


def collect_came(near, came_corner, came):
    half = near.shape[1] // 2
    corner = (near[3] + came_corner.astype(F32)).astype(LOW)
    by_across = swap(corner[:half], 2).astype(F32)
    by_along = swap(corner[half:], 4).astype(F32)
    across = near[1] + came[1].astype(F32)
    along = near[2] + came[2].astype(F32)
    across = jnp.concatenate([across[:half], across[half:] + by_along], axis=0).astype(LOW)
    along = jnp.concatenate([along[:half] + by_across, along[half:]], axis=0).astype(LOW)
    return near[0] + came[0].astype(F32), swap(across, 2), swap(along, 4)


def put_block(outs, k, m, value):
    if k == 0:
        outs[0][m] = value
    elif m < 3:
        outs[1][m] = value.astype(LOW)
    else:
        outs[2][...] = value.astype(LOW)


def total(terms):
    return terms[0] + terms[1].astype(F32) + terms[2].astype(F32)


def norm_parts(values):
    centre = values - jnp.mean(values, axis=-1, keepdims=True)
    spread_of = jnp.mean(centre * centre, axis=-1, keepdims=True)
    inverse = lax.rsqrt(spread_of + EPSILON)
    return centre * inverse, inverse


def norm_back(unit, inverse, gain, incoming):
    scaled = incoming * gain
    return inverse * (
        scaled
        - jnp.mean(scaled, axis=-1, keepdims=True)
        - unit * jnp.mean(scaled * unit, axis=-1, keepdims=True)
    )


def dot(a, b, dims=((1,), (0,))):
    return lax.dot_general(a, b, (dims, ((), ())), preferred_element_type=F32)


NT = ((1,), (1,))
TN = ((0,), (0,))


def block_rows(place, number):
    return pl.ds(pl.multiple_of(place * number, number), number)


def gather_planes(plane, refs, out):
    planes = len(refs)
    rows = refs[0].shape[0]
    for s, ref in enumerate(refs):
        out[block_rows(lax.rem(plane - s + planes, planes), rows), :] = ref[...]


def project_kernel(spot_ref, *refs):
    token_refs, refs = refs[:SPREAD], refs[SPREAD:]
    sent_ref, lots_ref, unit_ref, first_ref, query_ref, pair_ref, weight_ref, vector_ref, held = refs
    spot = spot_ref[0]
    number, columns = token_refs[0].shape
    devices = sent_ref.shape[0]
    rows = columns // devices
    for d in range(devices):
        weight_ref[pl.ds(d * rows, rows), :] = sent_ref[d, :rows, :]
    for g in range(lots_ref.shape[0]):
        lanes = slice(g * LANES, (g + 1) * LANES)
        vector_ref[:EXTRA, lanes] = lots_ref[g, :, :LANES]
        vector_ref[EXTRA:, lanes] = lots_ref[g, :, LANES : 2 * LANES]
    join(token_refs, held)
    gain, shift = vector_ref[0:1, :], vector_ref[1:2, :]
    for r in range(PLANE):
        here = pl.ds(r * number, number)
        unit, _ = norm_parts(held[here, :].astype(F32))
        first = (unit * gain + shift).astype(LOW)
        unit_ref[here, :] = unit.astype(LOW)
        held[here, :] = first
        first_ref[block_rows(spot ^ relative(r), number), :] = first
    joined = dot(held[...], weight_ref[...]).astype(LOW)
    wide = query_ref.shape[1]
    for r in range(PLANE):
        here = slice(r * number, (r + 1) * number)
        query_ref[block_rows(spot ^ relative(r), number), :] = joined[here, :wide]
        pair_ref[block_rows(spot ^ relative(r), number), :] = joined[here, wide:]


def relative(r):
    return 2 * (r % 4) + r // 4


def head_part(array, head):
    lanes = lax.broadcasted_iota(jnp.int32, array.shape, len(array.shape) - 1)
    return jnp.where(lanes // 64 == head, array, jnp.zeros_like(array))


def scene_marks(bound_ref, first, count, inside, outside):
    place = first + lax.broadcasted_iota(jnp.int32, (count, LANES), 0)
    here = (place >= bound_ref[0:1, :]) & (place < bound_ref[1:2, :])
    return jnp.where(here, inside, outside).astype(LOW)


def marked_queries(bound_ref, query_ref, first):
    queries = query_ref[...] * jnp.asarray(0.125, LOW)
    marks = scene_marks(bound_ref, first, queries.shape[0], MASK_FLOOR, 0.0)
    return [jnp.concatenate([head_part(queries, h), marks], axis=1) for h in range(2)]


def marked_keys(bound_ref, refs, keys):
    tokens = refs[0].shape[0]
    for place, ref in enumerate(refs):
        keys[pl.ds(place * tokens, tokens), :LANES] = ref[:, :LANES]
        keys[pl.ds(place * tokens, tokens), LANES:] = scene_marks(bound_ref, place * tokens, tokens, 0.0, 1.0)
    keys[3 * tokens :, :LANES] = jnp.zeros((keys.shape[0] - 3 * tokens, LANES), LOW)
    keys[3 * tokens :, LANES:] = jnp.ones((keys.shape[0] - 3 * tokens, LANES), LOW)


def attend_kernel(
    range_ref, query_ref, before_ref, own_ref, after_ref, bound_ref, mixed_ref, low_ref, log_ref, keys, values
):
    step = pl.program_id(0)
    tokens = own_ref.shape[0]
    here = query_ref.shape[0]

    @pl.when(step == 0)
    def _():
        refs = (before_ref, own_ref, after_ref)
        marked_keys(bound_ref, refs, keys)
        for place, ref in enumerate(refs):
            values[:, pl.ds(place * tokens, tokens)] = ref[:, LANES:].T
        values[:, 3 * tokens :] = jnp.zeros((LANES, values.shape[1] - 3 * tokens), LOW)

    queries = marked_queries(bound_ref, query_ref, tokens + step * here)
    origin = range_ref[0, step] * LANES

    def body(index, carry):
        start = pl.multiple_of(origin + index * KEY_TILE, LANES)
        block = keys[pl.ds(start, KEY_TILE), :]
        out = []
        for h in range(2):
            peak, whole, mixed = carry[h]
            scores = dot(block, queries[h], NT)
            raised_peak = jnp.maximum(peak, jnp.max(scores, axis=0, keepdims=True))
            raised = jnp.exp(scores - raised_peak)
            fade = jnp.exp(peak - raised_peak)
            whole = whole * fade + jnp.sum(raised, axis=0, keepdims=True)
            turned = values[64 * h : 64 * h + 64, pl.ds(start, KEY_TILE)]
            mixed = mixed * fade + dot(turned, raised.astype(LOW))
            out.append((raised_peak, whole, mixed))
        return tuple(out)

    init = tuple(
        (jnp.full((1, here), MASK_FLOOR, F32), jnp.zeros((1, here), F32), jnp.zeros((64, here), F32))
        for _ in range(2)
    )
    done = lax.fori_loop(0, range_ref[1, step], body, init)
    mixed = jnp.concatenate([m / t for _, t, m in done], axis=0).T
    mixed_ref[...] = mixed
    low_ref[...] = mixed.astype(LOW)
    log_ref[...] = jnp.concatenate([k + jnp.log(t) for k, t, _ in done], axis=0)


def attend_back_kernel(
    range_ref,
    query_ref,
    before_ref,
    own_ref,
    after_ref,
    bound_ref,
    mixed_ref,
    log_ref,
    grad_ref,
    query_grad_ref,
    before_grad_ref,
    own_grad_ref,
    after_grad_ref,
    keys,
    values,
    turned_keys,
    key_grad,
    value_grad,
):
    step = pl.program_id(0)
    tokens = own_ref.shape[0]
    here = query_ref.shape[0]

    @pl.when(step == 0)
    def _():
        refs = (before_ref, own_ref, after_ref)
        marked_keys(bound_ref, refs, keys)
        for place, ref in enumerate(refs):
            values[pl.ds(place * tokens, tokens), :] = ref[:, LANES:]
            turned_keys[:, pl.ds(place * tokens, tokens)] = ref[:, :LANES].T
        values[3 * tokens :, :] = jnp.zeros((values.shape[0] - 3 * tokens, LANES), LOW)
        turned_keys[:, 3 * tokens :] = jnp.zeros((LANES, values.shape[0] - 3 * tokens), LOW)
        key_grad[...] = jnp.zeros_like(key_grad)
        value_grad[...] = jnp.zeros_like(value_grad)

    queries = marked_queries(bound_ref, query_ref, tokens + step * here)
    grads = grad_ref[...]
    split_grads = [head_part(grads, h) for h in range(2)]
    product = (grads.astype(F32) * mixed_ref[...]).T
    centred = [jnp.sum(product[64 * h : 64 * h + 64], axis=0, keepdims=True) for h in range(2)]
    origin = range_ref[0, step] * LANES

    def body(index, carry):
        start = pl.multiple_of(origin + index * KEY_TILE, LANES)
        rows = pl.ds(start, KEY_TILE)
        out, key_part, value_part = [], 0, 0
        for h in range(2):
            shares = jnp.exp(dot(keys[rows, :], queries[h], NT) - log_ref[h : h + 1, :])
            value_part += dot(shares.astype(LOW), split_grads[h])
            share_grad = dot(values[rows, :], split_grads[h], NT)
            score_grad = (shares * (share_grad - centred[h])).astype(LOW)
            key_part += dot(score_grad, queries[h][:, :LANES])
            out.append(carry[h] + dot(turned_keys[64 * h : 64 * h + 64, rows], score_grad))
        key_grad[rows, :] += key_part
        value_grad[rows, :] += value_part
        return tuple(out)

    init = tuple(jnp.zeros((64, here), F32) for _ in range(2))
    done = lax.fori_loop(0, range_ref[1, step], body, init)
    query_grad_ref[...] = (jnp.concatenate(done, axis=0).T * 0.125).astype(LOW)

    @pl.when(step == pl.num_programs(0) - 1)
    def _():
        for place, ref in enumerate((before_grad_ref, own_grad_ref, after_grad_ref)):
            ref[:, :LANES] = key_grad[pl.ds(place * tokens, tokens), :].astype(ref.dtype)
            ref[:, LANES:] = value_grad[pl.ds(place * tokens, tokens), :].astype(ref.dtype)


def key_ranges(spans, query_tile, key_tile):
    first = spans[0, ::query_tile] // LANES
    return jnp.stack([first, (spans[1, query_tile - 1 :: query_tile] - first * LANES + key_tile - 1) // key_tile])


def attention(spans, bounds, queries, before, own, behind):
    tokens, wide = queries.shape
    whole = lambda shape: pl.BlockSpec(shape, lambda i, s: (0, 0))
    tile = pl.BlockSpec((QUERY_TILE, wide), lambda i, s: (i, 0))
    row = pl.BlockSpec((2, QUERY_TILE), lambda i, s: (0, i))
    window = 3 * tokens + KEY_TILE
    return pl.pallas_call(
        attend_kernel,
        grid_spec=pltpu.PrefetchScalarGridSpec(
            num_scalar_prefetch=1,
            grid=(tokens // QUERY_TILE,),
            in_specs=[tile] + [whole((tokens, 2 * wide))] * 3 + [whole(bounds.shape)],
            out_specs=[tile, tile, row],
            scratch_shapes=[pltpu.VMEM((window, 2 * wide), LOW), pltpu.VMEM((wide, window), LOW)],
        ),
        out_shape=[like((tokens, wide), F32), like((tokens, wide), LOW), like((2, tokens), F32)],
        cost_estimate=pl.CostEstimate(
            flops=40 * tokens * tokens * wide, bytes_accessed=16 * tokens * wide, transcendentals=2 * tokens * tokens
        ),
        compiler_params=pltpu.CompilerParams(vmem_limit_bytes=60 << 20),
    )(key_ranges(spans, QUERY_TILE, KEY_TILE), queries, before, own, behind, bounds)


def attention_back(spans, bounds, queries, before, own, behind, mixed, logs, grads):
    tokens, wide = queries.shape
    whole = lambda shape: pl.BlockSpec(shape, lambda i, s: (0, 0))
    tile = pl.BlockSpec((QUERY_TILE, wide), lambda i, s: (i, 0))
    row = pl.BlockSpec((2, QUERY_TILE), lambda i, s: (0, i))
    window = 3 * tokens + KEY_TILE
    return pl.pallas_call(
        attend_back_kernel,
        grid_spec=pltpu.PrefetchScalarGridSpec(
            num_scalar_prefetch=1,
            grid=(tokens // QUERY_TILE,),
            in_specs=[tile] + [whole((tokens, 2 * wide))] * 3 + [whole(bounds.shape), tile, row, tile],
            out_specs=[tile] + [whole((tokens, 2 * wide))] * 3,
            scratch_shapes=[
                pltpu.VMEM((window, 2 * wide), LOW),
                pltpu.VMEM((window, wide), LOW),
                pltpu.VMEM((wide, window), LOW),
                pltpu.VMEM((window, wide), F32),
                pltpu.VMEM((window, wide), F32),
            ],
        ),
        out_shape=[
            like((tokens, wide), LOW),
            like((tokens, 2 * wide), LOW),
            like((tokens, 2 * wide), F32),
            like((tokens, 2 * wide), LOW),
        ],
        cost_estimate=pl.CostEstimate(
            flops=60 * tokens * tokens * wide, bytes_accessed=32 * tokens * wide, transcendentals=2 * tokens * tokens
        ),
        compiler_params=pltpu.CompilerParams(vmem_limit_bytes=60 << 20),
    )(key_ranges(spans, QUERY_TILE, KEY_TILE), queries, before, own, behind, bounds, mixed, logs, grads)


def output_steps(planes):
    return [PLANE << i for i in range(planes.bit_length() - 1)] + [4, 2, 1]


def step_bits(index, steps):
    return sum(bit for i, bit in enumerate(steps) if index >> i & 1)


def place_output(planes, place_ref, refs, out):
    if len(refs) == 1:
        out[...] = refs[0][...]
        return
    devices = PLANE * planes
    rows = out.shape[0] // devices
    steps = output_steps(planes)
    device = place_ref[1] * PLANE + place_ref[0]
    for k, ref in enumerate(refs):
        for i in range(devices // 2):
            bits = step_bits(k * devices // 2 + i, steps)
            out[block_rows(device ^ bits, rows), :] = ref[pl.ds(i * rows, rows), :]


def ordered_output(device, planes, refs):
    devices = PLANE * planes
    rows = 2 * refs[0].shape[0] // devices
    if rows % 16 == 0:
        return refs
    whole = jnp.concatenate(refs, axis=0).reshape(devices, rows, -1)
    steps = output_steps(planes)
    bits = jnp.array([step_bits(i, steps) for i in range(devices)], jnp.int32)
    return [jnp.zeros_like(whole).at[device ^ bits].set(whole).reshape(devices * rows, -1)]


def mix_out_kernel(planes, place_ref, mixed_ref, tokens_ref, vector_ref, *refs):
    output_refs, (second_ref, normed_ref, output) = refs[:-3], refs[-3:]
    place_output(planes, place_ref, output_refs, output)
    mixed = jnp.concatenate([mixed_ref[j] for j in range(PLANE)], axis=1)
    second = tokens_ref[...].astype(F32) + dot(mixed, output[...])
    second_ref[...] = second
    unit, _ = norm_parts(second)
    normed_ref[...] = (unit * vector_ref[2:3, :] + vector_ref[3:4, :]).astype(LOW)


def feed_kernel(planes, place_ref, *refs):
    normed_refs, refs = refs[:SPREAD], refs[SPREAD:]
    cot_refs, refs = refs[:2], refs[2:]
    shrink_refs, refs = refs[:planes], refs[planes:]
    expand_refs, refs = refs[:2], refs[2:]
    bias_ref, near_out, far_out, corner_out, active_ref, grad_ref, bias_out, expand, shrink, x, c = refs
    part = expand.shape[1] // 2
    expand[:, :part] = expand_refs[0][...]
    expand[:, part:] = expand_refs[1][...]
    gather_planes(place_ref[1], shrink_refs, shrink)
    join(normed_refs, x)
    join(cot_refs, c)
    number = near_out.shape[1]
    sums = jnp.zeros(bias_ref.shape, F32)
    for k, m in ((1, 2), (1, 0), (0, 2), (0, 0)):
        rows = pl.ds((4 * k + m) * number, 2 * number)
        upper = dot(x[rows, :], expand[...]) + bias_ref[...]
        share = 0.5 + 0.5 * lax.erf(upper * 0.7071067811865476)
        density = 0.3989422804014327 * jnp.exp(-0.5 * upper * upper)
        active_ref[rows, :] = (upper * share).astype(LOW)
        grad = (dot(c[rows, :], shrink[...], NT) * (share + upper * density)).astype(LOW)
        grad_ref[rows, :] = grad
        sums += jnp.sum(grad.astype(F32), axis=0, keepdims=True)
        down = dot(grad, expand[...], NT)
        put_block((near_out, far_out, corner_out), k, m, down[:number])
        put_block((near_out, far_out, corner_out), k, m + 1, down[number:])
    bias_out[...] = sums


def plane_blocks(plane, whole, outs):
    planes = len(outs)
    tall = whole.shape[0] // planes
    for s, out in enumerate(outs):
        out[...] = whole[block_rows(lax.rem(plane + s, planes), tall), :].astype(out.dtype)


def shrink_grad_kernel(place_ref, active_ref, *refs):
    cot_refs, outs, (whole, cotangents) = refs[:2], refs[2:-2], refs[-2:]
    join(cot_refs, cotangents)
    whole[...] = dot(active_ref[...], cotangents[...], TN)
    plane_blocks(place_ref[1], whole, outs)


def expand_grad_kernel(grad_ref, *refs):
    normed_refs, (out_ref, normed) = refs[:SPREAD], refs[SPREAD:]
    join(normed_refs, normed)
    out_ref[...] = dot(normed[...], grad_ref[...], TN).astype(LOW)


def norm_two_back_kernel(
    planes, place_ref, one_ref, two_ref, three_ref, second_ref, cotangent_ref, vector_ref, *refs
):
    output_refs, (second_grad_ref, branch_ref, mixed_ref, sums_ref, output) = refs[:-5], refs[-5:]
    place_output(planes, place_ref, output_refs, output)
    incoming = one_ref[...] + two_ref[...].astype(F32) + three_ref[...].astype(F32)
    unit, inverse = norm_parts(second_ref[...])
    cotangent = cotangent_ref[...].astype(F32)
    second_grad = cotangent + norm_back(unit, inverse, vector_ref[2:3, :], incoming)
    second_grad_ref[...] = second_grad
    branch = second_grad.astype(LOW)
    branch_ref[...] = branch
    mixed = dot(branch, output[...], NT).astype(LOW)
    wide = mixed_ref.shape[2]
    for j in range(PLANE):
        mixed_ref[j] = mixed[:, wide * j : wide * j + wide]
    sums_ref[...] = jnp.concatenate(
        [
            jnp.sum(incoming * unit, axis=0, keepdims=True),
            jnp.sum(incoming, axis=0, keepdims=True),
            jnp.sum(cotangent, axis=0, keepdims=True),
        ],
        axis=0,
    )


def output_grad_kernel(place_ref, mixed_ref, *refs):
    branch_refs, outs, (whole, left, right) = refs[:2], refs[2:-3], refs[-3:]
    join(branch_refs, right)
    number = right.shape[0] // PLANE
    for r in range(PLANE):
        left[pl.ds(r * number, number), :] = mixed_ref[block_rows(place_ref[0] ^ relative(r), number), :]
    whole[...] = dot(left[...], right[...], TN)
    if len(outs) == 1:
        outs[0][...] = whole[...].astype(LOW)
    else:
        plane_blocks(place_ref[1], whole, outs)


def first_back_kernel(
    planes, place_ref, own_ref, from_after_ref, from_before_ref, query_ref, first_ref, unit_ref,
    weight, two_sums_ref, up_sums_ref, active_ref, *refs
):
    shrink_refs, (grad_ref, near_ref, far_ref, corner_ref, sums_ref, joined, vectors, shrink) = refs[:planes], refs[planes:]
    gather_planes(place_ref[1], shrink_refs, shrink)
    spot = place_ref[0]
    number, columns = near_ref.shape[1] // 2, near_ref.shape[2]
    wide = query_ref.shape[1]
    pairs = (own_ref[...] + from_after_ref[...].astype(F32) + from_before_ref[...].astype(F32)).astype(LOW)
    joined[:, :wide] = query_ref[...]
    joined[:, wide:] = pairs
    grad = dot(first_ref[...], joined[...], TN).astype(LOW)
    gain = jnp.zeros((1, columns), F32)
    shift = jnp.zeros((1, columns), F32)
    for k, m in ((1, 2), (1, 0), (0, 2), (0, 0)):
        part = jnp.concatenate(
            [joined[block_rows(spot ^ (2 * (m + i) + k), number), :] for i in range(2)], axis=0
        )
        down = dot(part, weight[...], NT)
        unit = unit_ref[pl.ds((4 * k + m) * number, 2 * number), :].astype(F32)
        gain += jnp.sum(down * unit, axis=0, keepdims=True)
        shift += jnp.sum(down, axis=0, keepdims=True)
        lower = dot(active_ref[pl.ds((4 * k + m) * number, 2 * number), :], shrink[...])
        outs = (near_ref, far_ref, corner_ref)
        put_block(outs, k, m, jnp.concatenate([down[:number], lower[:number]], axis=0))
        put_block(outs, k, m + 1, jnp.concatenate([down[number:], lower[number:]], axis=0))
    sums_ref[...] = jnp.concatenate([gain, shift], axis=0)
    if len(grad_ref.shape) == 2:
        grad_ref[...] = grad
        return
    devices, tall, _ = grad_ref.shape
    rows = tall - EXTRA
    vectors[...] = jnp.zeros_like(vectors)
    vectors[0:2, :] = sums_ref[...]
    vectors[2:5, :] = two_sums_ref[...]
    for g in range(up_sums_ref.shape[1] // LANES):
        lanes = pl.ds(pl.multiple_of(spot * LANES, LANES), LANES)
        vectors[5 + g : 6 + g, lanes] = up_sums_ref[:, g * LANES : (g + 1) * LANES]
    grad_ref[:, rows:, :] = jnp.zeros((devices, EXTRA, grad_ref.shape[2]), LOW)
    for d in range(devices):
        lot = slice(d * rows // LANES * LANES, (d * rows // LANES + 1) * LANES)
        grad_ref[d, :rows, :] = grad[d * rows : (d + 1) * rows]
        grad_ref[d, rows:, :LANES] = vectors[:EXTRA, lot].astype(LOW)
        grad_ref[d, rows:, LANES : 2 * LANES] = vectors[EXTRA:, lot].astype(LOW)


def first_norm_back_kernel(one_ref, two_ref, three_ref, tokens_ref, second_grad_ref, vector_ref, out_ref):
    incoming = one_ref[...] + two_ref[...].astype(F32) + three_ref[...].astype(F32)
    unit, inverse = norm_parts(tokens_ref[...].astype(F32))
    out_ref[...] = (second_grad_ref[...] + norm_back(unit, inverse, vector_ref[0:1, :], incoming)).astype(LOW)


def sum_kernel(wide, with_vectors, square_ref, *refs):
    part_ref, grad_ref, total_ref = refs[:3]
    devices = part_ref.shape[0]
    rows = grad_ref.shape[0]
    square = jnp.zeros((rows, wide), F32)
    start = 0
    for c in range(part_ref.shape[2] // wide):
        for j in range(PLANE):
            sources = range(j, devices, PLANE)
            whole = sum(part_ref[d, :rows, c * wide : (c + 1) * wide].astype(F32) for d in sources)
            grad_ref[:, start : start + wide] = whole
            square += whole * whole
            start += wide
    found = jnp.sum(square, keepdims=True) + square_ref[0]
    if with_vectors:
        vectors = sum(part_ref[d, rows:, : 2 * LANES].astype(F32) for d in range(devices))
        refs[3][:EXTRA, :] = vectors[:, :LANES]
        refs[3][EXTRA:, :] = vectors[:, LANES:]
        lanes = lax.broadcasted_iota(jnp.int32, (2 * EXTRA, LANES), 1)
        mine = lanes // rows == square_ref[1].astype(jnp.int32)
        found += jnp.sum(jnp.where(mine, refs[3][...] * refs[3][...], 0.0), keepdims=True)
    total_ref[...] = jnp.broadcast_to(found.reshape((1,) * len(total_ref.shape)), total_ref.shape)


def sum_parts(wide, rows, part, square, lot=None):
    n, _, columns = part.shape
    vectors = lot is not None
    if wide % LANES == 0 and rows % 16 == 0:
        outs = [like((rows, PLANE * columns), F32), like((n, 1, LANES) if vectors else (1, 1), F32)]
        found = kernel_call(
            functools.partial(sum_kernel, wide, vectors),
            outs + [like((2 * EXTRA, LANES), F32)] * vectors,
            part,
            scalars=(jnp.stack([square, lot.astype(F32) if vectors else square]),),
        )
        return found if vectors else (*found, None)
    whole = part[:, :rows].astype(F32).reshape(-1, PLANE, rows, columns // wide, wide).sum(0)
    whole = whole.transpose(1, 2, 0, 3).reshape(rows, -1)
    square = square + jnp.sum(whole * whole)
    if not vectors:
        return whole, square.reshape(1, 1), None
    found = part[:, rows:, : 2 * LANES].astype(F32).sum(0)
    found = jnp.concatenate([found[:, :LANES], found[:, LANES:]], axis=0)
    mine = lax.dynamic_slice_in_dim(found, rows * lot, rows, axis=1)
    square = square + jnp.sum(mine * mine)
    return whole, jnp.full((n, 1, LANES), square), found


def update_kernel(square_ref, *refs):
    norm = jnp.sqrt(jnp.sum(square_ref[...], axis=0)[:, :1])
    refs[-1][...] = norm
    refs = refs[:-1]
    factor = jnp.minimum(1.0, CLIP_NORM / (norm + 1e-06))
    smooth_rate = min(0.999, (1.0 + STEP) / (10.0 + STEP))
    count = len(LEARNING_RATES)
    states, grads, outs = refs[: 3 * count], refs[3 * count : 4 * count], refs[4 * count :]
    for place, rate in enumerate(LEARNING_RATES):
        weight, moment, average = (ref[...] for ref in states[3 * place : 3 * place + 3])
        clipped = factor * grads[place][...] + WEIGHT_DECAY * weight
        velocity = MOMENTUM * moment + clipped
        updated = weight - rate * (clipped + MOMENTUM * velocity)
        outs[3 * place][...] = velocity
        outs[3 * place + 1][...] = updated
        outs[3 * place + 2][...] = smooth_rate * average + (1.0 - smooth_rate) * updated


def with_vectors(attend_grad, one_sums, two_sums, up_sums, spot, n, rows, hidden):
    columns, wide = attend_grad.shape
    planes, lots, in_lot = n // PLANE, columns // LANES, LANES // rows
    up_sums = lax.dynamic_update_slice_in_dim(
        jnp.zeros((planes, PLANE, hidden), F32), up_sums.reshape(planes, 1, hidden), spot, axis=1
    )
    part = jnp.concatenate([one_sums, two_sums, up_sums.reshape(-1, columns)], axis=0).astype(LOW)
    part = jnp.moveaxis(part.reshape(-1, lots, LANES), 1, 0)
    part = jnp.pad(part, ((0, 0), (0, 2 * EXTRA - part.shape[1]), (0, 0)))
    part = jnp.concatenate([part[:, :EXTRA], part[:, EXTRA:]], axis=2)
    part = jnp.pad(part, ((0, 0), (0, 0), (0, wide - 2 * LANES)))
    return jnp.concatenate([attend_grad.reshape(n, rows, wide), jnp.repeat(part, in_lot, axis=0)], axis=1)


def on_device(
    tokens,
    scene_lengths,
    cotangent,
    attend_weight,
    output_weight,
    expand_weight,
    reduce_weight,
    vector_params,
    attend_momentum,
    output_momentum,
    expand_momentum,
    reduce_momentum,
    vector_momentum,
    attend_average,
    output_average,
    expand_average,
    reduce_average,
    vector_average,
):
    n = lax.axis_size("seq")
    planes = n // PLANE
    device = lax.axis_index("seq")
    plane, spot = device // PLANE, device % PLANE
    place = jnp.stack([spot, plane]).astype(jnp.int32)
    number, columns = tokens.shape
    shared = number * PLANE
    rows = columns // n
    hidden = reduce_weight.shape[0]
    wide = columns // PLANE
    lots = columns // LANES
    in_lot = LANES // rows
    inner = planes * hidden
    near_like, far_like = like((4, number, columns), F32), like((3, number, columns), LOW)
    block_like, block_exact = like((number, columns), LOW), like((number, columns), F32)
    shared_scratch = pltpu.VMEM((shared, columns), LOW)
    square_scratch = pltpu.VMEM((columns, columns), LOW)

    vector_low = vector_params.astype(LOW)
    sides = spread_sides(tokens)
    attend = attend_weight.astype(LOW).reshape(rows, 3, PLANE, wide).transpose(2, 0, 1, 3).reshape(PLANE, rows, 3 * wide)
    vector_part = lax.dynamic_update_slice(
        jnp.zeros((2 * EXTRA, LANES), LOW), vector_low, (0, rows * (device % in_lot))
    )
    vector_part = jnp.concatenate([vector_part[:EXTRA], vector_part[EXTRA:]], axis=1)
    vector_part = jnp.pad(vector_part, ((0, 0), (0, 3 * wide - 2 * LANES)))
    attend = jnp.concatenate(
        [
            jnp.broadcast_to(attend[None], (planes,) + attend.shape).reshape(n, rows, 3 * wide),
            jnp.broadcast_to(vector_part[None], (n,) + vector_part.shape),
        ],
        axis=1,
    )
    attend = exchange(after(attend, *sides))
    lot_vectors = attend[:, rows:].reshape(lots, in_lot, EXTRA, 3 * wide).astype(F32).sum(1)
    corner = spread_corner(*sides)
    output = after(output_weight.astype(LOW), *sides)
    for bit in output_steps(planes)[:-3]:
        output = grow(output, bit)
    expand = (
        expand_weight.astype(LOW)
        .reshape(rows, planes, PLANE, hidden)
        .transpose(2, 0, 1, 3)
        .reshape(PLANE, rows, inner)
    )
    expand = jnp.broadcast_to(expand[None], (planes,) + expand.shape).reshape(n, rows, inner)
    expand = [expand[:, :, : inner // 2], expand[:, :, inner // 2 :]]
    shrink = reduce_weight.astype(LOW)
    corner, expand, shrink = tie(corner, expand, shrink)
    gathered = spread_far(tokens, sides, corner)
    gathered, output = tie(gathered, output)

    units, first_low, queries, pairs, attend, vectors = kernel_call(
        project_kernel,
        [
            like((shared, columns), LOW),
            like((shared, columns), LOW),
            like((shared, wide), LOW),
            like((shared, 2 * wide), LOW),
            like((columns, 3 * wide), LOW),
            like((2 * EXTRA, columns), F32),
        ],
        *gathered,
        attend,
        lot_vectors,
        scalars=(place,),
        scratch=[shared_scratch],
        flops=6 * shared * columns * wide,
    )
    bias_up = lax.dynamic_index_in_dim(
        vectors[5 : vector_params.shape[0]].reshape(planes, PLANE, hidden), spot, axis=1, keepdims=False
    ).reshape(1, inner)

    before, behind = move(pairs, PLANE), move(pairs, -PLANE)
    expand[0] = exchange(after(expand[0], pairs)).reshape(columns, inner // 2)
    output = grow(after(output, pairs), 4)
    cotangents = grow(after(cotangent, pairs), 2)
    queries, output, cotangents = tie(queries, output, cotangents)

    finish = jnp.cumsum(scene_lengths)
    begin = finish - scene_lengths
    base = (plane - 1) * shared
    position = plane * shared + jnp.arange(shared, dtype=jnp.int32)
    past = begin[None, :] <= position[:, None]
    span_begin = jnp.max(jnp.where(past, begin[None, :], 0), axis=1) - base
    span_end = jnp.min(jnp.where(finish[None, :] > position[:, None], finish[None, :], 1 << 30), axis=1) - base
    spans = jnp.stack([span_begin, span_end])
    bounds = jnp.stack([begin, finish]) - base
    bounds = jnp.pad(bounds, ((0, 0), (0, LANES - bounds.shape[1])))
    output = grow(output, 2)
    cotangents = grow(cotangents, 4)
    shrink_turns = {1: turn(after(shrink, queries), 1)}
    mixed_exact, mixed_low, logs = attention(spans, bounds, queries, before, pairs, behind)
    mixed_low, output, cotangents, expand[0], shrink_turns = tie(
        mixed_low, output, cotangents, expand[0], shrink_turns
    )

    mixed = exchange(mixed_low.reshape(PLANE, number, wide), plane_groups())
    output = [output, swap(output, 1)]
    cotangents = [cotangents, swap(cotangents, 1)]
    shrink_turns.update({s: turn(after(shrink, mixed_low), s) for s in range(2, planes)})
    output = ordered_output(device, planes, output)
    second, normed = kernel_call(
        functools.partial(mix_out_kernel, planes),
        [block_exact, block_like],
        mixed,
        tokens,
        vectors,
        *output,
        scalars=(place,),
        scratch=[square_scratch],
        flops=2 * number * columns * columns,
    )

    expand[1] = exchange(after(expand[1], mixed)).reshape(columns, inner // 2)
    sides = spread_sides(normed)
    sides, shrink_turns, cotangents = tie(sides, shrink_turns, cotangents)
    corner = spread_corner(*sides)
    shrink = [shrink] + [shrink_turns[s] for s in range(1, planes)]
    normed_all = spread_far(normed, sides, corner)

    inner_low = like((shared, inner), LOW)
    grad_near, grad_far, grad_corner, active, upper_grad, up_sums = kernel_call(
        functools.partial(feed_kernel, planes),
        [near_like, far_like, block_like, inner_low, inner_low, like((1, inner), F32)],
        *normed_all,
        *cotangents,
        *shrink,
        *expand,
        bias_up,
        scalars=(place,),
        scratch=[pltpu.VMEM((columns, inner), LOW), pltpu.VMEM((inner, columns), LOW), shared_scratch, shared_scratch],
        flops=6 * shared * columns * inner,
    )

    normed_grad = collect(grad_near, grad_far, grad_corner)
    shrink_grad = kernel_call(
        shrink_grad_kernel,
        [like((hidden, columns), LOW)] * planes,
        active,
        *cotangents,
        scalars=(place,),
        scratch=[pltpu.VMEM((inner, columns), F32), shared_scratch],
        flops=2 * shared * columns * inner,
    )
    shrink_turns = [turn(shrink_grad[s], s) for s in range(1, planes)]
    normed_grad, shrink_turns[:1] = tie(normed_grad, shrink_turns[:1])
    second_grad, branch_grad, mixed_grad, two_sums = kernel_call(
        functools.partial(norm_two_back_kernel, planes),
        [block_exact, block_like, like((PLANE, number, wide), LOW), like((3, columns), F32)],
        *normed_grad,
        second,
        cotangent,
        vectors,
        *output,
        scalars=(place,),
        scratch=[square_scratch],
        flops=2 * number * columns * columns,
    )

    mixed_grad = exchange(mixed_grad, plane_groups()).reshape(shared, wide)
    (expand_grad,) = kernel_call(
        expand_grad_kernel,
        [like((columns, inner), LOW)],
        after(upper_grad, branch_grad),
        *normed_all,
        scratch=[shared_scratch],
        flops=2 * shared * columns * inner,
    )
    branch_sides = spread_sides(branch_grad)
    mixed_grad, expand_grad, branch_sides, shrink_turns[:2] = tie(
        mixed_grad, expand_grad, branch_sides, shrink_turns[:2]
    )

    expand_part = exchange(after(expand_grad, mixed_grad).reshape(n, rows, inner))
    branch_corner = spread_corner(*branch_sides)
    query_grad, before_grad, own_grad, behind_grad = attention_back(
        spans, bounds, queries, before, pairs, behind, mixed_exact, logs, mixed_grad
    )
    before_grad, behind_grad, branch_corner = tie(before_grad, behind_grad, branch_corner)

    from_after, from_before = move(before_grad, -PLANE), move(behind_grad, PLANE)
    branch = jnp.concatenate([branch_grad, *branch_sides, *branch_corner], axis=0)
    output_grad = kernel_call(
        output_grad_kernel,
        [like((rows, columns), LOW)] * planes if rows % 16 == 0 else [like((wide, columns), LOW)],
        mixed_low,
        branch,
        swap(branch, 1),
        scalars=(place,),
        scratch=[pltpu.VMEM((wide, columns), F32), pltpu.VMEM((shared, wide), LOW), shared_scratch],
        flops=2 * shared * columns * wide,
    )
    if len(output_grad) == 1:
        output_grad = jnp.take(
            output_grad[0].reshape(planes, rows, columns), (plane + jnp.arange(planes)) % planes, axis=0, mode="clip"
        )
    output_grad = sum(
        lax.ppermute(
            output_grad[s],
            "seq",
            [(g * PLANE + j, j * planes + (g + s) % planes) for g in range(planes) for j in range(PLANE)],
        ).astype(F32)
        for s in range(planes)
    )
    from_after, from_before, output_grad = tie(from_after, from_before, output_grad)

    fused = rows % 16 == 0 and hidden == LANES
    attend_grad, first_near, first_far, first_corner, one_sums = kernel_call(
        functools.partial(first_back_kernel, planes),
        [
            like((n, rows + EXTRA, 3 * wide) if fused else (columns, 3 * wide), LOW),
            like((4, 2 * number, columns), F32),
            like((3, 2 * number, columns), LOW),
            like((2 * number, columns), LOW),
            like((2, columns), F32),
        ],
        own_grad,
        from_after,
        from_before,
        query_grad,
        first_low,
        units,
        attend,
        two_sums,
        up_sums,
        active,
        *shrink,
        scalars=(place,),
        scratch=[
            pltpu.VMEM((shared, 3 * wide), LOW),
            pltpu.VMEM((2 * EXTRA, columns), F32),
            pltpu.VMEM((inner, columns), LOW),
        ],
        flops=2 * shared * columns * 6 * wide,
    )
    more = vector_params.shape[0] - EXTRA
    attend_part = attend_grad
    if not fused:
        attend_part = with_vectors(attend_grad, one_sums, two_sums, up_sums, spot, n, rows, hidden)
    attend_part, first_near, first_far, first_corner, expand_part, shrink_turns = tie(
        attend_part, first_near, first_far, first_corner, expand_part, shrink_turns
    )
    shrink_grad = sum(g.astype(F32) for g in [shrink_grad[0], *shrink_turns])
    attend_part = exchange(attend_part)
    both = collect(first_near, first_far, first_corner)
    first_grad, block_output = zip(*[(t[:number], t[number:]) for t in both])
    (input_gradient,) = kernel_call(
        first_norm_back_kernel, [block_like], *first_grad, tokens, second_grad, vectors
    )
    block_output = (second + total(block_output) + vectors[4:5]).astype(LOW)

    squares = sum(jnp.sum(g * g) for g in (output_grad, shrink_grad))
    expand_grad, squares, _ = sum_parts(hidden, rows, expand_part, squares)
    attend_grad, squares, vector_grad = sum_parts(wide, rows, attend_part, squares[0, 0], device % in_lot)
    vector_grad = lax.dynamic_slice_in_dim(vector_grad, rows * (device % in_lot), rows, axis=1)
    vector_grad = vector_grad[: vector_params.shape[0]]
    squares, input_gradient, block_output = tie(exchange(squares), input_gradient, block_output)
    states = (
        (attend_weight, attend_momentum, attend_average),
        (output_weight, output_momentum, output_average),
        (expand_weight, expand_momentum, expand_average),
        (reduce_weight, reduce_momentum, reduce_average),
        (vector_params, vector_momentum, vector_average),
    )
    *updates, gradient_norm = kernel_call(
        update_kernel,
        [like(g[0].shape, F32) for g in states for _ in range(3)] + [like((1, 1), F32)],
        squares,
        *[a for g in states for a in g],
        attend_grad,
        output_grad,
        expand_grad,
        shrink_grad,
        vector_grad,
    )
    return (block_output, input_gradient, gradient_norm.reshape(()), *updates)


def solution(mesh):
    split, turned = P("seq", None), P(None, "seq")
    return jax.shard_map(
        on_device,
        mesh=mesh,
        in_specs=(split, P()) + (split,) * 5 + (turned,) + ((split,) * 4 + (turned,)) * 2,
        out_specs=(split, split, P()) + (split,) * 12 + (turned,) * 3,
        check_vma=False,
    )
```

time: 330 us -> 304 us (0.921)
  starting transfers between devices: 134 us -> 119 us
  Pallas kernels: 88.4 us -> 80.1 us
  other arithmetic: 27.4 us -> 21.6 us
  waiting for transfers between devices: 55.8 us -> 61.4 us
  between operations: 7.24 us -> 3.24 us
  local copies, waits for them, and re-layouts: 14 us -> 17.4 us
    ppermute x53 -> x39, waiting for transfers between devices: 15.3 us -> 47.5 us  [swap(): return lax.ppermute(block, 'seq', [(i, i ^ bit) for i in range(n)])]
    ppermute x12 -> x6, waiting for transfers between devices: 24.5 us -> 0.02 us  [turn(): lax.ppermute(block, 'seq', [(i, (i + planes_on * PLANE) % n) for i in ran...]
    all_to_all x10 -> x8, starting transfers between devices: 51.9 us -> 36.5 us  [exchange(): return lax.all_to_all(blocks, 'seq', 0, 0, axis_index_groups=groups)]
    ppermute x1 -> x4, starting transfers between devices: 1.55 us -> 14.1 us  [on_device(): lax.ppermute(output_grad[s], 'seq', [(g * PLANE + j, j * planes + (g + s)...]
    ppermute x53 -> x39, starting transfers between devices: 48.6 us -> 39.1 us  [swap(): return lax.ppermute(block, 'seq', [(i, i ^ bit) for i in range(n)])]
    ppermute x4, waiting for transfers between devices: 10 us -> 2.64 us  [move(): lax.ppermute(block, 'seq', [(i, i + distance) for i in range(n) if 0 <= i...]
    pallas_call x1, Pallas kernels: 15.2 us -> 10.2 us  [attention(): pl.pallas_call(attend_kernel, grid_spec=pltpu.PrefetchScalarGridSpec(num_...]
    slice x16 -> x12, local copies, waits for them, and re-layouts: 0.35 us -> 4.92 us  [the longest x3 3.22 us: on_device(): first_grad, block_output = zip(*[(t[:number], t[number:]) for t in both])]
  transfers between devices with their start and end apart: 80 -> 61, of which waited for: 18 -> 21; matrix products, arithmetic and copies ran while one was open for 10% -> 10% of each run, Pallas kernels for 19% -> 20%
where the time goes in v3:
time: 304 us; the launch traced here: 302 us
  starting transfers between devices  119 us (39%)
  Pallas kernels  80.1 us (26%)
  waiting for transfers between devices  61.4 us (20%)
  other arithmetic  21.6 us (7%)
  local copies, waits for them, and re-layouts  17.4 us (6%)
  between operations  3.24 us (1%)
    pallas_call x12, Pallas kernels, kernel_call(): pl.pallas_call(body, in_specs=[SMEM] * len(scalars) + [WHOLE] * len(args)...  56.3 us
    ppermute x39, waiting for transfers between devices, swap(): return lax.ppermute(block, 'seq', [(i, i ^ bit) for i in range(n)])  47.5 us
    ppermute x39, starting transfers between devices, swap(): return lax.ppermute(block, 'seq', [(i, i ^ bit) for i in range(n)])  39.1 us
    all_to_all x8, starting transfers between devices, exchange(): return lax.all_to_all(blocks, 'seq', 0, 0, axis_index_groups=groups)  36.5 us
    ppermute x6, starting transfers between devices, turn(): lax.ppermute(block, 'seq', [(i, (i + planes_on * PLANE) % n) for i in ran...  18.9 us
    ppermute x4, starting transfers between devices, on_device(): lax.ppermute(output_grad[s], 'seq', [(g * PLANE + j, j * planes + (g + s)...  14.1 us
    pallas_call x1, Pallas kernels, attention_back(): pl.pallas_call(attend_back_kernel, grid_spec=pltpu.PrefetchScalarGridSpec...  13.5 us
    pallas_call x1, Pallas kernels, attention(): pl.pallas_call(attend_kernel, grid_spec=pltpu.PrefetchScalarGridSpec(num_...  10.2 us
  transfers between devices with their start and end apart: 61, of which 21 were waited for; matrix products, arithmetic and copies ran while one was open for 10% of the time, Pallas kernels for 20%

profile of v3, /device:TPU:0, one launch (start us, length us, event | category | flops | bytes accessed | tf_op | source)
XLA Modules:
  0.0 302.4 jit_solution(13048847300996653647)
XLA Ops:
  0.7 3.0 collective-permute-start
  11.6 4.9 %all-to-all-start = ((bf16[32,40,384]{2,1,0:T(8,128)(2,1)}), bf16[32,40,384]{2,1,0:T(8,128)(2,1)S(1)}, u32[]{:S(2)}, u32[]{:S(2)}) async-start(bf16[32,40,384]{2,1,0:T(8,128)(2,1)} %pad_maximum_fusion.2), calls=%async_computation | async-start | bytes 1966080 | tf_op jit(solution)/shard_map/all_to_all | solution.py:82
  23.7 10.9 %collective-permute-done.7 = bf16[32,1024]{1,0:T(8,128)(2,1)S(1)} collective-permute-done((bf16[32,1024]{1,0:T(8,128)(2,1)S(1)}, bf16[32,1024]{1,0:T(8,128)(2,1)S(1)}, u32[]{:S(2)}, u32[]{:S(2)}) %collective-permute-start.7) | collective-permute-done | bytes 65568 | tf_op jit(solution)/shard_map/ppermute | solution.py:56
  34.6 4.6 %collective-permute-start.8 = (bf16[64,1024]{1,0:T(8,128)(2,1)S(1)}, bf16[64,1024]{1,0:T(8,128)(2,1)S(1)}, u32[]{:S(2)}, u32[]{:S(2)}) collective-permute-start(bf16[64,1024]{1,0:T(8,128)(2,1)S(1)} %pad_maximum_fusion.12), channel_id=1, source_target_pairs={{0,16},{1,17},{2,18},{3,19},{4,20},{5,21},{6,22},{7,23},{8,24},{9,... | collective-permute-start | bytes 393224 | tf_op jit(solution)/shard_map/ppermute | solution.py:56
  40.6 6.4 %collective-permute-done.8 = bf16[64,1024]{1,0:T(8,128)(2,1)S(1)} collective-permute-done((bf16[64,1024]{1,0:T(8,128)(2,1)S(1)}, bf16[64,1024]{1,0:T(8,128)(2,1)S(1)}, u32[]{:S(2)}, u32[]{:S(2)}) %collective-permute-start.8) | collective-permute-done | bytes 131104 | tf_op jit(solution)/shard_map/ppermute | solution.py:56
  48.2 6.5 %shard_map.313 = (bf16[1024,1024]{1,0:T(8,128)(2,1)}, bf16[1024,1024]{1,0:T(8,128)(2,1)}, bf16[1024,128]{1,0:T(8,128)(2,1)}, bf16[1024,256]{1,0:T(8,128)(2,1)}, ...) custom-call(s32[2]{0:T(128)} %pad_add_fusion.1.spot_ref.place_ref, bf16[128,1024]{1,0:T(8,128)(2,1)} %tokens_ref.3, ...), custom_call_target="tpu_custom_call" | custom-call | flops 805306368 | bytes 9011200 | tf_op jit(solution)/shard_map/pallas_call | solution.py:35
  54.7 2.1 collective-permute-start.11
  61.7 5.0 %all-to-all-start.1 = ((bf16[32,32,256]{2,1,0:T(8,128)(2,1)}), bf16[32,32,256]{2,1,0:T(8,128)(2,1)S(1)}, u32[]{:S(2)}, u32[]{:S(2)}) async-start(bf16[32,32,256]{2,1,0:T(8,128)(2,1)} %get-tuple-element.167), calls=%async_computation.1 | async-start | bytes 1048576 | tf_op jit(solution)/shard_map/all_to_all | solution.py:82
  69.3 2.4 collective-permute-start.15
  72.3 2.6 collective-permute-done.12.after_ref
  74.9 10.2 %shard_map.314 = (f32[1024,128]{1,0:T(8,128)}, bf16[1024,128]{1,0:T(8,128)(2,1)}, f32[2,1024]{1,0:T(2,128)}) custom-call(s32[2,2]{1,0:T(2,128)} %pad_add_fusion.range_ref, bf16[1024,128]{1,0:T(8,128)(2,1)} %get-tuple-element.160.query_ref, bf16[1024,256]{1,0:T(8,128)(2,1)} %collective-permute-done.11.before_ref, ...), custom_call_target="tpu_custom_call" | custom-call | flops 5368709120 | bytes 2097152 | tf_op jit(solution)/shard_map/pallas_call | solution.py:373
  88.0 2.4 all-to-all-done.1
  91.7 3.4 %all-to-all-start.2 = ((bf16[8,128,128]{2,1,0:T(8,128)(2,1)}), bf16[8,128,128]{2,1,0:T(8,128)(2,1)S(1)}, u32[]{:S(2)}, u32[]{:S(2)}) async-start(bf16[8,128,128]{2,1,0:T(8,128)(2,1)} %bitcast.17), calls=%async_computation.2 | async-start | bytes 524288 | tf_op jit(solution)/shard_map/all_to_all | solution.py:82
  95.2 3.3 %collective-permute-start.20 = (bf16[128,1024]{1,0:T(8,128)(2,1)S(1)}, bf16[128,1024]{1,0:T(8,128)(2,1)S(1)}, u32[]{:S(2)}, u32[]{:S(2)}) collective-permute-start(bf16[128,1024]{1,0:T(8,128)(2,1)S(1)} %convert_element_type.112.refs_10_.refs_0_), channel_id=1, source_target_pairs={{0,24},{1,25},{2,26},{3,27},{4,28},{5,29},{6,30},{7,31},{8,0},{9,1... | collective-permute-start | bytes 786440 | tf_op jit(solution)/shard_map/ppermute | solution.py:68
  98.5 3.5 %all-to-all-done.2.mixed_ref = bf16[8,128,128]{2,1,0:T(8,128)(2,1)S(1)} async-done(((bf16[8,128,128]{2,1,0:T(8,128)(2,1)}), bf16[8,128,128]{2,1,0:T(8,128)(2,1)S(1)}, u32[]{:S(2)}, u32[]{:S(2)}) %all-to-all-start.2) | async-done | bytes 262176 | tf_op jit(solution)/shard_map/all_to_all | solution.py:82
  103.1 3.3 %shard_map.315 = (f32[128,1024]{1,0:T(8,128)}, bf16[128,1024]{1,0:T(8,128)(2,1)}) custom-call(s32[2]{0:T(128)} %pad_add_fusion.1.spot_ref.place_ref, bf16[8,128,128]{2,1,0:T(8,128)(2,1)} %copy-done.18, bf16[128,1024]{1,0:T(8,128)(2,1)} %tokens_ref.3, f32[16,1024]{1,0:T(8,128)} %get-tuple-element.171.vector_ref, bf16[512,1024]{1,0:T(8,128)(2,1)} %copy-done, ...), custom_call_target="tpu_custom_call" | custom-call | flops 268435456 | bytes 3473408 | tf_op jit(solution)/shard_map/pallas_call | solution.py:35
  107.4 3.3 %all-to-all-start.3 = ((bf16[32,32,256]{2,1,0:T(8,128)(2,1)}), bf16[32,32,256]{2,1,0:T(8,128)(2,1)S(1)}, u32[]{:S(2)}, u32[]{:S(2)}) async-start(bf16[32,32,256]{2,1,0:T(8,128)(2,1)} %get-tuple-element.186), calls=%async_computation.3 | async-start | bytes 1048576 | tf_op jit(solution)/shard_map/all_to_all | solution.py:82
  110.8 3.6 %collective-permute-done.17.refs_1_ = bf16[128,1024]{1,0:T(8,128)(2,1)S(1)} collective-permute-done((bf16[128,1024]{1,0:T(8,128)(2,1)}, bf16[128,1024]{1,0:T(8,128)(2,1)S(1)}, u32[]{:S(2)}, u32[]{:S(2)}) %collective-permute-start.17) | collective-permute-done | bytes 262176 | tf_op jit(solution)/shard_map/ppermute | solution.py:56
  114.4 2.5 collective-permute-done.18.refs_2_
  119.2 6.0 %collective-permute-done.22.refs_3_ = bf16[64,1024]{1,0:T(8,128)(2,1)S(1)} collective-permute-done((bf16[64,1024]{1,0:T(8,128)(2,1)S(1)}, bf16[64,1024]{1,0:T(8,128)(2,1)S(1)}, u32[]{:S(2)}, u32[]{:S(2)}) %collective-permute-start.22) | collective-permute-done | bytes 131104 | tf_op jit(solution)/shard_map/ppermute | solution.py:56
  129.0 8.8 %shard_map.316 = (f32[4,128,1024]{2,1,0:T(8,128)}, bf16[3,128,1024]{2,1,0:T(8,128)(2,1)}, bf16[128,1024]{1,0:T(8,128)(2,1)}, bf16[1024,512]{1,0:T(8,128)(2,1)}, ...) custom-call(s32[2]{0:T(128)} %pad_add_fusion.1.spot_ref.place_ref, bf16[128,1024]{1,0:T(8,128)(2,1)} %get-tuple-element.173.refs_0_, ...), custom_call_target="tpu_custom_call" | custom-call | flops 3221225472 | bytes 11538432 | tf_op jit(solution)/shard_map/pallas_call | solution.py:35
  138.4 4.4 %shard_map.317 = (bf16[128,1024]{1,0:T(8,128)(2,1)}, bf16[128,1024]{1,0:T(8,128)(2,1)}, bf16[128,1024]{1,0:T(8,128)(2,1)}, bf16[128,1024]{1,0:T(8,128)(2,1)}) custom-call(s32[2]{0:T(128)} %pad_add_fusion.1.spot_ref.place_ref, bf16[1024,512]{1,0:T(8,128)(2,1)} %get-tuple-element.190.active_ref, bf16[512,1024]{1,0:T(8,128)(2,1)} %pad_maximum_fusion.1.refs_8_.refs_0_, ...), custom_call_target="tpu_custom_call" | custom-call | flops 1073741824 | bytes 4194304 | tf_op jit(solution)/shard_map/pallas_call | solution.py:35
  142.8 2.8 collective-permute-start.33
  148.7 2.6 collective-permute-done.31
  155.4 3.5 %collective-permute-done.32.three_ref = bf16[128,1024]{1,0:T(8,128)(2,1)S(1)} collective-permute-done((bf16[128,1024]{1,0:T(8,128)(2,1)S(1)}, bf16[128,1024]{1,0:T(8,128)(2,1)S(1)}, u32[]{:S(2)}, u32[]{:S(2)}) %collective-permute-start.32) | collective-permute-done | bytes 262176 | tf_op jit(solution)/shard_map/ppermute | solution.py:56
  159.9 4.1 %shard_map.318 = (f32[128,1024]{1,0:T(8,128)}, bf16[128,1024]{1,0:T(8,128)(2,1)}, bf16[8,128,128]{2,1,0:T(8,128)(2,1)}, f32[3,1024]{1,0:T(4,128)}) custom-call(s32[2]{0:T(128)} %pad_add_fusion.1.spot_ref.place_ref, f32[128,1024]{1,0:T(8,128)} %get-tuple-element.192.one_ref, bf16[128,1024]{1,0:T(8,128)(2,1)} %copy-done.29, bf16[128,1024]{1,0:T(8,128)(2,1)} %copy-done.28, ...), custom_call_target="tpu_custom_call" | custom-call | flops 268435456 | bytes 5058560 | tf_op jit(solution)/shard_map/pallas_call | solution.py:35
  166.5 3.4 %all-to-all-start.4 = ((bf16[8,128,128]{2,1,0:T(8,128)(2,1)}), bf16[8,128,128]{2,1,0:T(8,128)(2,1)S(1)}, u32[]{:S(2)}, u32[]{:S(2)}) async-start(bf16[8,128,128]{2,1,0:T(8,128)(2,1)} %get-tuple-element.196), calls=%async_computation.4 | async-start | bytes 524288 | tf_op jit(solution)/shard_map/all_to_all | solution.py:82
  170.0 4.1 %shard_map.319 = bf16[1024,512]{1,0:T(8,128)(2,1)} custom-call(bf16[1024,512]{1,0:T(8,128)(2,1)} %get-tuple-element.199.grad_ref, bf16[128,1024]{1,0:T(8,128)(2,1)} %get-tuple-element.173.refs_0_, bf16[128,1024]{1,0:T(8,128)(2,1)} %copy-done.11, bf16[128,1024]{1,0:T(8,128)(2,1)} %copy-done.12, bf16[64,1024]{1,0:T(8,128)(2,1)} %copy-done.36, ...), custom_call_target="tpu_custom_call" | custom-call | flops 1073741824 | bytes 4194304 | tf_op jit(solution)/shard_map/pallas_call | solution.py:35
  174.1 2.7 all-to-all-done.4
  176.8 2.9 all-to-all-start.5
  182.8 13.5 %shard_map.320 = (bf16[1024,128]{1,0:T(8,128)(2,1)}, bf16[1024,256]{1,0:T(8,128)(2,1)}, f32[1024,256]{1,0:T(8,128)}, bf16[1024,256]{1,0:T(8,128)(2,1)}) custom-call(s32[2,2]{1,0:T(2,128)} %pad_add_fusion.range_ref, bf16[1024,128]{1,0:T(8,128)(2,1)} %get-tuple-element.160.query_ref, bf16[1024,256]{1,0:T(8,128)(2,1)} %collective-permute-done.11.before_ref, ...), custom_call_target="tpu_custom_call" | custom-call | flops 8053063680 | bytes 4194304 | tf_op jit(solution)/shard_map/pallas_call | solution.py:396
  197.8 5.4 %collective-permute-start.40 = (bf16[1024,256]{1,0:T(8,128)(2,1)}, bf16[1024,256]{1,0:T(8,128)(2,1)}, u32[]{:S(2)}, u32[]{:S(2)}) collective-permute-start(bf16[1024,256]{1,0:T(8,128)(2,1)} %get-tuple-element.208), channel_id=1, source_target_pairs={{0,8},{1,9},{2,10},{3,11},{4,12},{5,13},{6,14},{7,15},{8,16},{9,17... | collective-permute-start | bytes 1572872 | tf_op jit(solution)/shard_map/ppermute | solution.py:61
  204.2 2.9 shard_map.321
  208.5 3.0 collective-permute-start.43
  211.5 3.1 %collective-permute-start.44 = (bf16[32,1024]{1,0:T(8,128)(2,1)}, bf16[32,1024]{1,0:T(8,128)(2,1)S(1)}, u32[]{:S(2)}, u32[]{:S(2)}) collective-permute-start(bf16[32,1024]{1,0:T(8,128)(2,1)} %get-tuple-element.213), channel_id=1, source_target_pairs={{0,2},{1,6},{2,10},{3,14},{4,18},{5,22},{6,26},{7,30},{8,3},{9,7},... | collective-permute-start | bytes 196616 | tf_op jit(solution)/shard_map/ppermute | solution.py:906
  214.5 6.6 %collective-permute-start.45 = (bf16[32,1024]{1,0:T(8,128)(2,1)}, bf16[32,1024]{1,0:T(8,128)(2,1)S(1)}, u32[]{:S(2)}, u32[]{:S(2)}) collective-permute-start(bf16[32,1024]{1,0:T(8,128)(2,1)} %get-tuple-element.214), channel_id=1, source_target_pairs={{0,3},{1,7},{2,11},{3,15},{4,19},{5,23},{6,27},{7,31},{8,0},{9,4},... | collective-permute-start | bytes 196616 | tf_op jit(solution)/shard_map/ppermute | solution.py:906
  221.2 8.6 %collective-permute-start.46 = (bf16[128,1024]{1,0:T(8,128)(2,1)}, bf16[128,1024]{1,0:T(8,128)(2,1)S(1)}, u32[]{:S(2)}, u32[]{:S(2)}) collective-permute-start(bf16[128,1024]{1,0:T(8,128)(2,1)} %get-tuple-element.234), channel_id=1, source_target_pairs={{0,24},{1,25},{2,26},{3,27},{4,28},{5,29},{6,30},{7,31},{8,0},{9,1... | collective-permute-start | bytes 786440 | tf_op jit(solution)/shard_map/ppermute | solution.py:68
  229.7 1.9 collective-permute-done.45
  232.5 10.1 %shard_map.322 = (bf16[32,40,384]{2,1,0:T(8,128)(2,1)}, f32[4,256,1024]{2,1,0:T(8,128)}, bf16[3,256,1024]{2,1,0:T(8,128)(2,1)}, bf16[256,1024]{1,0:T(8,128)(2,1)}, f32[2,1024]{1,0:T(2,128)}) custom-call(s32[2]{0:T(128)} %pad_add_fusion.1.spot_ref.place_ref, f32[1024,256]{1,0:T(8,128)} %get-tuple-element.217.own_ref, bf16[1024,256]{1,0:T(8,128)(2,1)} %copy-done.24, ...), custom_call_target="tpu_custom_call" | custom-call | flops 1610612736 | bytes 16734208 | tf_op jit(solution)/shard_map/pallas_call | solution.py:35
  244.7 8.9 %all-to-all-start.6 = ((bf16[32,40,384]{2,1,0:T(8,128)(2,1)}), bf16[32,40,384]{2,1,0:T(8,128)(2,1)S(1)}, u32[]{:S(2)}, u32[]{:S(2)}) async-start(bf16[32,40,384]{2,1,0:T(8,128)(2,1)} %get-tuple-element.240), calls=%async_computation.6 | async-start | bytes 1966080 | tf_op jit(solution)/shard_map/all_to_all | solution.py:82
  253.6 2.5 multiply_reduce_fusion
  262.1 2.8 convert_add_fusion
  265.0 6.7 %collective-permute-done.51 = bf16[128,1024]{1,0:T(8,128)(2,1)S(1)} collective-permute-done((bf16[128,1024]{1,0:T(8,128)(2,1)S(1)}, bf16[128,1024]{1,0:T(8,128)(2,1)S(1)}, u32[]{:S(2)}, u32[]{:S(2)}) %collective-permute-start.51) | collective-permute-done | bytes 262176 | tf_op jit(solution)/shard_map/ppermute | solution.py:56
  276.1 2.2 shard_map.323
  281.3 2.1 shard_map.324
  283.4 4.7 %all-to-all-start.7 = ((f32[32,1,128]{2,1,0:T(1,128)}), f32[32,1,128]{2,1,0:T(1,128)S(1)}, u32[]{:S(2)}, u32[]{:S(2)}) async-start(f32[32,1,128]{2,1,0:T(1,128)} %get-tuple-element.241), calls=%async_computation.7 | async-start | bytes 32768 | tf_op jit(solution)/shard_map/all_to_all | solution.py:82
  293.7 2.6 shard_map.325
  296.9 5.3 %shard_map.326 = (f32[32,3072]{1,0:T(8,128)}, f32[32,3072]{1,0:T(8,128)}, f32[32,3072]{1,0:T(8,128)}, f32[32,1024]{1,0:T(8,128)}, f32[32,1024]{1,0:T(8,128)}, /*...) custom-call(f32[32,1,128]{2,1,0:T(1,128)} %copy-done.42, ...), custom_call_target="tpu_custom_call" | custom-call | bytes 11034500 | tf_op jit(solution)/shard_map/pallas_call | solution.py:35
  (261 shorter events, 77.3 us)
Async XLA Ops:
  0.7 9.5 %collective-permute-start = (bf16[128,1024]{1,0:T(8,128)(2,1)}, bf16[128,1024]{1,0:T(8,128)(2,1)S(1)}, u32[]{:S(2)}, u32[]{:S(2)}) collective-permute-start(bf16[128,1024]{1,0:T(8,128)(2,1)} %tokens_ref.3), channel_id=1, source_target_pairs={{0,2},{1,3},{2,0},{3,1},{4,6},{5,7},{6,4},{7,5},{8,10},{9,11},{10,... | collective-permute-start | bytes 786440 | tf_op jit(solution)/shard_map/ppermute | solution.py:56
  3.7 8.0 %collective-permute-start.1 = (bf16[128,1024]{1,0:T(8,128)(2,1)}, bf16[128,1024]{1,0:T(8,128)(2,1)S(1)}, u32[]{:S(2)}, u32[]{:S(2)}) collective-permute-start(bf16[128,1024]{1,0:T(8,128)(2,1)} %tokens_ref.3), channel_id=1, source_target_pairs={{0,4},{1,5},{2,6},{3,7},{4,0},{5,1},{6,2},{7,3},{8,12},{9,13},{10,... | collective-permute-start | bytes 786440 | tf_op jit(solution)/shard_map/ppermute | solution.py:56
  11.6 35.5 %all-to-all-start = ((bf16[32,40,384]{2,1,0:T(8,128)(2,1)}), bf16[32,40,384]{2,1,0:T(8,128)(2,1)S(1)}, u32[]{:S(2)}, u32[]{:S(2)}) async-start(bf16[32,40,384]{2,1,0:T(8,128)(2,1)} %pad_maximum_fusion.2), calls=%async_computation | async-start | bytes 1966080 | tf_op jit(solution)/shard_map/all_to_all | solution.py:82
  18.5 28.6 %collective-permute-start.4 = (bf16[3,128,1024]{2,1,0:T(8,128)(2,1)S(1)}, bf16[3,128,1024]{2,1,0:T(8,128)(2,1)}, u32[]{:S(2)}, u32[]{:S(2)}) collective-permute-start(bf16[3,128,1024]{2,1,0:T(8,128)(2,1)S(1)} %pad_maximum_fusion.3), channel_id=1, source_target_pairs={{0,1},{1,0},{2,3},{3,2},{4,5},{5,4},{6,7},{7,6},{8,9},{9,8},{10,11... | collective-permute-start | bytes 2359304 | tf_op jit(solution)/shard_map/ppermute | solution.py:56
  18.8 15.7 %collective-permute-start.7 = (bf16[32,1024]{1,0:T(8,128)(2,1)S(1)}, bf16[32,1024]{1,0:T(8,128)(2,1)S(1)}, u32[]{:S(2)}, u32[]{:S(2)}) collective-permute-start(bf16[32,1024]{1,0:T(8,128)(2,1)S(1)} %convert_element_type.113), channel_id=1, source_target_pairs={{0,8},{1,9},{2,10},{3,11},{4,12},{5,13},{6,14},{7,15},{8,0},{9,1},... | collective-permute-start | bytes 196616 | tf_op jit(solution)/shard_map/ppermute | solution.py:56
  20.6 18.6 %collective-permute-start.2 = (bf16[64,1024]{1,0:T(8,128)(2,1)S(1)}, bf16[64,1024]{1,0:T(8,128)(2,1)}, u32[]{:S(2)}, u32[]{:S(2)}) collective-permute-start(bf16[64,1024]{1,0:T(8,128)(2,1)S(1)} %slice.238), channel_id=1, source_target_pairs={{0,4},{1,5},{2,6},{3,7},{4,0},{5,1},{6,2},{7,3},{8,12},{9,13},{10,... | collective-permute-start | bytes 393224 | tf_op jit(solution)/shard_map/ppermute | solution.py:56
  22.2 17.0 %collective-permute-start.3 = (bf16[64,1024]{1,0:T(8,128)(2,1)S(1)}, bf16[64,1024]{1,0:T(8,128)(2,1)}, u32[]{:S(2)}, u32[]{:S(2)}) collective-permute-start(bf16[64,1024]{1,0:T(8,128)(2,1)S(1)} %slice.239), channel_id=1, source_target_pairs={{0,2},{1,3},{2,0},{3,1},{4,6},{5,7},{6,4},{7,5},{8,10},{9,11},{10,... | collective-permute-start | bytes 393224 | tf_op jit(solution)/shard_map/ppermute | solution.py:56
  34.6 12.4 %collective-permute-start.8 = (bf16[64,1024]{1,0:T(8,128)(2,1)S(1)}, bf16[64,1024]{1,0:T(8,128)(2,1)S(1)}, u32[]{:S(2)}, u32[]{:S(2)}) collective-permute-start(bf16[64,1024]{1,0:T(8,128)(2,1)S(1)} %pad_maximum_fusion.12), channel_id=1, source_target_pairs={{0,16},{1,17},{2,18},{3,19},{4,20},{5,21},{6,22},{7,23},{8,24},{9,... | collective-permute-start | bytes 393224 | tf_op jit(solution)/shard_map/ppermute | solution.py:56
  39.2 7.8 %collective-permute-start.5 = (bf16[64,1024]{1,0:T(8,128)(2,1)}, bf16[64,1024]{1,0:T(8,128)(2,1)S(1)}, u32[]{:S(2)}, u32[]{:S(2)}) collective-permute-start(bf16[64,1024]{1,0:T(8,128)(2,1)} %collective-permute-done.2.refs_3_), channel_id=1, source_target_pairs={{0,1},{1,0},{2,3},{3,2},{4,5},{5,4},{6,7},{7,6},{8,9},{9,8},{10,11... | collective-permute-start | bytes 393224 | tf_op jit(solution)/shard_map/ppermute | solution.py:56
  54.7 17.6 %collective-permute-start.11 = (bf16[1024,256]{1,0:T(8,128)(2,1)}, bf16[1024,256]{1,0:T(8,128)(2,1)}, u32[]{:S(2)}, u32[]{:S(2)}) collective-permute-start(bf16[1024,256]{1,0:T(8,128)(2,1)} %get-tuple-element.157.own_ref), channel_id=1, source_target_pairs={{0,8},{1,9},{2,10},{3,11},{4,12},{5,13},{6,14},{7,15},{8,16},{9,17... | collective-permute-start | bytes 1572872 | tf_op jit(solution)/shard_map/ppermute | solution.py:61
  56.8 18.1 %collective-permute-start.12 = (bf16[1024,256]{1,0:T(8,128)(2,1)}, bf16[1024,256]{1,0:T(8,128)(2,1)}, u32[]{:S(2)}, u32[]{:S(2)}) collective-permute-start(bf16[1024,256]{1,0:T(8,128)(2,1)} %get-tuple-element.157.own_ref), channel_id=1, source_target_pairs={{8,0},{9,1},{10,2},{11,3},{12,4},{13,5},{14,6},{15,7},{16,8},{17,9... | collective-permute-start | bytes 1572872 | tf_op jit(solution)/shard_map/ppermute | solution.py:61
  58.1 8.6 %collective-permute-start.10 = (bf16[128,1024]{1,0:T(8,128)(2,1)S(1)}, bf16[128,1024]{1,0:T(8,128)(2,1)S(1)}, u32[]{:S(2)}, u32[]{:S(2)}) collective-permute-start(bf16[128,1024]{1,0:T(8,128)(2,1)S(1)} %copy-done.19), channel_id=1, source_target_pairs={{0,2},{1,3},{2,0},{3,1},{4,6},{5,7},{6,4},{7,5},{8,10},{9,11},{10,... | collective-permute-start | bytes 786440 | tf_op jit(solution)/shard_map/ppermute | solution.py:56
  61.7 28.7 %all-to-all-start.1 = ((bf16[32,32,256]{2,1,0:T(8,128)(2,1)}), bf16[32,32,256]{2,1,0:T(8,128)(2,1)S(1)}, u32[]{:S(2)}, u32[]{:S(2)}) async-start(bf16[32,32,256]{2,1,0:T(8,128)(2,1)} %get-tuple-element.167), calls=%async_computation.1 | async-start | bytes 1048576 | tf_op jit(solution)/shard_map/all_to_all | solution.py:82
  67.2 18.8 %collective-permute-start.14 = (bf16[256,1024]{1,0:T(8,128)(2,1)S(1)}, bf16[256,1024]{1,0:T(8,128)(2,1)S(1)}, u32[]{:S(2)}, u32[]{:S(2)}) collective-permute-start(bf16[256,1024]{1,0:T(8,128)(2,1)S(1)} %pad_maximum_fusion.6), channel_id=1, source_target_pairs={{0,4},{1,5},{2,6},{3,7},{4,0},{5,1},{6,2},{7,3},{8,12},{9,13},{10,... | collective-permute-start | bytes 1572872 | tf_op jit(solution)/shard_map/ppermute | solution.py:56
  69.3 18.6 %collective-permute-start.15 = (bf16[128,1024]{1,0:T(8,128)(2,1)S(1)}, bf16[128,1024]{1,0:T(8,128)(2,1)S(1)}, u32[]{:S(2)}, u32[]{:S(2)}) collective-permute-start(bf16[128,1024]{1,0:T(8,128)(2,1)S(1)} %convert_element_type.112.refs_10_.refs_0_), channel_id=1, source_target_pairs={{0,8},{1,9},{2,10},{3,11},{4,12},{5,13},{6,14},{7,15},{8,16},{9,17... | collective-permute-start | bytes 786440 | tf_op jit(solution)/shard_map/ppermute | solution.py:68
  71.7 16.2 %collective-permute-start.13 = (bf16[256,1024]{1,0:T(8,128)(2,1)S(1)}, bf16[256,1024]{1,0:T(8,128)(2,1)S(1)}, u32[]{:S(2)}, u32[]{:S(2)}) collective-permute-start(bf16[256,1024]{1,0:T(8,128)(2,1)S(1)} %pad_maximum_fusion.5), channel_id=1, source_target_pairs={{0,2},{1,3},{2,0},{3,1},{4,6},{5,7},{6,4},{7,5},{8,10},{9,11},{10,... | collective-permute-start | bytes 1572872 | tf_op jit(solution)/shard_map/ppermute | solution.py:56
  91.2 10.8 %collective-permute-start.16 = (bf16[512,1024]{1,0:T(8,128)(2,1)S(1)}, bf16[512,1024]{1,0:T(8,128)(2,1)S(1)}, u32[]{:S(2)}, u32[]{:S(2)}) collective-permute-start(bf16[512,1024]{1,0:T(8,128)(2,1)S(1)} %pad_maximum_fusion.refs_0_), channel_id=1, source_target_pairs={{0,1},{1,0},{2,3},{3,2},{4,5},{5,4},{6,7},{7,6},{8,9},{9,8},{10,11... | collective-permute-start | bytes 3145736 | tf_op jit(solution)/shard_map/ppermute | solution.py:56
  91.2 19.6 %collective-permute-start.21 = (bf16[512,1024]{1,0:T(8,128)(2,1)}, bf16[512,1024]{1,0:T(8,128)(2,1)}, u32[]{:S(2)}, u32[]{:S(2)}) collective-permute-start(bf16[512,1024]{1,0:T(8,128)(2,1)} %pad_maximum_fusion.1.refs_8_.refs_0_), channel_id=1, source_target_pairs={{0,1},{1,0},{2,3},{3,2},{4,5},{5,4},{6,7},{7,6},{8,9},{9,8},{10,11... | collective-permute-start | bytes 3145736 | tf_op jit(solution)/shard_map/ppermute | solution.py:56
  91.7 10.3 %all-to-all-start.2 = ((bf16[8,128,128]{2,1,0:T(8,128)(2,1)}), bf16[8,128,128]{2,1,0:T(8,128)(2,1)S(1)}, u32[]{:S(2)}, u32[]{:S(2)}) async-start(bf16[8,128,128]{2,1,0:T(8,128)(2,1)} %bitcast.17), calls=%async_computation.2 | async-start | bytes 524288 | tf_op jit(solution)/shard_map/all_to_all | solution.py:82
  95.1 15.6 %collective-permute-start.19 = (bf16[128,1024]{1,0:T(8,128)(2,1)S(1)}, bf16[128,1024]{1,0:T(8,128)(2,1)S(1)}, u32[]{:S(2)}, u32[]{:S(2)}) collective-permute-start(bf16[128,1024]{1,0:T(8,128)(2,1)S(1)} %convert_element_type.112.refs_10_.refs_0_), channel_id=1, source_target_pairs={{0,16},{1,17},{2,18},{3,19},{4,20},{5,21},{6,22},{7,23},{8,24},{9,... | collective-permute-start | bytes 786440 | tf_op jit(solution)/shard_map/ppermute | solution.py:68
  95.2 15.5 %collective-permute-start.20 = (bf16[128,1024]{1,0:T(8,128)(2,1)S(1)}, bf16[128,1024]{1,0:T(8,128)(2,1)S(1)}, u32[]{:S(2)}, u32[]{:S(2)}) collective-permute-start(bf16[128,1024]{1,0:T(8,128)(2,1)S(1)} %convert_element_type.112.refs_10_.refs_0_), channel_id=1, source_target_pairs={{0,24},{1,25},{2,26},{3,27},{4,28},{5,29},{6,30},{7,31},{8,0},{9,1... | collective-permute-start | bytes 786440 | tf_op jit(solution)/shard_map/ppermute | solution.py:68
  106.3 8.1 %collective-permute-start.17 = (bf16[128,1024]{1,0:T(8,128)(2,1)}, bf16[128,1024]{1,0:T(8,128)(2,1)S(1)}, u32[]{:S(2)}, u32[]{:S(2)}) collective-permute-start(bf16[128,1024]{1,0:T(8,128)(2,1)} %get-tuple-element.173.refs_0_), channel_id=1, source_target_pairs={{0,2},{1,3},{2,0},{3,1},{4,6},{5,7},{6,4},{7,5},{8,10},{9,11},{10,... | collective-permute-start | bytes 786440 | tf_op jit(solution)/shard_map/ppermute | solution.py:56
  106.9 10.0 %collective-permute-start.18 = (bf16[128,1024]{1,0:T(8,128)(2,1)}, bf16[128,1024]{1,0:T(8,128)(2,1)S(1)}, u32[]{:S(2)}, u32[]{:S(2)}) collective-permute-start(bf16[128,1024]{1,0:T(8,128)(2,1)} %get-tuple-element.173.refs_0_), channel_id=1, source_target_pairs={{0,4},{1,5},{2,6},{3,7},{4,0},{5,1},{6,2},{7,3},{8,12},{9,13},{10,... | collective-permute-start | bytes 786440 | tf_op jit(solution)/shard_map/ppermute | solution.py:56
  107.4 20.4 %all-to-all-start.3 = ((bf16[32,32,256]{2,1,0:T(8,128)(2,1)}), bf16[32,32,256]{2,1,0:T(8,128)(2,1)S(1)}, u32[]{:S(2)}, u32[]{:S(2)}) async-start(bf16[32,32,256]{2,1,0:T(8,128)(2,1)} %get-tuple-element.186), calls=%async_computation.3 | async-start | bytes 1048576 | tf_op jit(solution)/shard_map/all_to_all | solution.py:82
  118.0 9.8 %collective-permute-start.24 = (bf16[3,128,1024]{2,1,0:T(8,128)(2,1)S(1)}, bf16[3,128,1024]{2,1,0:T(8,128)(2,1)S(1)}, u32[]{:S(2)}, u32[]{:S(2)}) collective-permute-start(bf16[3,128,1024]{2,1,0:T(8,128)(2,1)S(1)} %pad_maximum_fusion.4), channel_id=1, source_target_pairs={{0,1},{1,0},{2,3},{3,2},{4,5},{5,4},{6,7},{7,6},{8,9},{9,8},{10,11... | collective-permute-start | bytes 2359304 | tf_op jit(solution)/shard_map/ppermute | solution.py:56
  137.8 9.8 %collective-permute-start.27 = (bf16[3,128,1024]{2,1,0:T(8,128)(2,1)}, bf16[3,128,1024]{2,1,0:T(8,128)(2,1)S(1)}, u32[]{:S(2)}, u32[]{:S(2)}) collective-permute-start(bf16[3,128,1024]{2,1,0:T(8,128)(2,1)} %get-tuple-element.188), channel_id=1, source_target_pairs={{0,1},{1,0},{2,3},{3,2},{4,5},{5,4},{6,7},{7,6},{8,9},{9,8},{10,11... | collective-permute-start | bytes 2359304 | tf_op jit(solution)/shard_map/ppermute | solution.py:56
  142.8 12.6 %collective-permute-start.33 = (bf16[128,1024]{1,0:T(8,128)(2,1)}, bf16[128,1024]{1,0:T(8,128)(2,1)S(1)}, u32[]{:S(2)}, u32[]{:S(2)}) collective-permute-start(bf16[128,1024]{1,0:T(8,128)(2,1)} %get-tuple-element.191), channel_id=1, source_target_pairs={{0,8},{1,9},{2,10},{3,11},{4,12},{5,13},{6,14},{7,15},{8,16},{9,17... | collective-permute-start | bytes 786440 | tf_op jit(solution)/shard_map/ppermute | solution.py:68
  153.5 20.6 %collective-permute-start.36 = (bf16[128,1024]{1,0:T(8,128)(2,1)S(1)}, bf16[128,1024]{1,0:T(8,128)(2,1)S(1)}, u32[]{:S(2)}, u32[]{:S(2)}) collective-permute-start(bf16[128,1024]{1,0:T(8,128)(2,1)S(1)} %copy-done.43), channel_id=1, source_target_pairs={{0,16},{1,17},{2,18},{3,19},{4,20},{5,21},{6,22},{7,23},{8,24},{9,... | collective-permute-start | bytes 786440 | tf_op jit(solution)/shard_map/ppermute | solution.py:68
  164.0 12.8 %collective-permute-start.34 = (bf16[128,1024]{1,0:T(8,128)(2,1)}, bf16[128,1024]{1,0:T(8,128)(2,1)S(1)}, u32[]{:S(2)}, u32[]{:S(2)}) collective-permute-start(bf16[128,1024]{1,0:T(8,128)(2,1)} %get-tuple-element.198), channel_id=1, source_target_pairs={{0,2},{1,3},{2,0},{3,1},{4,6},{5,7},{6,4},{7,5},{8,10},{9,11},{10,... | collective-permute-start | bytes 786440 | tf_op jit(solution)/shard_map/ppermute | solution.py:56
  165.6 11.2 %collective-permute-start.35 = (bf16[128,1024]{1,0:T(8,128)(2,1)}, bf16[128,1024]{1,0:T(8,128)(2,1)S(1)}, u32[]{:S(2)}, u32[]{:S(2)}) collective-permute-start(bf16[128,1024]{1,0:T(8,128)(2,1)} %get-tuple-element.198), channel_id=1, source_target_pairs={{0,4},{1,5},{2,6},{3,7},{4,0},{5,1},{6,2},{7,3},{8,12},{9,13},{10,... | collective-permute-start | bytes 786440 | tf_op jit(solution)/shard_map/ppermute | solution.py:56
  166.5 10.3 %all-to-all-start.4 = ((bf16[8,128,128]{2,1,0:T(8,128)(2,1)}), bf16[8,128,128]{2,1,0:T(8,128)(2,1)S(1)}, u32[]{:S(2)}, u32[]{:S(2)}) async-start(bf16[8,128,128]{2,1,0:T(8,128)(2,1)} %get-tuple-element.196), calls=%async_computation.4 | async-start | bytes 524288 | tf_op jit(solution)/shard_map/all_to_all | solution.py:82
  176.8 65.8 %all-to-all-start.5 = ((bf16[32,32,512]{2,1,0:T(8,128)(2,1)}), bf16[32,32,512]{2,1,0:T(8,128)(2,1)S(1)}, u32[]{:S(2)}, u32[]{:S(2)}) async-start(bf16[32,32,512]{2,1,0:T(8,128)(2,1)} %bitcast.104), calls=%async_computation.5 | async-start | bytes 2097152 | tf_op jit(solution)/shard_map/all_to_all | solution.py:82
  179.7 16.6 %collective-permute-start.37 = (bf16[64,1024]{1,0:T(8,128)(2,1)S(1)}, bf16[64,1024]{1,0:T(8,128)(2,1)S(1)}, u32[]{:S(2)}, u32[]{:S(2)}) collective-permute-start(bf16[64,1024]{1,0:T(8,128)(2,1)S(1)} %slice.209), channel_id=1, source_target_pairs={{0,4},{1,5},{2,6},{3,7},{4,0},{5,1},{6,2},{7,3},{8,12},{9,13},{10,... | collective-permute-start | bytes 393224 | tf_op jit(solution)/shard_map/ppermute | solution.py:56
  181.3 15.1 %collective-permute-start.38 = (bf16[64,1024]{1,0:T(8,128)(2,1)S(1)}, bf16[64,1024]{1,0:T(8,128)(2,1)S(1)}, u32[]{:S(2)}, u32[]{:S(2)}) collective-permute-start(bf16[64,1024]{1,0:T(8,128)(2,1)S(1)} %slice.210), channel_id=1, source_target_pairs={{0,2},{1,3},{2,0},{3,1},{4,6},{5,7},{6,4},{7,5},{8,10},{9,11},{10,... | collective-permute-start | bytes 393224 | tf_op jit(solution)/shard_map/ppermute | solution.py:56
  196.5 35.2 %collective-permute-start.39 = (bf16[1024,256]{1,0:T(8,128)(2,1)}, bf16[1024,256]{1,0:T(8,128)(2,1)S(1)}, u32[]{:S(2)}, u32[]{:S(2)}) collective-permute-start(bf16[1024,256]{1,0:T(8,128)(2,1)} %get-tuple-element.207), channel_id=1, source_target_pairs={{8,0},{9,1},{10,2},{11,3},{12,4},{13,5},{14,6},{15,7},{16,8},{17,9... | collective-permute-start | bytes 1572872 | tf_op jit(solution)/shard_map/ppermute | solution.py:61
  197.8 33.9 %collective-permute-start.40 = (bf16[1024,256]{1,0:T(8,128)(2,1)}, bf16[1024,256]{1,0:T(8,128)(2,1)}, u32[]{:S(2)}, u32[]{:S(2)}) collective-permute-start(bf16[1024,256]{1,0:T(8,128)(2,1)} %get-tuple-element.208), channel_id=1, source_target_pairs={{0,8},{1,9},{2,10},{3,11},{4,12},{5,13},{6,14},{7,15},{8,16},{9,17... | collective-permute-start | bytes 1572872 | tf_op jit(solution)/shard_map/ppermute | solution.py:61
  208.5 12.6 %collective-permute-start.43 = (bf16[32,1024]{1,0:T(8,128)(2,1)}, bf16[32,1024]{1,0:T(8,128)(2,1)S(1)}, u32[]{:S(2)}, u32[]{:S(2)}) collective-permute-start(bf16[32,1024]{1,0:T(8,128)(2,1)} %get-tuple-element.212), channel_id=1, source_target_pairs={{0,1},{1,5},{2,9},{3,13},{4,17},{5,21},{6,25},{7,29},{8,2},{9,6},{... | collective-permute-start | bytes 196616 | tf_op jit(solution)/shard_map/ppermute | solution.py:906
  211.5 18.3 %collective-permute-start.44 = (bf16[32,1024]{1,0:T(8,128)(2,1)}, bf16[32,1024]{1,0:T(8,128)(2,1)S(1)}, u32[]{:S(2)}, u32[]{:S(2)}) collective-permute-start(bf16[32,1024]{1,0:T(8,128)(2,1)} %get-tuple-element.213), channel_id=1, source_target_pairs={{0,2},{1,6},{2,10},{3,14},{4,18},{5,22},{6,26},{7,30},{8,3},{9,7},... | collective-permute-start | bytes 196616 | tf_op jit(solution)/shard_map/ppermute | solution.py:906
  214.5 17.1 %collective-permute-start.45 = (bf16[32,1024]{1,0:T(8,128)(2,1)}, bf16[32,1024]{1,0:T(8,128)(2,1)S(1)}, u32[]{:S(2)}, u32[]{:S(2)}) collective-permute-start(bf16[32,1024]{1,0:T(8,128)(2,1)} %get-tuple-element.214), channel_id=1, source_target_pairs={{0,3},{1,7},{2,11},{3,15},{4,19},{5,23},{6,27},{7,31},{8,0},{9,4},... | collective-permute-start | bytes 196616 | tf_op jit(solution)/shard_map/ppermute | solution.py:906
  221.2 21.5 %collective-permute-start.46 = (bf16[128,1024]{1,0:T(8,128)(2,1)}, bf16[128,1024]{1,0:T(8,128)(2,1)S(1)}, u32[]{:S(2)}, u32[]{:S(2)}) collective-permute-start(bf16[128,1024]{1,0:T(8,128)(2,1)} %get-tuple-element.234), channel_id=1, source_target_pairs={{0,24},{1,25},{2,26},{3,27},{4,28},{5,29},{6,30},{7,31},{8,0},{9,1... | collective-permute-start | bytes 786440 | tf_op jit(solution)/shard_map/ppermute | solution.py:68
  242.7 19.4 %collective-permute-start.47 = (bf16[3,256,1024]{2,1,0:T(8,128)(2,1)}, bf16[3,256,1024]{2,1,0:T(8,128)(2,1)}, u32[]{:S(2)}, u32[]{:S(2)}) collective-permute-start(bf16[3,256,1024]{2,1,0:T(8,128)(2,1)} %get-tuple-element.243), channel_id=1, source_target_pairs={{0,1},{1,0},{2,3},{3,2},{4,5},{5,4},{6,7},{7,6},{8,9},{9,8},{10,11... | collective-permute-start | bytes 4718600 | tf_op jit(solution)/shard_map/ppermute | solution.py:56
  242.8 14.6 %collective-permute-start.48 = (bf16[256,1024]{1,0:T(8,128)(2,1)}, bf16[256,1024]{1,0:T(8,128)(2,1)S(1)}, u32[]{:S(2)}, u32[]{:S(2)}) collective-permute-start(bf16[256,1024]{1,0:T(8,128)(2,1)} %get-tuple-element.244), channel_id=1, source_target_pairs={{0,1},{1,0},{2,3},{3,2},{4,5},{5,4},{6,7},{7,6},{8,9},{9,8},{10,11... | collective-permute-start | bytes 1572872 | tf_op jit(solution)/shard_map/ppermute | solution.py:56
  244.7 35.7 %all-to-all-start.6 = ((bf16[32,40,384]{2,1,0:T(8,128)(2,1)}), bf16[32,40,384]{2,1,0:T(8,128)(2,1)S(1)}, u32[]{:S(2)}, u32[]{:S(2)}) async-start(bf16[32,40,384]{2,1,0:T(8,128)(2,1)} %get-tuple-element.240), calls=%async_computation.6 | async-start | bytes 1966080 | tf_op jit(solution)/shard_map/all_to_all | solution.py:82
  258.8 12.9 %collective-permute-start.51 = (bf16[128,1024]{1,0:T(8,128)(2,1)S(1)}, bf16[128,1024]{1,0:T(8,128)(2,1)S(1)}, u32[]{:S(2)}, u32[]{:S(2)}) collective-permute-start(bf16[128,1024]{1,0:T(8,128)(2,1)S(1)} %get-tuple-element.282), channel_id=1, source_target_pairs={{0,2},{1,3},{2,0},{3,1},{4,6},{5,7},{6,4},{7,5},{8,10},{9,11},{10,... | collective-permute-start | bytes 786440 | tf_op jit(solution)/shard_map/ppermute | solution.py:56
  260.6 12.7 %collective-permute-start.49 = (bf16[128,1024]{1,0:T(8,128)(2,1)S(1)}, bf16[128,1024]{1,0:T(8,128)(2,1)S(1)}, u32[]{:S(2)}, u32[]{:S(2)}) collective-permute-start(bf16[128,1024]{1,0:T(8,128)(2,1)S(1)} %get-tuple-element.283), channel_id=1, source_target_pairs={{0,4},{1,5},{2,6},{3,7},{4,0},{5,1},{6,2},{7,3},{8,12},{9,13},{10,... | collective-permute-start | bytes 786440 | tf_op jit(solution)/shard_map/ppermute | solution.py:56
  272.6 16.9 %collective-permute-start.52 = (bf16[256,1024]{1,0:T(8,128)(2,1)}, bf16[256,1024]{1,0:T(8,128)(2,1)S(1)}, u32[]{:S(2)}, u32[]{:S(2)}) collective-permute-start(bf16[256,1024]{1,0:T(8,128)(2,1)} %pad_maximum_fusion.8), channel_id=1, source_target_pairs={{0,4},{1,5},{2,6},{3,7},{4,0},{5,1},{6,2},{7,3},{8,12},{9,13},{10,... | collective-permute-start | bytes 1572872 | tf_op jit(solution)/shard_map/ppermute | solution.py:56
  274.2 15.3 %collective-permute-start.50 = (bf16[256,1024]{1,0:T(8,128)(2,1)}, bf16[256,1024]{1,0:T(8,128)(2,1)}, u32[]{:S(2)}, u32[]{:S(2)}) collective-permute-start(bf16[256,1024]{1,0:T(8,128)(2,1)} %pad_maximum_fusion.7), channel_id=1, source_target_pairs={{0,2},{1,3},{2,0},{3,1},{4,6},{5,7},{6,4},{7,5},{8,10},{9,11},{10,... | collective-permute-start | bytes 1572872 | tf_op jit(solution)/shard_map/ppermute | solution.py:56
  283.4 12.9 %all-to-all-start.7 = ((f32[32,1,128]{2,1,0:T(1,128)}), f32[32,1,128]{2,1,0:T(1,128)S(1)}, u32[]{:S(2)}, u32[]{:S(2)}) async-start(f32[32,1,128]{2,1,0:T(1,128)} %get-tuple-element.241), calls=%async_computation.7 | async-start | bytes 32768 | tf_op jit(solution)/shard_map/all_to_all | solution.py:82
  (58 other events, 457.4 us)

commit v4 on v3

--- a/solution.py
+++ b/solution.py
@@ -30,7 +30,7 @@
     return jax.ShapeDtypeStruct(shape, dtype)
 
 
-def kernel_call(body, outs, *args, scalars=(), scratch=(), flops=0, limit=60):
+def kernel_call(body, outs, *args, scalars=(), scratch=(), flops=0, limit=56):
     moved = sum(a.size * a.dtype.itemsize for a in list(args) + list(outs))
     return pl.pallas_call(
         body,
@@ -383,7 +383,7 @@
         cost_estimate=pl.CostEstimate(
             flops=40 * tokens * tokens * wide, bytes_accessed=16 * tokens * wide, transcendentals=2 * tokens * tokens
         ),
-        compiler_params=pltpu.CompilerParams(vmem_limit_bytes=60 << 20),
+        compiler_params=pltpu.CompilerParams(vmem_limit_bytes=56 << 20),
     )(key_ranges(spans, QUERY_TILE, KEY_TILE), queries, before, own, behind, bounds)
 
 
@@ -417,7 +417,7 @@
         cost_estimate=pl.CostEstimate(
             flops=60 * tokens * tokens * wide, bytes_accessed=32 * tokens * wide, transcendentals=2 * tokens * tokens
         ),
-        compiler_params=pltpu.CompilerParams(vmem_limit_bytes=60 << 20),
+        compiler_params=pltpu.CompilerParams(vmem_limit_bytes=56 << 20),
     )(key_ranges(spans, QUERY_TILE, KEY_TILE), queries, before, own, behind, bounds, mixed, logs, grads)
 
 
@@ -599,13 +599,17 @@
         grad_ref[d, rows:, LANES : 2 * LANES] = vectors[EXTRA:, lot].astype(LOW)
 
 
-def first_norm_back_kernel(one_ref, two_ref, three_ref, tokens_ref, second_grad_ref, vector_ref, out_ref):
-    incoming = one_ref[...] + two_ref[...].astype(F32) + three_ref[...].astype(F32)
+def last_kernel(one_ref, two_ref, three_ref, tokens_ref, second_grad_ref, second_ref, vector_ref, out_ref, block_ref):
+    number = tokens_ref.shape[0]
+    both = one_ref[...] + two_ref[...].astype(F32) + three_ref[...].astype(F32)
     unit, inverse = norm_parts(tokens_ref[...].astype(F32))
-    out_ref[...] = (second_grad_ref[...] + norm_back(unit, inverse, vector_ref[0:1, :], incoming)).astype(LOW)
-
-
-def sum_kernel(wide, with_vectors, square_ref, *refs):
+    back = norm_back(unit, inverse, vector_ref[0:1, :], both[:number])
+    out_ref[...] = (second_grad_ref[...] + back).astype(LOW)
+    block_ref[...] = (second_ref[...] + both[number:] + vector_ref[4:5, :]).astype(LOW)
+
+
+def sum_kernel(wide, with_vectors, whole_count, parts_count, square_ref, *refs):
+    others, parts, refs = refs[:whole_count], refs[whole_count : whole_count + parts_count], refs[whole_count + parts_count :]
     part_ref, grad_ref, total_ref = refs[:3]
     devices = part_ref.shape[0]
     rows = grad_ref.shape[0]
@@ -619,6 +623,12 @@
             square += whole * whole
             start += wide
     found = jnp.sum(square, keepdims=True) + square_ref[0]
+    for ref in others:
+        found += jnp.sum(ref[...] * ref[...], keepdims=True)
+    if parts:
+        whole = sum(ref[...].astype(F32) for ref in parts)
+        refs[-1][...] = whole
+        found += jnp.sum(whole * whole, keepdims=True)
     if with_vectors:
         vectors = sum(part_ref[d, rows:, : 2 * LANES].astype(F32) for d in range(devices))
         refs[3][:EXTRA, :] = vectors[:, :LANES]
@@ -629,23 +639,26 @@
     total_ref[...] = jnp.broadcast_to(found.reshape((1,) * len(total_ref.shape)), total_ref.shape)
 
 
-def sum_parts(wide, rows, part, square, lot=None):
+def sum_parts(wide, rows, part, square, lot=None, others=(), parts=()):
     n, _, columns = part.shape
     vectors = lot is not None
     if wide % LANES == 0 and rows % 16 == 0:
         outs = [like((rows, PLANE * columns), F32), like((n, 1, LANES) if vectors else (1, 1), F32)]
         found = kernel_call(
-            functools.partial(sum_kernel, wide, vectors),
-            outs + [like((2 * EXTRA, LANES), F32)] * vectors,
+            functools.partial(sum_kernel, wide, vectors, len(others), len(parts)),
+            outs + [like((2 * EXTRA, LANES), F32)] * vectors + [like(p.shape, F32) for p in parts[:1]],
+            *others,
+            *parts,
             part,
             scalars=(jnp.stack([square, lot.astype(F32) if vectors else square]),),
         )
-        return found if vectors else (*found, None)
+        return found
     whole = part[:, :rows].astype(F32).reshape(-1, PLANE, rows, columns // wide, wide).sum(0)
     whole = whole.transpose(1, 2, 0, 3).reshape(rows, -1)
-    square = square + jnp.sum(whole * whole)
+    square = square + jnp.sum(whole * whole) + sum(jnp.sum(g * g) for g in others)
     if not vectors:
-        return whole, square.reshape(1, 1), None
+        joined = sum(p.astype(F32) for p in parts)
+        return whole, (square + jnp.sum(joined * joined)).reshape(1, 1), joined
     found = part[:, rows:, : 2 * LANES].astype(F32).sum(0)
     found = jnp.concatenate([found[:, :LANES], found[:, LANES:]], axis=0)
     mine = lax.dynamic_slice_in_dim(found, rows * lot, rows, axis=1)
@@ -875,9 +888,8 @@
         flops=2 * shared * columns * inner,
     )
     branch_sides = spread_sides(branch_grad)
-    mixed_grad, expand_grad, branch_sides, shrink_turns[:2] = tie(
-        mixed_grad, expand_grad, branch_sides, shrink_turns[:2]
-    )
+    mixed_grad, expand_grad, branch_sides, shrink_turns = tie(mixed_grad, expand_grad, branch_sides, shrink_turns)
+    shrink_grad = sum(g.astype(F32) for g in [shrink_grad[0], *shrink_turns])
 
     expand_part = exchange(after(expand_grad, mixed_grad).reshape(n, rows, inner))
     branch_corner = spread_corner(*branch_sides)
@@ -902,15 +914,15 @@
         output_grad = jnp.take(
             output_grad[0].reshape(planes, rows, columns), (plane + jnp.arange(planes)) % planes, axis=0, mode="clip"
         )
-    output_grad = sum(
+    output_parts = [
         lax.ppermute(
             output_grad[s],
             "seq",
             [(g * PLANE + j, j * planes + (g + s) % planes) for g in range(planes) for j in range(PLANE)],
-        ).astype(F32)
+        )
         for s in range(planes)
-    )
-    from_after, from_before, output_grad = tie(from_after, from_before, output_grad)
+    ]
+    from_after, from_before, output_parts[:2] = tie(from_after, from_before, output_parts[:2])
 
     fused = rows % 16 == 0 and hidden == LANES
     attend_grad, first_near, first_far, first_corner, one_sums = kernel_call(
@@ -945,20 +957,17 @@
     attend_part = attend_grad
     if not fused:
         attend_part = with_vectors(attend_grad, one_sums, two_sums, up_sums, spot, n, rows, hidden)
-    attend_part, first_near, first_far, first_corner, expand_part, shrink_turns = tie(
-        attend_part, first_near, first_far, first_corner, expand_part, shrink_turns
-    )
-    shrink_grad = sum(g.astype(F32) for g in [shrink_grad[0], *shrink_turns])
+    attend_part, first_near, first_far, first_corner, expand_part, output_parts = tie(
+        attend_part, first_near, first_far, first_corner, expand_part, output_parts
+    )
     attend_part = exchange(attend_part)
     both = collect(first_near, first_far, first_corner)
-    first_grad, block_output = zip(*[(t[:number], t[number:]) for t in both])
-    (input_gradient,) = kernel_call(
-        first_norm_back_kernel, [block_like], *first_grad, tokens, second_grad, vectors
-    )
-    block_output = (second + total(block_output) + vectors[4:5]).astype(LOW)
-
-    squares = sum(jnp.sum(g * g) for g in (output_grad, shrink_grad))
-    expand_grad, squares, _ = sum_parts(hidden, rows, expand_part, squares)
+    input_gradient, block_output = kernel_call(
+        last_kernel, [block_like, block_like], *both, tokens, second_grad, second, vectors
+    )
+    expand_grad, squares, output_grad = sum_parts(
+        hidden, rows, expand_part, jnp.zeros((), F32), others=[shrink_grad], parts=output_parts
+    )
     attend_grad, squares, vector_grad = sum_parts(wide, rows, attend_part, squares[0, 0], device % in_lot)
     vector_grad = lax.dynamic_slice_in_dim(vector_grad, rows * (device % in_lot), rows, axis=1)
     vector_grad = vector_grad[: vector_params.shape[0]]

time: 304 us -> 294 us (0.967)
  starting transfers between devices: 119 us -> 112 us
  waiting for transfers between devices: 61.4 us -> 67 us
  local copies, waits for them, and re-layouts: 17.4 us -> 13.1 us
  other arithmetic: 21.6 us -> 17.5 us
    ppermute x6, starting transfers between devices: 18.9 us -> 10.7 us  [turn(): lax.ppermute(block, 'seq', [(i, (i + planes_on * PLANE) % n) for i in ran...]
    all_to_all x8, starting transfers between devices: 36.5 us -> 41.4 us  [exchange(): return lax.all_to_all(blocks, 'seq', 0, 0, axis_index_groups=groups)]
    slice x4 -> x0, local copies, waits for them, and re-layouts: 3.98 us -> none  [the longest x3 3.22 us: on_device(): first_grad, block_output = zip(*[(t[:number], t[number:]) for t in both])]
    reduce_sum x2 -> x0, other arithmetic: 3.15 us -> none  [on_device(): squares = sum((jnp.sum(g * g) for g in (output_grad, shrink_grad)))]
    unnamed x96 -> x102, local copies, waits for them, and re-layouts: 7.55 us -> 6.75 us
  transfers between devices with their start and end apart: 61 -> 61, of which waited for: 21 -> 24; matrix products, arithmetic and copies ran while one was open for 10% -> 8% of each run, Pallas kernels for 20% -> 21%
where the time goes in v4:
time: 294 us; the launch traced here: 293 us
  starting transfers between devices  112 us (38%)
  Pallas kernels  81 us (28%)
  waiting for transfers between devices  67 us (23%)
  other arithmetic  17.5 us (6%)
  local copies, waits for them, and re-layouts  13.1 us (4%)
    pallas_call x12, Pallas kernels, kernel_call(): pl.pallas_call(body, in_specs=[SMEM] * len(scalars) + [WHOLE] * len(args)...  57.3 us
    ppermute x39, waiting for transfers between devices, swap(): return lax.ppermute(block, 'seq', [(i, i ^ bit) for i in range(n)])  49 us
    all_to_all x8, starting transfers between devices, exchange(): return lax.all_to_all(blocks, 'seq', 0, 0, axis_index_groups=groups)  41.4 us
    ppermute x39, starting transfers between devices, swap(): return lax.ppermute(block, 'seq', [(i, i ^ bit) for i in range(n)])  39.3 us
    pallas_call x1, Pallas kernels, attention_back(): pl.pallas_call(attend_back_kernel, grid_spec=pltpu.PrefetchScalarGridSpec...  13.5 us
    ppermute x4, starting transfers between devices, on_device(): lax.ppermute(output_grad[s], 'seq', [(g * PLANE + j, j * planes + (g + s)...  11.3 us
    all_to_all x8, waiting for transfers between devices, exchange(): return lax.all_to_all(blocks, 'seq', 0, 0, axis_index_groups=groups)  10.8 us
    ppermute x6, starting transfers between devices, turn(): lax.ppermute(block, 'seq', [(i, (i + planes_on * PLANE) % n) for i in ran...  10.7 us
  transfers between devices with their start and end apart: 61, of which 24 were waited for; matrix products, arithmetic and copies ran while one was open for 8% of the time, Pallas kernels for 21%

profile of v4, /device:TPU:0, one launch (start us, length us, event | category | flops | bytes accessed | tf_op | source)
XLA Modules:
  0.0 292.5 jit_solution(12957745982466119423)
XLA Ops:
  0.7 3.0 %collective-permute-start = (bf16[128,1024]{1,0:T(8,128)(2,1)}, bf16[128,1024]{1,0:T(8,128)(2,1)S(1)}, u32[]{:S(2)}, u32[]{:S(2)}) collective-permute-start(bf16[128,1024]{1,0:T(8,128)(2,1)} %tokens_ref.3), channel_id=1, source_target_pairs={{0,2},{1,3},{2,0},{3,1},{4,6},{5,7},{6,4},{7,5},{8,10},{9,11},{10,... | collective-permute-start | bytes 786440 | tf_op jit(solution)/shard_map/ppermute | solution.py:56
  11.6 4.9 %all-to-all-start = ((bf16[32,40,384]{2,1,0:T(8,128)(2,1)}), bf16[32,40,384]{2,1,0:T(8,128)(2,1)S(1)}, u32[]{:S(2)}, u32[]{:S(2)}) async-start(bf16[32,40,384]{2,1,0:T(8,128)(2,1)} %pad_maximum_fusion.2), calls=%async_computation | async-start | bytes 1966080 | tf_op jit(solution)/shard_map/all_to_all | solution.py:82
  23.7 10.9 %collective-permute-done.7 = bf16[32,1024]{1,0:T(8,128)(2,1)S(1)} collective-permute-done((bf16[32,1024]{1,0:T(8,128)(2,1)S(1)}, bf16[32,1024]{1,0:T(8,128)(2,1)S(1)}, u32[]{:S(2)}, u32[]{:S(2)}) %collective-permute-start.7) | collective-permute-done | bytes 65568 | tf_op jit(solution)/shard_map/ppermute | solution.py:56
  34.6 4.6 %collective-permute-start.8 = (bf16[64,1024]{1,0:T(8,128)(2,1)S(1)}, bf16[64,1024]{1,0:T(8,128)(2,1)S(1)}, u32[]{:S(2)}, u32[]{:S(2)}) collective-permute-start(bf16[64,1024]{1,0:T(8,128)(2,1)S(1)} %pad_maximum_fusion.12), channel_id=1, source_target_pairs={{0,16},{1,17},{2,18},{3,19},{4,20},{5,21},{6,22},{7,23},{8,24},{9,... | collective-permute-start | bytes 393224 | tf_op jit(solution)/shard_map/ppermute | solution.py:56
  40.5 6.5 %collective-permute-done.8 = bf16[64,1024]{1,0:T(8,128)(2,1)S(1)} collective-permute-done((bf16[64,1024]{1,0:T(8,128)(2,1)S(1)}, bf16[64,1024]{1,0:T(8,128)(2,1)S(1)}, u32[]{:S(2)}, u32[]{:S(2)}) %collective-permute-start.8) | collective-permute-done | bytes 131104 | tf_op jit(solution)/shard_map/ppermute | solution.py:56
  48.1 6.5 %shard_map.313 = (bf16[1024,1024]{1,0:T(8,128)(2,1)}, bf16[1024,1024]{1,0:T(8,128)(2,1)}, bf16[1024,128]{1,0:T(8,128)(2,1)}, bf16[1024,256]{1,0:T(8,128)(2,1)}, ...) custom-call(s32[2]{0:T(128)} %pad_add_fusion.1.spot_ref.place_ref, bf16[128,1024]{1,0:T(8,128)(2,1)} %tokens_ref.3, ...), custom_call_target="tpu_custom_call" | custom-call | flops 805306368 | bytes 9011200 | tf_op jit(solution)/shard_map/pallas_call | solution.py:35
  54.6 2.1 collective-permute-start.11
  61.6 5.0 %all-to-all-start.1 = ((bf16[32,32,256]{2,1,0:T(8,128)(2,1)}), bf16[32,32,256]{2,1,0:T(8,128)(2,1)S(1)}, u32[]{:S(2)}, u32[]{:S(2)}) async-start(bf16[32,32,256]{2,1,0:T(8,128)(2,1)} %get-tuple-element.171), calls=%async_computation.1 | async-start | bytes 1048576 | tf_op jit(solution)/shard_map/all_to_all | solution.py:82
  69.2 2.4 collective-permute-start.15
  72.1 2.7 collective-permute-done.12.after_ref
  74.8 10.2 %shard_map.314 = (f32[1024,128]{1,0:T(8,128)}, bf16[1024,128]{1,0:T(8,128)(2,1)}, f32[2,1024]{1,0:T(2,128)}) custom-call(s32[2,2]{1,0:T(2,128)} %pad_add_fusion.range_ref, bf16[1024,128]{1,0:T(8,128)(2,1)} %get-tuple-element.166.query_ref, bf16[1024,256]{1,0:T(8,128)(2,1)} %collective-permute-done.11.before_ref, ...), custom_call_target="tpu_custom_call" | custom-call | flops 5368709120 | bytes 2097152 | tf_op jit(solution)/shard_map/pallas_call | solution.py:373
  87.9 2.4 all-to-all-done.1
  90.8 3.4 %all-to-all-start.2 = ((bf16[8,128,128]{2,1,0:T(8,128)(2,1)}), bf16[8,128,128]{2,1,0:T(8,128)(2,1)S(1)}, u32[]{:S(2)}, u32[]{:S(2)}) async-start(bf16[8,128,128]{2,1,0:T(8,128)(2,1)} %bitcast.17), calls=%async_computation.2 | async-start | bytes 524288 | tf_op jit(solution)/shard_map/all_to_all | solution.py:82
  94.3 3.3 %collective-permute-start.20 = (bf16[128,1024]{1,0:T(8,128)(2,1)S(1)}, bf16[128,1024]{1,0:T(8,128)(2,1)}, u32[]{:S(2)}, u32[]{:S(2)}) collective-permute-start(bf16[128,1024]{1,0:T(8,128)(2,1)S(1)} %convert_element_type.91.refs_10_.refs_0_), channel_id=1, source_target_pairs={{0,24},{1,25},{2,26},{3,27},{4,28},{5,29},{6,30},{7,31},{8,0},{9,1... | collective-permute-start | bytes 786440 | tf_op jit(solution)/shard_map/ppermute | solution.py:68
  97.6 3.5 %all-to-all-done.2.mixed_ref = bf16[8,128,128]{2,1,0:T(8,128)(2,1)S(1)} async-done(((bf16[8,128,128]{2,1,0:T(8,128)(2,1)}), bf16[8,128,128]{2,1,0:T(8,128)(2,1)S(1)}, u32[]{:S(2)}, u32[]{:S(2)}) %all-to-all-start.2) | async-done | bytes 262176 | tf_op jit(solution)/shard_map/all_to_all | solution.py:82
  102.2 3.2 %shard_map.315 = (f32[128,1024]{1,0:T(8,128)}, bf16[128,1024]{1,0:T(8,128)(2,1)}) custom-call(s32[2]{0:T(128)} %pad_add_fusion.1.spot_ref.place_ref, bf16[8,128,128]{2,1,0:T(8,128)(2,1)} %copy-done.16, bf16[128,1024]{1,0:T(8,128)(2,1)} %tokens_ref.3, f32[16,1024]{1,0:T(8,128)} %get-tuple-element.175.vector_ref, bf16[512,1024]{1,0:T(8,128)(2,1)} %copy-done, ...), custom_call_target="tpu_custom_call" | custom-call | flops 268435456 | bytes 3473408 | tf_op jit(solution)/shard_map/pallas_call | solution.py:35
  106.5 3.5 %all-to-all-start.3 = ((bf16[32,32,256]{2,1,0:T(8,128)(2,1)}), bf16[32,32,256]{2,1,0:T(8,128)(2,1)}, u32[]{:S(2)}, u32[]{:S(2)}) async-start(bf16[32,32,256]{2,1,0:T(8,128)(2,1)} %get-tuple-element.190), calls=%async_computation.3 | async-start | bytes 1048576 | tf_op jit(solution)/shard_map/all_to_all | solution.py:82
  110.1 3.5 %collective-permute-done.17.refs_1_ = bf16[128,1024]{1,0:T(8,128)(2,1)S(1)} collective-permute-done((bf16[128,1024]{1,0:T(8,128)(2,1)}, bf16[128,1024]{1,0:T(8,128)(2,1)S(1)}, u32[]{:S(2)}, u32[]{:S(2)}) %collective-permute-start.17) | collective-permute-done | bytes 262176 | tf_op jit(solution)/shard_map/ppermute | solution.py:56
  113.6 2.5 collective-permute-done.18.refs_2_
  118.4 6.0 %collective-permute-done.22.refs_3_ = bf16[64,1024]{1,0:T(8,128)(2,1)S(1)} collective-permute-done((bf16[64,1024]{1,0:T(8,128)(2,1)S(1)}, bf16[64,1024]{1,0:T(8,128)(2,1)S(1)}, u32[]{:S(2)}, u32[]{:S(2)}) %collective-permute-start.22) | collective-permute-done | bytes 131104 | tf_op jit(solution)/shard_map/ppermute | solution.py:56
  128.0 8.7 %shard_map.316 = (f32[4,128,1024]{2,1,0:T(8,128)}, bf16[3,128,1024]{2,1,0:T(8,128)(2,1)}, bf16[128,1024]{1,0:T(8,128)(2,1)}, bf16[1024,512]{1,0:T(8,128)(2,1)}, ...) custom-call(s32[2]{0:T(128)} %pad_add_fusion.1.spot_ref.place_ref, bf16[128,1024]{1,0:T(8,128)(2,1)} %get-tuple-element.177.refs_0_, ...), custom_call_target="tpu_custom_call" | custom-call | flops 3221225472 | bytes 11538432 | tf_op jit(solution)/shard_map/pallas_call | solution.py:35
  137.3 4.3 %shard_map.317 = (bf16[128,1024]{1,0:T(8,128)(2,1)}, bf16[128,1024]{1,0:T(8,128)(2,1)}, bf16[128,1024]{1,0:T(8,128)(2,1)}, bf16[128,1024]{1,0:T(8,128)(2,1)}) custom-call(s32[2]{0:T(128)} %pad_add_fusion.1.spot_ref.place_ref, bf16[1024,512]{1,0:T(8,128)(2,1)} %get-tuple-element.191.active_ref, bf16[512,1024]{1,0:T(8,128)(2,1)} %pad_maximum_fusion.1.refs_8_.refs_0_, ...), custom_call_target="tpu_custom_call" | custom-call | flops 1073741824 | bytes 4194304 | tf_op jit(solution)/shard_map/pallas_call | solution.py:35
  141.7 2.4 collective-permute-start.33
  147.3 2.5 collective-permute-done.31
  154.7 2.7 collective-permute-done.32.three_ref
  158.4 4.1 %shard_map.318 = (f32[128,1024]{1,0:T(8,128)}, bf16[128,1024]{1,0:T(8,128)(2,1)}, bf16[8,128,128]{2,1,0:T(8,128)(2,1)}, f32[3,1024]{1,0:T(4,128)}) custom-call(s32[2]{0:T(128)} %pad_add_fusion.1.spot_ref.place_ref, f32[128,1024]{1,0:T(8,128)} %get-tuple-element.197.one_ref, bf16[128,1024]{1,0:T(8,128)(2,1)} %copy-done.27, bf16[128,1024]{1,0:T(8,128)(2,1)} %copy-done.26, ...), custom_call_target="tpu_custom_call" | custom-call | flops 268435456 | bytes 5058560 | tf_op jit(solution)/shard_map/pallas_call | solution.py:35
  165.0 3.4 %all-to-all-start.4 = ((bf16[8,128,128]{2,1,0:T(8,128)(2,1)}), bf16[8,128,128]{2,1,0:T(8,128)(2,1)S(1)}, u32[]{:S(2)}, u32[]{:S(2)}) async-start(bf16[8,128,128]{2,1,0:T(8,128)(2,1)} %get-tuple-element.201), calls=%async_computation.4 | async-start | bytes 524288 | tf_op jit(solution)/shard_map/all_to_all | solution.py:82
  168.4 4.1 %shard_map.319 = bf16[1024,512]{1,0:T(8,128)(2,1)} custom-call(bf16[1024,512]{1,0:T(8,128)(2,1)} %get-tuple-element.204.grad_ref, bf16[128,1024]{1,0:T(8,128)(2,1)} %get-tuple-element.177.refs_0_, bf16[128,1024]{1,0:T(8,128)(2,1)} %copy-done.10, bf16[128,1024]{1,0:T(8,128)(2,1)} %copy-done.11, bf16[64,1024]{1,0:T(8,128)(2,1)} %copy-done.34, ...), custom_call_target="tpu_custom_call" | custom-call | flops 1073741824 | bytes 4194304 | tf_op jit(solution)/shard_map/pallas_call | solution.py:35
  172.6 2.7 all-to-all-done.4
  175.3 3.0 %all-to-all-start.5 = ((bf16[32,32,512]{2,1,0:T(8,128)(2,1)}), bf16[32,32,512]{2,1,0:T(8,128)(2,1)S(1)}, u32[]{:S(2)}, u32[]{:S(2)}) async-start(bf16[32,32,512]{2,1,0:T(8,128)(2,1)} %bitcast.90), calls=%async_computation.5 | async-start | bytes 2097152 | tf_op jit(solution)/shard_map/all_to_all | solution.py:82
  181.5 13.5 %shard_map.320 = (bf16[1024,128]{1,0:T(8,128)(2,1)}, bf16[1024,256]{1,0:T(8,128)(2,1)}, f32[1024,256]{1,0:T(8,128)}, bf16[1024,256]{1,0:T(8,128)(2,1)}) custom-call(s32[2,2]{1,0:T(2,128)} %pad_add_fusion.range_ref, bf16[1024,128]{1,0:T(8,128)(2,1)} %get-tuple-element.166.query_ref, bf16[1024,256]{1,0:T(8,128)(2,1)} %collective-permute-done.11.before_ref, ...), custom_call_target="tpu_custom_call" | custom-call | flops 8053063680 | bytes 4194304 | tf_op jit(solution)/shard_map/pallas_call | solution.py:396
  196.5 4.6 %collective-permute-start.41 = (bf16[1024,256]{1,0:T(8,128)(2,1)}, bf16[1024,256]{1,0:T(8,128)(2,1)S(1)}, u32[]{:S(2)}, u32[]{:S(2)}) collective-permute-start(bf16[1024,256]{1,0:T(8,128)(2,1)} %get-tuple-element.220), channel_id=1, source_target_pairs={{0,8},{1,9},{2,10},{3,11},{4,12},{5,13},{6,14},{7,15},{8,16},{9,17... | collective-permute-start | bytes 1572872 | tf_op jit(solution)/shard_map/ppermute | solution.py:61
  202.1 2.8 shard_map.321
  206.5 3.0 %collective-permute-start.44 = (bf16[32,1024]{1,0:T(8,128)(2,1)}, bf16[32,1024]{1,0:T(8,128)(2,1)S(1)}, u32[]{:S(2)}, u32[]{:S(2)}) collective-permute-start(bf16[32,1024]{1,0:T(8,128)(2,1)} %get-tuple-element.224), channel_id=1, source_target_pairs={{0,1},{1,5},{2,9},{3,13},{4,17},{5,21},{6,25},{7,29},{8,2},{9,6},{... | collective-permute-start | bytes 196616 | tf_op jit(solution)/shard_map/ppermute | solution.py:918
  209.5 3.7 %collective-permute-start.45 = (bf16[32,1024]{1,0:T(8,128)(2,1)}, bf16[32,1024]{1,0:T(8,128)(2,1)S(1)}, u32[]{:S(2)}, u32[]{:S(2)}) collective-permute-start(bf16[32,1024]{1,0:T(8,128)(2,1)} %get-tuple-element.241), channel_id=1, source_target_pairs={{0,2},{1,6},{2,10},{3,14},{4,18},{5,22},{6,26},{7,30},{8,3},{9,7},... | collective-permute-start | bytes 196616 | tf_op jit(solution)/shard_map/ppermute | solution.py:918
  214.4 3.1 %collective-permute-start.46 = (bf16[32,1024]{1,0:T(8,128)(2,1)}, bf16[32,1024]{1,0:T(8,128)(2,1)S(1)}, u32[]{:S(2)}, u32[]{:S(2)}) collective-permute-start(bf16[32,1024]{1,0:T(8,128)(2,1)} %get-tuple-element.242), channel_id=1, source_target_pairs={{0,3},{1,7},{2,11},{3,15},{4,19},{5,23},{6,27},{7,31},{8,0},{9,4},... | collective-permute-start | bytes 196616 | tf_op jit(solution)/shard_map/ppermute | solution.py:918
  218.8 10.1 %shard_map.322 = (bf16[32,40,384]{2,1,0:T(8,128)(2,1)}, f32[4,256,1024]{2,1,0:T(8,128)}, bf16[3,256,1024]{2,1,0:T(8,128)(2,1)}, bf16[256,1024]{1,0:T(8,128)(2,1)}, f32[2,1024]{1,0:T(2,128)}) custom-call(s32[2]{0:T(128)} %pad_add_fusion.1.spot_ref.place_ref, f32[1024,256]{1,0:T(8,128)} %get-tuple-element.214.own_ref, bf16[1024,256]{1,0:T(8,128)(2,1)} %copy-done.23, ...), custom_call_target="tpu_custom_call" | custom-call | flops 1610612736 | bytes 16734208 | tf_op jit(solution)/shard_map/pallas_call | solution.py:35
  229.0 2.0 collective-permute-done.46.refs_4_
  231.6 13.5 %all-to-all-start.6 = ((bf16[32,40,384]{2,1,0:T(8,128)(2,1)}), bf16[32,40,384]{2,1,0:T(8,128)(2,1)S(1)}, u32[]{:S(2)}, u32[]{:S(2)}) async-start(bf16[32,40,384]{2,1,0:T(8,128)(2,1)} %get-tuple-element.249), calls=%async_computation.6 | async-start | bytes 1966080 | tf_op jit(solution)/shard_map/all_to_all | solution.py:82
  246.6 1.8 collective-permute-start.51
  249.9 3.9 %convert_add_fusion = (f32[1,256,1024]{2,1,0:T(8,128)S(1)}, f32[1,256,1024]{2,1,0:T(8,128)S(1)}, f32[256,1024]{1,0:T(8,128)}) fusion(f32[4,256,1024]{2,1,0:T(8,128)} %get-tuple-element.251, bf16[3,256,1024]{2,1,0:T(8,128)(2,1)} %collective-permute-done.47), kind=kLoop, calls=%fused_computation.4 | loop fusion | flops 1572864 | bytes 7864320 | tf_op jit(solution)/shard_map/add | solution.py:134
  253.9 9.0 %collective-permute-done.51 = bf16[128,1024]{1,0:T(8,128)(2,1)S(1)} collective-permute-done((bf16[128,1024]{1,0:T(8,128)(2,1)S(1)}, bf16[128,1024]{1,0:T(8,128)(2,1)S(1)}, u32[]{:S(2)}, u32[]{:S(2)}) %collective-permute-start.51) | collective-permute-done | bytes 262176 | tf_op jit(solution)/shard_map/ppermute | solution.py:56
  265.3 2.1 convert_add_fusion.2.refs_0_.refs_18_
  267.9 2.6 shard_map.323
  272.7 2.1 shard_map.324
  274.8 4.6 %all-to-all-start.7 = ((f32[32,1,128]{2,1,0:T(1,128)}), f32[32,1,128]{2,1,0:T(1,128)S(1)}, u32[]{:S(2)}, u32[]{:S(2)}) async-start(f32[32,1,128]{2,1,0:T(1,128)} %get-tuple-element.250), calls=%async_computation.7 | async-start | bytes 32768 | tf_op jit(solution)/shard_map/all_to_all | solution.py:82
  281.7 3.2 %shard_map.325 = (bf16[128,1024]{1,0:T(8,128)(2,1)}, bf16[128,1024]{1,0:T(8,128)(2,1)}) custom-call(f32[256,1024]{1,0:T(8,128)} %get-tuple-element.286.one_ref, bf16[256,1024]{1,0:T(8,128)(2,1)} %copy-done.22, bf16[256,1024]{1,0:T(8,128)(2,1)} %copy-done.21, bf16[128,1024]{1,0:T(8,128)(2,1)} %tokens_ref.3, f32[128,1024]{1,0:T(8,128)} %get-tuple-element.254.second_grad_ref, ...), custom_call_target="tpu_custom_call" | custom-call | bytes 3997696 | tf_op jit(solution)/shard_map/pallas_call | solution.py:35
  287.1 5.3 %shard_map.326 = (f32[32,3072]{1,0:T(8,128)}, f32[32,3072]{1,0:T(8,128)}, f32[32,3072]{1,0:T(8,128)}, f32[32,1024]{1,0:T(8,128)}, f32[32,1024]{1,0:T(8,128)}, /*...) custom-call(f32[32,1,128]{2,1,0:T(1,128)} %copy-done.40, ...), custom_call_target="tpu_custom_call" | custom-call | bytes 11034500 | tf_op jit(solution)/shard_map/pallas_call | solution.py:35
  (260 shorter events, 71.4 us)
Async XLA Ops:
  0.7 9.5 %collective-permute-start = (bf16[128,1024]{1,0:T(8,128)(2,1)}, bf16[128,1024]{1,0:T(8,128)(2,1)S(1)}, u32[]{:S(2)}, u32[]{:S(2)}) collective-permute-start(bf16[128,1024]{1,0:T(8,128)(2,1)} %tokens_ref.3), channel_id=1, source_target_pairs={{0,2},{1,3},{2,0},{3,1},{4,6},{5,7},{6,4},{7,5},{8,10},{9,11},{10,... | collective-permute-start | bytes 786440 | tf_op jit(solution)/shard_map/ppermute | solution.py:56
  3.7 8.0 %collective-permute-start.1 = (bf16[128,1024]{1,0:T(8,128)(2,1)}, bf16[128,1024]{1,0:T(8,128)(2,1)S(1)}, u32[]{:S(2)}, u32[]{:S(2)}) collective-permute-start(bf16[128,1024]{1,0:T(8,128)(2,1)} %tokens_ref.3), channel_id=1, source_target_pairs={{0,4},{1,5},{2,6},{3,7},{4,0},{5,1},{6,2},{7,3},{8,12},{9,13},{10,... | collective-permute-start | bytes 786440 | tf_op jit(solution)/shard_map/ppermute | solution.py:56
  11.6 35.5 %all-to-all-start = ((bf16[32,40,384]{2,1,0:T(8,128)(2,1)}), bf16[32,40,384]{2,1,0:T(8,128)(2,1)S(1)}, u32[]{:S(2)}, u32[]{:S(2)}) async-start(bf16[32,40,384]{2,1,0:T(8,128)(2,1)} %pad_maximum_fusion.2), calls=%async_computation | async-start | bytes 1966080 | tf_op jit(solution)/shard_map/all_to_all | solution.py:82
  18.5 28.6 %collective-permute-start.4 = (bf16[3,128,1024]{2,1,0:T(8,128)(2,1)S(1)}, bf16[3,128,1024]{2,1,0:T(8,128)(2,1)}, u32[]{:S(2)}, u32[]{:S(2)}) collective-permute-start(bf16[3,128,1024]{2,1,0:T(8,128)(2,1)S(1)} %pad_maximum_fusion.3), channel_id=1, source_target_pairs={{0,1},{1,0},{2,3},{3,2},{4,5},{5,4},{6,7},{7,6},{8,9},{9,8},{10,11... | collective-permute-start | bytes 2359304 | tf_op jit(solution)/shard_map/ppermute | solution.py:56
  18.8 15.7 %collective-permute-start.7 = (bf16[32,1024]{1,0:T(8,128)(2,1)S(1)}, bf16[32,1024]{1,0:T(8,128)(2,1)S(1)}, u32[]{:S(2)}, u32[]{:S(2)}) collective-permute-start(bf16[32,1024]{1,0:T(8,128)(2,1)S(1)} %convert_element_type.92), channel_id=1, source_target_pairs={{0,8},{1,9},{2,10},{3,11},{4,12},{5,13},{6,14},{7,15},{8,0},{9,1},... | collective-permute-start | bytes 196616 | tf_op jit(solution)/shard_map/ppermute | solution.py:56
  20.6 18.6 %collective-permute-start.2 = (bf16[64,1024]{1,0:T(8,128)(2,1)S(1)}, bf16[64,1024]{1,0:T(8,128)(2,1)}, u32[]{:S(2)}, u32[]{:S(2)}) collective-permute-start(bf16[64,1024]{1,0:T(8,128)(2,1)S(1)} %slice.202), channel_id=1, source_target_pairs={{0,4},{1,5},{2,6},{3,7},{4,0},{5,1},{6,2},{7,3},{8,12},{9,13},{10,... | collective-permute-start | bytes 393224 | tf_op jit(solution)/shard_map/ppermute | solution.py:56
  22.2 17.0 %collective-permute-start.3 = (bf16[64,1024]{1,0:T(8,128)(2,1)S(1)}, bf16[64,1024]{1,0:T(8,128)(2,1)}, u32[]{:S(2)}, u32[]{:S(2)}) collective-permute-start(bf16[64,1024]{1,0:T(8,128)(2,1)S(1)} %slice.203), channel_id=1, source_target_pairs={{0,2},{1,3},{2,0},{3,1},{4,6},{5,7},{6,4},{7,5},{8,10},{9,11},{10,... | collective-permute-start | bytes 393224 | tf_op jit(solution)/shard_map/ppermute | solution.py:56
  34.6 12.4 %collective-permute-start.8 = (bf16[64,1024]{1,0:T(8,128)(2,1)S(1)}, bf16[64,1024]{1,0:T(8,128)(2,1)S(1)}, u32[]{:S(2)}, u32[]{:S(2)}) collective-permute-start(bf16[64,1024]{1,0:T(8,128)(2,1)S(1)} %pad_maximum_fusion.12), channel_id=1, source_target_pairs={{0,16},{1,17},{2,18},{3,19},{4,20},{5,21},{6,22},{7,23},{8,24},{9,... | collective-permute-start | bytes 393224 | tf_op jit(solution)/shard_map/ppermute | solution.py:56
  54.6 17.5 %collective-permute-start.11 = (bf16[1024,256]{1,0:T(8,128)(2,1)}, bf16[1024,256]{1,0:T(8,128)(2,1)}, u32[]{:S(2)}, u32[]{:S(2)}) collective-permute-start(bf16[1024,256]{1,0:T(8,128)(2,1)} %get-tuple-element.163.own_ref), channel_id=1, source_target_pairs={{0,8},{1,9},{2,10},{3,11},{4,12},{5,13},{6,14},{7,15},{8,16},{9,17... | collective-permute-start | bytes 1572872 | tf_op jit(solution)/shard_map/ppermute | solution.py:61
  56.7 18.1 %collective-permute-start.12 = (bf16[1024,256]{1,0:T(8,128)(2,1)}, bf16[1024,256]{1,0:T(8,128)(2,1)}, u32[]{:S(2)}, u32[]{:S(2)}) collective-permute-start(bf16[1024,256]{1,0:T(8,128)(2,1)} %get-tuple-element.163.own_ref), channel_id=1, source_target_pairs={{8,0},{9,1},{10,2},{11,3},{12,4},{13,5},{14,6},{15,7},{16,8},{17,9... | collective-permute-start | bytes 1572872 | tf_op jit(solution)/shard_map/ppermute | solution.py:61
  58.0 8.6 %collective-permute-start.10 = (bf16[128,1024]{1,0:T(8,128)(2,1)S(1)}, bf16[128,1024]{1,0:T(8,128)(2,1)S(1)}, u32[]{:S(2)}, u32[]{:S(2)}) collective-permute-start(bf16[128,1024]{1,0:T(8,128)(2,1)S(1)} %copy-done.17), channel_id=1, source_target_pairs={{0,2},{1,3},{2,0},{3,1},{4,6},{5,7},{6,4},{7,5},{8,10},{9,11},{10,... | collective-permute-start | bytes 786440 | tf_op jit(solution)/shard_map/ppermute | solution.py:56
  61.6 28.7 %all-to-all-start.1 = ((bf16[32,32,256]{2,1,0:T(8,128)(2,1)}), bf16[32,32,256]{2,1,0:T(8,128)(2,1)S(1)}, u32[]{:S(2)}, u32[]{:S(2)}) async-start(bf16[32,32,256]{2,1,0:T(8,128)(2,1)} %get-tuple-element.171), calls=%async_computation.1 | async-start | bytes 1048576 | tf_op jit(solution)/shard_map/all_to_all | solution.py:82
  67.1 18.9 %collective-permute-start.14 = (bf16[256,1024]{1,0:T(8,128)(2,1)S(1)}, bf16[256,1024]{1,0:T(8,128)(2,1)S(1)}, u32[]{:S(2)}, u32[]{:S(2)}) collective-permute-start(bf16[256,1024]{1,0:T(8,128)(2,1)S(1)} %pad_maximum_fusion.6), channel_id=1, source_target_pairs={{0,4},{1,5},{2,6},{3,7},{4,0},{5,1},{6,2},{7,3},{8,12},{9,13},{10,... | collective-permute-start | bytes 1572872 | tf_op jit(solution)/shard_map/ppermute | solution.py:56
  69.2 18.6 %collective-permute-start.15 = (bf16[128,1024]{1,0:T(8,128)(2,1)S(1)}, bf16[128,1024]{1,0:T(8,128)(2,1)S(1)}, u32[]{:S(2)}, u32[]{:S(2)}) collective-permute-start(bf16[128,1024]{1,0:T(8,128)(2,1)S(1)} %convert_element_type.91.refs_10_.refs_0_), channel_id=1, source_target_pairs={{0,8},{1,9},{2,10},{3,11},{4,12},{5,13},{6,14},{7,15},{8,16},{9,17... | collective-permute-start | bytes 786440 | tf_op jit(solution)/shard_map/ppermute | solution.py:68
  71.6 16.2 %collective-permute-start.13 = (bf16[256,1024]{1,0:T(8,128)(2,1)S(1)}, bf16[256,1024]{1,0:T(8,128)(2,1)S(1)}, u32[]{:S(2)}, u32[]{:S(2)}) collective-permute-start(bf16[256,1024]{1,0:T(8,128)(2,1)S(1)} %pad_maximum_fusion.5), channel_id=1, source_target_pairs={{0,2},{1,3},{2,0},{3,1},{4,6},{5,7},{6,4},{7,5},{8,10},{9,11},{10,... | collective-permute-start | bytes 1572872 | tf_op jit(solution)/shard_map/ppermute | solution.py:56
  90.3 10.8 %collective-permute-start.16 = (bf16[512,1024]{1,0:T(8,128)(2,1)S(1)}, bf16[512,1024]{1,0:T(8,128)(2,1)S(1)}, u32[]{:S(2)}, u32[]{:S(2)}) collective-permute-start(bf16[512,1024]{1,0:T(8,128)(2,1)S(1)} %pad_maximum_fusion.refs_0_), channel_id=1, source_target_pairs={{0,1},{1,0},{2,3},{3,2},{4,5},{5,4},{6,7},{7,6},{8,9},{9,8},{10,11... | collective-permute-start | bytes 3145736 | tf_op jit(solution)/shard_map/ppermute | solution.py:56
  90.3 19.8 %collective-permute-start.21 = (bf16[512,1024]{1,0:T(8,128)(2,1)}, bf16[512,1024]{1,0:T(8,128)(2,1)}, u32[]{:S(2)}, u32[]{:S(2)}) collective-permute-start(bf16[512,1024]{1,0:T(8,128)(2,1)} %pad_maximum_fusion.1.refs_8_.refs_0_), channel_id=1, source_target_pairs={{0,1},{1,0},{2,3},{3,2},{4,5},{5,4},{6,7},{7,6},{8,9},{9,8},{10,11... | collective-permute-start | bytes 3145736 | tf_op jit(solution)/shard_map/ppermute | solution.py:56
  90.8 10.3 %all-to-all-start.2 = ((bf16[8,128,128]{2,1,0:T(8,128)(2,1)}), bf16[8,128,128]{2,1,0:T(8,128)(2,1)S(1)}, u32[]{:S(2)}, u32[]{:S(2)}) async-start(bf16[8,128,128]{2,1,0:T(8,128)(2,1)} %bitcast.17), calls=%async_computation.2 | async-start | bytes 524288 | tf_op jit(solution)/shard_map/all_to_all | solution.py:82
  94.2 15.8 %collective-permute-start.19 = (bf16[128,1024]{1,0:T(8,128)(2,1)S(1)}, bf16[128,1024]{1,0:T(8,128)(2,1)}, u32[]{:S(2)}, u32[]{:S(2)}) collective-permute-start(bf16[128,1024]{1,0:T(8,128)(2,1)S(1)} %convert_element_type.91.refs_10_.refs_0_), channel_id=1, source_target_pairs={{0,16},{1,17},{2,18},{3,19},{4,20},{5,21},{6,22},{7,23},{8,24},{9,... | collective-permute-start | bytes 786440 | tf_op jit(solution)/shard_map/ppermute | solution.py:68
  94.3 15.7 %collective-permute-start.20 = (bf16[128,1024]{1,0:T(8,128)(2,1)S(1)}, bf16[128,1024]{1,0:T(8,128)(2,1)}, u32[]{:S(2)}, u32[]{:S(2)}) collective-permute-start(bf16[128,1024]{1,0:T(8,128)(2,1)S(1)} %convert_element_type.91.refs_10_.refs_0_), channel_id=1, source_target_pairs={{0,24},{1,25},{2,26},{3,27},{4,28},{5,29},{6,30},{7,31},{8,0},{9,1... | collective-permute-start | bytes 786440 | tf_op jit(solution)/shard_map/ppermute | solution.py:68
  105.4 8.2 %collective-permute-start.17 = (bf16[128,1024]{1,0:T(8,128)(2,1)}, bf16[128,1024]{1,0:T(8,128)(2,1)S(1)}, u32[]{:S(2)}, u32[]{:S(2)}) collective-permute-start(bf16[128,1024]{1,0:T(8,128)(2,1)} %get-tuple-element.177.refs_0_), channel_id=1, source_target_pairs={{0,2},{1,3},{2,0},{3,1},{4,6},{5,7},{6,4},{7,5},{8,10},{9,11},{10,... | collective-permute-start | bytes 786440 | tf_op jit(solution)/shard_map/ppermute | solution.py:56
  106.0 10.2 %collective-permute-start.18 = (bf16[128,1024]{1,0:T(8,128)(2,1)}, bf16[128,1024]{1,0:T(8,128)(2,1)S(1)}, u32[]{:S(2)}, u32[]{:S(2)}) collective-permute-start(bf16[128,1024]{1,0:T(8,128)(2,1)} %get-tuple-element.177.refs_0_), channel_id=1, source_target_pairs={{0,4},{1,5},{2,6},{3,7},{4,0},{5,1},{6,2},{7,3},{8,12},{9,13},{10,... | collective-permute-start | bytes 786440 | tf_op jit(solution)/shard_map/ppermute | solution.py:56
  106.5 20.5 %all-to-all-start.3 = ((bf16[32,32,256]{2,1,0:T(8,128)(2,1)}), bf16[32,32,256]{2,1,0:T(8,128)(2,1)}, u32[]{:S(2)}, u32[]{:S(2)}) async-start(bf16[32,32,256]{2,1,0:T(8,128)(2,1)} %get-tuple-element.190), calls=%async_computation.3 | async-start | bytes 1048576 | tf_op jit(solution)/shard_map/all_to_all | solution.py:82
  117.3 9.8 %collective-permute-start.24 = (bf16[3,128,1024]{2,1,0:T(8,128)(2,1)S(1)}, bf16[3,128,1024]{2,1,0:T(8,128)(2,1)S(1)}, u32[]{:S(2)}, u32[]{:S(2)}) collective-permute-start(bf16[3,128,1024]{2,1,0:T(8,128)(2,1)S(1)} %pad_maximum_fusion.4), channel_id=1, source_target_pairs={{0,1},{1,0},{2,3},{3,2},{4,5},{5,4},{6,7},{7,6},{8,9},{9,8},{10,11... | collective-permute-start | bytes 2359304 | tf_op jit(solution)/shard_map/ppermute | solution.py:56
  136.8 9.5 %collective-permute-start.27 = (bf16[3,128,1024]{2,1,0:T(8,128)(2,1)}, bf16[3,128,1024]{2,1,0:T(8,128)(2,1)S(1)}, u32[]{:S(2)}, u32[]{:S(2)}) collective-permute-start(bf16[3,128,1024]{2,1,0:T(8,128)(2,1)} %get-tuple-element.194), channel_id=1, source_target_pairs={{0,1},{1,0},{2,3},{3,2},{4,5},{5,4},{6,7},{7,6},{8,9},{9,8},{10,11... | collective-permute-start | bytes 2359304 | tf_op jit(solution)/shard_map/ppermute | solution.py:56
  141.7 13.1 %collective-permute-start.33 = (bf16[128,1024]{1,0:T(8,128)(2,1)}, bf16[128,1024]{1,0:T(8,128)(2,1)S(1)}, u32[]{:S(2)}, u32[]{:S(2)}) collective-permute-start(bf16[128,1024]{1,0:T(8,128)(2,1)} %get-tuple-element.196), channel_id=1, source_target_pairs={{0,8},{1,9},{2,10},{3,11},{4,12},{5,13},{6,14},{7,15},{8,16},{9,17... | collective-permute-start | bytes 786440 | tf_op jit(solution)/shard_map/ppermute | solution.py:68
  152.1 20.5 %collective-permute-start.36 = (bf16[128,1024]{1,0:T(8,128)(2,1)S(1)}, bf16[128,1024]{1,0:T(8,128)(2,1)S(1)}, u32[]{:S(2)}, u32[]{:S(2)}) collective-permute-start(bf16[128,1024]{1,0:T(8,128)(2,1)S(1)} %copy-done.46), channel_id=1, source_target_pairs={{0,16},{1,17},{2,18},{3,19},{4,20},{5,21},{6,22},{7,23},{8,24},{9,... | collective-permute-start | bytes 786440 | tf_op jit(solution)/shard_map/ppermute | solution.py:68
  153.8 18.8 %collective-permute-start.37 = (bf16[128,1024]{1,0:T(8,128)(2,1)S(1)}, bf16[128,1024]{1,0:T(8,128)(2,1)S(1)}, u32[]{:S(2)}, u32[]{:S(2)}) collective-permute-start(bf16[128,1024]{1,0:T(8,128)(2,1)S(1)} %copy-done.45), channel_id=1, source_target_pairs={{0,24},{1,25},{2,26},{3,27},{4,28},{5,29},{6,30},{7,31},{8,0},{9,1... | collective-permute-start | bytes 786440 | tf_op jit(solution)/shard_map/ppermute | solution.py:68
  162.5 12.8 %collective-permute-start.34 = (bf16[128,1024]{1,0:T(8,128)(2,1)}, bf16[128,1024]{1,0:T(8,128)(2,1)S(1)}, u32[]{:S(2)}, u32[]{:S(2)}) collective-permute-start(bf16[128,1024]{1,0:T(8,128)(2,1)} %get-tuple-element.203), channel_id=1, source_target_pairs={{0,2},{1,3},{2,0},{3,1},{4,6},{5,7},{6,4},{7,5},{8,10},{9,11},{10,... | collective-permute-start | bytes 786440 | tf_op jit(solution)/shard_map/ppermute | solution.py:56
  164.2 11.1 %collective-permute-start.35 = (bf16[128,1024]{1,0:T(8,128)(2,1)}, bf16[128,1024]{1,0:T(8,128)(2,1)S(1)}, u32[]{:S(2)}, u32[]{:S(2)}) collective-permute-start(bf16[128,1024]{1,0:T(8,128)(2,1)} %get-tuple-element.203), channel_id=1, source_target_pairs={{0,4},{1,5},{2,6},{3,7},{4,0},{5,1},{6,2},{7,3},{8,12},{9,13},{10,... | collective-permute-start | bytes 786440 | tf_op jit(solution)/shard_map/ppermute | solution.py:56
  165.0 10.3 %all-to-all-start.4 = ((bf16[8,128,128]{2,1,0:T(8,128)(2,1)}), bf16[8,128,128]{2,1,0:T(8,128)(2,1)S(1)}, u32[]{:S(2)}, u32[]{:S(2)}) async-start(bf16[8,128,128]{2,1,0:T(8,128)(2,1)} %get-tuple-element.201), calls=%async_computation.4 | async-start | bytes 524288 | tf_op jit(solution)/shard_map/all_to_all | solution.py:82
  175.3 55.7 %all-to-all-start.5 = ((bf16[32,32,512]{2,1,0:T(8,128)(2,1)}), bf16[32,32,512]{2,1,0:T(8,128)(2,1)S(1)}, u32[]{:S(2)}, u32[]{:S(2)}) async-start(bf16[32,32,512]{2,1,0:T(8,128)(2,1)} %bitcast.90), calls=%async_computation.5 | async-start | bytes 2097152 | tf_op jit(solution)/shard_map/all_to_all | solution.py:82
  178.4 16.7 %collective-permute-start.38 = (bf16[64,1024]{1,0:T(8,128)(2,1)S(1)}, bf16[64,1024]{1,0:T(8,128)(2,1)S(1)}, u32[]{:S(2)}, u32[]{:S(2)}) collective-permute-start(bf16[64,1024]{1,0:T(8,128)(2,1)S(1)} %slice.182), channel_id=1, source_target_pairs={{0,4},{1,5},{2,6},{3,7},{4,0},{5,1},{6,2},{7,3},{8,12},{9,13},{10,... | collective-permute-start | bytes 393224 | tf_op jit(solution)/shard_map/ppermute | solution.py:56
  180.0 15.1 %collective-permute-start.39 = (bf16[64,1024]{1,0:T(8,128)(2,1)S(1)}, bf16[64,1024]{1,0:T(8,128)(2,1)S(1)}, u32[]{:S(2)}, u32[]{:S(2)}) collective-permute-start(bf16[64,1024]{1,0:T(8,128)(2,1)S(1)} %slice.183), channel_id=1, source_target_pairs={{0,2},{1,3},{2,0},{3,1},{4,6},{5,7},{6,4},{7,5},{8,10},{9,11},{10,... | collective-permute-start | bytes 393224 | tf_op jit(solution)/shard_map/ppermute | solution.py:56
  195.2 19.1 %collective-permute-start.40 = (bf16[1024,256]{1,0:T(8,128)(2,1)}, bf16[1024,256]{1,0:T(8,128)(2,1)S(1)}, u32[]{:S(2)}, u32[]{:S(2)}) collective-permute-start(bf16[1024,256]{1,0:T(8,128)(2,1)} %get-tuple-element.219), channel_id=1, source_target_pairs={{8,0},{9,1},{10,2},{11,3},{12,4},{13,5},{14,6},{15,7},{16,8},{17,9... | collective-permute-start | bytes 1572872 | tf_op jit(solution)/shard_map/ppermute | solution.py:61
  196.5 21.0 %collective-permute-start.41 = (bf16[1024,256]{1,0:T(8,128)(2,1)}, bf16[1024,256]{1,0:T(8,128)(2,1)S(1)}, u32[]{:S(2)}, u32[]{:S(2)}) collective-permute-start(bf16[1024,256]{1,0:T(8,128)(2,1)} %get-tuple-element.220), channel_id=1, source_target_pairs={{0,8},{1,9},{2,10},{3,11},{4,12},{5,13},{6,14},{7,15},{8,16},{9,17... | collective-permute-start | bytes 1572872 | tf_op jit(solution)/shard_map/ppermute | solution.py:61
  205.0 12.6 %collective-permute-start.43 = (bf16[32,1024]{1,0:T(8,128)(2,1)}, bf16[32,1024]{1,0:T(8,128)(2,1)S(1)}, u32[]{:S(2)}, u32[]{:S(2)}) collective-permute-start(bf16[32,1024]{1,0:T(8,128)(2,1)} %get-tuple-element.223), channel_id=1, source_target_pairs={{0,0},{1,4},{2,8},{3,12},{4,16},{5,20},{6,24},{7,28},{8,1},{9,5},{... | collective-permute-start | bytes 196616 | tf_op jit(solution)/shard_map/ppermute | solution.py:918
  206.5 12.4 %collective-permute-start.44 = (bf16[32,1024]{1,0:T(8,128)(2,1)}, bf16[32,1024]{1,0:T(8,128)(2,1)S(1)}, u32[]{:S(2)}, u32[]{:S(2)}) collective-permute-start(bf16[32,1024]{1,0:T(8,128)(2,1)} %get-tuple-element.224), channel_id=1, source_target_pairs={{0,1},{1,5},{2,9},{3,13},{4,17},{5,21},{6,25},{7,29},{8,2},{9,6},{... | collective-permute-start | bytes 196616 | tf_op jit(solution)/shard_map/ppermute | solution.py:918
  209.5 19.5 %collective-permute-start.45 = (bf16[32,1024]{1,0:T(8,128)(2,1)}, bf16[32,1024]{1,0:T(8,128)(2,1)S(1)}, u32[]{:S(2)}, u32[]{:S(2)}) collective-permute-start(bf16[32,1024]{1,0:T(8,128)(2,1)} %get-tuple-element.241), channel_id=1, source_target_pairs={{0,2},{1,6},{2,10},{3,14},{4,18},{5,22},{6,26},{7,30},{8,3},{9,7},... | collective-permute-start | bytes 196616 | tf_op jit(solution)/shard_map/ppermute | solution.py:918
  214.4 16.6 %collective-permute-start.46 = (bf16[32,1024]{1,0:T(8,128)(2,1)}, bf16[32,1024]{1,0:T(8,128)(2,1)S(1)}, u32[]{:S(2)}, u32[]{:S(2)}) collective-permute-start(bf16[32,1024]{1,0:T(8,128)(2,1)} %get-tuple-element.242), channel_id=1, source_target_pairs={{0,3},{1,7},{2,11},{3,15},{4,19},{5,23},{6,27},{7,31},{8,0},{9,4},... | collective-permute-start | bytes 196616 | tf_op jit(solution)/shard_map/ppermute | solution.py:918
  231.0 18.9 %collective-permute-start.47 = (bf16[3,256,1024]{2,1,0:T(8,128)(2,1)}, bf16[3,256,1024]{2,1,0:T(8,128)(2,1)}, u32[]{:S(2)}, u32[]{:S(2)}) collective-permute-start(bf16[3,256,1024]{2,1,0:T(8,128)(2,1)} %get-tuple-element.252), channel_id=1, source_target_pairs={{0,1},{1,0},{2,3},{3,2},{4,5},{5,4},{6,7},{7,6},{8,9},{9,8},{10,11... | collective-permute-start | bytes 4718600 | tf_op jit(solution)/shard_map/ppermute | solution.py:56
  231.1 14.1 %collective-permute-start.48 = (bf16[256,1024]{1,0:T(8,128)(2,1)}, bf16[256,1024]{1,0:T(8,128)(2,1)S(1)}, u32[]{:S(2)}, u32[]{:S(2)}) collective-permute-start(bf16[256,1024]{1,0:T(8,128)(2,1)} %get-tuple-element.253), channel_id=1, source_target_pairs={{0,1},{1,0},{2,3},{3,2},{4,5},{5,4},{6,7},{7,6},{8,9},{9,8},{10,11... | collective-permute-start | bytes 1572872 | tf_op jit(solution)/shard_map/ppermute | solution.py:56
  231.6 40.1 %all-to-all-start.6 = ((bf16[32,40,384]{2,1,0:T(8,128)(2,1)}), bf16[32,40,384]{2,1,0:T(8,128)(2,1)S(1)}, u32[]{:S(2)}, u32[]{:S(2)}) async-start(bf16[32,40,384]{2,1,0:T(8,128)(2,1)} %get-tuple-element.249), calls=%async_computation.6 | async-start | bytes 1966080 | tf_op jit(solution)/shard_map/all_to_all | solution.py:82
  246.6 16.2 %collective-permute-start.51 = (bf16[128,1024]{1,0:T(8,128)(2,1)S(1)}, bf16[128,1024]{1,0:T(8,128)(2,1)S(1)}, u32[]{:S(2)}, u32[]{:S(2)}) collective-permute-start(bf16[128,1024]{1,0:T(8,128)(2,1)S(1)} %get-tuple-element.292), channel_id=1, source_target_pairs={{0,2},{1,3},{2,0},{3,1},{4,6},{5,7},{6,4},{7,5},{8,10},{9,11},{10,... | collective-permute-start | bytes 786440 | tf_op jit(solution)/shard_map/ppermute | solution.py:56
  248.4 15.8 %collective-permute-start.49 = (bf16[128,1024]{1,0:T(8,128)(2,1)S(1)}, bf16[128,1024]{1,0:T(8,128)(2,1)S(1)}, u32[]{:S(2)}, u32[]{:S(2)}) collective-permute-start(bf16[128,1024]{1,0:T(8,128)(2,1)S(1)} %get-tuple-element.293), channel_id=1, source_target_pairs={{0,4},{1,5},{2,6},{3,7},{4,0},{5,1},{6,2},{7,3},{8,12},{9,13},{10,... | collective-permute-start | bytes 786440 | tf_op jit(solution)/shard_map/ppermute | solution.py:56
  263.0 17.8 %collective-permute-start.52 = (bf16[256,1024]{1,0:T(8,128)(2,1)S(1)}, bf16[256,1024]{1,0:T(8,128)(2,1)S(1)}, u32[]{:S(2)}, u32[]{:S(2)}) collective-permute-start(bf16[256,1024]{1,0:T(8,128)(2,1)S(1)} %pad_maximum_fusion.8), channel_id=1, source_target_pairs={{0,4},{1,5},{2,6},{3,7},{4,0},{5,1},{6,2},{7,3},{8,12},{9,13},{10,... | collective-permute-start | bytes 1572872 | tf_op jit(solution)/shard_map/ppermute | solution.py:56
  264.3 16.4 %collective-permute-start.50 = (bf16[256,1024]{1,0:T(8,128)(2,1)S(1)}, bf16[256,1024]{1,0:T(8,128)(2,1)S(1)}, u32[]{:S(2)}, u32[]{:S(2)}) collective-permute-start(bf16[256,1024]{1,0:T(8,128)(2,1)S(1)} %pad_maximum_fusion.7), channel_id=1, source_target_pairs={{0,2},{1,3},{2,0},{3,1},{4,6},{5,7},{6,4},{7,5},{8,10},{9,11},{10,... | collective-permute-start | bytes 1572872 | tf_op jit(solution)/shard_map/ppermute | solution.py:56
  274.8 11.7 %all-to-all-start.7 = ((f32[32,1,128]{2,1,0:T(1,128)}), f32[32,1,128]{2,1,0:T(1,128)S(1)}, u32[]{:S(2)}, u32[]{:S(2)}) async-start(f32[32,1,128]{2,1,0:T(1,128)} %get-tuple-element.250), calls=%async_computation.7 | async-start | bytes 32768 | tf_op jit(solution)/shard_map/all_to_all | solution.py:82
  (61 other events, 442.4 us)

commit v5 on v4

--- a/solution.py
+++ b/solution.py
@@ -192,8 +192,12 @@
     number, columns = token_refs[0].shape
     devices = sent_ref.shape[0]
     rows = columns // devices
-    for d in range(devices):
-        weight_ref[pl.ds(d * rows, rows), :] = sent_ref[d, :rows, :]
+    if len(sent_ref.shape) == 2:
+        weight_ref[...] = sent_ref[...]
+    wide = query_ref.shape[1]
+    for d in range(devices if len(sent_ref.shape) == 3 else 0):
+        for c in range(3):
+            weight_ref[pl.ds(d * rows, rows), c * wide : (c + 1) * wide] = sent_ref[d, c * rows : (c + 1) * rows, :]
     for g in range(lots_ref.shape[0]):
         lanes = slice(g * LANES, (g + 1) * LANES)
         vector_ref[:EXTRA, lanes] = lots_ref[g, :, :LANES]
@@ -208,7 +212,6 @@
         held[here, :] = first
         first_ref[block_rows(spot ^ relative(r), number), :] = first
     joined = dot(held[...], weight_ref[...]).astype(LOW)
-    wide = query_ref.shape[1]
     for r in range(PLANE):
         here = slice(r * number, (r + 1) * number)
         query_ref[block_rows(spot ^ relative(r), number), :] = joined[here, :wide]
@@ -584,19 +587,28 @@
         grad_ref[...] = grad
         return
     devices, tall, _ = grad_ref.shape
-    rows = tall - EXTRA
+    rows = (tall - EXTRA) // 3
     vectors[...] = jnp.zeros_like(vectors)
     vectors[0:2, :] = sums_ref[...]
     vectors[2:5, :] = two_sums_ref[...]
     for g in range(up_sums_ref.shape[1] // LANES):
         lanes = pl.ds(pl.multiple_of(spot * LANES, LANES), LANES)
         vectors[5 + g : 6 + g, lanes] = up_sums_ref[:, g * LANES : (g + 1) * LANES]
-    grad_ref[:, rows:, :] = jnp.zeros((devices, EXTRA, grad_ref.shape[2]), LOW)
-    for d in range(devices):
-        lot = slice(d * rows // LANES * LANES, (d * rows // LANES + 1) * LANES)
-        grad_ref[d, :rows, :] = grad[d * rows : (d + 1) * rows]
-        grad_ref[d, rows:, :LANES] = vectors[:EXTRA, lot].astype(LOW)
-        grad_ref[d, rows:, LANES : 2 * LANES] = vectors[EXTRA:, lot].astype(LOW)
+    in_lot = LANES // rows
+    part = lax.broadcasted_iota(jnp.int32, (EXTRA, LANES), 1) // rows
+    top = lax.broadcasted_iota(jnp.int32, (EXTRA, LANES), 0) == 0
+    for lot in range(devices // in_lot):
+        values = vectors[:EXTRA, lot * LANES : (lot + 1) * LANES]
+        last = vectors[EXTRA : EXTRA + 1, lot * LANES : (lot + 1) * LANES]
+        last = jnp.concatenate([last[:, LANES - rows :], last[:, : LANES - rows]], axis=1)
+        for i in range(in_lot):
+            d = lot * in_lot + i
+            sums = jnp.where(part == i, values, jnp.where((part == (i + 1) % in_lot) & top, last, 0.0))
+            grad_ref[d, 3 * rows :, :] = sums.astype(LOW)
+            for c in range(3):
+                grad_ref[d, c * rows : (c + 1) * rows, :] = grad[
+                    d * rows : (d + 1) * rows, c * wide : (c + 1) * wide
+                ]
 
 
 def last_kernel(one_ref, two_ref, three_ref, tokens_ref, second_grad_ref, second_ref, vector_ref, out_ref, block_ref):
@@ -611,14 +623,16 @@
 def sum_kernel(wide, with_vectors, whole_count, parts_count, square_ref, *refs):
     others, parts, refs = refs[:whole_count], refs[whole_count : whole_count + parts_count], refs[whole_count + parts_count :]
     part_ref, grad_ref, total_ref = refs[:3]
+    stacked = with_vectors
     devices = part_ref.shape[0]
     rows = grad_ref.shape[0]
     square = jnp.zeros((rows, wide), F32)
     start = 0
-    for c in range(part_ref.shape[2] // wide):
+    for c in range(part_ref.shape[2] // wide if not stacked else part_ref.shape[1] // rows):
+        here = (slice(c * rows, (c + 1) * rows), slice(None)) if stacked else (slice(rows), slice(c * wide, (c + 1) * wide))
         for j in range(PLANE):
             sources = range(j, devices, PLANE)
-            whole = sum(part_ref[d, :rows, c * wide : (c + 1) * wide].astype(F32) for d in sources)
+            whole = sum(part_ref[(d, *here)].astype(F32) for d in sources)
             grad_ref[:, start : start + wide] = whole
             square += whole * whole
             start += wide
@@ -630,9 +644,10 @@
         refs[-1][...] = whole
         found += jnp.sum(whole * whole, keepdims=True)
     if with_vectors:
-        vectors = sum(part_ref[d, rows:, : 2 * LANES].astype(F32) for d in range(devices))
-        refs[3][:EXTRA, :] = vectors[:, :LANES]
-        refs[3][EXTRA:, :] = vectors[:, LANES:]
+        vectors = sum(part_ref[d, 3 * rows :, :].astype(F32) for d in range(devices))
+        refs[3][...] = jnp.zeros_like(refs[3])
+        refs[3][:EXTRA, :] = vectors
+        refs[3][EXTRA : EXTRA + 1, :] = jnp.concatenate([vectors[:1, rows:], vectors[:1, :rows]], axis=1)
         lanes = lax.broadcasted_iota(jnp.int32, (2 * EXTRA, LANES), 1)
         mine = lanes // rows == square_ref[1].astype(jnp.int32)
         found += jnp.sum(jnp.where(mine, refs[3][...] * refs[3][...], 0.0), keepdims=True)
@@ -640,8 +655,9 @@
 
 
 def sum_parts(wide, rows, part, square, lot=None, others=(), parts=()):
+    vectors = lot is not None
     n, _, columns = part.shape
-    vectors = lot is not None
+    columns = 3 * columns if vectors else columns
     if wide % LANES == 0 and rows % 16 == 0:
         outs = [like((rows, PLANE * columns), F32), like((n, 1, LANES) if vectors else (1, 1), F32)]
         found = kernel_call(
@@ -653,14 +669,17 @@
             scalars=(jnp.stack([square, lot.astype(F32) if vectors else square]),),
         )
         return found
-    whole = part[:, :rows].astype(F32).reshape(-1, PLANE, rows, columns // wide, wide).sum(0)
+    whole = part.astype(F32)
+    if vectors:
+        whole = whole[:, : 3 * rows].reshape(n, 3, rows, wide).transpose(0, 2, 1, 3)
+    whole = whole.reshape(-1, PLANE, rows, columns // wide, wide).sum(0)
     whole = whole.transpose(1, 2, 0, 3).reshape(rows, -1)
     square = square + jnp.sum(whole * whole) + sum(jnp.sum(g * g) for g in others)
     if not vectors:
         joined = sum(p.astype(F32) for p in parts)
         return whole, (square + jnp.sum(joined * joined)).reshape(1, 1), joined
-    found = part[:, rows:, : 2 * LANES].astype(F32).sum(0)
-    found = jnp.concatenate([found[:, :LANES], found[:, LANES:]], axis=0)
+    found = part[:, 3 * rows :].astype(F32).sum(0)
+    found = jnp.concatenate([found, jnp.roll(found[:1], -rows, axis=1)], axis=0)
     mine = lax.dynamic_slice_in_dim(found, rows * lot, rows, axis=1)
     square = square + jnp.sum(mine * mine)
     return whole, jnp.full((n, 1, LANES), square), found
@@ -685,17 +704,21 @@
 
 
 def with_vectors(attend_grad, one_sums, two_sums, up_sums, spot, n, rows, hidden):
-    columns, wide = attend_grad.shape
+    columns = attend_grad.shape[0]
     planes, lots, in_lot = n // PLANE, columns // LANES, LANES // rows
     up_sums = lax.dynamic_update_slice_in_dim(
         jnp.zeros((planes, PLANE, hidden), F32), up_sums.reshape(planes, 1, hidden), spot, axis=1
     )
-    part = jnp.concatenate([one_sums, two_sums, up_sums.reshape(-1, columns)], axis=0).astype(LOW)
-    part = jnp.moveaxis(part.reshape(-1, lots, LANES), 1, 0)
-    part = jnp.pad(part, ((0, 0), (0, 2 * EXTRA - part.shape[1]), (0, 0)))
-    part = jnp.concatenate([part[:, :EXTRA], part[:, EXTRA:]], axis=2)
-    part = jnp.pad(part, ((0, 0), (0, 0), (0, wide - 2 * LANES)))
-    return jnp.concatenate([attend_grad.reshape(n, rows, wide), jnp.repeat(part, in_lot, axis=0)], axis=1)
+    sums = jnp.concatenate([one_sums, two_sums, up_sums.reshape(-1, columns)], axis=0)
+    sums = jnp.moveaxis(sums.reshape(-1, lots, LANES), 1, 0)
+    last = jnp.roll(sums[:, EXTRA:], rows, axis=2)
+    each, part = jnp.arange(in_lot)[:, None, None], jnp.arange(LANES) // rows
+    top = jnp.arange(EXTRA)[:, None] == 0
+    sums = jnp.where(
+        part == each, sums[:, None, :EXTRA], jnp.where((part == (each + 1) % in_lot) & top, last[:, None], 0.0)
+    )
+    grad = attend_grad.reshape(n, rows, 3, -1).transpose(0, 2, 1, 3).reshape(n, 3 * rows, -1)
+    return jnp.concatenate([grad, sums.astype(LOW).reshape(n, EXTRA, LANES)], axis=1)
 
 
 def on_device(
@@ -738,21 +761,27 @@
 
     vector_low = vector_params.astype(LOW)
     sides = spread_sides(tokens)
-    attend = attend_weight.astype(LOW).reshape(rows, 3, PLANE, wide).transpose(2, 0, 1, 3).reshape(PLANE, rows, 3 * wide)
-    vector_part = lax.dynamic_update_slice(
-        jnp.zeros((2 * EXTRA, LANES), LOW), vector_low, (0, rows * (device % in_lot))
-    )
-    vector_part = jnp.concatenate([vector_part[:EXTRA], vector_part[EXTRA:]], axis=1)
-    vector_part = jnp.pad(vector_part, ((0, 0), (0, 3 * wide - 2 * LANES)))
+    attend = attend_weight.astype(LOW).reshape(rows, 3, PLANE, wide).transpose(2, 1, 0, 3).reshape(PLANE, 3 * rows, wide)
+    part, following = device % in_lot, (device + 1) % in_lot
+    vector_part = lax.dynamic_update_slice(jnp.zeros((EXTRA, LANES), LOW), vector_low[:EXTRA], (0, rows * part))
+    vector_part = lax.dynamic_update_slice(vector_part, vector_low[EXTRA:], (0, rows * following))
     attend = jnp.concatenate(
         [
-            jnp.broadcast_to(attend[None], (planes,) + attend.shape).reshape(n, rows, 3 * wide),
+            jnp.broadcast_to(attend[None], (planes,) + attend.shape).reshape(n, 3 * rows, wide),
             jnp.broadcast_to(vector_part[None], (n,) + vector_part.shape),
         ],
         axis=1,
     )
     attend = exchange(after(attend, *sides))
-    lot_vectors = attend[:, rows:].reshape(lots, in_lot, EXTRA, 3 * wide).astype(F32).sum(1)
+    pieces = attend[:, 3 * rows :].reshape(lots, in_lot, EXTRA, LANES).astype(F32)
+    lane_part = jnp.arange(LANES) // rows
+    each = jnp.arange(in_lot)[:, None, None]
+    main = jnp.sum(jnp.where(lane_part == each, pieces, 0.0), axis=1)
+    last = jnp.sum(jnp.where(lane_part == (each + 1) % in_lot, pieces[:, :, :1], 0.0), axis=1)
+    last = jnp.concatenate([last[:, :, rows:], last[:, :, :rows]], axis=2)
+    lot_vectors = jnp.concatenate([main, jnp.broadcast_to(last, main.shape)], axis=2)
+    if rows % 16:
+        attend = attend[:, : 3 * rows].reshape(n, 3, rows, wide).transpose(0, 2, 1, 3).reshape(columns, 3 * wide)
     corner = spread_corner(*sides)
     output = after(output_weight.astype(LOW), *sides)
     for bit in output_steps(planes)[:-3]:
@@ -928,7 +957,7 @@
     attend_grad, first_near, first_far, first_corner, one_sums = kernel_call(
         functools.partial(first_back_kernel, planes),
         [
-            like((n, rows + EXTRA, 3 * wide) if fused else (columns, 3 * wide), LOW),
+            like((n, 3 * rows + EXTRA, wide) if fused else (columns, 3 * wide), LOW),
             like((4, 2 * number, columns), F32),
             like((3, 2 * number, columns), LOW),
             like((2 * number, columns), LOW),

time: 294 us -> 289 us (0.983)
  waiting for transfers between devices: 67 us -> 63.1 us
    all_to_all x8, starting transfers between devices: 41.4 us -> 34.6 us  [exchange(): return lax.all_to_all(blocks, 'seq', 0, 0, axis_index_groups=groups)]
    ppermute x39, starting transfers between devices: 39.3 us -> 45.8 us  [swap(): return lax.ppermute(block, 'seq', [(i, i ^ bit) for i in range(n)])]
    ppermute x39, waiting for transfers between devices: 49 us -> 45.4 us  [swap(): return lax.ppermute(block, 'seq', [(i, i ^ bit) for i in range(n)])]
    unnamed x102 -> x110, local copies, waits for them, and re-layouts: 6.75 us -> 7.17 us
  transfers between devices with their start and end apart: 61 -> 61, of which waited for: 24 -> 22; matrix products, arithmetic and copies ran while one was open for 8% -> 8% of each run, Pallas kernels for 21% -> 21%
where the time goes in v5:
time: 289 us; the launch traced here: 287 us
  starting transfers between devices  110 us (38%)
  Pallas kernels  81 us (28%)
  waiting for transfers between devices  63.1 us (22%)
  other arithmetic  18.1 us (6%)
  local copies, waits for them, and re-layouts  13.5 us (5%)
    pallas_call x12, Pallas kernels, kernel_call(): pl.pallas_call(body, in_specs=[SMEM] * len(scalars) + [WHOLE] * len(args)...  57.2 us
    ppermute x39, starting transfers between devices, swap(): return lax.ppermute(block, 'seq', [(i, i ^ bit) for i in range(n)])  45.8 us
    ppermute x39, waiting for transfers between devices, swap(): return lax.ppermute(block, 'seq', [(i, i ^ bit) for i in range(n)])  45.4 us
    all_to_all x8, starting transfers between devices, exchange(): return lax.all_to_all(blocks, 'seq', 0, 0, axis_index_groups=groups)  34.6 us
    pallas_call x1, Pallas kernels, attention_back(): pl.pallas_call(attend_back_kernel, grid_spec=pltpu.PrefetchScalarGridSpec...  13.5 us
    all_to_all x8, waiting for transfers between devices, exchange(): return lax.all_to_all(blocks, 'seq', 0, 0, axis_index_groups=groups)  10.7 us
    pallas_call x1, Pallas kernels, attention(): pl.pallas_call(attend_kernel, grid_spec=pltpu.PrefetchScalarGridSpec(num_...  10.2 us
    ppermute x6, starting transfers between devices, turn(): lax.ppermute(block, 'seq', [(i, (i + planes_on * PLANE) % n) for i in ran...  10.1 us
  transfers between devices with their start and end apart: 61, of which 22 were waited for; matrix products, arithmetic and copies ran while one was open for 8% of the time, Pallas kernels for 21%

profile of v5, /device:TPU:0, one launch (start us, length us, event | category | flops | bytes accessed | tf_op | source)
XLA Modules:
  0.0 287.3 jit_solution(17839830357114441687)
XLA Ops:
  0.7 3.0 %collective-permute-start = (bf16[128,1024]{1,0:T(8,128)(2,1)}, bf16[128,1024]{1,0:T(8,128)(2,1)S(1)}, u32[]{:S(2)}, u32[]{:S(2)}) collective-permute-start(bf16[128,1024]{1,0:T(8,128)(2,1)} %tokens_ref.3), channel_id=1, source_target_pairs={{0,2},{1,3},{2,0},{3,1},{4,6},{5,7},{6,4},{7,5},{8,10},{9,11},{10,... | collective-permute-start | bytes 786440 | tf_op jit(solution)/shard_map/ppermute | solution.py:56
  11.6 4.9 %all-to-all-start = ((bf16[32,104,128]{2,1,0:T(8,128)(2,1)}), bf16[32,104,128]{2,1,0:T(8,128)(2,1)S(1)}, u32[]{:S(2)}, u32[]{:S(2)}) async-start(bf16[32,104,128]{2,1,0:T(8,128)(2,1)} %pad_maximum_fusion.2), calls=%async_computation | async-start | bytes 1703936 | tf_op jit(solution)/shard_map/all_to_all | solution.py:82
  23.5 9.0 %collective-permute-done.7 = bf16[32,1024]{1,0:T(8,128)(2,1)S(1)} collective-permute-done((bf16[32,1024]{1,0:T(8,128)(2,1)S(1)}, bf16[32,1024]{1,0:T(8,128)(2,1)S(1)}, u32[]{:S(2)}, u32[]{:S(2)}) %collective-permute-start.7) | collective-permute-done | bytes 65568 | tf_op jit(solution)/shard_map/ppermute | solution.py:56
  32.5 4.6 %collective-permute-start.8 = (bf16[64,1024]{1,0:T(8,128)(2,1)S(1)}, bf16[64,1024]{1,0:T(8,128)(2,1)}, u32[]{:S(2)}, u32[]{:S(2)}) collective-permute-start(bf16[64,1024]{1,0:T(8,128)(2,1)S(1)} %pad_maximum_fusion.12), channel_id=1, source_target_pairs={{0,16},{1,17},{2,18},{3,19},{4,20},{5,21},{6,22},{7,23},{8,24},{9,... | collective-permute-start | bytes 393224 | tf_op jit(solution)/shard_map/ppermute | solution.py:56
  38.6 5.7 %collective-permute-done.8 = bf16[64,1024]{1,0:T(8,128)(2,1)} collective-permute-done((bf16[64,1024]{1,0:T(8,128)(2,1)S(1)}, bf16[64,1024]{1,0:T(8,128)(2,1)}, u32[]{:S(2)}, u32[]{:S(2)}) %collective-permute-start.8) | collective-permute-done | bytes 131104 | tf_op jit(solution)/shard_map/ppermute | solution.py:56
  46.3 6.5 %shard_map.313 = (bf16[1024,1024]{1,0:T(8,128)(2,1)}, bf16[1024,1024]{1,0:T(8,128)(2,1)}, bf16[1024,128]{1,0:T(8,128)(2,1)}, bf16[1024,256]{1,0:T(8,128)(2,1)}, ...) custom-call(s32[2]{0:T(128)} %pad_add_fusion.1.spot_ref.place_ref, bf16[128,1024]{1,0:T(8,128)(2,1)} %tokens_ref.3, ...), custom_call_target="tpu_custom_call" | custom-call | flops 805306368 | bytes 8847360 | tf_op jit(solution)/shard_map/pallas_call | solution.py:35
  58.9 5.8 %all-to-all-start.1 = ((bf16[32,32,256]{2,1,0:T(8,128)(2,1)}), bf16[32,32,256]{2,1,0:T(8,128)(2,1)S(1)}, u32[]{:S(2)}, u32[]{:S(2)}) async-start(bf16[32,32,256]{2,1,0:T(8,128)(2,1)} %get-tuple-element.171), calls=%async_computation.1 | async-start | bytes 1048576 | tf_op jit(solution)/shard_map/all_to_all | solution.py:82
  64.8 1.8 collective-permute-start.14
  70.2 2.0 collective-permute-done.12.after_ref
  72.2 10.2 %shard_map.314 = (f32[1024,128]{1,0:T(8,128)}, bf16[1024,128]{1,0:T(8,128)(2,1)}, f32[2,1024]{1,0:T(2,128)}) custom-call(s32[2,2]{1,0:T(2,128)} %pad_add_fusion.range_ref, bf16[1024,128]{1,0:T(8,128)(2,1)} %get-tuple-element.166.query_ref, bf16[1024,256]{1,0:T(8,128)(2,1)} %copy-done.48, bf16[1024,256]{1,0:T(8,128)(2,1)} %get-tuple-element.163.own_ref, ...), custom_call_target="tpu_custom_call" | custom-call | flops 5368709120 | bytes 2097152 | tf_op jit(solution)/shard_map/pallas_call | solution.py:376
  85.7 2.3 all-to-all-done.1
  88.5 3.4 %all-to-all-start.2 = ((bf16[8,128,128]{2,1,0:T(8,128)(2,1)}), bf16[8,128,128]{2,1,0:T(8,128)(2,1)S(1)}, u32[]{:S(2)}, u32[]{:S(2)}) async-start(bf16[8,128,128]{2,1,0:T(8,128)(2,1)} %bitcast.21), calls=%async_computation.2 | async-start | bytes 524288 | tf_op jit(solution)/shard_map/all_to_all | solution.py:82
  92.1 3.2 %collective-permute-start.20 = (bf16[128,1024]{1,0:T(8,128)(2,1)S(1)}, bf16[128,1024]{1,0:T(8,128)(2,1)}, u32[]{:S(2)}, u32[]{:S(2)}) collective-permute-start(bf16[128,1024]{1,0:T(8,128)(2,1)S(1)} %convert_element_type.89.refs_10_.refs_0_), channel_id=1, source_target_pairs={{0,24},{1,25},{2,26},{3,27},{4,28},{5,29},{6,30},{7,31},{8,0},{9,1... | collective-permute-start | bytes 786440 | tf_op jit(solution)/shard_map/ppermute | solution.py:68
  95.2 3.5 %all-to-all-done.2.mixed_ref = bf16[8,128,128]{2,1,0:T(8,128)(2,1)S(1)} async-done(((bf16[8,128,128]{2,1,0:T(8,128)(2,1)}), bf16[8,128,128]{2,1,0:T(8,128)(2,1)S(1)}, u32[]{:S(2)}, u32[]{:S(2)}) %all-to-all-start.2) | async-done | bytes 262176 | tf_op jit(solution)/shard_map/all_to_all | solution.py:82
  99.8 3.3 %shard_map.315 = (f32[128,1024]{1,0:T(8,128)}, bf16[128,1024]{1,0:T(8,128)(2,1)}) custom-call(s32[2]{0:T(128)} %pad_add_fusion.1.spot_ref.place_ref, bf16[8,128,128]{2,1,0:T(8,128)(2,1)} %copy-done.16, bf16[128,1024]{1,0:T(8,128)(2,1)} %tokens_ref.3, f32[16,1024]{1,0:T(8,128)} %get-tuple-element.175.vector_ref, bf16[512,1024]{1,0:T(8,128)(2,1)} %copy-done, ...), custom_call_target="tpu_custom_call" | custom-call | flops 268435456 | bytes 3473408 | tf_op jit(solution)/shard_map/pallas_call | solution.py:35
  104.2 3.6 %all-to-all-start.3 = ((bf16[32,32,256]{2,1,0:T(8,128)(2,1)}), bf16[32,32,256]{2,1,0:T(8,128)(2,1)}, u32[]{:S(2)}, u32[]{:S(2)}) async-start(bf16[32,32,256]{2,1,0:T(8,128)(2,1)} %get-tuple-element.190), calls=%async_computation.3 | async-start | bytes 1048576 | tf_op jit(solution)/shard_map/all_to_all | solution.py:82
  107.8 3.3 %collective-permute-done.17.refs_1_ = bf16[128,1024]{1,0:T(8,128)(2,1)S(1)} collective-permute-done((bf16[128,1024]{1,0:T(8,128)(2,1)}, bf16[128,1024]{1,0:T(8,128)(2,1)S(1)}, u32[]{:S(2)}, u32[]{:S(2)}) %collective-permute-start.17) | collective-permute-done | bytes 262176 | tf_op jit(solution)/shard_map/ppermute | solution.py:56
  111.1 2.6 collective-permute-done.18.refs_2_
  116.0 6.0 %collective-permute-done.22.refs_3_ = bf16[64,1024]{1,0:T(8,128)(2,1)S(1)} collective-permute-done((bf16[64,1024]{1,0:T(8,128)(2,1)S(1)}, bf16[64,1024]{1,0:T(8,128)(2,1)S(1)}, u32[]{:S(2)}, u32[]{:S(2)}) %collective-permute-start.22) | collective-permute-done | bytes 131104 | tf_op jit(solution)/shard_map/ppermute | solution.py:56
  125.7 8.8 %shard_map.316 = (f32[4,128,1024]{2,1,0:T(8,128)}, bf16[3,128,1024]{2,1,0:T(8,128)(2,1)}, bf16[128,1024]{1,0:T(8,128)(2,1)}, bf16[1024,512]{1,0:T(8,128)(2,1)}, ...) custom-call(s32[2]{0:T(128)} %pad_add_fusion.1.spot_ref.place_ref, bf16[128,1024]{1,0:T(8,128)(2,1)} %get-tuple-element.177.refs_0_, ...), custom_call_target="tpu_custom_call" | custom-call | flops 3221225472 | bytes 11538432 | tf_op jit(solution)/shard_map/pallas_call | solution.py:35
  135.0 4.3 %shard_map.317 = (bf16[128,1024]{1,0:T(8,128)(2,1)}, bf16[128,1024]{1,0:T(8,128)(2,1)}, bf16[128,1024]{1,0:T(8,128)(2,1)}, bf16[128,1024]{1,0:T(8,128)(2,1)}) custom-call(s32[2]{0:T(128)} %pad_add_fusion.1.spot_ref.place_ref, bf16[1024,512]{1,0:T(8,128)(2,1)} %get-tuple-element.191.active_ref, bf16[512,1024]{1,0:T(8,128)(2,1)} %pad_maximum_fusion.1.refs_8_.refs_0_, ...), custom_call_target="tpu_custom_call" | custom-call | flops 1073741824 | bytes 4194304 | tf_op jit(solution)/shard_map/pallas_call | solution.py:35
  139.3 2.3 collective-permute-start.33
  144.9 2.5 collective-permute-done.31
  152.3 2.7 collective-permute-done.32.three_ref
  156.0 4.1 %shard_map.318 = (f32[128,1024]{1,0:T(8,128)}, bf16[128,1024]{1,0:T(8,128)(2,1)}, bf16[8,128,128]{2,1,0:T(8,128)(2,1)}, f32[3,1024]{1,0:T(4,128)}) custom-call(s32[2]{0:T(128)} %pad_add_fusion.1.spot_ref.place_ref, f32[128,1024]{1,0:T(8,128)} %get-tuple-element.197.one_ref, bf16[128,1024]{1,0:T(8,128)(2,1)} %copy-done.27, bf16[128,1024]{1,0:T(8,128)(2,1)} %copy-done.26, ...), custom_call_target="tpu_custom_call" | custom-call | flops 268435456 | bytes 5058560 | tf_op jit(solution)/shard_map/pallas_call | solution.py:35
  162.6 3.4 %all-to-all-start.4 = ((bf16[8,128,128]{2,1,0:T(8,128)(2,1)}), bf16[8,128,128]{2,1,0:T(8,128)(2,1)S(1)}, u32[]{:S(2)}, u32[]{:S(2)}) async-start(bf16[8,128,128]{2,1,0:T(8,128)(2,1)} %get-tuple-element.201), calls=%async_computation.4 | async-start | bytes 524288 | tf_op jit(solution)/shard_map/all_to_all | solution.py:82
  166.1 4.1 %shard_map.319 = bf16[1024,512]{1,0:T(8,128)(2,1)} custom-call(bf16[1024,512]{1,0:T(8,128)(2,1)} %get-tuple-element.204.grad_ref, bf16[128,1024]{1,0:T(8,128)(2,1)} %get-tuple-element.177.refs_0_, bf16[128,1024]{1,0:T(8,128)(2,1)} %copy-done.12, bf16[128,1024]{1,0:T(8,128)(2,1)} %copy-done.13, bf16[64,1024]{1,0:T(8,128)(2,1)} %copy-done.35, ...), custom_call_target="tpu_custom_call" | custom-call | flops 1073741824 | bytes 4194304 | tf_op jit(solution)/shard_map/pallas_call | solution.py:35
  170.3 2.7 all-to-all-done.4
  172.9 3.2 %all-to-all-start.5 = ((bf16[32,32,512]{2,1,0:T(8,128)(2,1)}), bf16[32,32,512]{2,1,0:T(8,128)(2,1)S(1)}, u32[]{:S(2)}, u32[]{:S(2)}) async-start(bf16[32,32,512]{2,1,0:T(8,128)(2,1)} %bitcast.95), calls=%async_computation.5 | async-start | bytes 2097152 | tf_op jit(solution)/shard_map/all_to_all | solution.py:82
  179.3 13.5 %shard_map.320 = (bf16[1024,128]{1,0:T(8,128)(2,1)}, bf16[1024,256]{1,0:T(8,128)(2,1)}, f32[1024,256]{1,0:T(8,128)}, bf16[1024,256]{1,0:T(8,128)(2,1)}) custom-call(s32[2,2]{1,0:T(2,128)} %pad_add_fusion.range_ref, bf16[1024,128]{1,0:T(8,128)(2,1)} %get-tuple-element.166.query_ref, bf16[1024,256]{1,0:T(8,128)(2,1)} %copy-done.48, ...), custom_call_target="tpu_custom_call" | custom-call | flops 8053063680 | bytes 4194304 | tf_op jit(solution)/shard_map/pallas_call | solution.py:399
  194.4 5.9 %collective-permute-start.41 = (bf16[1024,256]{1,0:T(8,128)(2,1)}, bf16[1024,256]{1,0:T(8,128)(2,1)S(1)}, u32[]{:S(2)}, u32[]{:S(2)}) collective-permute-start(bf16[1024,256]{1,0:T(8,128)(2,1)} %get-tuple-element.220), channel_id=1, source_target_pairs={{0,8},{1,9},{2,10},{3,11},{4,12},{5,13},{6,14},{7,15},{8,16},{9,17... | collective-permute-start | bytes 1572872 | tf_op jit(solution)/shard_map/ppermute | solution.py:61
  201.3 2.8 shard_map.321
  205.7 3.0 %collective-permute-start.44 = (bf16[32,1024]{1,0:T(8,128)(2,1)}, bf16[32,1024]{1,0:T(8,128)(2,1)S(1)}, u32[]{:S(2)}, u32[]{:S(2)}) collective-permute-start(bf16[32,1024]{1,0:T(8,128)(2,1)} %get-tuple-element.224), channel_id=1, source_target_pairs={{0,1},{1,5},{2,9},{3,13},{4,17},{5,21},{6,25},{7,29},{8,2},{9,6},{... | collective-permute-start | bytes 196616 | tf_op jit(solution)/shard_map/ppermute | solution.py:947
  208.7 2.8 collective-permute-start.45
  211.5 3.3 %collective-permute-done.40.from_after_ref = bf16[1024,256]{1,0:T(8,128)(2,1)S(1)} collective-permute-done((bf16[1024,256]{1,0:T(8,128)(2,1)}, bf16[1024,256]{1,0:T(8,128)(2,1)S(1)}, u32[]{:S(2)}, u32[]{:S(2)}) %collective-permute-start.40) | collective-permute-done | bytes 524320 | tf_op jit(solution)/shard_map/ppermute | solution.py:61
  214.8 1.9 collective-permute-start.46
  217.6 10.1 %shard_map.322 = (bf16[32,104,128]{2,1,0:T(8,128)(2,1)}, f32[4,256,1024]{2,1,0:T(8,128)}, bf16[3,256,1024]{2,1,0:T(8,128)(2,1)}, bf16[256,1024]{1,0:T(8,128)(2,1)}, f32[2,1024]{1,0:T(2,128)}) custom-call(s32[2]{0:T(128)} %pad_add_fusion.1.spot_ref.place_ref, f32[1024,256]{1,0:T(8,128)} %get-tuple-element.214.own_ref, bf16[1024,256]{1,0:T(8,128)(2,1)} %copy-done.23, ...), custom_call_target="tpu_custom_call" | custom-call | flops 1610612736 | bytes 16603136 | tf_op jit(solution)/shard_map/pallas_call | solution.py:35
  229.4 6.1 %collective-permute-start.47 = (bf16[3,256,1024]{2,1,0:T(8,128)(2,1)}, bf16[3,256,1024]{2,1,0:T(8,128)(2,1)S(1)}, u32[]{:S(2)}, u32[]{:S(2)}) collective-permute-start(bf16[3,256,1024]{2,1,0:T(8,128)(2,1)} %get-tuple-element.252), channel_id=1, source_target_pairs={{0,1},{1,0},{2,3},{3,2},{4,5},{5,4},{6,7},{7,6},{8,9},{9,8},{10,11... | collective-permute-start | bytes 4718600 | tf_op jit(solution)/shard_map/ppermute | solution.py:56
  235.6 5.8 %all-to-all-start.6 = ((bf16[32,104,128]{2,1,0:T(8,128)(2,1)}), bf16[32,104,128]{2,1,0:T(8,128)(2,1)S(1)}, u32[]{:S(2)}, u32[]{:S(2)}) async-start(bf16[32,104,128]{2,1,0:T(8,128)(2,1)} %get-tuple-element.249), calls=%async_computation.6 | async-start | bytes 1703936 | tf_op jit(solution)/shard_map/all_to_all | solution.py:82
  242.9 1.8 collective-permute-start.51
  246.2 3.4 %convert_add_fusion = (f32[1,256,1024]{2,1,0:T(8,128)S(1)}, f32[1,256,1024]{2,1,0:T(8,128)S(1)}, f32[256,1024]{1,0:T(8,128)}) fusion(f32[4,256,1024]{2,1,0:T(8,128)} %get-tuple-element.251, bf16[3,256,1024]{2,1,0:T(8,128)(2,1)S(1)} %collective-permute-done.47), kind=kLoop, calls=%fused_computation.4 | loop fusion | flops 1572864 | bytes 7864320 | tf_op jit(solution)/shard_map/add | solution.py:134
  249.7 8.1 %collective-permute-done.51 = bf16[128,1024]{1,0:T(8,128)(2,1)S(1)} collective-permute-done((bf16[128,1024]{1,0:T(8,128)(2,1)S(1)}, bf16[128,1024]{1,0:T(8,128)(2,1)S(1)}, u32[]{:S(2)}, u32[]{:S(2)}) %collective-permute-start.51) | collective-permute-done | bytes 262176 | tf_op jit(solution)/shard_map/ppermute | solution.py:56
  260.2 2.0 convert_add_fusion.2.refs_0_.refs_18_
  262.7 2.6 shard_map.323
  267.5 2.0 shard_map.324
  269.5 4.6 %all-to-all-start.7 = ((f32[32,1,128]{2,1,0:T(1,128)}), f32[32,1,128]{2,1,0:T(1,128)S(1)}, u32[]{:S(2)}, u32[]{:S(2)}) async-start(f32[32,1,128]{2,1,0:T(1,128)} %get-tuple-element.250), calls=%async_computation.7 | async-start | bytes 32768 | tf_op jit(solution)/shard_map/all_to_all | solution.py:82
  276.5 3.2 %shard_map.325 = (bf16[128,1024]{1,0:T(8,128)(2,1)}, bf16[128,1024]{1,0:T(8,128)(2,1)}) custom-call(f32[256,1024]{1,0:T(8,128)} %get-tuple-element.286.one_ref, bf16[256,1024]{1,0:T(8,128)(2,1)} %copy-done.22, bf16[256,1024]{1,0:T(8,128)(2,1)} %copy-done.21, bf16[128,1024]{1,0:T(8,128)(2,1)} %tokens_ref.3, f32[128,1024]{1,0:T(8,128)} %get-tuple-element.254.second_grad_ref, ...), custom_call_target="tpu_custom_call" | custom-call | bytes 3997696 | tf_op jit(solution)/shard_map/pallas_call | solution.py:35
  281.8 5.3 %shard_map.326 = (f32[32,3072]{1,0:T(8,128)}, f32[32,3072]{1,0:T(8,128)}, f32[32,3072]{1,0:T(8,128)}, f32[32,1024]{1,0:T(8,128)}, f32[32,1024]{1,0:T(8,128)}, /*...) custom-call(f32[32,1,128]{2,1,0:T(1,128)} %copy-done.43, ...), custom_call_target="tpu_custom_call" | custom-call | bytes 11034500 | tf_op jit(solution)/shard_map/pallas_call | solution.py:35
  (277 shorter events, 74.1 us)
Async XLA Ops:
  0.7 9.5 %collective-permute-start = (bf16[128,1024]{1,0:T(8,128)(2,1)}, bf16[128,1024]{1,0:T(8,128)(2,1)S(1)}, u32[]{:S(2)}, u32[]{:S(2)}) collective-permute-start(bf16[128,1024]{1,0:T(8,128)(2,1)} %tokens_ref.3), channel_id=1, source_target_pairs={{0,2},{1,3},{2,0},{3,1},{4,6},{5,7},{6,4},{7,5},{8,10},{9,11},{10,... | collective-permute-start | bytes 786440 | tf_op jit(solution)/shard_map/ppermute | solution.py:56
  11.6 33.7 %all-to-all-start = ((bf16[32,104,128]{2,1,0:T(8,128)(2,1)}), bf16[32,104,128]{2,1,0:T(8,128)(2,1)S(1)}, u32[]{:S(2)}, u32[]{:S(2)}) async-start(bf16[32,104,128]{2,1,0:T(8,128)(2,1)} %pad_maximum_fusion.2), calls=%async_computation | async-start | bytes 1703936 | tf_op jit(solution)/shard_map/all_to_all | solution.py:82
  18.4 26.9 %collective-permute-start.4 = (bf16[3,128,1024]{2,1,0:T(8,128)(2,1)S(1)}, bf16[3,128,1024]{2,1,0:T(8,128)(2,1)}, u32[]{:S(2)}, u32[]{:S(2)}) collective-permute-start(bf16[3,128,1024]{2,1,0:T(8,128)(2,1)S(1)} %pad_maximum_fusion.3), channel_id=1, source_target_pairs={{0,1},{1,0},{2,3},{3,2},{4,5},{5,4},{6,7},{7,6},{8,9},{9,8},{10,11... | collective-permute-start | bytes 2359304 | tf_op jit(solution)/shard_map/ppermute | solution.py:56
  18.7 13.7 %collective-permute-start.7 = (bf16[32,1024]{1,0:T(8,128)(2,1)S(1)}, bf16[32,1024]{1,0:T(8,128)(2,1)S(1)}, u32[]{:S(2)}, u32[]{:S(2)}) collective-permute-start(bf16[32,1024]{1,0:T(8,128)(2,1)S(1)} %convert_element_type.90), channel_id=1, source_target_pairs={{0,8},{1,9},{2,10},{3,11},{4,12},{5,13},{6,14},{7,15},{8,0},{9,1},... | collective-permute-start | bytes 196616 | tf_op jit(solution)/shard_map/ppermute | solution.py:56
  20.4 16.8 %collective-permute-start.2 = (bf16[64,1024]{1,0:T(8,128)(2,1)S(1)}, bf16[64,1024]{1,0:T(8,128)(2,1)S(1)}, u32[]{:S(2)}, u32[]{:S(2)}) collective-permute-start(bf16[64,1024]{1,0:T(8,128)(2,1)S(1)} %slice.214), channel_id=1, source_target_pairs={{0,4},{1,5},{2,6},{3,7},{4,0},{5,1},{6,2},{7,3},{8,12},{9,13},{10,... | collective-permute-start | bytes 393224 | tf_op jit(solution)/shard_map/ppermute | solution.py:56
  21.9 15.2 %collective-permute-start.3 = (bf16[64,1024]{1,0:T(8,128)(2,1)S(1)}, bf16[64,1024]{1,0:T(8,128)(2,1)S(1)}, u32[]{:S(2)}, u32[]{:S(2)}) collective-permute-start(bf16[64,1024]{1,0:T(8,128)(2,1)S(1)} %slice.215), channel_id=1, source_target_pairs={{0,2},{1,3},{2,0},{3,1},{4,6},{5,7},{6,4},{7,5},{8,10},{9,11},{10,... | collective-permute-start | bytes 393224 | tf_op jit(solution)/shard_map/ppermute | solution.py:56
  32.5 11.9 %collective-permute-start.8 = (bf16[64,1024]{1,0:T(8,128)(2,1)S(1)}, bf16[64,1024]{1,0:T(8,128)(2,1)}, u32[]{:S(2)}, u32[]{:S(2)}) collective-permute-start(bf16[64,1024]{1,0:T(8,128)(2,1)S(1)} %pad_maximum_fusion.12), channel_id=1, source_target_pairs={{0,16},{1,17},{2,18},{3,19},{4,20},{5,21},{6,22},{7,23},{8,24},{9,... | collective-permute-start | bytes 393224 | tf_op jit(solution)/shard_map/ppermute | solution.py:56
  37.2 8.0 %collective-permute-start.5 = (bf16[64,1024]{1,0:T(8,128)(2,1)S(1)}, bf16[64,1024]{1,0:T(8,128)(2,1)S(1)}, u32[]{:S(2)}, u32[]{:S(2)}) collective-permute-start(bf16[64,1024]{1,0:T(8,128)(2,1)S(1)} %collective-permute-done.2.refs_3_), channel_id=1, source_target_pairs={{0,1},{1,0},{2,3},{3,2},{4,5},{5,4},{6,7},{7,6},{8,9},{9,8},{10,11... | collective-permute-start | bytes 393224 | tf_op jit(solution)/shard_map/ppermute | solution.py:56
  37.3 8.0 %collective-permute-start.6 = (bf16[64,1024]{1,0:T(8,128)(2,1)S(1)}, bf16[64,1024]{1,0:T(8,128)(2,1)S(1)}, u32[]{:S(2)}, u32[]{:S(2)}) collective-permute-start(bf16[64,1024]{1,0:T(8,128)(2,1)S(1)} %collective-permute-done.3.refs_4_), channel_id=1, source_target_pairs={{0,1},{1,0},{2,3},{3,2},{4,5},{5,4},{6,7},{7,6},{8,9},{9,8},{10,11... | collective-permute-start | bytes 393224 | tf_op jit(solution)/shard_map/ppermute | solution.py:56
  52.7 17.5 %collective-permute-start.11 = (bf16[1024,256]{1,0:T(8,128)(2,1)}, bf16[1024,256]{1,0:T(8,128)(2,1)S(1)}, u32[]{:S(2)}, u32[]{:S(2)}) collective-permute-start(bf16[1024,256]{1,0:T(8,128)(2,1)} %get-tuple-element.163.own_ref), channel_id=1, source_target_pairs={{0,8},{1,9},{2,10},{3,11},{4,12},{5,13},{6,14},{7,15},{8,16},{9,17... | collective-permute-start | bytes 1572872 | tf_op jit(solution)/shard_map/ppermute | solution.py:61
  54.1 18.1 %collective-permute-start.12 = (bf16[1024,256]{1,0:T(8,128)(2,1)}, bf16[1024,256]{1,0:T(8,128)(2,1)}, u32[]{:S(2)}, u32[]{:S(2)}) collective-permute-start(bf16[1024,256]{1,0:T(8,128)(2,1)} %get-tuple-element.163.own_ref), channel_id=1, source_target_pairs={{8,0},{9,1},{10,2},{11,3},{12,4},{13,5},{14,6},{15,7},{16,8},{17,9... | collective-permute-start | bytes 1572872 | tf_op jit(solution)/shard_map/ppermute | solution.py:61
  55.4 9.4 %collective-permute-start.10 = (bf16[128,1024]{1,0:T(8,128)(2,1)S(1)}, bf16[128,1024]{1,0:T(8,128)(2,1)S(1)}, u32[]{:S(2)}, u32[]{:S(2)}) collective-permute-start(bf16[128,1024]{1,0:T(8,128)(2,1)S(1)} %copy-done.17), channel_id=1, source_target_pairs={{0,2},{1,3},{2,0},{3,1},{4,6},{5,7},{6,4},{7,5},{8,10},{9,11},{10,... | collective-permute-start | bytes 786440 | tf_op jit(solution)/shard_map/ppermute | solution.py:56
  58.9 29.0 %all-to-all-start.1 = ((bf16[32,32,256]{2,1,0:T(8,128)(2,1)}), bf16[32,32,256]{2,1,0:T(8,128)(2,1)S(1)}, u32[]{:S(2)}, u32[]{:S(2)}) async-start(bf16[32,32,256]{2,1,0:T(8,128)(2,1)} %get-tuple-element.171), calls=%async_computation.1 | async-start | bytes 1048576 | tf_op jit(solution)/shard_map/all_to_all | solution.py:82
  64.8 19.3 %collective-permute-start.14 = (bf16[256,1024]{1,0:T(8,128)(2,1)S(1)}, bf16[256,1024]{1,0:T(8,128)(2,1)S(1)}, u32[]{:S(2)}, u32[]{:S(2)}) collective-permute-start(bf16[256,1024]{1,0:T(8,128)(2,1)S(1)} %pad_maximum_fusion.6), channel_id=1, source_target_pairs={{0,4},{1,5},{2,6},{3,7},{4,0},{5,1},{6,2},{7,3},{8,12},{9,13},{10,... | collective-permute-start | bytes 1572872 | tf_op jit(solution)/shard_map/ppermute | solution.py:56
  67.3 18.4 %collective-permute-start.15 = (bf16[128,1024]{1,0:T(8,128)(2,1)S(1)}, bf16[128,1024]{1,0:T(8,128)(2,1)S(1)}, u32[]{:S(2)}, u32[]{:S(2)}) collective-permute-start(bf16[128,1024]{1,0:T(8,128)(2,1)S(1)} %convert_element_type.89.refs_10_.refs_0_), channel_id=1, source_target_pairs={{0,8},{1,9},{2,10},{3,11},{4,12},{5,13},{6,14},{7,15},{8,16},{9,17... | collective-permute-start | bytes 786440 | tf_op jit(solution)/shard_map/ppermute | solution.py:68
  69.0 16.5 %collective-permute-start.13 = (bf16[256,1024]{1,0:T(8,128)(2,1)S(1)}, bf16[256,1024]{1,0:T(8,128)(2,1)S(1)}, u32[]{:S(2)}, u32[]{:S(2)}) collective-permute-start(bf16[256,1024]{1,0:T(8,128)(2,1)S(1)} %pad_maximum_fusion.5), channel_id=1, source_target_pairs={{0,2},{1,3},{2,0},{3,1},{4,6},{5,7},{6,4},{7,5},{8,10},{9,11},{10,... | collective-permute-start | bytes 1572872 | tf_op jit(solution)/shard_map/ppermute | solution.py:56
  87.9 10.8 %collective-permute-start.16 = (bf16[512,1024]{1,0:T(8,128)(2,1)S(1)}, bf16[512,1024]{1,0:T(8,128)(2,1)S(1)}, u32[]{:S(2)}, u32[]{:S(2)}) collective-permute-start(bf16[512,1024]{1,0:T(8,128)(2,1)S(1)} %pad_maximum_fusion.refs_0_), channel_id=1, source_target_pairs={{0,1},{1,0},{2,3},{3,2},{4,5},{5,4},{6,7},{7,6},{8,9},{9,8},{10,11... | collective-permute-start | bytes 3145736 | tf_op jit(solution)/shard_map/ppermute | solution.py:56
  87.9 19.8 %collective-permute-start.21 = (bf16[512,1024]{1,0:T(8,128)(2,1)}, bf16[512,1024]{1,0:T(8,128)(2,1)}, u32[]{:S(2)}, u32[]{:S(2)}) collective-permute-start(bf16[512,1024]{1,0:T(8,128)(2,1)} %pad_maximum_fusion.1.refs_8_.refs_0_), channel_id=1, source_target_pairs={{0,1},{1,0},{2,3},{3,2},{4,5},{5,4},{6,7},{7,6},{8,9},{9,8},{10,11... | collective-permute-start | bytes 3145736 | tf_op jit(solution)/shard_map/ppermute | solution.py:56
  88.5 10.3 %all-to-all-start.2 = ((bf16[8,128,128]{2,1,0:T(8,128)(2,1)}), bf16[8,128,128]{2,1,0:T(8,128)(2,1)S(1)}, u32[]{:S(2)}, u32[]{:S(2)}) async-start(bf16[8,128,128]{2,1,0:T(8,128)(2,1)} %bitcast.21), calls=%async_computation.2 | async-start | bytes 524288 | tf_op jit(solution)/shard_map/all_to_all | solution.py:82
  91.9 15.9 %collective-permute-start.19 = (bf16[128,1024]{1,0:T(8,128)(2,1)S(1)}, bf16[128,1024]{1,0:T(8,128)(2,1)}, u32[]{:S(2)}, u32[]{:S(2)}) collective-permute-start(bf16[128,1024]{1,0:T(8,128)(2,1)S(1)} %convert_element_type.89.refs_10_.refs_0_), channel_id=1, source_target_pairs={{0,16},{1,17},{2,18},{3,19},{4,20},{5,21},{6,22},{7,23},{8,24},{9,... | collective-permute-start | bytes 786440 | tf_op jit(solution)/shard_map/ppermute | solution.py:68
  92.1 15.7 %collective-permute-start.20 = (bf16[128,1024]{1,0:T(8,128)(2,1)S(1)}, bf16[128,1024]{1,0:T(8,128)(2,1)}, u32[]{:S(2)}, u32[]{:S(2)}) collective-permute-start(bf16[128,1024]{1,0:T(8,128)(2,1)S(1)} %convert_element_type.89.refs_10_.refs_0_), channel_id=1, source_target_pairs={{0,24},{1,25},{2,26},{3,27},{4,28},{5,29},{6,30},{7,31},{8,0},{9,1... | collective-permute-start | bytes 786440 | tf_op jit(solution)/shard_map/ppermute | solution.py:68
  103.0 8.0 %collective-permute-start.17 = (bf16[128,1024]{1,0:T(8,128)(2,1)}, bf16[128,1024]{1,0:T(8,128)(2,1)S(1)}, u32[]{:S(2)}, u32[]{:S(2)}) collective-permute-start(bf16[128,1024]{1,0:T(8,128)(2,1)} %get-tuple-element.177.refs_0_), channel_id=1, source_target_pairs={{0,2},{1,3},{2,0},{3,1},{4,6},{5,7},{6,4},{7,5},{8,10},{9,11},{10,... | collective-permute-start | bytes 786440 | tf_op jit(solution)/shard_map/ppermute | solution.py:56
  103.6 10.1 %collective-permute-start.18 = (bf16[128,1024]{1,0:T(8,128)(2,1)}, bf16[128,1024]{1,0:T(8,128)(2,1)S(1)}, u32[]{:S(2)}, u32[]{:S(2)}) collective-permute-start(bf16[128,1024]{1,0:T(8,128)(2,1)} %get-tuple-element.177.refs_0_), channel_id=1, source_target_pairs={{0,4},{1,5},{2,6},{3,7},{4,0},{5,1},{6,2},{7,3},{8,12},{9,13},{10,... | collective-permute-start | bytes 786440 | tf_op jit(solution)/shard_map/ppermute | solution.py:56
  104.2 20.5 %all-to-all-start.3 = ((bf16[32,32,256]{2,1,0:T(8,128)(2,1)}), bf16[32,32,256]{2,1,0:T(8,128)(2,1)}, u32[]{:S(2)}, u32[]{:S(2)}) async-start(bf16[32,32,256]{2,1,0:T(8,128)(2,1)} %get-tuple-element.190), calls=%async_computation.3 | async-start | bytes 1048576 | tf_op jit(solution)/shard_map/all_to_all | solution.py:82
  114.8 9.8 %collective-permute-start.24 = (bf16[3,128,1024]{2,1,0:T(8,128)(2,1)S(1)}, bf16[3,128,1024]{2,1,0:T(8,128)(2,1)S(1)}, u32[]{:S(2)}, u32[]{:S(2)}) collective-permute-start(bf16[3,128,1024]{2,1,0:T(8,128)(2,1)S(1)} %pad_maximum_fusion.4), channel_id=1, source_target_pairs={{0,1},{1,0},{2,3},{3,2},{4,5},{5,4},{6,7},{7,6},{8,9},{9,8},{10,11... | collective-permute-start | bytes 2359304 | tf_op jit(solution)/shard_map/ppermute | solution.py:56
  134.4 9.4 %collective-permute-start.27 = (bf16[3,128,1024]{2,1,0:T(8,128)(2,1)}, bf16[3,128,1024]{2,1,0:T(8,128)(2,1)S(1)}, u32[]{:S(2)}, u32[]{:S(2)}) collective-permute-start(bf16[3,128,1024]{2,1,0:T(8,128)(2,1)} %get-tuple-element.194), channel_id=1, source_target_pairs={{0,1},{1,0},{2,3},{3,2},{4,5},{5,4},{6,7},{7,6},{8,9},{9,8},{10,11... | collective-permute-start | bytes 2359304 | tf_op jit(solution)/shard_map/ppermute | solution.py:56
  139.3 13.0 %collective-permute-start.33 = (bf16[128,1024]{1,0:T(8,128)(2,1)}, bf16[128,1024]{1,0:T(8,128)(2,1)S(1)}, u32[]{:S(2)}, u32[]{:S(2)}) collective-permute-start(bf16[128,1024]{1,0:T(8,128)(2,1)} %get-tuple-element.196), channel_id=1, source_target_pairs={{0,8},{1,9},{2,10},{3,11},{4,12},{5,13},{6,14},{7,15},{8,16},{9,17... | collective-permute-start | bytes 786440 | tf_op jit(solution)/shard_map/ppermute | solution.py:68
  149.7 20.6 %collective-permute-start.36 = (bf16[128,1024]{1,0:T(8,128)(2,1)S(1)}, bf16[128,1024]{1,0:T(8,128)(2,1)S(1)}, u32[]{:S(2)}, u32[]{:S(2)}) collective-permute-start(bf16[128,1024]{1,0:T(8,128)(2,1)S(1)} %copy-done.50), channel_id=1, source_target_pairs={{0,16},{1,17},{2,18},{3,19},{4,20},{5,21},{6,22},{7,23},{8,24},{9,... | collective-permute-start | bytes 786440 | tf_op jit(solution)/shard_map/ppermute | solution.py:68
  151.2 19.1 %collective-permute-start.37 = (bf16[128,1024]{1,0:T(8,128)(2,1)S(1)}, bf16[128,1024]{1,0:T(8,128)(2,1)S(1)}, u32[]{:S(2)}, u32[]{:S(2)}) collective-permute-start(bf16[128,1024]{1,0:T(8,128)(2,1)S(1)} %copy-done.49), channel_id=1, source_target_pairs={{0,24},{1,25},{2,26},{3,27},{4,28},{5,29},{6,30},{7,31},{8,0},{9,1... | collective-permute-start | bytes 786440 | tf_op jit(solution)/shard_map/ppermute | solution.py:68
  160.1 12.8 %collective-permute-start.34 = (bf16[128,1024]{1,0:T(8,128)(2,1)}, bf16[128,1024]{1,0:T(8,128)(2,1)S(1)}, u32[]{:S(2)}, u32[]{:S(2)}) collective-permute-start(bf16[128,1024]{1,0:T(8,128)(2,1)} %get-tuple-element.203), channel_id=1, source_target_pairs={{0,2},{1,3},{2,0},{3,1},{4,6},{5,7},{6,4},{7,5},{8,10},{9,11},{10,... | collective-permute-start | bytes 786440 | tf_op jit(solution)/shard_map/ppermute | solution.py:56
  161.8 11.2 %collective-permute-start.35 = (bf16[128,1024]{1,0:T(8,128)(2,1)}, bf16[128,1024]{1,0:T(8,128)(2,1)S(1)}, u32[]{:S(2)}, u32[]{:S(2)}) collective-permute-start(bf16[128,1024]{1,0:T(8,128)(2,1)} %get-tuple-element.203), channel_id=1, source_target_pairs={{0,4},{1,5},{2,6},{3,7},{4,0},{5,1},{6,2},{7,3},{8,12},{9,13},{10,... | collective-permute-start | bytes 786440 | tf_op jit(solution)/shard_map/ppermute | solution.py:56
  162.6 10.3 %all-to-all-start.4 = ((bf16[8,128,128]{2,1,0:T(8,128)(2,1)}), bf16[8,128,128]{2,1,0:T(8,128)(2,1)S(1)}, u32[]{:S(2)}, u32[]{:S(2)}) async-start(bf16[8,128,128]{2,1,0:T(8,128)(2,1)} %get-tuple-element.201), calls=%async_computation.4 | async-start | bytes 524288 | tf_op jit(solution)/shard_map/all_to_all | solution.py:82
  172.9 56.4 %all-to-all-start.5 = ((bf16[32,32,512]{2,1,0:T(8,128)(2,1)}), bf16[32,32,512]{2,1,0:T(8,128)(2,1)S(1)}, u32[]{:S(2)}, u32[]{:S(2)}) async-start(bf16[32,32,512]{2,1,0:T(8,128)(2,1)} %bitcast.95), calls=%async_computation.5 | async-start | bytes 2097152 | tf_op jit(solution)/shard_map/all_to_all | solution.py:82
  176.2 16.8 %collective-permute-start.38 = (bf16[64,1024]{1,0:T(8,128)(2,1)S(1)}, bf16[64,1024]{1,0:T(8,128)(2,1)S(1)}, u32[]{:S(2)}, u32[]{:S(2)}) collective-permute-start(bf16[64,1024]{1,0:T(8,128)(2,1)S(1)} %slice.194), channel_id=1, source_target_pairs={{0,4},{1,5},{2,6},{3,7},{4,0},{5,1},{6,2},{7,3},{8,12},{9,13},{10,... | collective-permute-start | bytes 393224 | tf_op jit(solution)/shard_map/ppermute | solution.py:56
  177.8 15.1 %collective-permute-start.39 = (bf16[64,1024]{1,0:T(8,128)(2,1)S(1)}, bf16[64,1024]{1,0:T(8,128)(2,1)S(1)}, u32[]{:S(2)}, u32[]{:S(2)}) collective-permute-start(bf16[64,1024]{1,0:T(8,128)(2,1)S(1)} %slice.195), channel_id=1, source_target_pairs={{0,2},{1,3},{2,0},{3,1},{4,6},{5,7},{6,4},{7,5},{8,10},{9,11},{10,... | collective-permute-start | bytes 393224 | tf_op jit(solution)/shard_map/ppermute | solution.py:56
  193.1 21.8 %collective-permute-start.40 = (bf16[1024,256]{1,0:T(8,128)(2,1)}, bf16[1024,256]{1,0:T(8,128)(2,1)S(1)}, u32[]{:S(2)}, u32[]{:S(2)}) collective-permute-start(bf16[1024,256]{1,0:T(8,128)(2,1)} %get-tuple-element.219), channel_id=1, source_target_pairs={{8,0},{9,1},{10,2},{11,3},{12,4},{13,5},{14,6},{15,7},{16,8},{17,9... | collective-permute-start | bytes 1572872 | tf_op jit(solution)/shard_map/ppermute | solution.py:61
  194.4 22.4 %collective-permute-start.41 = (bf16[1024,256]{1,0:T(8,128)(2,1)}, bf16[1024,256]{1,0:T(8,128)(2,1)S(1)}, u32[]{:S(2)}, u32[]{:S(2)}) collective-permute-start(bf16[1024,256]{1,0:T(8,128)(2,1)} %get-tuple-element.220), channel_id=1, source_target_pairs={{0,8},{1,9},{2,10},{3,11},{4,12},{5,13},{6,14},{7,15},{8,16},{9,17... | collective-permute-start | bytes 1572872 | tf_op jit(solution)/shard_map/ppermute | solution.py:61
  204.2 12.6 %collective-permute-start.43 = (bf16[32,1024]{1,0:T(8,128)(2,1)}, bf16[32,1024]{1,0:T(8,128)(2,1)S(1)}, u32[]{:S(2)}, u32[]{:S(2)}) collective-permute-start(bf16[32,1024]{1,0:T(8,128)(2,1)} %get-tuple-element.223), channel_id=1, source_target_pairs={{0,0},{1,4},{2,8},{3,12},{4,16},{5,20},{6,24},{7,28},{8,1},{9,5},{... | collective-permute-start | bytes 196616 | tf_op jit(solution)/shard_map/ppermute | solution.py:947
  205.7 11.1 %collective-permute-start.44 = (bf16[32,1024]{1,0:T(8,128)(2,1)}, bf16[32,1024]{1,0:T(8,128)(2,1)S(1)}, u32[]{:S(2)}, u32[]{:S(2)}) collective-permute-start(bf16[32,1024]{1,0:T(8,128)(2,1)} %get-tuple-element.224), channel_id=1, source_target_pairs={{0,1},{1,5},{2,9},{3,13},{4,17},{5,21},{6,25},{7,29},{8,2},{9,6},{... | collective-permute-start | bytes 196616 | tf_op jit(solution)/shard_map/ppermute | solution.py:947
  208.7 19.0 %collective-permute-start.45 = (bf16[32,1024]{1,0:T(8,128)(2,1)}, bf16[32,1024]{1,0:T(8,128)(2,1)S(1)}, u32[]{:S(2)}, u32[]{:S(2)}) collective-permute-start(bf16[32,1024]{1,0:T(8,128)(2,1)} %get-tuple-element.241), channel_id=1, source_target_pairs={{0,2},{1,6},{2,10},{3,14},{4,18},{5,22},{6,26},{7,30},{8,3},{9,7},... | collective-permute-start | bytes 196616 | tf_op jit(solution)/shard_map/ppermute | solution.py:947
  214.8 14.5 %collective-permute-start.46 = (bf16[32,1024]{1,0:T(8,128)(2,1)}, bf16[32,1024]{1,0:T(8,128)(2,1)S(1)}, u32[]{:S(2)}, u32[]{:S(2)}) collective-permute-start(bf16[32,1024]{1,0:T(8,128)(2,1)} %get-tuple-element.242), channel_id=1, source_target_pairs={{0,3},{1,7},{2,11},{3,15},{4,19},{5,23},{6,27},{7,31},{8,0},{9,4},... | collective-permute-start | bytes 196616 | tf_op jit(solution)/shard_map/ppermute | solution.py:947
  229.4 16.8 %collective-permute-start.47 = (bf16[3,256,1024]{2,1,0:T(8,128)(2,1)}, bf16[3,256,1024]{2,1,0:T(8,128)(2,1)S(1)}, u32[]{:S(2)}, u32[]{:S(2)}) collective-permute-start(bf16[3,256,1024]{2,1,0:T(8,128)(2,1)} %get-tuple-element.252), channel_id=1, source_target_pairs={{0,1},{1,0},{2,3},{3,2},{4,5},{5,4},{6,7},{7,6},{8,9},{9,8},{10,11... | collective-permute-start | bytes 4718600 | tf_op jit(solution)/shard_map/ppermute | solution.py:56
  235.6 31.0 %all-to-all-start.6 = ((bf16[32,104,128]{2,1,0:T(8,128)(2,1)}), bf16[32,104,128]{2,1,0:T(8,128)(2,1)S(1)}, u32[]{:S(2)}, u32[]{:S(2)}) async-start(bf16[32,104,128]{2,1,0:T(8,128)(2,1)} %get-tuple-element.249), calls=%async_computation.6 | async-start | bytes 1703936 | tf_op jit(solution)/shard_map/all_to_all | solution.py:82
  242.9 14.9 %collective-permute-start.51 = (bf16[128,1024]{1,0:T(8,128)(2,1)S(1)}, bf16[128,1024]{1,0:T(8,128)(2,1)S(1)}, u32[]{:S(2)}, u32[]{:S(2)}) collective-permute-start(bf16[128,1024]{1,0:T(8,128)(2,1)S(1)} %get-tuple-element.292), channel_id=1, source_target_pairs={{0,2},{1,3},{2,0},{3,1},{4,6},{5,7},{6,4},{7,5},{8,10},{9,11},{10,... | collective-permute-start | bytes 786440 | tf_op jit(solution)/shard_map/ppermute | solution.py:56
  244.8 14.4 %collective-permute-start.49 = (bf16[128,1024]{1,0:T(8,128)(2,1)S(1)}, bf16[128,1024]{1,0:T(8,128)(2,1)S(1)}, u32[]{:S(2)}, u32[]{:S(2)}) collective-permute-start(bf16[128,1024]{1,0:T(8,128)(2,1)S(1)} %get-tuple-element.293), channel_id=1, source_target_pairs={{0,4},{1,5},{2,6},{3,7},{4,0},{5,1},{6,2},{7,3},{8,12},{9,13},{10,... | collective-permute-start | bytes 786440 | tf_op jit(solution)/shard_map/ppermute | solution.py:56
  257.9 17.6 %collective-permute-start.52 = (bf16[256,1024]{1,0:T(8,128)(2,1)S(1)}, bf16[256,1024]{1,0:T(8,128)(2,1)S(1)}, u32[]{:S(2)}, u32[]{:S(2)}) collective-permute-start(bf16[256,1024]{1,0:T(8,128)(2,1)S(1)} %pad_maximum_fusion.8), channel_id=1, source_target_pairs={{0,4},{1,5},{2,6},{3,7},{4,0},{5,1},{6,2},{7,3},{8,12},{9,13},{10,... | collective-permute-start | bytes 1572872 | tf_op jit(solution)/shard_map/ppermute | solution.py:56
  259.3 16.2 %collective-permute-start.50 = (bf16[256,1024]{1,0:T(8,128)(2,1)S(1)}, bf16[256,1024]{1,0:T(8,128)(2,1)S(1)}, u32[]{:S(2)}, u32[]{:S(2)}) collective-permute-start(bf16[256,1024]{1,0:T(8,128)(2,1)S(1)} %pad_maximum_fusion.7), channel_id=1, source_target_pairs={{0,2},{1,3},{2,0},{3,1},{4,6},{5,7},{6,4},{7,5},{8,10},{9,11},{10,... | collective-permute-start | bytes 1572872 | tf_op jit(solution)/shard_map/ppermute | solution.py:56
  269.5 11.7 %all-to-all-start.7 = ((f32[32,1,128]{2,1,0:T(1,128)}), f32[32,1,128]{2,1,0:T(1,128)S(1)}, u32[]{:S(2)}, u32[]{:S(2)}) async-start(f32[32,1,128]{2,1,0:T(1,128)} %get-tuple-element.250), calls=%async_computation.7 | async-start | bytes 32768 | tf_op jit(solution)/shard_map/all_to_all | solution.py:82
  (65 other events, 444.2 us)

commit v6 on v5

--- a/solution.py
+++ b/solution.py
@@ -552,7 +552,9 @@
     if len(outs) == 1:
         outs[0][...] = whole[...].astype(LOW)
     else:
-        plane_blocks(place_ref[1], whole, outs)
+        for q, out in enumerate(outs):
+            pair = block_rows((place_ref[1] >> 1) ^ q, whole.shape[0] // len(outs))
+            out[...] = whole[pair, :].astype(LOW)
 
 
 def first_back_kernel(
@@ -620,7 +622,7 @@
     block_ref[...] = (second_ref[...] + both[number:] + vector_ref[4:5, :]).astype(LOW)
 
 
-def sum_kernel(wide, with_vectors, whole_count, parts_count, square_ref, *refs):
+def sum_kernel(wide, with_vectors, whole_count, parts_count, place_ref, square_ref, *refs):
     others, parts, refs = refs[:whole_count], refs[whole_count : whole_count + parts_count], refs[whole_count + parts_count :]
     part_ref, grad_ref, total_ref = refs[:3]
     stacked = with_vectors
@@ -636,7 +638,7 @@
             grad_ref[:, start : start + wide] = whole
             square += whole * whole
             start += wide
-    found = jnp.sum(square, keepdims=True) + square_ref[0]
+    found = jnp.sum(square, keepdims=True) + square_ref[...]
     for ref in others:
         found += jnp.sum(ref[...] * ref[...], keepdims=True)
     if parts:
@@ -649,12 +651,12 @@
         refs[3][:EXTRA, :] = vectors
         refs[3][EXTRA : EXTRA + 1, :] = jnp.concatenate([vectors[:1, rows:], vectors[:1, :rows]], axis=1)
         lanes = lax.broadcasted_iota(jnp.int32, (2 * EXTRA, LANES), 1)
-        mine = lanes // rows == square_ref[1].astype(jnp.int32)
+        mine = lanes // rows == lax.rem(place_ref[1] * PLANE + place_ref[0], LANES // rows)
         found += jnp.sum(jnp.where(mine, refs[3][...] * refs[3][...], 0.0), keepdims=True)
     total_ref[...] = jnp.broadcast_to(found.reshape((1,) * len(total_ref.shape)), total_ref.shape)
 
 
-def sum_parts(wide, rows, part, square, lot=None, others=(), parts=()):
+def sum_parts(wide, rows, part, square, place, lot=None, others=(), parts=()):
     vectors = lot is not None
     n, _, columns = part.shape
     columns = 3 * columns if vectors else columns
@@ -663,10 +665,11 @@
         found = kernel_call(
             functools.partial(sum_kernel, wide, vectors, len(others), len(parts)),
             outs + [like((2 * EXTRA, LANES), F32)] * vectors + [like(p.shape, F32) for p in parts[:1]],
+            square,
             *others,
             *parts,
             part,
-            scalars=(jnp.stack([square, lot.astype(F32) if vectors else square]),),
+            scalars=(place,),
         )
         return found
     whole = part.astype(F32)
@@ -674,15 +677,15 @@
         whole = whole[:, : 3 * rows].reshape(n, 3, rows, wide).transpose(0, 2, 1, 3)
     whole = whole.reshape(-1, PLANE, rows, columns // wide, wide).sum(0)
     whole = whole.transpose(1, 2, 0, 3).reshape(rows, -1)
-    square = square + jnp.sum(whole * whole) + sum(jnp.sum(g * g) for g in others)
+    square = square[0, 0] + jnp.sum(whole * whole) + sum(jnp.sum(g * g) for g in others)
     if not vectors:
-        joined = sum(p.astype(F32) for p in parts)
-        return whole, (square + jnp.sum(joined * joined)).reshape(1, 1), joined
+        return whole, square.reshape(1, 1)
+    joined = sum(p.astype(F32) for p in parts)
     found = part[:, 3 * rows :].astype(F32).sum(0)
     found = jnp.concatenate([found, jnp.roll(found[:1], -rows, axis=1)], axis=0)
     mine = lax.dynamic_slice_in_dim(found, rows * lot, rows, axis=1)
-    square = square + jnp.sum(mine * mine)
-    return whole, jnp.full((n, 1, LANES), square), found
+    square = square + jnp.sum(mine * mine) + jnp.sum(joined * joined)
+    return whole, jnp.full((n, 1, LANES), square), found, joined
 
 
 def update_kernel(square_ref, *refs):
@@ -931,7 +934,7 @@
     branch = jnp.concatenate([branch_grad, *branch_sides, *branch_corner], axis=0)
     output_grad = kernel_call(
         output_grad_kernel,
-        [like((rows, columns), LOW)] * planes if rows % 16 == 0 else [like((wide, columns), LOW)],
+        [like((2 * rows, columns), LOW)] * (planes // 2) if rows % 16 == 0 else [like((wide, columns), LOW)],
         mixed_low,
         branch,
         swap(branch, 1),
@@ -940,18 +943,20 @@
         flops=2 * shared * columns * wide,
     )
     if len(output_grad) == 1:
-        output_grad = jnp.take(
-            output_grad[0].reshape(planes, rows, columns), (plane + jnp.arange(planes)) % planes, axis=0, mode="clip"
+        pairs_of = (plane >> 1) ^ jnp.arange(planes // 2)
+        output_grad = jnp.take(output_grad[0].reshape(-1, 2 * rows, columns), pairs_of, axis=0, mode="clip")
+    expand_grad, squares = sum_parts(hidden, rows, expand_part, jnp.zeros((1, 1), F32), place, others=[shrink_grad])
+    from_after, from_before, output_grad, expand_grad, squares = tie(
+        from_after, from_before, output_grad, expand_grad, squares
+    )
+    output_pairs = [
+        lax.ppermute(
+            output_grad[q],
+            "seq",
+            [(g * PLANE + j, j * planes + 2 * ((g >> 1) ^ q) + (g & 1)) for g in range(planes) for j in range(PLANE)],
         )
-    output_parts = [
-        lax.ppermute(
-            output_grad[s],
-            "seq",
-            [(g * PLANE + j, j * planes + (g + s) % planes) for g in range(planes) for j in range(PLANE)],
-        )
-        for s in range(planes)
+        for q in range(planes // 2)
     ]
-    from_after, from_before, output_parts[:2] = tie(from_after, from_before, output_parts[:2])
 
     fused = rows % 16 == 0 and hidden == LANES
     attend_grad, first_near, first_far, first_corner, one_sums = kernel_call(
@@ -986,18 +991,22 @@
     attend_part = attend_grad
     if not fused:
         attend_part = with_vectors(attend_grad, one_sums, two_sums, up_sums, spot, n, rows, hidden)
-    attend_part, first_near, first_far, first_corner, expand_part, output_parts = tie(
-        attend_part, first_near, first_far, first_corner, expand_part, output_parts
-    )
+    attend_part, first_near, first_far, first_corner, output_pairs = tie(
+        attend_part, first_near, first_far, first_corner, output_pairs
+    )
+    both_cores = sum(g.astype(F32) for g in output_pairs)
+    output_parts = [
+        lax.dynamic_slice_in_dim(both_cores, rows * (device & 1), rows, axis=0),
+        swap(lax.dynamic_slice_in_dim(both_cores, rows * (1 - (device & 1)), rows, axis=0).astype(LOW), 1),
+    ]
     attend_part = exchange(attend_part)
     both = collect(first_near, first_far, first_corner)
     input_gradient, block_output = kernel_call(
         last_kernel, [block_like, block_like], *both, tokens, second_grad, second, vectors
     )
-    expand_grad, squares, output_grad = sum_parts(
-        hidden, rows, expand_part, jnp.zeros((), F32), others=[shrink_grad], parts=output_parts
-    )
-    attend_grad, squares, vector_grad = sum_parts(wide, rows, attend_part, squares[0, 0], device % in_lot)
+    attend_grad, squares, vector_grad, output_grad = sum_parts(
+        wide, rows, attend_part, squares, place, device % in_lot, parts=output_parts
+    )
     vector_grad = lax.dynamic_slice_in_dim(vector_grad, rows * (device % in_lot), rows, axis=1)
     vector_grad = vector_grad[: vector_params.shape[0]]
     squares, input_gradient, block_output = tie(exchange(squares), input_gradient, block_output)

time: 289 us -> 284 us (0.983)
  starting transfers between devices: 110 us -> 101 us
  waiting for transfers between devices: 63.1 us -> 67.5 us
    ppermute x39 -> x40, starting transfers between devices: 45.8 us -> 41 us  [swap(): return lax.ppermute(block, 'seq', [(i, i ^ bit) for i in range(n)])]
    ppermute x4 -> x2, starting transfers between devices: 9.24 us -> 5.39 us  [on_device(): lax.ppermute(output_grad[q], 'seq', [(g * PLANE + j, j * planes + 2 * (g...]
    ppermute x39 -> x40, waiting for transfers between devices: 45.4 us -> 47.8 us  [swap(): return lax.ppermute(block, 'seq', [(i, i ^ bit) for i in range(n)])]
    unnamed x110 -> x102, local copies, waits for them, and re-layouts: 7.17 us -> 7.23 us
  transfers between devices with their start and end apart: 61 -> 60, of which waited for: 22 -> 25; matrix products, arithmetic and copies ran while one was open for 8% -> 8% of each run, Pallas kernels for 21% -> 22%
where the time goes in v6:
time: 284 us; the launch traced here: 282 us
  starting transfers between devices  101 us (36%)
  Pallas kernels  81.6 us (29%)
  waiting for transfers between devices  67.5 us (24%)
  other arithmetic  16.8 us (6%)
  local copies, waits for them, and re-layouts  13.8 us (5%)
    pallas_call x12, Pallas kernels, kernel_call(): pl.pallas_call(body, in_specs=[SMEM] * len(scalars) + [WHOLE] * len(args)...  57.7 us
    ppermute x40, waiting for transfers between devices, swap(): return lax.ppermute(block, 'seq', [(i, i ^ bit) for i in range(n)])  47.8 us
    ppermute x40, starting transfers between devices, swap(): return lax.ppermute(block, 'seq', [(i, i ^ bit) for i in range(n)])  41 us
    all_to_all x8, starting transfers between devices, exchange(): return lax.all_to_all(blocks, 'seq', 0, 0, axis_index_groups=groups)  36 us
    pallas_call x1, Pallas kernels, attention_back(): pl.pallas_call(attend_back_kernel, grid_spec=pltpu.PrefetchScalarGridSpec...  13.6 us
    all_to_all x8, waiting for transfers between devices, exchange(): return lax.all_to_all(blocks, 'seq', 0, 0, axis_index_groups=groups)  11.5 us
    pallas_call x1, Pallas kernels, attention(): pl.pallas_call(attend_kernel, grid_spec=pltpu.PrefetchScalarGridSpec(num_...  10.2 us
    ppermute x6, starting transfers between devices, turn(): lax.ppermute(block, 'seq', [(i, (i + planes_on * PLANE) % n) for i in ran...  9.95 us
  transfers between devices with their start and end apart: 60, of which 25 were waited for; matrix products, arithmetic and copies ran while one was open for 8% of the time, Pallas kernels for 22%

profile of v6, /device:TPU:0, one launch (start us, length us, event | category | flops | bytes accessed | tf_op | source)
XLA Modules:
  0.0 282.4 jit_solution(901931531641257420)
XLA Ops:
  0.7 3.0 %collective-permute-start = (bf16[128,1024]{1,0:T(8,128)(2,1)}, bf16[128,1024]{1,0:T(8,128)(2,1)S(1)}, u32[]{:S(2)}, u32[]{:S(2)}) collective-permute-start(bf16[128,1024]{1,0:T(8,128)(2,1)} %tokens_ref.3), channel_id=1, source_target_pairs={{0,2},{1,3},{2,0},{3,1},{4,6},{5,7},{6,4},{7,5},{8,10},{9,11},{10,... | collective-permute-start | bytes 786440 | tf_op jit(solution)/shard_map/ppermute | solution.py:56
  11.6 4.9 %all-to-all-start = ((bf16[32,104,128]{2,1,0:T(8,128)(2,1)}), bf16[32,104,128]{2,1,0:T(8,128)(2,1)S(1)}, u32[]{:S(2)}, u32[]{:S(2)}) async-start(bf16[32,104,128]{2,1,0:T(8,128)(2,1)} %pad_maximum_fusion.2), calls=%async_computation | async-start | bytes 1703936 | tf_op jit(solution)/shard_map/all_to_all | solution.py:82
  23.5 9.0 %collective-permute-done.7 = bf16[32,1024]{1,0:T(8,128)(2,1)S(1)} collective-permute-done((bf16[32,1024]{1,0:T(8,128)(2,1)S(1)}, bf16[32,1024]{1,0:T(8,128)(2,1)S(1)}, u32[]{:S(2)}, u32[]{:S(2)}) %collective-permute-start.7) | collective-permute-done | bytes 65568 | tf_op jit(solution)/shard_map/ppermute | solution.py:56
  32.5 4.6 %collective-permute-start.8 = (bf16[64,1024]{1,0:T(8,128)(2,1)S(1)}, bf16[64,1024]{1,0:T(8,128)(2,1)}, u32[]{:S(2)}, u32[]{:S(2)}) collective-permute-start(bf16[64,1024]{1,0:T(8,128)(2,1)S(1)} %pad_maximum_fusion.12), channel_id=1, source_target_pairs={{0,16},{1,17},{2,18},{3,19},{4,20},{5,21},{6,22},{7,23},{8,24},{9,... | collective-permute-start | bytes 393224 | tf_op jit(solution)/shard_map/ppermute | solution.py:56
  38.6 5.8 %collective-permute-done.8 = bf16[64,1024]{1,0:T(8,128)(2,1)} collective-permute-done((bf16[64,1024]{1,0:T(8,128)(2,1)S(1)}, bf16[64,1024]{1,0:T(8,128)(2,1)}, u32[]{:S(2)}, u32[]{:S(2)}) %collective-permute-start.8) | collective-permute-done | bytes 131104 | tf_op jit(solution)/shard_map/ppermute | solution.py:56
  46.3 6.5 %shard_map.313 = (bf16[1024,1024]{1,0:T(8,128)(2,1)}, bf16[1024,1024]{1,0:T(8,128)(2,1)}, bf16[1024,128]{1,0:T(8,128)(2,1)}, bf16[1024,256]{1,0:T(8,128)(2,1)}, ...) custom-call(s32[2]{0:T(128)} %pad_add_fusion.1.spot_ref.place_ref, bf16[128,1024]{1,0:T(8,128)(2,1)} %tokens_ref.3, ...), custom_call_target="tpu_custom_call" | custom-call | flops 805306368 | bytes 8847360 | tf_op jit(solution)/shard_map/pallas_call | solution.py:35
  59.0 5.8 %all-to-all-start.1 = ((bf16[32,32,256]{2,1,0:T(8,128)(2,1)}), bf16[32,32,256]{2,1,0:T(8,128)(2,1)S(1)}, u32[]{:S(2)}, u32[]{:S(2)}) async-start(bf16[32,32,256]{2,1,0:T(8,128)(2,1)} %get-tuple-element.170), calls=%async_computation.1 | async-start | bytes 1048576 | tf_op jit(solution)/shard_map/all_to_all | solution.py:82
  64.9 1.8 collective-permute-start.14
  70.3 1.9 collective-permute-done.12.after_ref
  72.2 10.2 %shard_map.314 = (f32[1024,128]{1,0:T(8,128)}, bf16[1024,128]{1,0:T(8,128)(2,1)}, f32[2,1024]{1,0:T(2,128)}) custom-call(s32[2,2]{1,0:T(2,128)} %pad_add_fusion.range_ref, bf16[1024,128]{1,0:T(8,128)(2,1)} %get-tuple-element.163.query_ref, bf16[1024,256]{1,0:T(8,128)(2,1)} %copy-done.44, bf16[1024,256]{1,0:T(8,128)(2,1)} %get-tuple-element.160.own_ref, ...), custom_call_target="tpu_custom_call" | custom-call | flops 5368709120 | bytes 2097152 | tf_op jit(solution)/shard_map/pallas_call | solution.py:376
  85.7 2.2 all-to-all-done.1
  88.5 3.4 %all-to-all-start.2 = ((bf16[8,128,128]{2,1,0:T(8,128)(2,1)}), bf16[8,128,128]{2,1,0:T(8,128)(2,1)S(1)}, u32[]{:S(2)}, u32[]{:S(2)}) async-start(bf16[8,128,128]{2,1,0:T(8,128)(2,1)} %bitcast.21), calls=%async_computation.2 | async-start | bytes 524288 | tf_op jit(solution)/shard_map/all_to_all | solution.py:82
  92.2 3.1 %collective-permute-start.20 = (bf16[128,1024]{1,0:T(8,128)(2,1)S(1)}, bf16[128,1024]{1,0:T(8,128)(2,1)}, u32[]{:S(2)}, u32[]{:S(2)}) collective-permute-start(bf16[128,1024]{1,0:T(8,128)(2,1)S(1)} %convert_element_type.95.refs_10_.refs_0_), channel_id=1, source_target_pairs={{0,24},{1,25},{2,26},{3,27},{4,28},{5,29},{6,30},{7,31},{8,0},{9,1... | collective-permute-start | bytes 786440 | tf_op jit(solution)/shard_map/ppermute | solution.py:68
  95.2 3.5 %all-to-all-done.2.mixed_ref = bf16[8,128,128]{2,1,0:T(8,128)(2,1)S(1)} async-done(((bf16[8,128,128]{2,1,0:T(8,128)(2,1)}), bf16[8,128,128]{2,1,0:T(8,128)(2,1)S(1)}, u32[]{:S(2)}, u32[]{:S(2)}) %all-to-all-start.2) | async-done | bytes 262176 | tf_op jit(solution)/shard_map/all_to_all | solution.py:82
  99.8 3.2 %shard_map.315 = (f32[128,1024]{1,0:T(8,128)}, bf16[128,1024]{1,0:T(8,128)(2,1)}) custom-call(s32[2]{0:T(128)} %pad_add_fusion.1.spot_ref.place_ref, bf16[8,128,128]{2,1,0:T(8,128)(2,1)} %copy-done.16, bf16[128,1024]{1,0:T(8,128)(2,1)} %tokens_ref.3, f32[16,1024]{1,0:T(8,128)} %get-tuple-element.174.vector_ref, bf16[512,1024]{1,0:T(8,128)(2,1)} %copy-done, ...), custom_call_target="tpu_custom_call" | custom-call | flops 268435456 | bytes 3473408 | tf_op jit(solution)/shard_map/pallas_call | solution.py:35
  104.2 3.7 %all-to-all-start.3 = ((bf16[32,32,256]{2,1,0:T(8,128)(2,1)}), bf16[32,32,256]{2,1,0:T(8,128)(2,1)}, u32[]{:S(2)}, u32[]{:S(2)}) async-start(bf16[32,32,256]{2,1,0:T(8,128)(2,1)} %get-tuple-element.189), calls=%async_computation.3 | async-start | bytes 1048576 | tf_op jit(solution)/shard_map/all_to_all | solution.py:82
  107.9 3.0 %collective-permute-done.17.refs_1_ = bf16[128,1024]{1,0:T(8,128)(2,1)S(1)} collective-permute-done((bf16[128,1024]{1,0:T(8,128)(2,1)}, bf16[128,1024]{1,0:T(8,128)(2,1)S(1)}, u32[]{:S(2)}, u32[]{:S(2)}) %collective-permute-start.17) | collective-permute-done | bytes 262176 | tf_op jit(solution)/shard_map/ppermute | solution.py:56
  110.9 2.9 %collective-permute-done.18.refs_2_ = bf16[128,1024]{1,0:T(8,128)(2,1)S(1)} collective-permute-done((bf16[128,1024]{1,0:T(8,128)(2,1)}, bf16[128,1024]{1,0:T(8,128)(2,1)S(1)}, u32[]{:S(2)}, u32[]{:S(2)}) %collective-permute-start.18) | collective-permute-done | bytes 262176 | tf_op jit(solution)/shard_map/ppermute | solution.py:56
  115.3 6.7 %collective-permute-done.22.refs_3_ = bf16[64,1024]{1,0:T(8,128)(2,1)S(1)} collective-permute-done((bf16[64,1024]{1,0:T(8,128)(2,1)S(1)}, bf16[64,1024]{1,0:T(8,128)(2,1)S(1)}, u32[]{:S(2)}, u32[]{:S(2)}) %collective-permute-start.22) | collective-permute-done | bytes 131104 | tf_op jit(solution)/shard_map/ppermute | solution.py:56
  125.7 8.8 %shard_map.316 = (f32[4,128,1024]{2,1,0:T(8,128)}, bf16[3,128,1024]{2,1,0:T(8,128)(2,1)}, bf16[128,1024]{1,0:T(8,128)(2,1)}, bf16[1024,512]{1,0:T(8,128)(2,1)}, ...) custom-call(s32[2]{0:T(128)} %pad_add_fusion.1.spot_ref.place_ref, bf16[128,1024]{1,0:T(8,128)(2,1)} %get-tuple-element.176.refs_0_, ...), custom_call_target="tpu_custom_call" | custom-call | flops 3221225472 | bytes 11538432 | tf_op jit(solution)/shard_map/pallas_call | solution.py:35
  135.0 4.3 %shard_map.317 = (bf16[128,1024]{1,0:T(8,128)(2,1)}, bf16[128,1024]{1,0:T(8,128)(2,1)}, bf16[128,1024]{1,0:T(8,128)(2,1)}, bf16[128,1024]{1,0:T(8,128)(2,1)}) custom-call(s32[2]{0:T(128)} %pad_add_fusion.1.spot_ref.place_ref, bf16[1024,512]{1,0:T(8,128)(2,1)} %get-tuple-element.193.active_ref, bf16[512,1024]{1,0:T(8,128)(2,1)} %pad_maximum_fusion.1.refs_8_.refs_0_, ...), custom_call_target="tpu_custom_call" | custom-call | flops 1073741824 | bytes 4194304 | tf_op jit(solution)/shard_map/pallas_call | solution.py:35
  139.3 2.3 collective-permute-start.33
  144.8 2.6 collective-permute-done.31
  152.1 2.9 %collective-permute-done.32.three_ref = bf16[128,1024]{1,0:T(8,128)(2,1)S(1)} collective-permute-done((bf16[128,1024]{1,0:T(8,128)(2,1)S(1)}, bf16[128,1024]{1,0:T(8,128)(2,1)S(1)}, u32[]{:S(2)}, u32[]{:S(2)}) %collective-permute-start.32) | collective-permute-done | bytes 262176 | tf_op jit(solution)/shard_map/ppermute | solution.py:56
  156.0 4.1 %shard_map.318 = (f32[128,1024]{1,0:T(8,128)}, bf16[128,1024]{1,0:T(8,128)(2,1)}, bf16[8,128,128]{2,1,0:T(8,128)(2,1)}, f32[3,1024]{1,0:T(4,128)}) custom-call(s32[2]{0:T(128)} %pad_add_fusion.1.spot_ref.place_ref, f32[128,1024]{1,0:T(8,128)} %get-tuple-element.195.one_ref, bf16[128,1024]{1,0:T(8,128)(2,1)} %copy-done.27, bf16[128,1024]{1,0:T(8,128)(2,1)} %copy-done.26, ...), custom_call_target="tpu_custom_call" | custom-call | flops 268435456 | bytes 5058560 | tf_op jit(solution)/shard_map/pallas_call | solution.py:35
  162.7 3.4 %all-to-all-start.4 = ((bf16[8,128,128]{2,1,0:T(8,128)(2,1)}), bf16[8,128,128]{2,1,0:T(8,128)(2,1)S(1)}, u32[]{:S(2)}, u32[]{:S(2)}) async-start(bf16[8,128,128]{2,1,0:T(8,128)(2,1)} %get-tuple-element.199), calls=%async_computation.4 | async-start | bytes 524288 | tf_op jit(solution)/shard_map/all_to_all | solution.py:82
  166.1 4.1 %shard_map.319 = bf16[1024,512]{1,0:T(8,128)(2,1)} custom-call(bf16[1024,512]{1,0:T(8,128)(2,1)} %get-tuple-element.202.grad_ref, bf16[128,1024]{1,0:T(8,128)(2,1)} %get-tuple-element.176.refs_0_, bf16[128,1024]{1,0:T(8,128)(2,1)} %copy-done.12, bf16[128,1024]{1,0:T(8,128)(2,1)} %copy-done.13, bf16[64,1024]{1,0:T(8,128)(2,1)} %copy-done.34, ...), custom_call_target="tpu_custom_call" | custom-call | flops 1073741824 | bytes 4194304 | tf_op jit(solution)/shard_map/pallas_call | solution.py:35
  170.3 2.7 all-to-all-done.4
  173.0 3.1 %all-to-all-start.5 = ((bf16[32,32,512]{2,1,0:T(8,128)(2,1)}), bf16[32,32,512]{2,1,0:T(8,128)(2,1)S(1)}, u32[]{:S(2)}, u32[]{:S(2)}) async-start(bf16[32,32,512]{2,1,0:T(8,128)(2,1)} %bitcast.93), calls=%async_computation.5 | async-start | bytes 2097152 | tf_op jit(solution)/shard_map/all_to_all | solution.py:82
  179.2 13.6 %shard_map.320 = (bf16[1024,128]{1,0:T(8,128)(2,1)}, bf16[1024,256]{1,0:T(8,128)(2,1)}, f32[1024,256]{1,0:T(8,128)}, bf16[1024,256]{1,0:T(8,128)(2,1)}) custom-call(s32[2,2]{1,0:T(2,128)} %pad_add_fusion.range_ref, bf16[1024,128]{1,0:T(8,128)(2,1)} %get-tuple-element.163.query_ref, bf16[1024,256]{1,0:T(8,128)(2,1)} %copy-done.44, ...), custom_call_target="tpu_custom_call" | custom-call | flops 8053063680 | bytes 4194304 | tf_op jit(solution)/shard_map/pallas_call | solution.py:399
  194.4 4.6 %collective-permute-start.41 = (bf16[1024,256]{1,0:T(8,128)(2,1)}, bf16[1024,256]{1,0:T(8,128)(2,1)S(1)}, u32[]{:S(2)}, u32[]{:S(2)}) collective-permute-start(bf16[1024,256]{1,0:T(8,128)(2,1)} %get-tuple-element.212), channel_id=1, source_target_pairs={{0,8},{1,9},{2,10},{3,11},{4,12},{5,13},{6,14},{7,15},{8,16},{9,17... | collective-permute-start | bytes 1572872 | tf_op jit(solution)/shard_map/ppermute | solution.py:61
  199.0 1.9 convert_add_fusion.2.refs_0_.refs_18_
  201.9 2.8 %shard_map.321 = (bf16[64,1024]{1,0:T(8,128)(2,1)}, bf16[64,1024]{1,0:T(8,128)(2,1)}) custom-call(s32[2]{0:T(128)} %pad_add_fusion.1.spot_ref.place_ref, bf16[1024,128]{1,0:T(8,128)(2,1)} %get-tuple-element.173.mixed_ref, bf16[512,1024]{1,0:T(8,128)(2,1)} %copy-done.9, bf16[512,1024]{1,0:T(8,128)(2,1)} %copy-done.15), custom_call_target="tpu_custom_call" | custom-call | flops 268435456 | bytes 2621440 | tf_op jit(solution)/shard_map/pallas_call | solution.py:35
  205.7 2.4 shard_map.322
  208.1 3.9 %collective-permute-done.40.from_after_ref = bf16[1024,256]{1,0:T(8,128)(2,1)S(1)} collective-permute-done((bf16[1024,256]{1,0:T(8,128)(2,1)}, bf16[1024,256]{1,0:T(8,128)(2,1)S(1)}, u32[]{:S(2)}, u32[]{:S(2)}) %collective-permute-start.40) | collective-permute-done | bytes 524320 | tf_op jit(solution)/shard_map/ppermute | solution.py:61
  213.5 3.8 %collective-permute-start.44 = (bf16[64,1024]{1,0:T(8,128)(2,1)}, bf16[64,1024]{1,0:T(8,128)(2,1)S(1)}, u32[]{:S(2)}, u32[]{:S(2)}) collective-permute-start(bf16[64,1024]{1,0:T(8,128)(2,1)} %get-tuple-element.240), channel_id=1, source_target_pairs={{0,2},{1,6},{2,10},{3,14},{4,18},{5,22},{6,26},{7,30},{8,3},{9,7},... | collective-permute-start | bytes 393224 | tf_op jit(solution)/shard_map/ppermute | solution.py:953
  217.4 10.1 %shard_map.323 = (bf16[32,104,128]{2,1,0:T(8,128)(2,1)}, f32[4,256,1024]{2,1,0:T(8,128)}, bf16[3,256,1024]{2,1,0:T(8,128)(2,1)}, bf16[256,1024]{1,0:T(8,128)(2,1)}, f32[2,1024]{1,0:T(2,128)}) custom-call(s32[2]{0:T(128)} %pad_add_fusion.1.spot_ref.place_ref, f32[1024,256]{1,0:T(8,128)} %get-tuple-element.226.own_ref, bf16[1024,256]{1,0:T(8,128)(2,1)} %copy-done.23, ...), custom_call_target="tpu_custom_call" | custom-call | flops 1610612736 | bytes 16603136 | tf_op jit(solution)/shard_map/pallas_call | solution.py:35
  227.5 2.3 collective-permute-done.44
  229.8 1.8 collective-permute-start.46
  231.7 8.1 %all-to-all-start.6 = ((bf16[32,104,128]{2,1,0:T(8,128)(2,1)}), bf16[32,104,128]{2,1,0:T(8,128)(2,1)S(1)}, u32[]{:S(2)}, u32[]{:S(2)}) async-start(bf16[32,104,128]{2,1,0:T(8,128)(2,1)} %get-tuple-element.243), calls=%async_computation.6 | async-start | bytes 1703936 | tf_op jit(solution)/shard_map/all_to_all | solution.py:82
  241.2 1.8 collective-permute-start.50
  244.5 3.4 %convert_add_fusion = (f32[1,256,1024]{2,1,0:T(8,128)S(1)}, f32[1,256,1024]{2,1,0:T(8,128)S(1)}, f32[256,1024]{1,0:T(8,128)}) fusion(f32[4,256,1024]{2,1,0:T(8,128)} %get-tuple-element.245, bf16[3,256,1024]{2,1,0:T(8,128)(2,1)S(1)} %collective-permute-done.46), kind=kLoop, calls=%fused_computation.4 | loop fusion | flops 1572864 | bytes 7864320 | tf_op jit(solution)/shard_map/add | solution.py:134
  247.9 8.3 %collective-permute-done.50 = bf16[128,1024]{1,0:T(8,128)(2,1)S(1)} collective-permute-done((bf16[128,1024]{1,0:T(8,128)(2,1)S(1)}, bf16[128,1024]{1,0:T(8,128)(2,1)S(1)}, u32[]{:S(2)}, u32[]{:S(2)}) %collective-permute-start.50) | collective-permute-done | bytes 262176 | tf_op jit(solution)/shard_map/ppermute | solution.py:56
  260.0 1.8 all-to-all-done.6.refs_2_
  262.7 2.9 %shard_map.324 = (f32[32,3072]{1,0:T(8,128)}, f32[32,1,128]{2,1,0:T(1,128)}, f32[16,128]{1,0:T(8,128)}, f32[32,1024]{1,0:T(8,128)}) custom-call(s32[2]{0:T(128)} %pad_add_fusion.1.spot_ref.place_ref, f32[1,1]{1,0:T(1,128)} %get-tuple-element.225.square_ref, f32[32,1024]{1,0:T(8,128)} %constant_dynamic-slice_fusion.1.refs_0_, bf16[32,1024]{1,0:T(8,128)(2,1)} %copy-done.43, ...), custom_call_target="tpu_custom_call" | custom-call | bytes 1597444 | tf_op jit(solution)/shard_map/pallas_call | solution.py:35
  265.6 3.6 %all-to-all-start.7 = ((f32[32,1,128]{2,1,0:T(1,128)}), f32[32,1,128]{2,1,0:T(1,128)S(1)}, u32[]{:S(2)}, u32[]{:S(2)}) async-start(f32[32,1,128]{2,1,0:T(1,128)} %get-tuple-element.244), calls=%async_computation.7 | async-start | bytes 32768 | tf_op jit(solution)/shard_map/all_to_all | solution.py:82
  272.4 3.2 %shard_map.325 = (bf16[128,1024]{1,0:T(8,128)(2,1)}, bf16[128,1024]{1,0:T(8,128)(2,1)}) custom-call(f32[256,1024]{1,0:T(8,128)} %get-tuple-element.280.one_ref, bf16[256,1024]{1,0:T(8,128)(2,1)} %copy-done.22, bf16[256,1024]{1,0:T(8,128)(2,1)} %copy-done.21, bf16[128,1024]{1,0:T(8,128)(2,1)} %tokens_ref.3, f32[128,1024]{1,0:T(8,128)} %get-tuple-element.248.second_grad_ref, ...), custom_call_target="tpu_custom_call" | custom-call | bytes 3997696 | tf_op jit(solution)/shard_map/pallas_call | solution.py:35
  276.9 5.3 %shard_map.326 = (f32[32,3072]{1,0:T(8,128)}, f32[32,3072]{1,0:T(8,128)}, f32[32,3072]{1,0:T(8,128)}, f32[32,1024]{1,0:T(8,128)}, f32[32,1024]{1,0:T(8,128)}, /*...) custom-call(f32[32,1,128]{2,1,0:T(1,128)} %copy-done.42, ...), custom_call_target="tpu_custom_call" | custom-call | bytes 11034500 | tf_op jit(solution)/shard_map/pallas_call | solution.py:35
  (268 shorter events, 71.4 us)
Async XLA Ops:
  0.7 9.5 %collective-permute-start = (bf16[128,1024]{1,0:T(8,128)(2,1)}, bf16[128,1024]{1,0:T(8,128)(2,1)S(1)}, u32[]{:S(2)}, u32[]{:S(2)}) collective-permute-start(bf16[128,1024]{1,0:T(8,128)(2,1)} %tokens_ref.3), channel_id=1, source_target_pairs={{0,2},{1,3},{2,0},{3,1},{4,6},{5,7},{6,4},{7,5},{8,10},{9,11},{10,... | collective-permute-start | bytes 786440 | tf_op jit(solution)/shard_map/ppermute | solution.py:56
  3.7 8.0 %collective-permute-start.1 = (bf16[128,1024]{1,0:T(8,128)(2,1)}, bf16[128,1024]{1,0:T(8,128)(2,1)S(1)}, u32[]{:S(2)}, u32[]{:S(2)}) collective-permute-start(bf16[128,1024]{1,0:T(8,128)(2,1)} %tokens_ref.3), channel_id=1, source_target_pairs={{0,4},{1,5},{2,6},{3,7},{4,0},{5,1},{6,2},{7,3},{8,12},{9,13},{10,... | collective-permute-start | bytes 786440 | tf_op jit(solution)/shard_map/ppermute | solution.py:56
  11.6 33.7 %all-to-all-start = ((bf16[32,104,128]{2,1,0:T(8,128)(2,1)}), bf16[32,104,128]{2,1,0:T(8,128)(2,1)S(1)}, u32[]{:S(2)}, u32[]{:S(2)}) async-start(bf16[32,104,128]{2,1,0:T(8,128)(2,1)} %pad_maximum_fusion.2), calls=%async_computation | async-start | bytes 1703936 | tf_op jit(solution)/shard_map/all_to_all | solution.py:82
  18.4 26.9 %collective-permute-start.4 = (bf16[3,128,1024]{2,1,0:T(8,128)(2,1)S(1)}, bf16[3,128,1024]{2,1,0:T(8,128)(2,1)}, u32[]{:S(2)}, u32[]{:S(2)}) collective-permute-start(bf16[3,128,1024]{2,1,0:T(8,128)(2,1)S(1)} %pad_maximum_fusion.3), channel_id=1, source_target_pairs={{0,1},{1,0},{2,3},{3,2},{4,5},{5,4},{6,7},{7,6},{8,9},{9,8},{10,11... | collective-permute-start | bytes 2359304 | tf_op jit(solution)/shard_map/ppermute | solution.py:56
  18.7 13.7 %collective-permute-start.7 = (bf16[32,1024]{1,0:T(8,128)(2,1)S(1)}, bf16[32,1024]{1,0:T(8,128)(2,1)S(1)}, u32[]{:S(2)}, u32[]{:S(2)}) collective-permute-start(bf16[32,1024]{1,0:T(8,128)(2,1)S(1)} %convert_element_type.96), channel_id=1, source_target_pairs={{0,8},{1,9},{2,10},{3,11},{4,12},{5,13},{6,14},{7,15},{8,0},{9,1},... | collective-permute-start | bytes 196616 | tf_op jit(solution)/shard_map/ppermute | solution.py:56
  20.4 16.8 %collective-permute-start.2 = (bf16[64,1024]{1,0:T(8,128)(2,1)S(1)}, bf16[64,1024]{1,0:T(8,128)(2,1)S(1)}, u32[]{:S(2)}, u32[]{:S(2)}) collective-permute-start(bf16[64,1024]{1,0:T(8,128)(2,1)S(1)} %slice.214), channel_id=1, source_target_pairs={{0,4},{1,5},{2,6},{3,7},{4,0},{5,1},{6,2},{7,3},{8,12},{9,13},{10,... | collective-permute-start | bytes 393224 | tf_op jit(solution)/shard_map/ppermute | solution.py:56
  21.9 15.2 %collective-permute-start.3 = (bf16[64,1024]{1,0:T(8,128)(2,1)S(1)}, bf16[64,1024]{1,0:T(8,128)(2,1)S(1)}, u32[]{:S(2)}, u32[]{:S(2)}) collective-permute-start(bf16[64,1024]{1,0:T(8,128)(2,1)S(1)} %slice.215), channel_id=1, source_target_pairs={{0,2},{1,3},{2,0},{3,1},{4,6},{5,7},{6,4},{7,5},{8,10},{9,11},{10,... | collective-permute-start | bytes 393224 | tf_op jit(solution)/shard_map/ppermute | solution.py:56
  32.5 11.9 %collective-permute-start.8 = (bf16[64,1024]{1,0:T(8,128)(2,1)S(1)}, bf16[64,1024]{1,0:T(8,128)(2,1)}, u32[]{:S(2)}, u32[]{:S(2)}) collective-permute-start(bf16[64,1024]{1,0:T(8,128)(2,1)S(1)} %pad_maximum_fusion.12), channel_id=1, source_target_pairs={{0,16},{1,17},{2,18},{3,19},{4,20},{5,21},{6,22},{7,23},{8,24},{9,... | collective-permute-start | bytes 393224 | tf_op jit(solution)/shard_map/ppermute | solution.py:56
  37.2 8.0 %collective-permute-start.5 = (bf16[64,1024]{1,0:T(8,128)(2,1)S(1)}, bf16[64,1024]{1,0:T(8,128)(2,1)S(1)}, u32[]{:S(2)}, u32[]{:S(2)}) collective-permute-start(bf16[64,1024]{1,0:T(8,128)(2,1)S(1)} %collective-permute-done.2.refs_3_), channel_id=1, source_target_pairs={{0,1},{1,0},{2,3},{3,2},{4,5},{5,4},{6,7},{7,6},{8,9},{9,8},{10,11... | collective-permute-start | bytes 393224 | tf_op jit(solution)/shard_map/ppermute | solution.py:56
  37.3 8.0 %collective-permute-start.6 = (bf16[64,1024]{1,0:T(8,128)(2,1)S(1)}, bf16[64,1024]{1,0:T(8,128)(2,1)S(1)}, u32[]{:S(2)}, u32[]{:S(2)}) collective-permute-start(bf16[64,1024]{1,0:T(8,128)(2,1)S(1)} %collective-permute-done.3.refs_4_), channel_id=1, source_target_pairs={{0,1},{1,0},{2,3},{3,2},{4,5},{5,4},{6,7},{7,6},{8,9},{9,8},{10,11... | collective-permute-start | bytes 393224 | tf_op jit(solution)/shard_map/ppermute | solution.py:56
  52.7 17.5 %collective-permute-start.11 = (bf16[1024,256]{1,0:T(8,128)(2,1)}, bf16[1024,256]{1,0:T(8,128)(2,1)S(1)}, u32[]{:S(2)}, u32[]{:S(2)}) collective-permute-start(bf16[1024,256]{1,0:T(8,128)(2,1)} %get-tuple-element.160.own_ref), channel_id=1, source_target_pairs={{0,8},{1,9},{2,10},{3,11},{4,12},{5,13},{6,14},{7,15},{8,16},{9,17... | collective-permute-start | bytes 1572872 | tf_op jit(solution)/shard_map/ppermute | solution.py:61
  54.0 18.1 %collective-permute-start.12 = (bf16[1024,256]{1,0:T(8,128)(2,1)}, bf16[1024,256]{1,0:T(8,128)(2,1)}, u32[]{:S(2)}, u32[]{:S(2)}) collective-permute-start(bf16[1024,256]{1,0:T(8,128)(2,1)} %get-tuple-element.160.own_ref), channel_id=1, source_target_pairs={{8,0},{9,1},{10,2},{11,3},{12,4},{13,5},{14,6},{15,7},{16,8},{17,9... | collective-permute-start | bytes 1572872 | tf_op jit(solution)/shard_map/ppermute | solution.py:61
  55.4 9.4 %collective-permute-start.10 = (bf16[128,1024]{1,0:T(8,128)(2,1)S(1)}, bf16[128,1024]{1,0:T(8,128)(2,1)S(1)}, u32[]{:S(2)}, u32[]{:S(2)}) collective-permute-start(bf16[128,1024]{1,0:T(8,128)(2,1)S(1)} %copy-done.17), channel_id=1, source_target_pairs={{0,2},{1,3},{2,0},{3,1},{4,6},{5,7},{6,4},{7,5},{8,10},{9,11},{10,... | collective-permute-start | bytes 786440 | tf_op jit(solution)/shard_map/ppermute | solution.py:56
  56.9 8.0 %collective-permute-start.9 = (bf16[128,1024]{1,0:T(8,128)(2,1)S(1)}, bf16[128,1024]{1,0:T(8,128)(2,1)S(1)}, u32[]{:S(2)}, u32[]{:S(2)}) collective-permute-start(bf16[128,1024]{1,0:T(8,128)(2,1)S(1)} %pad_maximum_fusion.9), channel_id=1, source_target_pairs={{0,4},{1,5},{2,6},{3,7},{4,0},{5,1},{6,2},{7,3},{8,12},{9,13},{10,... | collective-permute-start | bytes 786440 | tf_op jit(solution)/shard_map/ppermute | solution.py:56
  59.0 28.9 %all-to-all-start.1 = ((bf16[32,32,256]{2,1,0:T(8,128)(2,1)}), bf16[32,32,256]{2,1,0:T(8,128)(2,1)S(1)}, u32[]{:S(2)}, u32[]{:S(2)}) async-start(bf16[32,32,256]{2,1,0:T(8,128)(2,1)} %get-tuple-element.170), calls=%async_computation.1 | async-start | bytes 1048576 | tf_op jit(solution)/shard_map/all_to_all | solution.py:82
  64.9 19.3 %collective-permute-start.14 = (bf16[256,1024]{1,0:T(8,128)(2,1)S(1)}, bf16[256,1024]{1,0:T(8,128)(2,1)S(1)}, u32[]{:S(2)}, u32[]{:S(2)}) collective-permute-start(bf16[256,1024]{1,0:T(8,128)(2,1)S(1)} %pad_maximum_fusion.6), channel_id=1, source_target_pairs={{0,4},{1,5},{2,6},{3,7},{4,0},{5,1},{6,2},{7,3},{8,12},{9,13},{10,... | collective-permute-start | bytes 1572872 | tf_op jit(solution)/shard_map/ppermute | solution.py:56
  67.3 18.4 %collective-permute-start.15 = (bf16[128,1024]{1,0:T(8,128)(2,1)S(1)}, bf16[128,1024]{1,0:T(8,128)(2,1)S(1)}, u32[]{:S(2)}, u32[]{:S(2)}) collective-permute-start(bf16[128,1024]{1,0:T(8,128)(2,1)S(1)} %convert_element_type.95.refs_10_.refs_0_), channel_id=1, source_target_pairs={{0,8},{1,9},{2,10},{3,11},{4,12},{5,13},{6,14},{7,15},{8,16},{9,17... | collective-permute-start | bytes 786440 | tf_op jit(solution)/shard_map/ppermute | solution.py:68
  69.0 16.6 %collective-permute-start.13 = (bf16[256,1024]{1,0:T(8,128)(2,1)S(1)}, bf16[256,1024]{1,0:T(8,128)(2,1)S(1)}, u32[]{:S(2)}, u32[]{:S(2)}) collective-permute-start(bf16[256,1024]{1,0:T(8,128)(2,1)S(1)} %pad_maximum_fusion.5), channel_id=1, source_target_pairs={{0,2},{1,3},{2,0},{3,1},{4,6},{5,7},{6,4},{7,5},{8,10},{9,11},{10,... | collective-permute-start | bytes 1572872 | tf_op jit(solution)/shard_map/ppermute | solution.py:56
  87.9 10.8 %collective-permute-start.16 = (bf16[512,1024]{1,0:T(8,128)(2,1)S(1)}, bf16[512,1024]{1,0:T(8,128)(2,1)S(1)}, u32[]{:S(2)}, u32[]{:S(2)}) collective-permute-start(bf16[512,1024]{1,0:T(8,128)(2,1)S(1)} %pad_maximum_fusion.refs_0_), channel_id=1, source_target_pairs={{0,1},{1,0},{2,3},{3,2},{4,5},{5,4},{6,7},{7,6},{8,9},{9,8},{10,11... | collective-permute-start | bytes 3145736 | tf_op jit(solution)/shard_map/ppermute | solution.py:56
  87.9 19.9 %collective-permute-start.21 = (bf16[512,1024]{1,0:T(8,128)(2,1)}, bf16[512,1024]{1,0:T(8,128)(2,1)}, u32[]{:S(2)}, u32[]{:S(2)}) collective-permute-start(bf16[512,1024]{1,0:T(8,128)(2,1)} %pad_maximum_fusion.1.refs_8_.refs_0_), channel_id=1, source_target_pairs={{0,1},{1,0},{2,3},{3,2},{4,5},{5,4},{6,7},{7,6},{8,9},{9,8},{10,11... | collective-permute-start | bytes 3145736 | tf_op jit(solution)/shard_map/ppermute | solution.py:56
  88.5 10.3 %all-to-all-start.2 = ((bf16[8,128,128]{2,1,0:T(8,128)(2,1)}), bf16[8,128,128]{2,1,0:T(8,128)(2,1)S(1)}, u32[]{:S(2)}, u32[]{:S(2)}) async-start(bf16[8,128,128]{2,1,0:T(8,128)(2,1)} %bitcast.21), calls=%async_computation.2 | async-start | bytes 524288 | tf_op jit(solution)/shard_map/all_to_all | solution.py:82
  91.9 16.0 %collective-permute-start.19 = (bf16[128,1024]{1,0:T(8,128)(2,1)S(1)}, bf16[128,1024]{1,0:T(8,128)(2,1)}, u32[]{:S(2)}, u32[]{:S(2)}) collective-permute-start(bf16[128,1024]{1,0:T(8,128)(2,1)S(1)} %convert_element_type.95.refs_10_.refs_0_), channel_id=1, source_target_pairs={{0,16},{1,17},{2,18},{3,19},{4,20},{5,21},{6,22},{7,23},{8,24},{9,... | collective-permute-start | bytes 786440 | tf_op jit(solution)/shard_map/ppermute | solution.py:68
  92.2 15.7 %collective-permute-start.20 = (bf16[128,1024]{1,0:T(8,128)(2,1)S(1)}, bf16[128,1024]{1,0:T(8,128)(2,1)}, u32[]{:S(2)}, u32[]{:S(2)}) collective-permute-start(bf16[128,1024]{1,0:T(8,128)(2,1)S(1)} %convert_element_type.95.refs_10_.refs_0_), channel_id=1, source_target_pairs={{0,24},{1,25},{2,26},{3,27},{4,28},{5,29},{6,30},{7,31},{8,0},{9,1... | collective-permute-start | bytes 786440 | tf_op jit(solution)/shard_map/ppermute | solution.py:68
  103.6 10.1 %collective-permute-start.18 = (bf16[128,1024]{1,0:T(8,128)(2,1)}, bf16[128,1024]{1,0:T(8,128)(2,1)S(1)}, u32[]{:S(2)}, u32[]{:S(2)}) collective-permute-start(bf16[128,1024]{1,0:T(8,128)(2,1)} %get-tuple-element.176.refs_0_), channel_id=1, source_target_pairs={{0,4},{1,5},{2,6},{3,7},{4,0},{5,1},{6,2},{7,3},{8,12},{9,13},{10,... | collective-permute-start | bytes 786440 | tf_op jit(solution)/shard_map/ppermute | solution.py:56
  104.2 20.5 %all-to-all-start.3 = ((bf16[32,32,256]{2,1,0:T(8,128)(2,1)}), bf16[32,32,256]{2,1,0:T(8,128)(2,1)}, u32[]{:S(2)}, u32[]{:S(2)}) async-start(bf16[32,32,256]{2,1,0:T(8,128)(2,1)} %get-tuple-element.189), calls=%async_computation.3 | async-start | bytes 1048576 | tf_op jit(solution)/shard_map/all_to_all | solution.py:82
  114.8 9.8 %collective-permute-start.24 = (bf16[3,128,1024]{2,1,0:T(8,128)(2,1)S(1)}, bf16[3,128,1024]{2,1,0:T(8,128)(2,1)S(1)}, u32[]{:S(2)}, u32[]{:S(2)}) collective-permute-start(bf16[3,128,1024]{2,1,0:T(8,128)(2,1)S(1)} %pad_maximum_fusion.4), channel_id=1, source_target_pairs={{0,1},{1,0},{2,3},{3,2},{4,5},{5,4},{6,7},{7,6},{8,9},{9,8},{10,11... | collective-permute-start | bytes 2359304 | tf_op jit(solution)/shard_map/ppermute | solution.py:56
  134.4 9.3 %collective-permute-start.27 = (bf16[3,128,1024]{2,1,0:T(8,128)(2,1)}, bf16[3,128,1024]{2,1,0:T(8,128)(2,1)S(1)}, u32[]{:S(2)}, u32[]{:S(2)}) collective-permute-start(bf16[3,128,1024]{2,1,0:T(8,128)(2,1)} %get-tuple-element.191), channel_id=1, source_target_pairs={{0,1},{1,0},{2,3},{3,2},{4,5},{5,4},{6,7},{7,6},{8,9},{9,8},{10,11... | collective-permute-start | bytes 2359304 | tf_op jit(solution)/shard_map/ppermute | solution.py:56
  139.3 12.8 %collective-permute-start.33 = (bf16[128,1024]{1,0:T(8,128)(2,1)}, bf16[128,1024]{1,0:T(8,128)(2,1)S(1)}, u32[]{:S(2)}, u32[]{:S(2)}) collective-permute-start(bf16[128,1024]{1,0:T(8,128)(2,1)} %get-tuple-element.194), channel_id=1, source_target_pairs={{0,8},{1,9},{2,10},{3,11},{4,12},{5,13},{6,14},{7,15},{8,16},{9,17... | collective-permute-start | bytes 786440 | tf_op jit(solution)/shard_map/ppermute | solution.py:68
  149.4 20.8 %collective-permute-start.36 = (bf16[128,1024]{1,0:T(8,128)(2,1)S(1)}, bf16[128,1024]{1,0:T(8,128)(2,1)S(1)}, u32[]{:S(2)}, u32[]{:S(2)}) collective-permute-start(bf16[128,1024]{1,0:T(8,128)(2,1)S(1)} %copy-done.46), channel_id=1, source_target_pairs={{0,16},{1,17},{2,18},{3,19},{4,20},{5,21},{6,22},{7,23},{8,24},{9,... | collective-permute-start | bytes 786440 | tf_op jit(solution)/shard_map/ppermute | solution.py:68
  151.1 19.1 %collective-permute-start.37 = (bf16[128,1024]{1,0:T(8,128)(2,1)S(1)}, bf16[128,1024]{1,0:T(8,128)(2,1)S(1)}, u32[]{:S(2)}, u32[]{:S(2)}) collective-permute-start(bf16[128,1024]{1,0:T(8,128)(2,1)S(1)} %copy-done.45), channel_id=1, source_target_pairs={{0,24},{1,25},{2,26},{3,27},{4,28},{5,29},{6,30},{7,31},{8,0},{9,1... | collective-permute-start | bytes 786440 | tf_op jit(solution)/shard_map/ppermute | solution.py:68
  160.1 12.8 %collective-permute-start.34 = (bf16[128,1024]{1,0:T(8,128)(2,1)}, bf16[128,1024]{1,0:T(8,128)(2,1)S(1)}, u32[]{:S(2)}, u32[]{:S(2)}) collective-permute-start(bf16[128,1024]{1,0:T(8,128)(2,1)} %get-tuple-element.201), channel_id=1, source_target_pairs={{0,2},{1,3},{2,0},{3,1},{4,6},{5,7},{6,4},{7,5},{8,10},{9,11},{10,... | collective-permute-start | bytes 786440 | tf_op jit(solution)/shard_map/ppermute | solution.py:56
  161.4 11.5 %collective-permute-start.35 = (bf16[128,1024]{1,0:T(8,128)(2,1)}, bf16[128,1024]{1,0:T(8,128)(2,1)S(1)}, u32[]{:S(2)}, u32[]{:S(2)}) collective-permute-start(bf16[128,1024]{1,0:T(8,128)(2,1)} %get-tuple-element.201), channel_id=1, source_target_pairs={{0,4},{1,5},{2,6},{3,7},{4,0},{5,1},{6,2},{7,3},{8,12},{9,13},{10,... | collective-permute-start | bytes 786440 | tf_op jit(solution)/shard_map/ppermute | solution.py:56
  162.7 10.3 %all-to-all-start.4 = ((bf16[8,128,128]{2,1,0:T(8,128)(2,1)}), bf16[8,128,128]{2,1,0:T(8,128)(2,1)S(1)}, u32[]{:S(2)}, u32[]{:S(2)}) async-start(bf16[8,128,128]{2,1,0:T(8,128)(2,1)} %get-tuple-element.199), calls=%async_computation.4 | async-start | bytes 524288 | tf_op jit(solution)/shard_map/all_to_all | solution.py:82
  173.0 31.8 %all-to-all-start.5 = ((bf16[32,32,512]{2,1,0:T(8,128)(2,1)}), bf16[32,32,512]{2,1,0:T(8,128)(2,1)S(1)}, u32[]{:S(2)}, u32[]{:S(2)}) async-start(bf16[32,32,512]{2,1,0:T(8,128)(2,1)} %bitcast.93), calls=%async_computation.5 | async-start | bytes 2097152 | tf_op jit(solution)/shard_map/all_to_all | solution.py:82
  176.1 16.9 %collective-permute-start.38 = (bf16[64,1024]{1,0:T(8,128)(2,1)S(1)}, bf16[64,1024]{1,0:T(8,128)(2,1)S(1)}, u32[]{:S(2)}, u32[]{:S(2)}) collective-permute-start(bf16[64,1024]{1,0:T(8,128)(2,1)S(1)} %slice.194), channel_id=1, source_target_pairs={{0,4},{1,5},{2,6},{3,7},{4,0},{5,1},{6,2},{7,3},{8,12},{9,13},{10,... | collective-permute-start | bytes 393224 | tf_op jit(solution)/shard_map/ppermute | solution.py:56
  177.7 15.3 %collective-permute-start.39 = (bf16[64,1024]{1,0:T(8,128)(2,1)S(1)}, bf16[64,1024]{1,0:T(8,128)(2,1)S(1)}, u32[]{:S(2)}, u32[]{:S(2)}) collective-permute-start(bf16[64,1024]{1,0:T(8,128)(2,1)S(1)} %slice.195), channel_id=1, source_target_pairs={{0,2},{1,3},{2,0},{3,1},{4,6},{5,7},{6,4},{7,5},{8,10},{9,11},{10,... | collective-permute-start | bytes 393224 | tf_op jit(solution)/shard_map/ppermute | solution.py:56
  193.1 18.9 %collective-permute-start.40 = (bf16[1024,256]{1,0:T(8,128)(2,1)}, bf16[1024,256]{1,0:T(8,128)(2,1)S(1)}, u32[]{:S(2)}, u32[]{:S(2)}) collective-permute-start(bf16[1024,256]{1,0:T(8,128)(2,1)} %get-tuple-element.211), channel_id=1, source_target_pairs={{8,0},{9,1},{10,2},{11,3},{12,4},{13,5},{14,6},{15,7},{16,8},{17,9... | collective-permute-start | bytes 1572872 | tf_op jit(solution)/shard_map/ppermute | solution.py:61
  194.4 17.6 %collective-permute-start.41 = (bf16[1024,256]{1,0:T(8,128)(2,1)}, bf16[1024,256]{1,0:T(8,128)(2,1)S(1)}, u32[]{:S(2)}, u32[]{:S(2)}) collective-permute-start(bf16[1024,256]{1,0:T(8,128)(2,1)} %get-tuple-element.212), channel_id=1, source_target_pairs={{0,8},{1,9},{2,10},{3,11},{4,12},{5,13},{6,14},{7,15},{8,16},{9,17... | collective-permute-start | bytes 1572872 | tf_op jit(solution)/shard_map/ppermute | solution.py:61
  212.0 15.5 %collective-permute-start.43 = (bf16[64,1024]{1,0:T(8,128)(2,1)}, bf16[64,1024]{1,0:T(8,128)(2,1)S(1)}, u32[]{:S(2)}, u32[]{:S(2)}) collective-permute-start(bf16[64,1024]{1,0:T(8,128)(2,1)} %get-tuple-element.239), channel_id=1, source_target_pairs={{0,0},{1,4},{2,8},{3,12},{4,16},{5,20},{6,24},{7,28},{8,1},{9,5},{... | collective-permute-start | bytes 393224 | tf_op jit(solution)/shard_map/ppermute | solution.py:953
  213.5 16.3 %collective-permute-start.44 = (bf16[64,1024]{1,0:T(8,128)(2,1)}, bf16[64,1024]{1,0:T(8,128)(2,1)S(1)}, u32[]{:S(2)}, u32[]{:S(2)}) collective-permute-start(bf16[64,1024]{1,0:T(8,128)(2,1)} %get-tuple-element.240), channel_id=1, source_target_pairs={{0,2},{1,6},{2,10},{3,14},{4,18},{5,22},{6,26},{7,30},{8,3},{9,7},... | collective-permute-start | bytes 393224 | tf_op jit(solution)/shard_map/ppermute | solution.py:953
  229.8 14.7 %collective-permute-start.46 = (bf16[3,256,1024]{2,1,0:T(8,128)(2,1)}, bf16[3,256,1024]{2,1,0:T(8,128)(2,1)S(1)}, u32[]{:S(2)}, u32[]{:S(2)}) collective-permute-start(bf16[3,256,1024]{2,1,0:T(8,128)(2,1)} %get-tuple-element.246), channel_id=1, source_target_pairs={{0,1},{1,0},{2,3},{3,2},{4,5},{5,4},{6,7},{7,6},{8,9},{9,8},{10,11... | collective-permute-start | bytes 4718600 | tf_op jit(solution)/shard_map/ppermute | solution.py:56
  231.6 8.2 %collective-permute-start.47 = (bf16[256,1024]{1,0:T(8,128)(2,1)}, bf16[256,1024]{1,0:T(8,128)(2,1)S(1)}, u32[]{:S(2)}, u32[]{:S(2)}) collective-permute-start(bf16[256,1024]{1,0:T(8,128)(2,1)} %get-tuple-element.247), channel_id=1, source_target_pairs={{0,1},{1,0},{2,3},{3,2},{4,5},{5,4},{6,7},{7,6},{8,9},{9,8},{10,11... | collective-permute-start | bytes 1572872 | tf_op jit(solution)/shard_map/ppermute | solution.py:56
  231.7 30.1 %all-to-all-start.6 = ((bf16[32,104,128]{2,1,0:T(8,128)(2,1)}), bf16[32,104,128]{2,1,0:T(8,128)(2,1)S(1)}, u32[]{:S(2)}, u32[]{:S(2)}) async-start(bf16[32,104,128]{2,1,0:T(8,128)(2,1)} %get-tuple-element.243), calls=%async_computation.6 | async-start | bytes 1703936 | tf_op jit(solution)/shard_map/all_to_all | solution.py:82
  241.2 15.0 %collective-permute-start.50 = (bf16[128,1024]{1,0:T(8,128)(2,1)S(1)}, bf16[128,1024]{1,0:T(8,128)(2,1)S(1)}, u32[]{:S(2)}, u32[]{:S(2)}) collective-permute-start(bf16[128,1024]{1,0:T(8,128)(2,1)S(1)} %get-tuple-element.286), channel_id=1, source_target_pairs={{0,2},{1,3},{2,0},{3,1},{4,6},{5,7},{6,4},{7,5},{8,10},{9,11},{10,... | collective-permute-start | bytes 786440 | tf_op jit(solution)/shard_map/ppermute | solution.py:56
  243.0 14.6 %collective-permute-start.48 = (bf16[128,1024]{1,0:T(8,128)(2,1)S(1)}, bf16[128,1024]{1,0:T(8,128)(2,1)S(1)}, u32[]{:S(2)}, u32[]{:S(2)}) collective-permute-start(bf16[128,1024]{1,0:T(8,128)(2,1)S(1)} %get-tuple-element.287), channel_id=1, source_target_pairs={{0,4},{1,5},{2,6},{3,7},{4,0},{5,1},{6,2},{7,3},{8,12},{9,13},{10,... | collective-permute-start | bytes 786440 | tf_op jit(solution)/shard_map/ppermute | solution.py:56
  256.3 14.7 %collective-permute-start.51 = (bf16[256,1024]{1,0:T(8,128)(2,1)S(1)}, bf16[256,1024]{1,0:T(8,128)(2,1)S(1)}, u32[]{:S(2)}, u32[]{:S(2)}) collective-permute-start(bf16[256,1024]{1,0:T(8,128)(2,1)S(1)} %pad_maximum_fusion.8), channel_id=1, source_target_pairs={{0,4},{1,5},{2,6},{3,7},{4,0},{5,1},{6,2},{7,3},{8,12},{9,13},{10,... | collective-permute-start | bytes 1572872 | tf_op jit(solution)/shard_map/ppermute | solution.py:56
  257.7 13.9 %collective-permute-start.49 = (bf16[256,1024]{1,0:T(8,128)(2,1)S(1)}, bf16[256,1024]{1,0:T(8,128)(2,1)S(1)}, u32[]{:S(2)}, u32[]{:S(2)}) collective-permute-start(bf16[256,1024]{1,0:T(8,128)(2,1)S(1)} %pad_maximum_fusion.7), channel_id=1, source_target_pairs={{0,2},{1,3},{2,0},{3,1},{4,6},{5,7},{6,4},{7,5},{8,10},{9,11},{10,... | collective-permute-start | bytes 1572872 | tf_op jit(solution)/shard_map/ppermute | solution.py:56
  265.6 10.7 %all-to-all-start.7 = ((f32[32,1,128]{2,1,0:T(1,128)}), f32[32,1,128]{2,1,0:T(1,128)S(1)}, u32[]{:S(2)}, u32[]{:S(2)}) async-start(f32[32,1,128]{2,1,0:T(1,128)} %get-tuple-element.244), calls=%async_computation.7 | async-start | bytes 32768 | tf_op jit(solution)/shard_map/all_to_all | solution.py:82
  (60 other events, 446.5 us)

commit v7 on v6

--- a/solution.py
+++ b/solution.py
@@ -30,7 +30,7 @@
     return jax.ShapeDtypeStruct(shape, dtype)
 
 
-def kernel_call(body, outs, *args, scalars=(), scratch=(), flops=0, limit=56):
+def kernel_call(body, outs, *args, scalars=(), scratch=(), flops=0, limit=53):
     moved = sum(a.size * a.dtype.itemsize for a in list(args) + list(outs))
     return pl.pallas_call(
         body,
@@ -386,7 +386,7 @@
         cost_estimate=pl.CostEstimate(
             flops=40 * tokens * tokens * wide, bytes_accessed=16 * tokens * wide, transcendentals=2 * tokens * tokens
         ),
-        compiler_params=pltpu.CompilerParams(vmem_limit_bytes=56 << 20),
+        compiler_params=pltpu.CompilerParams(vmem_limit_bytes=53 << 20),
     )(key_ranges(spans, QUERY_TILE, KEY_TILE), queries, before, own, behind, bounds)
 
 
@@ -420,7 +420,7 @@
         cost_estimate=pl.CostEstimate(
             flops=60 * tokens * tokens * wide, bytes_accessed=32 * tokens * wide, transcendentals=2 * tokens * tokens
         ),
-        compiler_params=pltpu.CompilerParams(vmem_limit_bytes=56 << 20),
+        compiler_params=pltpu.CompilerParams(vmem_limit_bytes=53 << 20),
     )(key_ranges(spans, QUERY_TILE, KEY_TILE), queries, before, own, behind, bounds, mixed, logs, grads)
 
 

time: 284 us -> 283 us (level)
  starting transfers between devices: 101 us -> 106 us
  local copies, waits for them, and re-layouts: 13.8 us -> 9.52 us
  waiting for transfers between devices: 67.5 us -> 71 us
    all_to_all x8, waiting for transfers between devices: 11.5 us -> 15.6 us  [exchange(): return lax.all_to_all(blocks, 'seq', 0, 0, axis_index_groups=groups)]
    ppermute x6, starting transfers between devices: 9.95 us -> 13 us  [turn(): lax.ppermute(block, 'seq', [(i, (i + planes_on * PLANE) % n) for i in ran...]
    ppermute x4, starting transfers between devices: 8.47 us -> 11.4 us  [move(): lax.ppermute(block, 'seq', [(i, i + distance) for i in range(n) if 0 <= i...]
    unnamed x102 -> x82, local copies, waits for them, and re-layouts: 7.23 us -> 6.91 us
  transfers between devices with their start and end apart: 60 -> 60, of which waited for: 25 -> 26; matrix products, arithmetic and copies ran while one was open for 8% -> 7% of each run, Pallas kernels for 22% -> 21%
where the time goes in v7:
time: 283 us
  starting transfers between devices  106 us (37%)
  Pallas kernels  78.9 us (28%)
  waiting for transfers between devices  71 us (25%)
  other arithmetic  16.2 us (6%)
  local copies, waits for them, and re-layouts  9.52 us (3%)
    pallas_call x12, Pallas kernels, kernel_call(): pl.pallas_call(body, in_specs=[SMEM] * len(scalars) + [WHOLE] * len(args)...  55.8 us
    ppermute x40, waiting for transfers between devices, swap(): return lax.ppermute(block, 'seq', [(i, i ^ bit) for i in range(n)])  45.8 us
    ppermute x40, starting transfers between devices, swap(): return lax.ppermute(block, 'seq', [(i, i ^ bit) for i in range(n)])  39.9 us
    all_to_all x8, starting transfers between devices, exchange(): return lax.all_to_all(blocks, 'seq', 0, 0, axis_index_groups=groups)  34.9 us
    all_to_all x8, waiting for transfers between devices, exchange(): return lax.all_to_all(blocks, 'seq', 0, 0, axis_index_groups=groups)  15.6 us
    pallas_call x1, Pallas kernels, attention_back(): pl.pallas_call(attend_back_kernel, grid_spec=pltpu.PrefetchScalarGridSpec...  13.1 us
    ppermute x6, starting transfers between devices, turn(): lax.ppermute(block, 'seq', [(i, (i + planes_on * PLANE) % n) for i in ran...  13 us
    ppermute x4, starting transfers between devices, move(): lax.ppermute(block, 'seq', [(i, i + distance) for i in range(n) if 0 <= i...  11.4 us
  transfers between devices with their start and end apart: 60, of which 26 were waited for; matrix products, arithmetic and copies ran while one was open for 7% of the time, Pallas kernels for 21%

profile of v7, /device:TPU:0, one launch (start us, length us, event | category | flops | bytes accessed | tf_op | source)
XLA Modules:
  0.0 283.1 jit_solution(11220367412004372513)
XLA Ops:
  0.7 3.0 %collective-permute-start = (bf16[128,1024]{1,0:T(8,128)(2,1)}, bf16[128,1024]{1,0:T(8,128)(2,1)S(1)}, u32[]{:S(2)}, u32[]{:S(2)}) collective-permute-start(bf16[128,1024]{1,0:T(8,128)(2,1)} %tokens_ref.3), channel_id=1, source_target_pairs={{0,2},{1,3},{2,0},{3,1},{4,6},{5,7},{6,4},{7,5},{8,10},{9,11},{10,... | collective-permute-start | bytes 786440 | tf_op jit(solution)/shard_map/ppermute | solution.py:56
  11.6 4.9 %all-to-all-start = ((bf16[32,104,128]{2,1,0:T(8,128)(2,1)}), bf16[32,104,128]{2,1,0:T(8,128)(2,1)S(1)}, u32[]{:S(2)}, u32[]{:S(2)}) async-start(bf16[32,104,128]{2,1,0:T(8,128)(2,1)} %pad_maximum_fusion.2), calls=%async_computation | async-start | bytes 1703936 | tf_op jit(solution)/shard_map/all_to_all | solution.py:82
  24.3 8.2 %collective-permute-done.7 = bf16[32,1024]{1,0:T(8,128)(2,1)S(1)} collective-permute-done((bf16[32,1024]{1,0:T(8,128)(2,1)S(1)}, bf16[32,1024]{1,0:T(8,128)(2,1)S(1)}, u32[]{:S(2)}, u32[]{:S(2)}) %collective-permute-start.7) | collective-permute-done | bytes 65568 | tf_op jit(solution)/shard_map/ppermute | solution.py:56
  32.5 4.6 %collective-permute-start.8 = (bf16[64,1024]{1,0:T(8,128)(2,1)S(1)}, bf16[64,1024]{1,0:T(8,128)(2,1)S(1)}, u32[]{:S(2)}, u32[]{:S(2)}) collective-permute-start(bf16[64,1024]{1,0:T(8,128)(2,1)S(1)} %pad_maximum_fusion.12), channel_id=1, source_target_pairs={{0,16},{1,17},{2,18},{3,19},{4,20},{5,21},{6,22},{7,23},{8,24},{9,... | collective-permute-start | bytes 393224 | tf_op jit(solution)/shard_map/ppermute | solution.py:56
  38.0 6.2 %collective-permute-done.8 = bf16[64,1024]{1,0:T(8,128)(2,1)S(1)} collective-permute-done((bf16[64,1024]{1,0:T(8,128)(2,1)S(1)}, bf16[64,1024]{1,0:T(8,128)(2,1)S(1)}, u32[]{:S(2)}, u32[]{:S(2)}) %collective-permute-start.8) | collective-permute-done | bytes 131104 | tf_op jit(solution)/shard_map/ppermute | solution.py:56
  45.2 6.5 %shard_map.313 = (bf16[1024,1024]{1,0:T(8,128)(2,1)}, bf16[1024,1024]{1,0:T(8,128)(2,1)}, bf16[1024,128]{1,0:T(8,128)(2,1)S(1)}, bf16[1024,256]{1,0:T(8,128)(2,1...) custom-call(s32[2]{0:T(128)S(1)} %pad_add_fusion.1.spot_ref.place_ref, bf16[128,1024]{1,0:T(8,128)(2,1)} %tokens_ref.3, ...), custom_call_target="tpu_custom_call" | custom-call | flops 805306368 | bytes 8847360 | tf_op jit(solution)/shard_map/pallas_call | solution.py:35
  51.7 2.1 collective-permute-start.11
  58.2 5.2 %all-to-all-start.1 = ((bf16[32,32,256]{2,1,0:T(8,128)(2,1)}), bf16[32,32,256]{2,1,0:T(8,128)(2,1)}, u32[]{:S(2)}, u32[]{:S(2)}) async-start(bf16[32,32,256]{2,1,0:T(8,128)(2,1)} %get-tuple-element.170), calls=%async_computation.1 | async-start | bytes 1048576 | tf_op jit(solution)/shard_map/all_to_all | solution.py:82
  65.8 2.4 collective-permute-start.15
  68.8 3.7 %collective-permute-done.12.after_ref = bf16[1024,256]{1,0:T(8,128)(2,1)} collective-permute-done((bf16[1024,256]{1,0:T(8,128)(2,1)}, bf16[1024,256]{1,0:T(8,128)(2,1)}, u32[]{:S(2)}, u32[]{:S(2)}) %collective-permute-start.12) | collective-permute-done | bytes 524320 | tf_op jit(solution)/shard_map/ppermute | solution.py:61
  72.5 10.0 %shard_map.314 = (f32[1024,128]{1,0:T(8,128)}, bf16[1024,128]{1,0:T(8,128)(2,1)}, f32[2,1024]{1,0:T(2,128)S(1)}) custom-call(s32[2,2]{1,0:T(2,128)S(1)} %pad_add_fusion.range_ref, bf16[1024,128]{1,0:T(8,128)(2,1)S(1)} %get-tuple-element.163.query_ref, bf16[1024,256]{1,0:T(8,128)(2,1)} %collective-permute-done.11.before_ref, ...), custom_call_target="tpu_custom_call" | custom-call | flops 5368709120 | bytes 2097152 | tf_op jit(solution)/shard_map/pallas_call | solution.py:376
  84.1 2.9 %all-to-all-done.1 = bf16[32,32,256]{2,1,0:T(8,128)(2,1)} async-done(((bf16[32,32,256]{2,1,0:T(8,128)(2,1)}), bf16[32,32,256]{2,1,0:T(8,128)(2,1)}, u32[]{:S(2)}, u32[]{:S(2)}) %all-to-all-start.1) | async-done | bytes 524320 | tf_op jit(solution)/shard_map/all_to_all | solution.py:82
  87.5 3.4 %all-to-all-start.2 = ((bf16[8,128,128]{2,1,0:T(8,128)(2,1)}), bf16[8,128,128]{2,1,0:T(8,128)(2,1)S(1)}, u32[]{:S(2)}, u32[]{:S(2)}) async-start(bf16[8,128,128]{2,1,0:T(8,128)(2,1)} %bitcast.21), calls=%async_computation.2 | async-start | bytes 524288 | tf_op jit(solution)/shard_map/all_to_all | solution.py:82
  91.2 3.1 %collective-permute-start.20 = (bf16[128,1024]{1,0:T(8,128)(2,1)S(1)}, bf16[128,1024]{1,0:T(8,128)(2,1)S(1)}, u32[]{:S(2)}, u32[]{:S(2)}) collective-permute-start(bf16[128,1024]{1,0:T(8,128)(2,1)S(1)} %convert_element_type.95.refs_10_.refs_0_), channel_id=1, source_target_pairs={{0,24},{1,25},{2,26},{3,27},{4,28},{5,29},{6,30},{7,31},{8,0},{9,1... | collective-permute-start | bytes 786440 | tf_op jit(solution)/shard_map/ppermute | solution.py:68
  94.3 3.5 %all-to-all-done.2.mixed_ref = bf16[8,128,128]{2,1,0:T(8,128)(2,1)S(1)} async-done(((bf16[8,128,128]{2,1,0:T(8,128)(2,1)}), bf16[8,128,128]{2,1,0:T(8,128)(2,1)S(1)}, u32[]{:S(2)}, u32[]{:S(2)}) %all-to-all-start.2) | async-done | bytes 262176 | tf_op jit(solution)/shard_map/all_to_all | solution.py:82
  97.8 3.0 %shard_map.315 = (f32[128,1024]{1,0:T(8,128)}, bf16[128,1024]{1,0:T(8,128)(2,1)S(1)}) custom-call(s32[2]{0:T(128)S(1)} %pad_add_fusion.1.spot_ref.place_ref, bf16[8,128,128]{2,1,0:T(8,128)(2,1)S(1)} %all-to-all-done.2.mixed_ref, bf16[128,1024]{1,0:T(8,128)(2,1)S(1)} %copy-done.1, f32[16,1024]{1,0:T(8,128)S(1)} %get-tuple-element.174.vector_ref, ...), custom_call_target="tpu_custom_call" | custom-call | flops 268435456 | bytes 3473408 | tf_op jit(solution)/shard_map/pallas_call | solution.py:35
  101.9 3.5 %all-to-all-start.3 = ((bf16[32,32,256]{2,1,0:T(8,128)(2,1)}), bf16[32,32,256]{2,1,0:T(8,128)(2,1)}, u32[]{:S(2)}, u32[]{:S(2)}) async-start(bf16[32,32,256]{2,1,0:T(8,128)(2,1)} %get-tuple-element.189), calls=%async_computation.3 | async-start | bytes 1048576 | tf_op jit(solution)/shard_map/all_to_all | solution.py:82
  106.5 2.0 collective-permute-done.17.refs_1_
  108.5 2.7 collective-permute-done.18.refs_2_
  113.1 6.0 %collective-permute-done.22.refs_3_ = bf16[64,1024]{1,0:T(8,128)(2,1)S(1)} collective-permute-done((bf16[64,1024]{1,0:T(8,128)(2,1)S(1)}, bf16[64,1024]{1,0:T(8,128)(2,1)S(1)}, u32[]{:S(2)}, u32[]{:S(2)}) %collective-permute-start.22) | collective-permute-done | bytes 131104 | tf_op jit(solution)/shard_map/ppermute | solution.py:56
  119.6 4.2 %all-to-all-done.3 = bf16[32,32,256]{2,1,0:T(8,128)(2,1)} async-done(((bf16[32,32,256]{2,1,0:T(8,128)(2,1)}), bf16[32,32,256]{2,1,0:T(8,128)(2,1)}, u32[]{:S(2)}, u32[]{:S(2)}) %all-to-all-start.3) | async-done | bytes 524320 | tf_op jit(solution)/shard_map/all_to_all | solution.py:82
  124.7 8.9 %shard_map.316 = (f32[4,128,1024]{2,1,0:T(8,128)}, bf16[3,128,1024]{2,1,0:T(8,128)(2,1)}, bf16[128,1024]{1,0:T(8,128)(2,1)S(1)}, bf16[1024,512]{1,0:T(8,128)(2,1...) custom-call(s32[2]{0:T(128)S(1)} %pad_add_fusion.1.spot_ref.place_ref, bf16[128,1024]{1,0:T(8,128)(2,1)} %copy-done.5, ...), custom_call_target="tpu_custom_call" | custom-call | flops 3221225472 | bytes 11538432 | tf_op jit(solution)/shard_map/pallas_call | solution.py:35
  134.1 4.1 %shard_map.317 = (bf16[128,1024]{1,0:T(8,128)(2,1)S(1)}, bf16[128,1024]{1,0:T(8,128)(2,1)S(1)}, bf16[128,1024]{1,0:T(8,128)(2,1)S(1)}, bf16[128,1024]{1,0:T(8,128)(2,1)}) custom-call(s32[2]{0:T(128)S(1)} %pad_add_fusion.1.spot_ref.place_ref, bf16[1024,512]{1,0:T(8,128)(2,1)} %get-tuple-element.193.active_ref, ...), custom_call_target="tpu_custom_call" | custom-call | flops 1073741824 | bytes 4194304 | tf_op jit(solution)/shard_map/pallas_call | solution.py:35
  138.2 4.6 %collective-permute-start.33 = (bf16[128,1024]{1,0:T(8,128)(2,1)S(1)}, bf16[128,1024]{1,0:T(8,128)(2,1)S(1)}, u32[]{:S(2)}, u32[]{:S(2)}) collective-permute-start(bf16[128,1024]{1,0:T(8,128)(2,1)S(1)} %get-tuple-element.194), channel_id=1, source_target_pairs={{0,8},{1,9},{2,10},{3,11},{4,12},{5,13},{6,14},{7,15},{8,16},{9,17... | collective-permute-start | bytes 786440 | tf_op jit(solution)/shard_map/ppermute | solution.py:68
  146.0 2.3 collective-permute-done.31
  153.1 2.6 collective-permute-done.32.three_ref
  156.3 4.1 %shard_map.318 = (f32[128,1024]{1,0:T(8,128)}, bf16[128,1024]{1,0:T(8,128)(2,1)S(1)}, bf16[8,128,128]{2,1,0:T(8,128)(2,1)}, f32[3,1024]{1,0:T(4,128)S(1)}) custom-call(s32[2]{0:T(128)S(1)} %pad_add_fusion.1.spot_ref.place_ref, f32[128,1024]{1,0:T(8,128)} %get-tuple-element.195.one_ref, bf16[128,1024]{1,0:T(8,128)(2,1)S(1)} %collective-permute-done.30.two_ref, ...), custom_call_target="tpu_custom_call" | custom-call | flops 268435456 | bytes 5058560 | tf_op jit(solution)/shard_map/pallas_call | solution.py:35
  162.5 3.4 %all-to-all-start.4 = ((bf16[8,128,128]{2,1,0:T(8,128)(2,1)}), bf16[8,128,128]{2,1,0:T(8,128)(2,1)S(1)}, u32[]{:S(2)}, u32[]{:S(2)}) async-start(bf16[8,128,128]{2,1,0:T(8,128)(2,1)} %get-tuple-element.199), calls=%async_computation.4 | async-start | bytes 524288 | tf_op jit(solution)/shard_map/all_to_all | solution.py:82
  165.9 3.9 %shard_map.319 = bf16[1024,512]{1,0:T(8,128)(2,1)} custom-call(bf16[1024,512]{1,0:T(8,128)(2,1)} %get-tuple-element.202.grad_ref, bf16[128,1024]{1,0:T(8,128)(2,1)S(1)} %copy-done.6, bf16[128,1024]{1,0:T(8,128)(2,1)} %copy-done.28, bf16[128,1024]{1,0:T(8,128)(2,1)} %copy-done.29, bf16[64,1024]{1,0:T(8,128)(2,1)S(1)} %collective-permute-done.22.refs_3_, ...), custom_call_target="tpu_custom_call" | custom-call | flops 1073741824 | bytes 4194304 | tf_op jit(solution)/shard_map/pallas_call | solution.py:35
  170.5 2.3 all-to-all-done.4
  172.8 2.9 %all-to-all-start.5 = ((bf16[32,32,512]{2,1,0:T(8,128)(2,1)}), bf16[32,32,512]{2,1,0:T(8,128)(2,1)S(1)}, u32[]{:S(2)}, u32[]{:S(2)}) async-start(bf16[32,32,512]{2,1,0:T(8,128)(2,1)} %bitcast.97), calls=%async_computation.5 | async-start | bytes 2097152 | tf_op jit(solution)/shard_map/all_to_all | solution.py:82
  178.7 13.1 %shard_map.320 = (bf16[1024,128]{1,0:T(8,128)(2,1)S(1)}, bf16[1024,256]{1,0:T(8,128)(2,1)}, f32[1024,256]{1,0:T(8,128)}, bf16[1024,256]{1,0:T(8,128)(2,1)}) custom-call(s32[2,2]{1,0:T(2,128)S(1)} %pad_add_fusion.range_ref, bf16[1024,128]{1,0:T(8,128)(2,1)S(1)} %get-tuple-element.163.query_ref, bf16[1024,256]{1,0:T(8,128)(2,1)} %collective-permute-done.11.before_ref, ...), custom_call_target="tpu_custom_call" | custom-call | flops 8053063680 | bytes 4194304 | tf_op jit(solution)/shard_map/pallas_call | solution.py:399
  193.3 6.8 %collective-permute-start.41 = (bf16[1024,256]{1,0:T(8,128)(2,1)}, bf16[1024,256]{1,0:T(8,128)(2,1)}, u32[]{:S(2)}, u32[]{:S(2)}) collective-permute-start(bf16[1024,256]{1,0:T(8,128)(2,1)} %get-tuple-element.212), channel_id=1, source_target_pairs={{0,8},{1,9},{2,10},{3,11},{4,12},{5,13},{6,14},{7,15},{8,16},{9,17... | collective-permute-start | bytes 1572872 | tf_op jit(solution)/shard_map/ppermute | solution.py:61
  200.1 2.0 convert_add_fusion.2.refs_0_.refs_18_
  203.0 2.1 shard_map.321
  206.2 2.3 shard_map.322
  209.3 2.5 collective-permute-done.40.from_after_ref
  212.5 5.8 %collective-permute-start.44 = (bf16[64,1024]{1,0:T(8,128)(2,1)S(1)}, bf16[64,1024]{1,0:T(8,128)(2,1)S(1)}, u32[]{:S(2)}, u32[]{:S(2)}) collective-permute-start(bf16[64,1024]{1,0:T(8,128)(2,1)S(1)} %get-tuple-element.240), channel_id=1, source_target_pairs={{0,2},{1,6},{2,10},{3,14},{4,18},{5,22},{6,26},{7,30},{8,3},{9,7},... | collective-permute-start | bytes 393224 | tf_op jit(solution)/shard_map/ppermute | solution.py:953
  218.3 9.9 %shard_map.323 = (bf16[32,104,128]{2,1,0:T(8,128)(2,1)}, f32[4,256,1024]{2,1,0:T(8,128)}, bf16[3,256,1024]{2,1,0:T(8,128)(2,1)}, bf16[256,1024]{1,0:T(8,128)(2,1)}, f32[2,1024]{1,0:T(2,128)}) custom-call(s32[2]{0:T(128)S(1)} %pad_add_fusion.1.spot_ref.place_ref, f32[1024,256]{1,0:T(8,128)} %get-tuple-element.226.own_ref, bf16[1024,256]{1,0:T(8,128)(2,1)} %copy-done.33, ...), custom_call_target="tpu_custom_call" | custom-call | flops 1610612736 | bytes 16603136 | tf_op jit(solution)/shard_map/pallas_call | solution.py:35
  228.2 2.4 collective-permute-done.44
  230.6 1.8 collective-permute-start.46
  232.5 8.0 %all-to-all-start.6 = ((bf16[32,104,128]{2,1,0:T(8,128)(2,1)}), bf16[32,104,128]{2,1,0:T(8,128)(2,1)S(1)}, u32[]{:S(2)}, u32[]{:S(2)}) async-start(bf16[32,104,128]{2,1,0:T(8,128)(2,1)} %get-tuple-element.243), calls=%async_computation.6 | async-start | bytes 1703936 | tf_op jit(solution)/shard_map/all_to_all | solution.py:82
  245.3 3.9 %convert_add_fusion = (f32[1,256,1024]{2,1,0:T(8,128)S(1)}, f32[1,256,1024]{2,1,0:T(8,128)S(1)}, f32[256,1024]{1,0:T(8,128)}) fusion(f32[4,256,1024]{2,1,0:T(8,128)} %get-tuple-element.245, bf16[3,256,1024]{2,1,0:T(8,128)(2,1)} %collective-permute-done.46), kind=kLoop, calls=%fused_computation.4 | loop fusion | flops 1572864 | bytes 7864320 | tf_op jit(solution)/shard_map/add | solution.py:134
  249.2 7.8 %collective-permute-done.50 = bf16[128,1024]{1,0:T(8,128)(2,1)S(1)} collective-permute-done((bf16[128,1024]{1,0:T(8,128)(2,1)S(1)}, bf16[128,1024]{1,0:T(8,128)(2,1)S(1)}, u32[]{:S(2)}, u32[]{:S(2)}) %collective-permute-start.50) | collective-permute-done | bytes 262176 | tf_op jit(solution)/shard_map/ppermute | solution.py:56
  263.5 2.8 shard_map.324
  267.0 3.6 %all-to-all-start.7 = ((f32[32,1,128]{2,1,0:T(1,128)}), f32[32,1,128]{2,1,0:T(1,128)S(1)}, u32[]{:S(2)}, u32[]{:S(2)}) async-start(f32[32,1,128]{2,1,0:T(1,128)} %get-tuple-element.244), calls=%async_computation.7 | async-start | bytes 32768 | tf_op jit(solution)/shard_map/all_to_all | solution.py:82
  273.0 3.0 %shard_map.325 = (bf16[128,1024]{1,0:T(8,128)(2,1)}, bf16[128,1024]{1,0:T(8,128)(2,1)}) custom-call(f32[256,1024]{1,0:T(8,128)} %get-tuple-element.280.one_ref, bf16[256,1024]{1,0:T(8,128)(2,1)S(1)} %collective-permute-done.49.two_ref, bf16[256,1024]{1,0:T(8,128)(2,1)} %collective-permute-done.51.three_ref, bf16[128,1024]{1,0:T(8,128)(2,1)S(1)} %copy-done.1, ...), custom_call_target="tpu_custom_call" | custom-call | bytes 3997696 | tf_op jit(solution)/shard_map/pallas_call | solution.py:35
  277.7 5.2 %shard_map.326 = (f32[32,3072]{1,0:T(8,128)}, f32[32,3072]{1,0:T(8,128)}, f32[32,3072]{1,0:T(8,128)}, f32[32,1024]{1,0:T(8,128)}, f32[32,1024]{1,0:T(8,128)}, /*...) custom-call(f32[32,1,128]{2,1,0:T(1,128)S(1)} %all-to-all-done.7.squ, ...), custom_call_target="tpu_custom_call" | custom-call | bytes 11034500 | tf_op jit(solution)/shard_map/pallas_call | solution.py:35
  (248 shorter events, 68.4 us)
Async XLA Ops:
  0.7 9.5 %collective-permute-start = (bf16[128,1024]{1,0:T(8,128)(2,1)}, bf16[128,1024]{1,0:T(8,128)(2,1)S(1)}, u32[]{:S(2)}, u32[]{:S(2)}) collective-permute-start(bf16[128,1024]{1,0:T(8,128)(2,1)} %tokens_ref.3), channel_id=1, source_target_pairs={{0,2},{1,3},{2,0},{3,1},{4,6},{5,7},{6,4},{7,5},{8,10},{9,11},{10,... | collective-permute-start | bytes 786440 | tf_op jit(solution)/shard_map/ppermute | solution.py:56
  3.7 8.0 %collective-permute-start.1 = (bf16[128,1024]{1,0:T(8,128)(2,1)}, bf16[128,1024]{1,0:T(8,128)(2,1)S(1)}, u32[]{:S(2)}, u32[]{:S(2)}) collective-permute-start(bf16[128,1024]{1,0:T(8,128)(2,1)} %tokens_ref.3), channel_id=1, source_target_pairs={{0,4},{1,5},{2,6},{3,7},{4,0},{5,1},{6,2},{7,3},{8,12},{9,13},{10,... | collective-permute-start | bytes 786440 | tf_op jit(solution)/shard_map/ppermute | solution.py:56
  11.6 32.6 %all-to-all-start = ((bf16[32,104,128]{2,1,0:T(8,128)(2,1)}), bf16[32,104,128]{2,1,0:T(8,128)(2,1)S(1)}, u32[]{:S(2)}, u32[]{:S(2)}) async-start(bf16[32,104,128]{2,1,0:T(8,128)(2,1)} %pad_maximum_fusion.2), calls=%async_computation | async-start | bytes 1703936 | tf_op jit(solution)/shard_map/all_to_all | solution.py:82
  19.3 25.0 %collective-permute-start.4 = (bf16[3,128,1024]{2,1,0:T(8,128)(2,1)}, bf16[3,128,1024]{2,1,0:T(8,128)(2,1)}, u32[]{:S(2)}, u32[]{:S(2)}) collective-permute-start(bf16[3,128,1024]{2,1,0:T(8,128)(2,1)} %pad_maximum_fusion.3), channel_id=1, source_target_pairs={{0,1},{1,0},{2,3},{3,2},{4,5},{5,4},{6,7},{7,6},{8,9},{9,8},{10,11... | collective-permute-start | bytes 2359304 | tf_op jit(solution)/shard_map/ppermute | solution.py:56
  19.5 12.9 %collective-permute-start.7 = (bf16[32,1024]{1,0:T(8,128)(2,1)S(1)}, bf16[32,1024]{1,0:T(8,128)(2,1)S(1)}, u32[]{:S(2)}, u32[]{:S(2)}) collective-permute-start(bf16[32,1024]{1,0:T(8,128)(2,1)S(1)} %convert_element_type.96), channel_id=1, source_target_pairs={{0,8},{1,9},{2,10},{3,11},{4,12},{5,13},{6,14},{7,15},{8,0},{9,1},... | collective-permute-start | bytes 196616 | tf_op jit(solution)/shard_map/ppermute | solution.py:56
  21.2 15.9 %collective-permute-start.2 = (bf16[64,1024]{1,0:T(8,128)(2,1)S(1)}, bf16[64,1024]{1,0:T(8,128)(2,1)S(1)}, u32[]{:S(2)}, u32[]{:S(2)}) collective-permute-start(bf16[64,1024]{1,0:T(8,128)(2,1)S(1)} %slice.214), channel_id=1, source_target_pairs={{0,4},{1,5},{2,6},{3,7},{4,0},{5,1},{6,2},{7,3},{8,12},{9,13},{10,... | collective-permute-start | bytes 393224 | tf_op jit(solution)/shard_map/ppermute | solution.py:56
  22.8 14.4 %collective-permute-start.3 = (bf16[64,1024]{1,0:T(8,128)(2,1)S(1)}, bf16[64,1024]{1,0:T(8,128)(2,1)S(1)}, u32[]{:S(2)}, u32[]{:S(2)}) collective-permute-start(bf16[64,1024]{1,0:T(8,128)(2,1)S(1)} %slice.215), channel_id=1, source_target_pairs={{0,2},{1,3},{2,0},{3,1},{4,6},{5,7},{6,4},{7,5},{8,10},{9,11},{10,... | collective-permute-start | bytes 393224 | tf_op jit(solution)/shard_map/ppermute | solution.py:56
  32.5 11.7 %collective-permute-start.8 = (bf16[64,1024]{1,0:T(8,128)(2,1)S(1)}, bf16[64,1024]{1,0:T(8,128)(2,1)S(1)}, u32[]{:S(2)}, u32[]{:S(2)}) collective-permute-start(bf16[64,1024]{1,0:T(8,128)(2,1)S(1)} %pad_maximum_fusion.12), channel_id=1, source_target_pairs={{0,16},{1,17},{2,18},{3,19},{4,20},{5,21},{6,22},{7,23},{8,24},{9,... | collective-permute-start | bytes 393224 | tf_op jit(solution)/shard_map/ppermute | solution.py:56
  51.7 17.1 %collective-permute-start.11 = (bf16[1024,256]{1,0:T(8,128)(2,1)}, bf16[1024,256]{1,0:T(8,128)(2,1)}, u32[]{:S(2)}, u32[]{:S(2)}) collective-permute-start(bf16[1024,256]{1,0:T(8,128)(2,1)} %get-tuple-element.160.own_ref), channel_id=1, source_target_pairs={{0,8},{1,9},{2,10},{3,11},{4,12},{5,13},{6,14},{7,15},{8,16},{9,17... | collective-permute-start | bytes 1572872 | tf_op jit(solution)/shard_map/ppermute | solution.py:61
  53.8 18.7 %collective-permute-start.12 = (bf16[1024,256]{1,0:T(8,128)(2,1)}, bf16[1024,256]{1,0:T(8,128)(2,1)}, u32[]{:S(2)}, u32[]{:S(2)}) collective-permute-start(bf16[1024,256]{1,0:T(8,128)(2,1)} %get-tuple-element.160.own_ref), channel_id=1, source_target_pairs={{8,0},{9,1},{10,2},{11,3},{12,4},{13,5},{14,6},{15,7},{16,8},{17,9... | collective-permute-start | bytes 1572872 | tf_op jit(solution)/shard_map/ppermute | solution.py:61
  55.1 8.2 %collective-permute-start.10 = (bf16[128,1024]{1,0:T(8,128)(2,1)S(1)}, bf16[128,1024]{1,0:T(8,128)(2,1)S(1)}, u32[]{:S(2)}, u32[]{:S(2)}) collective-permute-start(bf16[128,1024]{1,0:T(8,128)(2,1)S(1)} %copy-done.31), channel_id=1, source_target_pairs={{0,2},{1,3},{2,0},{3,1},{4,6},{5,7},{6,4},{7,5},{8,10},{9,11},{10,... | collective-permute-start | bytes 786440 | tf_op jit(solution)/shard_map/ppermute | solution.py:56
  58.2 28.9 %all-to-all-start.1 = ((bf16[32,32,256]{2,1,0:T(8,128)(2,1)}), bf16[32,32,256]{2,1,0:T(8,128)(2,1)}, u32[]{:S(2)}, u32[]{:S(2)}) async-start(bf16[32,32,256]{2,1,0:T(8,128)(2,1)} %get-tuple-element.170), calls=%async_computation.1 | async-start | bytes 1048576 | tf_op jit(solution)/shard_map/all_to_all | solution.py:82
  64.2 18.3 %collective-permute-start.14 = (bf16[256,1024]{1,0:T(8,128)(2,1)S(1)}, bf16[256,1024]{1,0:T(8,128)(2,1)S(1)}, u32[]{:S(2)}, u32[]{:S(2)}) collective-permute-start(bf16[256,1024]{1,0:T(8,128)(2,1)S(1)} %pad_maximum_fusion.6), channel_id=1, source_target_pairs={{0,4},{1,5},{2,6},{3,7},{4,0},{5,1},{6,2},{7,3},{8,12},{9,13},{10,... | collective-permute-start | bytes 1572872 | tf_op jit(solution)/shard_map/ppermute | solution.py:56
  65.8 18.3 %collective-permute-start.15 = (bf16[128,1024]{1,0:T(8,128)(2,1)S(1)}, bf16[128,1024]{1,0:T(8,128)(2,1)S(1)}, u32[]{:S(2)}, u32[]{:S(2)}) collective-permute-start(bf16[128,1024]{1,0:T(8,128)(2,1)S(1)} %convert_element_type.95.refs_10_.refs_0_), channel_id=1, source_target_pairs={{0,8},{1,9},{2,10},{3,11},{4,12},{5,13},{6,14},{7,15},{8,16},{9,17... | collective-permute-start | bytes 786440 | tf_op jit(solution)/shard_map/ppermute | solution.py:68
  68.2 15.8 %collective-permute-start.13 = (bf16[256,1024]{1,0:T(8,128)(2,1)S(1)}, bf16[256,1024]{1,0:T(8,128)(2,1)S(1)}, u32[]{:S(2)}, u32[]{:S(2)}) collective-permute-start(bf16[256,1024]{1,0:T(8,128)(2,1)S(1)} %pad_maximum_fusion.5), channel_id=1, source_target_pairs={{0,2},{1,3},{2,0},{3,1},{4,6},{5,7},{6,4},{7,5},{8,10},{9,11},{10,... | collective-permute-start | bytes 1572872 | tf_op jit(solution)/shard_map/ppermute | solution.py:56
  87.0 10.8 %collective-permute-start.16 = (bf16[512,1024]{1,0:T(8,128)(2,1)S(1)}, bf16[512,1024]{1,0:T(8,128)(2,1)}, u32[]{:S(2)}, u32[]{:S(2)}) collective-permute-start(bf16[512,1024]{1,0:T(8,128)(2,1)S(1)} %pad_maximum_fusion.refs_0_), channel_id=1, source_target_pairs={{0,1},{1,0},{2,3},{3,2},{4,5},{5,4},{6,7},{7,6},{8,9},{9,8},{10,11... | collective-permute-start | bytes 3145736 | tf_op jit(solution)/shard_map/ppermute | solution.py:56
  87.0 19.5 %collective-permute-start.21 = (bf16[512,1024]{1,0:T(8,128)(2,1)}, bf16[512,1024]{1,0:T(8,128)(2,1)}, u32[]{:S(2)}, u32[]{:S(2)}) collective-permute-start(bf16[512,1024]{1,0:T(8,128)(2,1)} %pad_maximum_fusion.1.refs_8_.refs_0_), channel_id=1, source_target_pairs={{0,1},{1,0},{2,3},{3,2},{4,5},{5,4},{6,7},{7,6},{8,9},{9,8},{10,11... | collective-permute-start | bytes 3145736 | tf_op jit(solution)/shard_map/ppermute | solution.py:56
  87.5 10.3 %all-to-all-start.2 = ((bf16[8,128,128]{2,1,0:T(8,128)(2,1)}), bf16[8,128,128]{2,1,0:T(8,128)(2,1)S(1)}, u32[]{:S(2)}, u32[]{:S(2)}) async-start(bf16[8,128,128]{2,1,0:T(8,128)(2,1)} %bitcast.21), calls=%async_computation.2 | async-start | bytes 524288 | tf_op jit(solution)/shard_map/all_to_all | solution.py:82
  91.0 15.5 %collective-permute-start.19 = (bf16[128,1024]{1,0:T(8,128)(2,1)S(1)}, bf16[128,1024]{1,0:T(8,128)(2,1)S(1)}, u32[]{:S(2)}, u32[]{:S(2)}) collective-permute-start(bf16[128,1024]{1,0:T(8,128)(2,1)S(1)} %convert_element_type.95.refs_10_.refs_0_), channel_id=1, source_target_pairs={{0,16},{1,17},{2,18},{3,19},{4,20},{5,21},{6,22},{7,23},{8,24},{9,... | collective-permute-start | bytes 786440 | tf_op jit(solution)/shard_map/ppermute | solution.py:68
  91.2 15.3 %collective-permute-start.20 = (bf16[128,1024]{1,0:T(8,128)(2,1)S(1)}, bf16[128,1024]{1,0:T(8,128)(2,1)S(1)}, u32[]{:S(2)}, u32[]{:S(2)}) collective-permute-start(bf16[128,1024]{1,0:T(8,128)(2,1)S(1)} %convert_element_type.95.refs_10_.refs_0_), channel_id=1, source_target_pairs={{0,24},{1,25},{2,26},{3,27},{4,28},{5,29},{6,30},{7,31},{8,0},{9,1... | collective-permute-start | bytes 786440 | tf_op jit(solution)/shard_map/ppermute | solution.py:68
  100.8 7.7 %collective-permute-start.17 = (bf16[128,1024]{1,0:T(8,128)(2,1)S(1)}, bf16[128,1024]{1,0:T(8,128)(2,1)S(1)}, u32[]{:S(2)}, u32[]{:S(2)}) collective-permute-start(bf16[128,1024]{1,0:T(8,128)(2,1)S(1)} %get-tuple-element.176.refs_0_), channel_id=1, source_target_pairs={{0,2},{1,3},{2,0},{3,1},{4,6},{5,7},{6,4},{7,5},{8,10},{9,11},{10,... | collective-permute-start | bytes 786440 | tf_op jit(solution)/shard_map/ppermute | solution.py:56
  101.4 9.8 %collective-permute-start.18 = (bf16[128,1024]{1,0:T(8,128)(2,1)S(1)}, bf16[128,1024]{1,0:T(8,128)(2,1)S(1)}, u32[]{:S(2)}, u32[]{:S(2)}) collective-permute-start(bf16[128,1024]{1,0:T(8,128)(2,1)S(1)} %get-tuple-element.176.refs_0_), channel_id=1, source_target_pairs={{0,4},{1,5},{2,6},{3,7},{4,0},{5,1},{6,2},{7,3},{8,12},{9,13},{10,... | collective-permute-start | bytes 786440 | tf_op jit(solution)/shard_map/ppermute | solution.py:56
  101.9 21.8 %all-to-all-start.3 = ((bf16[32,32,256]{2,1,0:T(8,128)(2,1)}), bf16[32,32,256]{2,1,0:T(8,128)(2,1)}, u32[]{:S(2)}, u32[]{:S(2)}) async-start(bf16[32,32,256]{2,1,0:T(8,128)(2,1)} %get-tuple-element.189), calls=%async_computation.3 | async-start | bytes 1048576 | tf_op jit(solution)/shard_map/all_to_all | solution.py:82
  112.1 11.6 %collective-permute-start.24 = (bf16[3,128,1024]{2,1,0:T(8,128)(2,1)}, bf16[3,128,1024]{2,1,0:T(8,128)(2,1)S(1)}, u32[]{:S(2)}, u32[]{:S(2)}) collective-permute-start(bf16[3,128,1024]{2,1,0:T(8,128)(2,1)} %pad_maximum_fusion.4), channel_id=1, source_target_pairs={{0,1},{1,0},{2,3},{3,2},{4,5},{5,4},{6,7},{7,6},{8,9},{9,8},{10,11... | collective-permute-start | bytes 2359304 | tf_op jit(solution)/shard_map/ppermute | solution.py:56
  133.6 11.3 %collective-permute-start.27 = (bf16[3,128,1024]{2,1,0:T(8,128)(2,1)}, bf16[3,128,1024]{2,1,0:T(8,128)(2,1)S(1)}, u32[]{:S(2)}, u32[]{:S(2)}) collective-permute-start(bf16[3,128,1024]{2,1,0:T(8,128)(2,1)} %get-tuple-element.191), channel_id=1, source_target_pairs={{0,1},{1,0},{2,3},{3,2},{4,5},{5,4},{6,7},{7,6},{8,9},{9,8},{10,11... | collective-permute-start | bytes 2359304 | tf_op jit(solution)/shard_map/ppermute | solution.py:56
  133.6 9.2 %collective-permute-start.28 = (bf16[128,1024]{1,0:T(8,128)(2,1)S(1)}, bf16[128,1024]{1,0:T(8,128)(2,1)S(1)}, u32[]{:S(2)}, u32[]{:S(2)}) collective-permute-start(bf16[128,1024]{1,0:T(8,128)(2,1)S(1)} %get-tuple-element.192), channel_id=1, source_target_pairs={{0,1},{1,0},{2,3},{3,2},{4,5},{5,4},{6,7},{7,6},{8,9},{9,8},{10,11... | collective-permute-start | bytes 786440 | tf_op jit(solution)/shard_map/ppermute | solution.py:56
  138.2 14.8 %collective-permute-start.33 = (bf16[128,1024]{1,0:T(8,128)(2,1)S(1)}, bf16[128,1024]{1,0:T(8,128)(2,1)S(1)}, u32[]{:S(2)}, u32[]{:S(2)}) collective-permute-start(bf16[128,1024]{1,0:T(8,128)(2,1)S(1)} %get-tuple-element.194), channel_id=1, source_target_pairs={{0,8},{1,9},{2,10},{3,11},{4,12},{5,13},{6,14},{7,15},{8,16},{9,17... | collective-permute-start | bytes 786440 | tf_op jit(solution)/shard_map/ppermute | solution.py:68
  150.4 20.1 %collective-permute-start.36 = (bf16[128,1024]{1,0:T(8,128)(2,1)S(1)}, bf16[128,1024]{1,0:T(8,128)(2,1)}, u32[]{:S(2)}, u32[]{:S(2)}) collective-permute-start(bf16[128,1024]{1,0:T(8,128)(2,1)S(1)} %get-tuple-element.204), channel_id=1, source_target_pairs={{0,16},{1,17},{2,18},{3,19},{4,20},{5,21},{6,22},{7,23},{8,24},{9,... | collective-permute-start | bytes 786440 | tf_op jit(solution)/shard_map/ppermute | solution.py:68
  151.9 18.5 %collective-permute-start.37 = (bf16[128,1024]{1,0:T(8,128)(2,1)}, bf16[128,1024]{1,0:T(8,128)(2,1)}, u32[]{:S(2)}, u32[]{:S(2)}) collective-permute-start(bf16[128,1024]{1,0:T(8,128)(2,1)} %get-tuple-element.205), channel_id=1, source_target_pairs={{0,24},{1,25},{2,26},{3,27},{4,28},{5,29},{6,30},{7,31},{8,0},{9,1... | collective-permute-start | bytes 786440 | tf_op jit(solution)/shard_map/ppermute | solution.py:68
  160.4 12.4 %collective-permute-start.34 = (bf16[128,1024]{1,0:T(8,128)(2,1)S(1)}, bf16[128,1024]{1,0:T(8,128)(2,1)S(1)}, u32[]{:S(2)}, u32[]{:S(2)}) collective-permute-start(bf16[128,1024]{1,0:T(8,128)(2,1)S(1)} %get-tuple-element.201), channel_id=1, source_target_pairs={{0,2},{1,3},{2,0},{3,1},{4,6},{5,7},{6,4},{7,5},{8,10},{9,11},{10,... | collective-permute-start | bytes 786440 | tf_op jit(solution)/shard_map/ppermute | solution.py:56
  161.4 11.4 %collective-permute-start.35 = (bf16[128,1024]{1,0:T(8,128)(2,1)S(1)}, bf16[128,1024]{1,0:T(8,128)(2,1)S(1)}, u32[]{:S(2)}, u32[]{:S(2)}) collective-permute-start(bf16[128,1024]{1,0:T(8,128)(2,1)S(1)} %get-tuple-element.201), channel_id=1, source_target_pairs={{0,4},{1,5},{2,6},{3,7},{4,0},{5,1},{6,2},{7,3},{8,12},{9,13},{10,... | collective-permute-start | bytes 786440 | tf_op jit(solution)/shard_map/ppermute | solution.py:56
  162.5 10.3 %all-to-all-start.4 = ((bf16[8,128,128]{2,1,0:T(8,128)(2,1)}), bf16[8,128,128]{2,1,0:T(8,128)(2,1)S(1)}, u32[]{:S(2)}, u32[]{:S(2)}) async-start(bf16[8,128,128]{2,1,0:T(8,128)(2,1)} %get-tuple-element.199), calls=%async_computation.4 | async-start | bytes 524288 | tf_op jit(solution)/shard_map/all_to_all | solution.py:82
  172.8 32.4 %all-to-all-start.5 = ((bf16[32,32,512]{2,1,0:T(8,128)(2,1)}), bf16[32,32,512]{2,1,0:T(8,128)(2,1)S(1)}, u32[]{:S(2)}, u32[]{:S(2)}) async-start(bf16[32,32,512]{2,1,0:T(8,128)(2,1)} %bitcast.97), calls=%async_computation.5 | async-start | bytes 2097152 | tf_op jit(solution)/shard_map/all_to_all | solution.py:82
  175.7 16.2 %collective-permute-start.38 = (bf16[64,1024]{1,0:T(8,128)(2,1)S(1)}, bf16[64,1024]{1,0:T(8,128)(2,1)S(1)}, u32[]{:S(2)}, u32[]{:S(2)}) collective-permute-start(bf16[64,1024]{1,0:T(8,128)(2,1)S(1)} %slice.194), channel_id=1, source_target_pairs={{0,4},{1,5},{2,6},{3,7},{4,0},{5,1},{6,2},{7,3},{8,12},{9,13},{10,... | collective-permute-start | bytes 393224 | tf_op jit(solution)/shard_map/ppermute | solution.py:56
  177.2 14.7 %collective-permute-start.39 = (bf16[64,1024]{1,0:T(8,128)(2,1)S(1)}, bf16[64,1024]{1,0:T(8,128)(2,1)S(1)}, u32[]{:S(2)}, u32[]{:S(2)}) collective-permute-start(bf16[64,1024]{1,0:T(8,128)(2,1)S(1)} %slice.195), channel_id=1, source_target_pairs={{0,2},{1,3},{2,0},{3,1},{4,6},{5,7},{6,4},{7,5},{8,10},{9,11},{10,... | collective-permute-start | bytes 393224 | tf_op jit(solution)/shard_map/ppermute | solution.py:56
  191.9 10.1 %collective-permute-start.42 = (bf16[512,1024]{1,0:T(8,128)(2,1)S(1)}, bf16[512,1024]{1,0:T(8,128)(2,1)S(1)}, u32[]{:S(2)}, u32[]{:S(2)}) collective-permute-start(bf16[512,1024]{1,0:T(8,128)(2,1)S(1)} %constant_dynamic-update-slice_fusion.refs_0_), channel_id=1, source_target_pairs={{0,1},{1,0},{2,3},{3,2},{4,5},{5,4},{6,7},{7,6},{8,9},{9,8},{10,11... | collective-permute-start | bytes 3145736 | tf_op jit(solution)/shard_map/ppermute | solution.py:56
  192.0 19.8 %collective-permute-start.40 = (bf16[1024,256]{1,0:T(8,128)(2,1)}, bf16[1024,256]{1,0:T(8,128)(2,1)S(1)}, u32[]{:S(2)}, u32[]{:S(2)}) collective-permute-start(bf16[1024,256]{1,0:T(8,128)(2,1)} %get-tuple-element.211), channel_id=1, source_target_pairs={{8,0},{9,1},{10,2},{11,3},{12,4},{13,5},{14,6},{15,7},{16,8},{17,9... | collective-permute-start | bytes 1572872 | tf_op jit(solution)/shard_map/ppermute | solution.py:61
  193.3 18.5 %collective-permute-start.41 = (bf16[1024,256]{1,0:T(8,128)(2,1)}, bf16[1024,256]{1,0:T(8,128)(2,1)}, u32[]{:S(2)}, u32[]{:S(2)}) collective-permute-start(bf16[1024,256]{1,0:T(8,128)(2,1)} %get-tuple-element.212), channel_id=1, source_target_pairs={{0,8},{1,9},{2,10},{3,11},{4,12},{5,13},{6,14},{7,15},{8,16},{9,17... | collective-permute-start | bytes 1572872 | tf_op jit(solution)/shard_map/ppermute | solution.py:61
  211.8 16.4 %collective-permute-start.43 = (bf16[64,1024]{1,0:T(8,128)(2,1)S(1)}, bf16[64,1024]{1,0:T(8,128)(2,1)S(1)}, u32[]{:S(2)}, u32[]{:S(2)}) collective-permute-start(bf16[64,1024]{1,0:T(8,128)(2,1)S(1)} %get-tuple-element.239), channel_id=1, source_target_pairs={{0,0},{1,4},{2,8},{3,12},{4,16},{5,20},{6,24},{7,28},{8,1},{9,5},{... | collective-permute-start | bytes 393224 | tf_op jit(solution)/shard_map/ppermute | solution.py:953
  212.5 18.1 %collective-permute-start.44 = (bf16[64,1024]{1,0:T(8,128)(2,1)S(1)}, bf16[64,1024]{1,0:T(8,128)(2,1)S(1)}, u32[]{:S(2)}, u32[]{:S(2)}) collective-permute-start(bf16[64,1024]{1,0:T(8,128)(2,1)S(1)} %get-tuple-element.240), channel_id=1, source_target_pairs={{0,2},{1,6},{2,10},{3,14},{4,18},{5,22},{6,26},{7,30},{8,3},{9,7},... | collective-permute-start | bytes 393224 | tf_op jit(solution)/shard_map/ppermute | solution.py:953
  230.6 14.7 %collective-permute-start.46 = (bf16[3,256,1024]{2,1,0:T(8,128)(2,1)}, bf16[3,256,1024]{2,1,0:T(8,128)(2,1)}, u32[]{:S(2)}, u32[]{:S(2)}) collective-permute-start(bf16[3,256,1024]{2,1,0:T(8,128)(2,1)} %get-tuple-element.246), channel_id=1, source_target_pairs={{0,1},{1,0},{2,3},{3,2},{4,5},{5,4},{6,7},{7,6},{8,9},{9,8},{10,11... | collective-permute-start | bytes 4718600 | tf_op jit(solution)/shard_map/ppermute | solution.py:56
  232.4 8.1 %collective-permute-start.47 = (bf16[256,1024]{1,0:T(8,128)(2,1)}, bf16[256,1024]{1,0:T(8,128)(2,1)S(1)}, u32[]{:S(2)}, u32[]{:S(2)}) collective-permute-start(bf16[256,1024]{1,0:T(8,128)(2,1)} %get-tuple-element.247), channel_id=1, source_target_pairs={{0,1},{1,0},{2,3},{3,2},{4,5},{5,4},{6,7},{7,6},{8,9},{9,8},{10,11... | collective-permute-start | bytes 1572872 | tf_op jit(solution)/shard_map/ppermute | solution.py:56
  232.5 30.0 %all-to-all-start.6 = ((bf16[32,104,128]{2,1,0:T(8,128)(2,1)}), bf16[32,104,128]{2,1,0:T(8,128)(2,1)S(1)}, u32[]{:S(2)}, u32[]{:S(2)}) async-start(bf16[32,104,128]{2,1,0:T(8,128)(2,1)} %get-tuple-element.243), calls=%async_computation.6 | async-start | bytes 1703936 | tf_op jit(solution)/shard_map/all_to_all | solution.py:82
  242.0 15.0 %collective-permute-start.50 = (bf16[128,1024]{1,0:T(8,128)(2,1)S(1)}, bf16[128,1024]{1,0:T(8,128)(2,1)S(1)}, u32[]{:S(2)}, u32[]{:S(2)}) collective-permute-start(bf16[128,1024]{1,0:T(8,128)(2,1)S(1)} %get-tuple-element.286), channel_id=1, source_target_pairs={{0,2},{1,3},{2,0},{3,1},{4,6},{5,7},{6,4},{7,5},{8,10},{9,11},{10,... | collective-permute-start | bytes 786440 | tf_op jit(solution)/shard_map/ppermute | solution.py:56
  243.8 14.6 %collective-permute-start.48 = (bf16[128,1024]{1,0:T(8,128)(2,1)S(1)}, bf16[128,1024]{1,0:T(8,128)(2,1)S(1)}, u32[]{:S(2)}, u32[]{:S(2)}) collective-permute-start(bf16[128,1024]{1,0:T(8,128)(2,1)S(1)} %get-tuple-element.287), channel_id=1, source_target_pairs={{0,4},{1,5},{2,6},{3,7},{4,0},{5,1},{6,2},{7,3},{8,12},{9,13},{10,... | collective-permute-start | bytes 786440 | tf_op jit(solution)/shard_map/ppermute | solution.py:56
  257.1 14.8 %collective-permute-start.51 = (bf16[256,1024]{1,0:T(8,128)(2,1)S(1)}, bf16[256,1024]{1,0:T(8,128)(2,1)}, u32[]{:S(2)}, u32[]{:S(2)}) collective-permute-start(bf16[256,1024]{1,0:T(8,128)(2,1)S(1)} %pad_maximum_fusion.8), channel_id=1, source_target_pairs={{0,4},{1,5},{2,6},{3,7},{4,0},{5,1},{6,2},{7,3},{8,12},{9,13},{10,... | collective-permute-start | bytes 1572872 | tf_op jit(solution)/shard_map/ppermute | solution.py:56
  259.3 13.7 %collective-permute-start.49 = (bf16[256,1024]{1,0:T(8,128)(2,1)}, bf16[256,1024]{1,0:T(8,128)(2,1)S(1)}, u32[]{:S(2)}, u32[]{:S(2)}) collective-permute-start(bf16[256,1024]{1,0:T(8,128)(2,1)} %pad_maximum_fusion.7), channel_id=1, source_target_pairs={{0,2},{1,3},{2,0},{3,1},{4,6},{5,7},{6,4},{7,5},{8,10},{9,11},{10,... | collective-permute-start | bytes 1572872 | tf_op jit(solution)/shard_map/ppermute | solution.py:56
  267.0 10.7 %all-to-all-start.7 = ((f32[32,1,128]{2,1,0:T(1,128)}), f32[32,1,128]{2,1,0:T(1,128)S(1)}, u32[]{:S(2)}, u32[]{:S(2)}) async-start(f32[32,1,128]{2,1,0:T(1,128)} %get-tuple-element.244), calls=%async_computation.7 | async-start | bytes 32768 | tf_op jit(solution)/shard_map/all_to_all | solution.py:82
  (50 other events, 502.1 us)
